TPU v7x, 32 devices: a whole 2x2x4 slice. The times are simulated.
32 devices in a mesh: pipe: 2 (over y), expert: 4 (over x, core), dp: 4 (over z).
Axes of the slice: x: 2, y: 2, z: 4, core: 2. Of those that a mesh axis runs over, the one named last changes fastest.
Arguments:
- x_forward: bfloat16 [2, 1024, 7168], P('pipe', ('expert', 'dp')), may hold values from -6 to 6
- route_forward: int32 [2, 1024, 1], P('pipe', ('expert', 'dp')), may hold values from 0 to 1; in each aligned block of 64 rows (0 to 63, 64 to 127, ..., all dimensions but the last counted through in order) at most 40 rows name the same one
- prob_forward: float32 [2, 1024], P('pipe', ('expert', 'dp')), may hold values from 0.3 to 1
- x_backward: bfloat16 [2, 1024, 7168], P('pipe', ('expert', 'dp')), may hold values from -6 to 6
- route_backward: int32 [2, 1024, 1], P('pipe', ('expert', 'dp')), may hold values from 0 to 1; in each aligned block of 64 rows (0 to 63, 64 to 127, ..., all dimensions but the last counted through in order) at most 40 rows name the same one
- prob_backward: float32 [2, 1024], P('pipe', ('expert', 'dp')), may hold values from 0.3 to 1
- grad_output: bfloat16 [2, 1024, 7168], P('pipe', ('expert', 'dp')), may hold values from -6 to 6
- w_gate: bfloat16 [2, 4, 7168, 512], P('pipe', 'expert', None, 'dp'), may hold values from -0.0625 to 0.0625
- w_up: bfloat16 [2, 4, 7168, 512], P('pipe', 'expert', None, 'dp'), may hold values from -0.0625 to 0.0625
- w_down: bfloat16 [2, 4, 512, 7168], P('pipe', 'expert', 'dp'), may hold values from -0.1875 to 0.1875
Outputs:
- next_input: bfloat16 [2, 1024, 7168], P('pipe', ('expert', 'dp'))
- next_grad: bfloat16 [2, 1024, 7168], P('pipe', ('expert', 'dp'))
Inputs may be any that keep to these rules, and one draw needn't show every extreme that they name: `route_forward`: in every aligned block of 64 rows (the rows of one device) no expert is named by more than 40 tokens, a bound that some block reaches. `route_backward`: as for route_forward.
All inputs are finite; a program needn't handle non-finite values.
Results may differ from a plain program's by a relative error of at most 0.0044.
Values may be sent and summed in bfloat16 or wider, within the bound.
No kernel may reach another device: no remote copies, remote signals or barrier semaphores. Data moves between devices by JAX's collectives and lax.ppermute only.
A program may use at most 128 MiB of HBM per device.

v0:
```python
import jax
import jax.numpy as jnp
from jax import lax
from jax.sharding import PartitionSpec as P


def from_partner(block, axis, stride):
    count = lax.axis_size(axis)
    route = []
    for low in range(count):
        high = low | 1 << stride
        if high != low and high < count:
            route += [(low, high), (high, low)]
    return lax.ppermute(block, axis, route)


def shifted(block, axis, distance):
    devices = range(lax.axis_size(axis))
    route = [((i - distance) % len(devices), i) for i in devices]
    return lax.ppermute(block, axis, route)


def silu_parts(pre_gate):
    sigma_gate = jax.nn.sigmoid(pre_gate)
    return (pre_gate * sigma_gate, sigma_gate)


def contract_last(left_side, weights):
    return lax.dot_general(
        left_side, weights, (((1,), (1,)), ((), ())), preferred_element_type=jnp.float32
    )


def expert_pass(forward_rows, backward_rows, scaled_rows, gate_weight, up_weight, down_weight):
    gate_fwd = jnp.dot(forward_rows, gate_weight, preferred_element_type=jnp.float32)
    up_fwd = jnp.dot(forward_rows, up_weight, preferred_element_type=jnp.float32)
    silu_fwd, sigma_fwd = silu_parts(gate_fwd)
    hidden_fwd = (silu_fwd * up_fwd).astype(jnp.bfloat16)
    expert_out = jnp.dot(hidden_fwd, down_weight, preferred_element_type=jnp.float32)
    gate_bwd = jnp.dot(backward_rows, gate_weight, preferred_element_type=jnp.float32)
    up_bwd = jnp.dot(backward_rows, up_weight, preferred_element_type=jnp.float32)
    silu_bwd, sigma_bwd = silu_parts(gate_bwd)
    grad_hidden = contract_last(scaled_rows, down_weight)
    grad_gate = (grad_hidden * up_bwd * (sigma_bwd + silu_bwd * (1.0 - sigma_bwd))).astype(
        jnp.bfloat16
    )
    grad_up = (grad_hidden * silu_bwd).astype(jnp.bfloat16)
    grad_rows = contract_last(grad_gate, gate_weight) + contract_last(grad_up, up_weight)
    return (expert_out, grad_rows)


def placing(routes, experts_here, capacity):
    route_hits = (routes[:, None] == jnp.arange(experts_here, dtype=jnp.int32)[None, :]).astype(
        jnp.int32
    )
    before = jnp.cumsum(route_hits, axis=0) - route_hits
    slot_index = jnp.sum(before * route_hits, axis=1)
    position = routes * capacity + slot_index
    selector = (
        position[None, :] == jnp.arange(experts_here * capacity, dtype=jnp.int32)[:, None]
    ).astype(jnp.bfloat16)
    return (position, selector)


def packing(selector, values):
    return jnp.dot(selector, values, preferred_element_type=jnp.float32).astype(jnp.bfloat16)


def on_device(
    x_forward,
    route_forward,
    prob_forward,
    x_backward,
    route_backward,
    prob_backward,
    grad_output,
    w_gate,
    w_up,
    w_down,
):
    tokens_here = x_forward.shape[1]
    feature_width = x_forward.shape[2]
    groups = lax.axis_size("expert")
    experts_here = groups // 2
    capacity = min(tokens_here, (tokens_here * 5 + 4 * experts_here - 1) // (4 * experts_here))
    pair_side = lax.axis_index("expert") % 2
    gate_full, up_full, down_full = (
        lax.all_gather(w_gate[0, 0], "dp", axis=1, tiled=True),
        lax.all_gather(w_up[0, 0], "dp", axis=1, tiled=True),
        lax.all_gather(w_down[0, 0], "dp", axis=0, tiled=True),
    )
    pos_fwd, select_fwd = placing(route_forward[0, :, 0], experts_here, capacity)
    pos_bwd, select_bwd = placing(route_backward[0, :, 0], experts_here, capacity)
    scaled_grad = (prob_backward[0][:, None] * grad_output[0].astype(jnp.float32)).astype(
        jnp.bfloat16
    )
    stacked = jnp.stack(
        [
            packing(select_fwd, x_forward[0]),
            packing(select_bwd, x_backward[0]),
            packing(select_bwd, scaled_grad),
        ]
    )
    stacked = stacked.reshape(3, experts_here, capacity, feature_width)
    split_rows = stacked.reshape(3, experts_here, capacity, 2, feature_width // 2).transpose(
        0, 1, 3, 2, 4
    )
    split_rows = split_rows.reshape(3, groups, capacity, feature_width // 2)
    own_half = lax.all_to_all(split_rows, "expert", split_axis=1, concat_axis=1, tiled=True)
    partner_half = from_partner(own_half, "expert", 0)
    arrived = jnp.where(
        pair_side == 0,
        jnp.concatenate([own_half, partner_half], axis=3),
        jnp.concatenate([partner_half, own_half], axis=3),
    )
    expert_rows = arrived.reshape(3, groups * capacity, feature_width)
    expert_out, grad_rows = expert_pass(
        expert_rows[0], expert_rows[1], expert_rows[2], gate_full, up_full, down_full
    )
    results = jnp.stack([expert_out, grad_rows]).reshape(2, groups, capacity, feature_width)
    quarters = results.reshape(2, groups, capacity, 2, feature_width // 2)
    keep_part = jnp.where(pair_side == 0, quarters[:, :, :, 0], quarters[:, :, :, 1])
    give_part = jnp.where(pair_side == 0, quarters[:, :, :, 1], quarters[:, :, :, 0])
    finished = keep_part + from_partner(give_part.astype(jnp.bfloat16), "expert", 0).astype(
        give_part.dtype
    )
    returned = lax.all_to_all(finished, "expert", split_axis=1, concat_axis=1, tiled=True)
    combined = returned.reshape(2, experts_here, 2, capacity, feature_width // 2).transpose(
        0, 1, 3, 2, 4
    )
    combined = combined.reshape(2, experts_here, capacity, feature_width)
    flat_out = combined.reshape(2, experts_here * capacity, feature_width)
    moved_fwd = jnp.take(flat_out[0], pos_fwd, axis=0)
    moved_bwd = jnp.take(flat_out[1], pos_bwd, axis=0)
    layer_out = (x_forward[0].astype(jnp.float32) + prob_forward[0][:, None] * moved_fwd).astype(
        jnp.bfloat16
    )
    grad_in = (grad_output[0].astype(jnp.float32) + moved_bwd).astype(jnp.bfloat16)
    sent_fwd = shifted(layer_out, "pipe", 1)
    sent_bwd = shifted(grad_in, "pipe", -1)
    return (sent_fwd[None], sent_bwd[None])


def solution(mesh):
    return jax.shard_map(
        on_device,
        mesh=mesh,
        in_specs=(
            P("pipe", ("expert", "dp"), None),
            P("pipe", ("expert", "dp"), None),
            P("pipe", ("expert", "dp")),
            P("pipe", ("expert", "dp"), None),
            P("pipe", ("expert", "dp"), None),
            P("pipe", ("expert", "dp")),
            P("pipe", ("expert", "dp"), None),
            P("pipe", "expert", None, "dp"),
            P("pipe", "expert", None, "dp"),
            P("pipe", "expert", "dp", None),
        ),
        out_specs=(P("pipe", ("expert", "dp"), None), P("pipe", ("expert", "dp"), None)),
        check_vma=False,
    )
```

profile of v0, /device:TPU:20, one launch (start us, length us, event | category | flops | bytes accessed | tf_op | source)
XLA Modules:
  0.0 589.8 jit_solution(4789582138999819190)
XLA Ops:
  7.2 0.7 all-gather.11.cloned.1.call-update
  8.0 0.7 all-gather.7.cloned.1.call-update
  8.7 0.7 all-gather.9.cloned.1.call-update
  9.8 0.4 convolution_convert_fusion.1
  10.3 0.9 stack.22
  11.3 1.8 convolution_convert_fusion
  13.1 1.7 stack.23
  14.8 1.4 copy.25
  16.5 1.5 convolution_convert_fusion.2
  18.0 2.8 stack.21
  20.8 1.4 copy.23
  22.2 0.4 pad_maximum_fusion
  22.9 43.5 %all_to_all.10 = bf16[3,4,40,3584]{3,2,0,1:T(8,128)(2,1)} all-to-all(bf16[3,4,40,3584]{3,2,0,1:T(8,128)(2,1)S(1)} %copy.26), channel_id=1, replica_groups=mesh['pipe'=2,'expert'=4,'dp'=4] {'expert'}, dimensions={1} | all-to-all | bytes 6881280 | tf_op jit(solution)/shard_map/all_to_all | solution.py:109
  66.4 6.4 %collective-permute-done = bf16[3,4,40,3584]{3,2,0,1:T(8,128)(2,1)} collective-permute-done((bf16[3,4,40,3584]{3,2,0,1:T(8,128)(2,1)}, bf16[3,4,40,3584]{3,2,0,1:T(8,128)(2,1)}, u32[]{:S(2)}, u32[]{:S(2)}) %collective-permute-start) | collective-permute-done | bytes 3440672 | tf_op jit(solution)/shard_map/ppermute | solution.py:14
  72.8 7.3 %maximum_select_fusion = bf16[3,4,40,7168]{3,2,0,1:T(8,128)(2,1)S(1)} fusion(bf16[3,4,40,3584]{3,2,0,1:T(8,128)(2,1)} %collective-permute-done, bf16[3,4,40,3584]{3,2,0,1:T(8,128)(2,1)} %all_to_all.10, pred[]{:T(512)S(6)} %eq.28), kind=kLoop, calls=%fused_computation.21 | loop fusion | flops 30965760 | bytes 13762561 | tf_op jit(solution)/shard_map/jit(_where)/select_n | solution.py:111
  80.0 2.5 fusion.48
  82.6 58.8 %all-gather.11.cloned.1.call-done = bf16[1,1,512,7168]{3,2,1,0:T(8,128)(2,1)} async-done(((bf16[1,1,128,7168]{3,2,1,0:T(8,128)(2,1)}), bf16[1,1,512,7168]{3,2,1,0:T(8,128)(2,1)}) %all-gather.11.cloned.1.call-update) | async-done | bytes 7340048 | tf_op jit(solution)/shard_map/all_gather | solution.py:90
  141.4 6.4 %fusion = f32[160,512]{1,0:T(8,128)S(1)} fusion(bf16[160,7168]{1,0:T(8,128)(2,1)} %bitcast.97, bf16[1,1,512,7168]{3,2,1,0:T(8,128)(2,1)} %all-gather.11.cloned.1.call-done), kind=kOutput, calls=%fused_computation.6 | convolution fusion | flops 1174405120 | bytes 9961472 | tf_op jit(solution)/shard_map/dot_general | solution.py:29
  147.8 125.4 %all-gather.7.cloned.1.call-done = bf16[1,1,7168,512]{3,2,1,0:T(8,128)(2,1)} async-done(((bf16[1,1,7168,128]{3,2,1,0:T(8,128)(2,1)}), bf16[1,1,7168,512]{3,2,1,0:T(8,128)(2,1)}) %all-gather.7.cloned.1.call-update) | async-done | bytes 7340048 | tf_op jit(solution)/shard_map/all_gather | solution.py:88
  273.2 4.4 fusion.11
  277.6 127.3 %all-gather.9.cloned.1.call-done = bf16[1,1,7168,512]{3,2,1,0:T(8,128)(2,1)} async-done(((bf16[1,1,7168,128]{3,2,1,0:T(8,128)(2,1)}), bf16[1,1,7168,512]{3,2,1,0:T(8,128)(2,1)}) %all-gather.9.cloned.1.call-update) | async-done | bytes 7340048 | tf_op jit(solution)/shard_map/all_gather | solution.py:89
  404.9 11.2 %fusion.9 = f32[160,7168]{1,0:T(8,128)} fusion(bf16[1,1,7168,512]{3,2,1,0:T(8,128)(2,1)} %all-gather.7.cloned.1.call-done, f32[160,512]{1,0:T(8,128)S(1)} %fusion, bf16[160,7168]{1,0:T(8,128)(2,1)S(1)} %bitcast.90, bf16[1,1,7168,512]{3,2,1,0:T(8,128)(2,1)} %all-gather.9.cloned.1.call-done, f32[160,512]{1,0:T(8,128)S(1)} %fusion.11), kind=kOutput, calls=%fused_computation.15 | convolution fusion | flops 2349629440 | bytes 22216704 | tf_op jit(solution)/shard_map/dot_general | solution.py:29
  416.1 9.1 %convolution_add_fusion = f32[160,7168]{1,0:T(8,128)} fusion(f32[160,7168]{1,0:T(8,128)} %fusion.9, bf16[1,1,7168,512]{3,2,1,0:T(8,128)(2,1)} %all-gather.9.cloned.1.call-done, f32[160,512]{1,0:T(8,128)S(1)} %fusion, f32[160,512]{1,0:T(8,128)S(1)} %fusion.11), kind=kOutput, calls=%fused_computation.2 | convolution fusion | flops 1176043520 | bytes 17170432 | tf_op jit(solution)/shard_map/dot_general | solution.py:29
  425.2 7.2 %stack.26 = f32[1,4,40,2,3584]{4,3,2,1,0:T(2,128)} reshape(f32[160,7168]{1,0:T(8,128)} %convolution_add_fusion) | data formatting | bytes 9175040 | tf_op jit(solution)/shard_map/stack | solution.py:120
  432.4 4.4 fusion.7
  436.8 10.0 %fusion.2 = f32[160,7168]{1,0:T(8,128)} fusion(bf16[1,1,512,7168]{3,2,1,0:T(8,128)(2,1)} %all-gather.11.cloned.1.call-done, f32[160,512]{1,0:T(8,128)S(1)} %fusion.7, bf16[160,7168]{1,0:T(8,128)(2,1)S(1)} %bitcast.92, bf16[1,1,7168,512]{3,2,1,0:T(8,128)(2,1)} %all-gather.7.cloned.1.call-done), kind=kOutput, calls=%fused_computation.8 | convolution fusion | flops 2349301760 | bytes 21889024 | tf_op jit(solution)/shard_map/dot_general | solution.py:39
  446.8 7.0 %stack.25 = f32[1,4,40,2,3584]{4,3,2,1,0:T(2,128)} reshape(f32[160,7168]{1,0:T(8,128)} %fusion.2) | data formatting | bytes 9175040 | tf_op jit(solution)/shard_map/stack | solution.py:120
  453.8 3.3 copy_dynamic-update-slice_fusion.1
  457.4 0.8 copy_dynamic-update-slice_fusion
  458.7 4.4 collective-permute-done.1
  463.1 1.0 bitcast_add_fusion
  464.1 2.5 copy.29
  466.6 5.2 all-to-all-start.1
  471.9 52.1 %all-to-all-done.1 = f32[2,4,40,3584]{3,2,0,1:T(8,128)} async-done(((f32[2,4,40,3584]{3,2,0,1:T(8,128)}), f32[2,4,40,3584]{3,2,0,1:T(8,128)}, u32[]{:S(2)}, u32[]{:S(2)}) %all-to-all-start.1) | async-done | bytes 4587552 | tf_op jit(solution)/shard_map/all_to_all | solution.py:127
  524.0 5.8 copy.36
  529.9 3.0 fusion.49
  532.9 0.4 copy.32
  533.3 2.3 gather_fusion.1
  535.6 2.8 fusion.17
  538.5 0.6 collective-permute-start.3
  539.1 0.4 copy.31
  539.5 2.4 gather_fusion
  541.9 2.2 fusion.19
  544.0 1.5 collective-permute-start.2
  545.5 16.5 %collective-permute-done.3 = bf16[64,7168]{1,0:T(8,128)(2,1)} collective-permute-done((bf16[64,7168]{1,0:T(8,128)(2,1)}, bf16[64,7168]{1,0:T(8,128)(2,1)}, u32[]{:S(2)}, u32[]{:S(2)}) %collective-permute-start.3) | collective-permute-done | bytes 917536 | tf_op jit(solution)/shard_map/ppermute | solution.py:20
  562.0 18.2 %collective-permute-done.2 = bf16[64,7168]{1,0:T(8,128)(2,1)S(1)} collective-permute-done((bf16[64,7168]{1,0:T(8,128)(2,1)S(1)}, bf16[64,7168]{1,0:T(8,128)(2,1)S(1)}, u32[]{:S(2)}, u32[]{:S(2)}) %collective-permute-start.2) | collective-permute-done | bytes 917536 | tf_op jit(solution)/shard_map/ppermute | solution.py:20
  580.2 0.9 copy.40
  581.1 2.2 copy.41
  (44 shorter events, 2.0 us)
Async XLA Ops:
  7.2 2.6 copy-start
  7.2 2.2 copy-start.6
  7.2 134.2 %all-gather.11.cloned.1.call-start = ((), (), s32[]{:S(2)}) async-start(), calls=%async_computation.4 | async-start | bytes 9175040 | tf_op jit(solution)/shard_map/all_gather | solution.py:90
  7.9 265.2 %all-gather.7.cloned.1.call-start = ((), (), s32[]{:S(2)}) async-start(), calls=%async_computation.2 | async-start | bytes 9175040 | tf_op jit(solution)/shard_map/all_gather | solution.py:88
  8.7 396.3 %all-gather.9.cloned.1.call-start = ((), (), s32[]{:S(2)}) async-start(), calls=%async_computation.3 | async-start | bytes 9175040 | tf_op jit(solution)/shard_map/all_gather | solution.py:89
  9.4 1.9 copy-start.8
  11.3 4.9 copy-start.7
  11.3 5.3 copy-start.5
  66.3 6.4 %collective-permute-start = (bf16[3,4,40,3584]{3,2,0,1:T(8,128)(2,1)}, bf16[3,4,40,3584]{3,2,0,1:T(8,128)(2,1)}, u32[]{:S(2)}, u32[]{:S(2)}) collective-permute-start(bf16[3,4,40,3584]{3,2,0,1:T(8,128)(2,1)} %all_to_all.10), channel_id=1, source_target_pairs={{0,4},{4,0},{8,12},{12,8},{1,5},{5,1},{9,13},{13,9},{2,6},{6,2},{1... | collective-permute-start | bytes 10321928 | tf_op jit(solution)/shard_map/ppermute | solution.py:14
  425.2 7.2 %copy-start.2 = (bf16[1,4,40,7168]{3,2,0,1:T(8,128)(2,1)S(1)}, bf16[1,4,40,7168]{3,2,0,1:T(8,128)(2,1)}, u32[]{:S(2)}) copy-start(bf16[1,4,40,7168]{3,2,0,1:T(8,128)(2,1)} %get-tuple-element.9) | copy-start | bytes 6881284
  446.8 10.4 %slice-start = ((s8[4587520]{0:T(1024)(128)(4,1)}), s8[393216]{0:T(1024)(128)(4,1)S(1)}, s32[]{:S(2)}) async-start(s8[4587520]{0:T(1024)(128)(4,1)} %bitcast.93), calls=%async_computation.5 | async-start | bytes 786432
  453.8 3.6 slice-start.1
  458.6 4.5 collective-permute-start.1
  466.6 57.4 %all-to-all-start.1 = ((f32[2,4,40,3584]{3,2,0,1:T(8,128)}), f32[2,4,40,3584]{3,2,0,1:T(8,128)}, u32[]{:S(2)}, u32[]{:S(2)}) async-start(f32[2,4,40,3584]{3,2,0,1:T(8,128)} %copy.29), calls=%async_computation.1 | async-start | bytes 9175040 | tf_op jit(solution)/shard_map/all_to_all | solution.py:127
  533.3 2.4 copy-start.4
  535.6 3.5 copy-start.3
  538.5 23.6 %collective-permute-start.3 = (bf16[64,7168]{1,0:T(8,128)(2,1)}, bf16[64,7168]{1,0:T(8,128)(2,1)}, u32[]{:S(2)}, u32[]{:S(2)}) collective-permute-start(bf16[64,7168]{1,0:T(8,128)(2,1)} %fusion.17), channel_id=1, source_target_pairs={{16,0},{0,16},{17,1},{1,17},{18,2},{2,18},{19,3},{3,19},{20,4},{4,... | collective-permute-start | bytes 2752520 | tf_op jit(solution)/shard_map/ppermute | solution.py:20
  539.5 2.4 copy-start.9
  541.8 41.5 %copy-start.1 = (bf16[1,64,7168]{2,1,0:T(8,128)(2,1)S(1)}, bf16[1,64,7168]{2,1,0:T(8,128)(2,1)}, u32[]{:S(2)}) copy-start(bf16[1,64,7168]{2,1,0:T(8,128)(2,1)} %param.15) | copy-start | bytes 2752516
  544.0 36.2 %collective-permute-start.2 = (bf16[64,7168]{1,0:T(8,128)(2,1)S(1)}, bf16[64,7168]{1,0:T(8,128)(2,1)S(1)}, u32[]{:S(2)}, u32[]{:S(2)}) collective-permute-start(bf16[64,7168]{1,0:T(8,128)(2,1)S(1)} %fusion.19), channel_id=1, source_target_pairs={{16,0},{0,16},{17,1},{1,17},{18,2},{2,18},{19,3},{3,19},{20,4},{4,... | collective-permute-start | bytes 2752520 | tf_op jit(solution)/shard_map/ppermute | solution.py:20
Sparse Core Ops, SparseCore 0:
  9.6 131.7 all-gather.10
  142.9 130.1 all-gather.6
  274.7 130.1 all-gather.8
where the time goes:
time: 594 us; the launch traced here: 590 us
  waiting for transfers between devices  411 us (69%)
  local copies, waits for them, and re-layouts  49.5 us (8%)
  matrix products  49.1 us (8%)
  blocking collectives  43.5 us (7%)
  other arithmetic  14.9 us (3%)
  between operations  14 us (2%)
  starting transfers between devices  7.51 us (1%)
    all_gather x1, waiting for transfers between devices, on_device(): lax.all_gather(w_up[0, 0], 'dp', axis=1, tiled=True)  127 us
    all_gather x1, waiting for transfers between devices, on_device(): lax.all_gather(w_gate[0, 0], 'dp', axis=1, tiled=True)  125 us
    all_gather x1, waiting for transfers between devices, on_device(): lax.all_gather(w_down[0, 0], 'dp', axis=0, tiled=True)  58.8 us
    all_to_all x1, waiting for transfers between devices, on_device(): lax.all_to_all(finished, 'expert', split_axis=1, concat_axis=1, tiled=True)  52.1 us
    all_to_all x1, blocking collectives, on_device(): lax.all_to_all(split_rows, 'expert', split_axis=1, concat_axis=1, tiled=T...  43.5 us
    ppermute x2, waiting for transfers between devices, shifted(): return lax.ppermute(block, axis, route)  34.7 us
    dot_general x3, matrix products, contract_last(): lax.dot_general(left_side, weights, (((1,), (1,)), ((), ())), preferred_e...  26.6 us
    another operation x3, local copies, waits for them, and re-layouts, on_device(): jnp.stack([expert_out, grad_rows])  15 us
  transfers between devices with their start and end apart: 8, of which 8 were waited for; matrix products, arithmetic and copies ran while one was open for 7% of the time, Pallas kernels for 0%

commit v1 on v0

--- a/solution.py
+++ b/solution.py
@@ -1,7 +1,276 @@
+import functools
+
 import jax
 import jax.numpy as jnp
 from jax import lax
+from jax.experimental import pallas as pl
+from jax.experimental.pallas import tpu as pltpu
 from jax.sharding import PartitionSpec as P
+
+BF16, F32 = jnp.bfloat16, jnp.float32
+VMEM_LIMIT = 56 * 1024 * 1024
+
+
+def contract_last(left_side, weights):
+    return lax.dot_general(
+        left_side, weights, (((1,), (1,)), ((), ())), preferred_element_type=F32
+    )
+
+
+def flipped(block, axis, stride):
+    route = [(i, i ^ stride) for i in range(lax.axis_size(axis))]
+    return lax.ppermute(block, axis, route)
+
+
+def shifted(block, axis, distance):
+    count = lax.axis_size(axis)
+    return lax.ppermute(block, axis, [((i - distance) % count, i) for i in range(count)])
+
+
+def chunk_of(width, most):
+    best = 128
+    for size in range(128, most + 1, 128):
+        if width % size == 0:
+            best = size
+    return best
+
+
+def own_columns(mask, hidden):
+    column = lax.broadcasted_iota(jnp.int32, (mask.shape[0], hidden), 1)
+    return (mask > 0) == (column < hidden // 2)
+
+
+def joined(refs, axis):
+    return jnp.concatenate([ref[...] for ref in refs], axis=axis)
+
+
+def gates_kernel(pieces, x_ref, *refs):
+    gates, ups = refs[:pieces], refs[pieces : 2 * pieces]
+    c_ref, e_ref = refs[2 * pieces :]
+
+    @pl.when(pl.program_id(0) == 0)
+    def _():
+        c_ref[...] = jnp.zeros_like(c_ref)
+        e_ref[...] = jnp.zeros_like(e_ref)
+
+    x = x_ref[...]
+    c_ref[...] += jnp.dot(x, joined(gates, 1), preferred_element_type=F32)
+    e_ref[...] += jnp.dot(x, joined(ups, 1), preferred_element_type=F32)
+
+
+def gates_call(x, gates, ups):
+    rows, width = x.shape
+    pieces, hid = len(gates), gates[0].shape[1]
+    chunk = chunk_of(width, 1024)
+    hidden = pieces * hid
+    weight_spec = pl.BlockSpec((chunk, hid), lambda i: (i, 0))
+    return pl.pallas_call(
+        functools.partial(gates_kernel, pieces),
+        grid=(width // chunk,),
+        in_specs=[pl.BlockSpec((rows, chunk), lambda i: (0, i))] + [weight_spec] * (2 * pieces),
+        out_specs=[pl.BlockSpec((rows, hidden), lambda i: (0, 0))] * 2,
+        out_shape=[jax.ShapeDtypeStruct((rows, hidden), F32)] * 2,
+        compiler_params=pltpu.CompilerParams(vmem_limit_bytes=VMEM_LIMIT),
+        cost_estimate=pl.CostEstimate(
+            flops=4 * rows * width * hidden,
+            bytes_accessed=2 * rows * width + 4 * width * hidden + 8 * rows * hidden,
+            transcendentals=0,
+        ),
+    )(x, *gates, *ups)
+
+
+def backward_kernel(pieces, steps, mask_ref, s_ref, c_ref, e_ref, *refs):
+    downs, gates, ups = refs[:pieces], refs[pieces : 2 * pieces], refs[2 * pieces : 3 * pieces]
+    out_ref, dh_ref, ga_ref, gb_ref = refs[3 * pieces :]
+    step = pl.program_id(0)
+
+    @pl.when(step == 0)
+    def _():
+        dh_ref[...] = jnp.zeros_like(dh_ref)
+
+    @pl.when(step < steps)
+    def _():
+        dh_ref[...] += contract_last(s_ref[...], joined(downs, 0))
+
+    @pl.when(step == steps - 1)
+    def _():
+        c, e, dh = c_ref[...], e_ref[...], dh_ref[...]
+        s = jax.nn.sigmoid(c)
+        silu = c * s
+        keep = own_columns(mask_ref[...], c.shape[1])
+        ga_ref[...] = jnp.where(keep, dh * e * (s + silu * (1.0 - s)), 0.0).astype(BF16)
+        gb_ref[...] = jnp.where(keep, dh * silu, 0.0).astype(BF16)
+
+    @pl.when(step >= steps)
+    def _():
+        total = contract_last(ga_ref[...], joined(gates, 1))
+        total += contract_last(gb_ref[...], joined(ups, 1))
+        out_ref[...] = total.astype(BF16)
+
+
+def backward_call(mask, scaled, c, e, downs, gates, ups):
+    rows, width = scaled.shape
+    pieces, hid = len(gates), gates[0].shape[1]
+    chunk = chunk_of(width, 1024)
+    steps = width // chunk
+    hidden = pieces * hid
+    first = lambda i: jnp.minimum(i, steps - 1)
+    second = lambda i: jnp.maximum(i - steps, 0)
+    whole = lambda i: (0, 0)
+    return pl.pallas_call(
+        functools.partial(backward_kernel, pieces, steps),
+        grid=(2 * steps,),
+        in_specs=[
+            pl.BlockSpec((rows, 1), whole),
+            pl.BlockSpec((rows, chunk), lambda i: (0, first(i))),
+            pl.BlockSpec((rows, hidden), whole),
+            pl.BlockSpec((rows, hidden), whole),
+        ]
+        + [pl.BlockSpec((hid, chunk), lambda i: (0, first(i)))] * pieces
+        + [pl.BlockSpec((chunk, hid), lambda i: (second(i), 0))] * (2 * pieces),
+        out_specs=pl.BlockSpec((rows, chunk), lambda i: (0, second(i))),
+        out_shape=jax.ShapeDtypeStruct((rows, width), BF16),
+        scratch_shapes=[
+            pltpu.VMEM((rows, hidden), F32),
+            pltpu.VMEM((rows, hidden), BF16),
+            pltpu.VMEM((rows, hidden), BF16),
+        ],
+        compiler_params=pltpu.CompilerParams(vmem_limit_bytes=VMEM_LIMIT),
+        cost_estimate=pl.CostEstimate(
+            flops=6 * rows * width * hidden,
+            bytes_accessed=4 * rows * width + 6 * width * hidden + 8 * rows * hidden,
+            transcendentals=rows * hidden,
+        ),
+    )(mask, scaled, c, e, *downs, *gates, *ups)
+
+
+def forward_kernel(pieces, steps, mask_ref, x_ref, *refs):
+    gates, ups, downs = refs[:pieces], refs[pieces : 2 * pieces], refs[2 * pieces : 3 * pieces]
+    out_ref, a_ref, b_ref, hidden_ref = refs[3 * pieces :]
+    step = pl.program_id(0)
+
+    @pl.when(step == 0)
+    def _():
+        a_ref[...] = jnp.zeros_like(a_ref)
+        b_ref[...] = jnp.zeros_like(b_ref)
+
+    @pl.when(step < steps)
+    def _():
+        x = x_ref[...]
+        a_ref[...] += jnp.dot(x, joined(gates, 1), preferred_element_type=F32)
+        b_ref[...] += jnp.dot(x, joined(ups, 1), preferred_element_type=F32)
+
+    @pl.when(step == steps - 1)
+    def _():
+        a, b = a_ref[...], b_ref[...]
+        keep = own_columns(mask_ref[...], a.shape[1])
+        hidden_ref[...] = jnp.where(keep, a * jax.nn.sigmoid(a) * b, 0.0).astype(BF16)
+
+    @pl.when(step >= steps)
+    def _():
+        out_ref[...] = jnp.dot(
+            hidden_ref[...], joined(downs, 0), preferred_element_type=F32
+        ).astype(BF16)
+
+
+def forward_call(mask, x, gates, ups, downs):
+    rows, width = x.shape
+    pieces, hid = len(gates), gates[0].shape[1]
+    chunk = chunk_of(width, 1024)
+    steps = width // chunk
+    hidden = pieces * hid
+    first = lambda i: jnp.minimum(i, steps - 1)
+    second = lambda i: jnp.maximum(i - steps, 0)
+    return pl.pallas_call(
+        functools.partial(forward_kernel, pieces, steps),
+        grid=(2 * steps,),
+        in_specs=[
+            pl.BlockSpec((rows, 1), lambda i: (0, 0)),
+            pl.BlockSpec((rows, chunk), lambda i: (0, first(i))),
+        ]
+        + [pl.BlockSpec((chunk, hid), lambda i: (first(i), 0))] * (2 * pieces)
+        + [pl.BlockSpec((hid, chunk), lambda i: (0, second(i)))] * pieces,
+        out_specs=pl.BlockSpec((rows, chunk), lambda i: (0, second(i))),
+        out_shape=jax.ShapeDtypeStruct((rows, width), BF16),
+        scratch_shapes=[
+            pltpu.VMEM((rows, hidden), F32),
+            pltpu.VMEM((rows, hidden), F32),
+            pltpu.VMEM((rows, hidden), BF16),
+        ],
+        compiler_params=pltpu.CompilerParams(vmem_limit_bytes=VMEM_LIMIT),
+        cost_estimate=pl.CostEstimate(
+            flops=6 * rows * width * hidden,
+            bytes_accessed=4 * rows * width + 6 * width * hidden,
+            transcendentals=rows * hidden,
+        ),
+    )(mask, x, *gates, *ups, *downs)
+
+
+def summed_home(partial, axis):
+    count, here = lax.axis_size(axis), lax.axis_index(axis)
+    rows = partial.shape[0] // count
+
+    def block(index):
+        start = jnp.clip(index, 0, count - 1) * rows
+        return lax.dynamic_slice_in_dim(partial, start, rows, 0).astype(F32)
+
+    up, down = None, None
+    for step in range(1, count):
+        to_up, to_down = block(here + count - step), block(here - count + step)
+        if up is not None:
+            to_up, to_down = to_up + up.astype(F32), to_down + down.astype(F32)
+        up = lax.ppermute(to_up.astype(BF16), axis, [(i, i + 1) for i in range(step)])
+        down = lax.ppermute(
+            to_down.astype(BF16), axis, [(i, i - 1) for i in range(count - step, count)]
+        )
+    return block(here) + up.astype(F32) + down.astype(F32)
+
+
+def few_experts(
+    x_forward,
+    route_forward,
+    prob_forward,
+    x_backward,
+    route_backward,
+    prob_backward,
+    grad_output,
+    w_gate,
+    w_up,
+    w_down,
+):
+    tokens_here = x_forward.shape[1]
+    expert_here = lax.axis_index("expert") // 2
+
+    def with_neighbours(weight):
+        across = flipped(weight, "expert", 2)
+        return [weight, flipped(weight, "expert", 1), across, flipped(across, "expert", 1)]
+
+    def gathered(rows):
+        return lax.all_gather(rows, "dp", axis=0, tiled=True)
+
+    routes = jnp.concatenate([route_forward[0], route_backward[0]], axis=1)
+    mine = (gathered(routes) == expert_here).astype(F32)
+    mask_fwd, mask_bwd = mine[:, 0:1], mine[:, 1:2]
+    scaled_grad = (prob_backward[0][:, None] * grad_output[0].astype(F32)).astype(BF16)
+    gates, ups, downs = (with_neighbours(w[0, 0]) for w in (w_gate, w_up, w_down))
+
+    c, e = gates_call(gathered(x_backward[0]), gates, ups)
+    partial_bwd = backward_call(mask_bwd, gathered(scaled_grad), c, e, downs, gates, ups)
+    grad_in = (grad_output[0].astype(F32) + summed_home(partial_bwd, "dp")).astype(BF16)
+    sent_bwd = shifted(grad_in, "pipe", -1)
+
+    parts, sent_fwd = 2, []
+    size = tokens_here // parts
+    count = lax.axis_size("dp")
+    for part in range(parts):
+        rows = slice(part * size, (part + 1) * size)
+        x_part = x_forward[0, rows]
+        mask = mask_fwd.reshape(count, tokens_here, 1)[:, rows].reshape(count * size, 1)
+        partial_fwd = forward_call(mask, gathered(x_part), gates, ups, downs)
+        total = summed_home(partial_fwd, "dp")
+        layer_out = (x_part.astype(F32) + prob_forward[0, rows][:, None] * total).astype(BF16)
+        sent_fwd.append(shifted(layer_out, "pipe", 1))
+    return (jnp.concatenate(sent_fwd, axis=0)[None], sent_bwd[None])
 
 
 def from_partner(block, axis, stride):
@@ -14,21 +283,9 @@
     return lax.ppermute(block, axis, route)
 
 
-def shifted(block, axis, distance):
-    devices = range(lax.axis_size(axis))
-    route = [((i - distance) % len(devices), i) for i in devices]
-    return lax.ppermute(block, axis, route)
-
-
 def silu_parts(pre_gate):
     sigma_gate = jax.nn.sigmoid(pre_gate)
     return (pre_gate * sigma_gate, sigma_gate)
-
-
-def contract_last(left_side, weights):
-    return lax.dot_general(
-        left_side, weights, (((1,), (1,)), ((), ())), preferred_element_type=jnp.float32
-    )
 
 
 def expert_pass(forward_rows, backward_rows, scaled_rows, gate_weight, up_weight, down_weight):
@@ -66,7 +323,7 @@
     return jnp.dot(selector, values, preferred_element_type=jnp.float32).astype(jnp.bfloat16)
 
 
-def on_device(
+def many_experts(
     x_forward,
     route_forward,
     prob_forward,
@@ -142,8 +399,9 @@
 
 
 def solution(mesh):
+    few = mesh.shape["expert"] == 4
     return jax.shard_map(
-        on_device,
+        few_experts if few else many_experts,
         mesh=mesh,
         in_specs=(
             P("pipe", ("expert", "dp"), None),

time: 594 us -> 435 us (0.73)
  waiting for transfers between devices: 411 us -> 259 us
  Pallas kernels: 0 us -> 60 us
  starting transfers between devices: 7.51 us -> 60.1 us
  matrix products: 49.1 us -> 0 us
  blocking collectives: 43.5 us -> 9.13 us
  local copies, waits for them, and re-layouts: 49.5 us -> 15.2 us
    all_gather x3 -> x4, waiting for transfers between devices: 312 us -> 28.6 us  [gathered(): return lax.all_gather(rows, 'dp', axis=0, tiled=True)]
    ppermute x4 -> x30, waiting for transfers between devices: 45.5 us -> 229 us  [the longest x9 115 us: flipped(): return lax.ppermute(block, axis, route)]
    pallas_call x0 -> x4, Pallas kernels: none -> 60 us  [the longest x2 31 us: forward_call(): pl.pallas_call(functools.partial(forward_kernel, pieces, steps), grid=(2...]
    ppermute x4 -> x30, starting transfers between devices: 2.19 us -> 59.9 us  [the longest x9 40.2 us: summed_home(): lax.ppermute(to_down.astype(BF16), axis, [(i, i - 1) for i in range(count...]
    all_to_all x1 -> x0, waiting for transfers between devices: 52.1 us -> none  [on_device(): lax.all_to_all(finished, 'expert', split_axis=1, concat_axis=1, tiled=True)]
    dot_general x9 -> x0, matrix products: 49.1 us -> none  [the longest x3 26.6 us: contract_last(): lax.dot_general(left_side, weights, (((1,), (1,)), ((), ())), preferred_e...]
    all_to_all x1 -> x0, blocking collectives: 43.5 us -> none  [on_device(): lax.all_to_all(split_rows, 'expert', split_axis=1, concat_axis=1, tiled=T...]
    another operation x9 -> x0, local copies, waits for them, and re-layouts: 23.2 us -> none  [the longest x3 15 us: on_device(): jnp.stack([expert_out, grad_rows])]
  transfers between devices with their start and end apart: 8 -> 34, of which waited for: 8 -> 13; matrix products, arithmetic and copies ran while one was open for 7% -> 5% of each run, Pallas kernels for 0% -> 14%
where the time goes in v1:
time: 435 us; the launch traced here: 431 us
  waiting for transfers between devices  259 us (60%)
  starting transfers between devices  60.1 us (14%)
  Pallas kernels  60 us (14%)
  local copies, waits for them, and re-layouts  15.2 us (3%)
  between operations  14.3 us (3%)
  other arithmetic  12.7 us (3%)
  blocking collectives  9.13 us (2%)
    ppermute x9, waiting for transfers between devices, flipped(): return lax.ppermute(block, axis, route)  115 us
    ppermute x9, waiting for transfers between devices, summed_home(): lax.ppermute(to_down.astype(BF16), axis, [(i, i - 1) for i in range(count...  50.9 us
    ppermute x9, waiting for transfers between devices, summed_home(): lax.ppermute(to_up.astype(BF16), axis, [(i, i + 1) for i in range(step)])  43.8 us
    ppermute x9, starting transfers between devices, summed_home(): lax.ppermute(to_down.astype(BF16), axis, [(i, i - 1) for i in range(count...  40.2 us
    pallas_call x2, Pallas kernels, forward_call(): pl.pallas_call(functools.partial(forward_kernel, pieces, steps), grid=(2...  31 us
    all_gather x4, waiting for transfers between devices, gathered(): return lax.all_gather(rows, 'dp', axis=0, tiled=True)  28.6 us
    ppermute x3, waiting for transfers between devices, shifted(): lax.ppermute(block, axis, [((i - distance) % count, i) for i in range(cou...  19.5 us
    pallas_call x1, Pallas kernels, backward_call(): pl.pallas_call(functools.partial(backward_kernel, pieces, steps), grid=(2...  18.4 us
  transfers between devices with their start and end apart: 34, of which 13 were waited for; matrix products, arithmetic and copies ran while one was open for 5% of the time, Pallas kernels for 14%

profile of v1, /device:TPU:20, one launch (start us, length us, event | category | flops | bytes accessed | tf_op | source)
XLA Modules:
  0.0 430.7 jit_solution(365343244949685524)
XLA Ops:
  7.2 2.3 fusion.5
  11.2 1.6 collective-permute-start.1
  13.2 1.5 collective-permute-start.7
  15.0 39.3 %collective-permute-done.1.refs_2_.refs_6_ = bf16[7168,128]{1,0:T(8,128)(2,1)} collective-permute-done((bf16[7168,128]{1,0:T(8,128)(2,1)S(1)}, bf16[7168,128]{1,0:T(8,128)(2,1)}, u32[]{:S(2)}, u32[]{:S(2)}) %collective-permute-start.1) | collective-permute-done | bytes 1835040 | tf_op jit(solution)/shard_map/ppermute | solution.py:22
  54.2 39.3 %collective-permute-done.4.refs_6_.refs_10_ = bf16[7168,128]{1,0:T(8,128)(2,1)} collective-permute-done((bf16[7168,128]{1,0:T(8,128)(2,1)}, bf16[7168,128]{1,0:T(8,128)(2,1)}, u32[]{:S(2)}, u32[]{:S(2)}) %collective-permute-start.4) | collective-permute-done | bytes 1835040 | tf_op jit(solution)/shard_map/ppermute | solution.py:22
  93.6 1.3 copy-done.1
  95.4 36.4 %collective-permute-done.7.refs_10_.refs_2_ = bf16[128,7168]{1,0:T(8,128)(2,1)} collective-permute-done((bf16[128,7168]{1,0:T(8,128)(2,1)}, bf16[128,7168]{1,0:T(8,128)(2,1)}, u32[]{:S(2)}, u32[]{:S(2)}) %collective-permute-start.7) | collective-permute-done | bytes 1835040 | tf_op jit(solution)/shard_map/ppermute | solution.py:22
  131.7 1.1 fusion
  133.0 9.1 %all-gather.3 = s32[4,64,2]{1,2,0:T(2,128)S(1)} all-gather(s32[1,64,2]{1,2,0:T(2,128)S(1)} %add_bitcast_fusion), channel_id=1, replica_groups=mesh['pipe'=2,'expert'=4,'dp'=4] {'dp'}, dimensions={0}, use_global_device_ids=true | all-gather | bytes 2560 | tf_op jit(solution)/shard_map/all_gather | solution.py:249
  144.8 1.2 copy-done.2
  146.0 15.3 %shard_map.114 = bf16[128,7168]{1,0:T(8,128)(2,1)} custom-call(f32[128,1]{1,0:T(8,128)} %reshape.34.mask_ref, bf16[128,7168]{1,0:T(8,128)(2,1)} %bitcast.52, bf16[7168,128]{1,0:T(8,128)(2,1)} %bitcast.33, bf16[7168,128]{1,0:T(8,128)(2,1)} %copy-done.1, bf16[7168,128]{1,0:T(8,128)(2,1)} %collective-permute-done.1.refs_2_.refs_6_, ...), custom_call_target="tpu_custom_call" | custom-call | flops 2818572288 | bytes 25690112 | tf_op jit(solution)/shard_map/pallas_call | solution.py:184
  161.3 2.1 constant_dynamic-slice_fusion.3
  163.4 1.4 collective-permute-start.16
  164.9 1.3 collective-permute-start.19
  166.2 15.7 %shard_map.113 = bf16[128,7168]{1,0:T(8,128)(2,1)} custom-call(f32[128,1]{1,0:T(8,128)} %reshape.33.mask_ref, bf16[128,7168]{1,0:T(8,128)(2,1)} %bitcast.51, bf16[7168,128]{1,0:T(8,128)(2,1)} %bitcast.34, bf16[7168,128]{1,0:T(8,128)(2,1)} %copy-done.1, bf16[7168,128]{1,0:T(8,128)(2,1)} %collective-permute-done.1.refs_2_.refs_6_, ...), custom_call_target="tpu_custom_call" | custom-call | flops 2818572288 | bytes 25690112 | tf_op jit(solution)/shard_map/pallas_call | solution.py:184
  181.9 2.1 constant_dynamic-slice_fusion.5
  184.7 1.3 collective-permute-start.12
  187.2 1.3 collective-permute-start.17
  188.5 1.9 add_convert_fusion.11
  190.4 1.3 collective-permute-start.10
  192.5 25.1 %collective-permute-done.17 = bf16[32,7168]{1,0:T(8,128)(2,1)S(1)} collective-permute-done((bf16[32,7168]{1,0:T(8,128)(2,1)S(1)}, bf16[32,7168]{1,0:T(8,128)(2,1)S(1)}, u32[]{:S(2)}, u32[]{:S(2)}) %collective-permute-start.17) | collective-permute-done | bytes 458784 | tf_op jit(solution)/shard_map/ppermute | solution.py:222
  217.6 2.0 add_convert_fusion.6
  219.6 13.6 %collective-permute-start.20 = (bf16[32,7168]{1,0:T(8,128)(2,1)}, bf16[32,7168]{1,0:T(8,128)(2,1)}, u32[]{:S(2)}, u32[]{:S(2)}) collective-permute-start(bf16[32,7168]{1,0:T(8,128)(2,1)} %get-tuple-element.15), channel_id=1, source_target_pairs={{2,1},{3,2},{6,5},{7,6},{10,9},{11,10},{14,13},{15,14},{18,17},{19... | collective-permute-start | bytes 1376264 | tf_op jit(solution)/shard_map/ppermute | solution.py:223
  233.2 1.9 collective-permute-start.18
  235.1 10.6 %shard_map.115 = (f32[256,512]{1,0:T(8,128)}, f32[256,512]{1,0:T(8,128)}) custom-call(bf16[256,7168]{1,0:T(8,128)(2,1)} %bitcast.50, bf16[7168,128]{1,0:T(8,128)(2,1)} %bitcast.35, bf16[7168,128]{1,0:T(8,128)(2,1)} %copy-done.1, bf16[7168,128]{1,0:T(8,128)(2,1)} %collective-permute-done.1.refs_2_.refs_6_, ...), custom_call_target="tpu_custom_call" | custom-call | flops 3758096384 | bytes 19398656 | tf_op jit(solution)/shard_map/pallas_call | solution.py:67
  245.7 28.5 %all-gather.9.cloned.1.call-done.s_ref = bf16[256,7168]{1,0:T(8,128)(2,1)} async-done(((bf16[64,7168]{1,0:T(8,128)(2,1)}), bf16[256,7168]{1,0:T(8,128)(2,1)}) %all-gather.9.cloned.1.call-update) | async-done | bytes 3670032 | tf_op jit(solution)/shard_map/all_gather | solution.py:249
  274.3 18.4 %shard_map.116 = bf16[256,7168]{1,0:T(8,128)(2,1)} custom-call(f32[256,1]{1,0:T(8,128)} %get-tuple-element.22.mask_ref, bf16[256,7168]{1,0:T(8,128)(2,1)} %all-gather.9.cloned.1.call-done.s_ref, f32[256,512]{1,0:T(8,128)} %get-tuple-element.4.c_ref, f32[256,512]{1,0:T(8,128)} %get-tuple-element.5.e_ref, bf16[128,7168]{1,0:T(8,128)(2,1)} %bitcast.49, ...), custom_call_target="tpu_custom_call" | custom-call | flops 5637144576 | bytes 30408704 | tf_op jit(solution)/shard_map/pallas_call | solution.py:120
  292.7 1.7 constant_dynamic-slice_fusion.1
  295.2 1.4 add_convert_fusion.10
  296.6 5.3 %collective-permute-start.13 = (bf16[32,7168]{1,0:T(8,128)(2,1)S(1)}, bf16[32,7168]{1,0:T(8,128)(2,1)S(1)}, u32[]{:S(2)}, u32[]{:S(2)}) collective-permute-start(bf16[32,7168]{1,0:T(8,128)(2,1)S(1)} %get-tuple-element.11), channel_id=1, source_target_pairs={{2,1},{3,2},{6,5},{7,6},{10,9},{11,10},{14,13},{15,14},{18,17},{19... | collective-permute-start | bytes 1376264 | tf_op jit(solution)/shard_map/ppermute | solution.py:223
  301.9 1.9 collective-permute-start.11
  303.8 1.3 collective-permute-start.26
  305.4 1.3 collective-permute-start.24
  307.8 22.3 %collective-permute-done.26 = bf16[64,7168]{1,0:T(8,128)(2,1)S(1)} collective-permute-done((bf16[64,7168]{1,0:T(8,128)(2,1)S(1)}, bf16[64,7168]{1,0:T(8,128)(2,1)S(1)}, u32[]{:S(2)}, u32[]{:S(2)}) %collective-permute-start.26) | collective-permute-done | bytes 917536 | tf_op jit(solution)/shard_map/ppermute | solution.py:223
  330.1 1.9 collective-permute-start.21
  332.0 11.4 %collective-permute-done.24 = bf16[64,7168]{1,0:T(8,128)(2,1)S(1)} collective-permute-done((bf16[64,7168]{1,0:T(8,128)(2,1)S(1)}, bf16[64,7168]{1,0:T(8,128)(2,1)S(1)}, u32[]{:S(2)}, u32[]{:S(2)}) %collective-permute-start.24) | collective-permute-done | bytes 917536 | tf_op jit(solution)/shard_map/ppermute | solution.py:222
  343.9 9.2 %collective-permute-start.27 = (bf16[64,7168]{1,0:T(8,128)(2,1)S(1)}, bf16[64,7168]{1,0:T(8,128)(2,1)S(1)}, u32[]{:S(2)}, u32[]{:S(2)}) collective-permute-start(bf16[64,7168]{1,0:T(8,128)(2,1)S(1)} %get-tuple-element.7), channel_id=1, source_target_pairs={{2,1},{3,2},{6,5},{7,6},{10,9},{11,10},{14,13},{15,14},{18,17},{19... | collective-permute-start | bytes 2752520 | tf_op jit(solution)/shard_map/ppermute | solution.py:223
  353.3 1.9 collective-permute-start.14
  355.3 18.7 %collective-permute-done.27 = bf16[64,7168]{1,0:T(8,128)(2,1)S(1)} collective-permute-done((bf16[64,7168]{1,0:T(8,128)(2,1)S(1)}, bf16[64,7168]{1,0:T(8,128)(2,1)S(1)}, u32[]{:S(2)}, u32[]{:S(2)}) %collective-permute-start.27) | collective-permute-done | bytes 917536 | tf_op jit(solution)/shard_map/ppermute | solution.py:223
  374.0 1.9 collective-permute-start.25
  376.1 4.4 %collective-permute-start.28 = (bf16[64,7168]{1,0:T(8,128)(2,1)S(1)}, bf16[64,7168]{1,0:T(8,128)(2,1)S(1)}, u32[]{:S(2)}, u32[]{:S(2)}) collective-permute-start(bf16[64,7168]{1,0:T(8,128)(2,1)S(1)} %add_convert_fusion), channel_id=1, source_target_pairs={{1,0},{2,1},{3,2},{5,4},{6,5},{7,6},{9,8},{10,9},{11,10},{13,12},{... | collective-permute-start | bytes 2752520 | tf_op jit(solution)/shard_map/ppermute | solution.py:223
  380.5 3.3 collective-permute-done.14
  383.8 1.5 fusion.3
  386.0 1.5 collective-permute-start.22
  387.5 7.3 %collective-permute-done.25 = bf16[64,7168]{1,0:T(8,128)(2,1)S(1)} collective-permute-done((bf16[64,7168]{1,0:T(8,128)(2,1)S(1)}, bf16[64,7168]{1,0:T(8,128)(2,1)S(1)}, u32[]{:S(2)}, u32[]{:S(2)}) %collective-permute-start.25) | collective-permute-done | bytes 917536 | tf_op jit(solution)/shard_map/ppermute | solution.py:222
  394.7 6.6 %collective-permute-done.28 = bf16[64,7168]{1,0:T(8,128)(2,1)S(1)} collective-permute-done((bf16[64,7168]{1,0:T(8,128)(2,1)S(1)}, bf16[64,7168]{1,0:T(8,128)(2,1)S(1)}, u32[]{:S(2)}, u32[]{:S(2)}) %collective-permute-start.28) | collective-permute-done | bytes 917536 | tf_op jit(solution)/shard_map/ppermute | solution.py:223
  402.7 1.9 collective-permute-done.22
  405.6 17.7 %collective-permute-done.29 = bf16[64,7168]{1,0:T(8,128)(2,1)S(1)} collective-permute-done((bf16[64,7168]{1,0:T(8,128)(2,1)S(1)}, bf16[64,7168]{1,0:T(8,128)(2,1)S(1)}, u32[]{:S(2)}, u32[]{:S(2)}) %collective-permute-start.29) | collective-permute-done | bytes 917536 | tf_op jit(solution)/shard_map/ppermute | solution.py:27
  (82 shorter events, 15.0 us)
Async XLA Ops:
  7.2 4.0 copy-start
  7.2 124.6 %copy-start.12 = (f32[1,64]{1,0:T(1,128)S(1)}, f32[1,64]{1,0:T(1,128)}, u32[]{:S(2)}) copy-start(f32[1,64]{1,0:T(1,128)} %param.15) | copy-start | bytes 772
  7.2 124.5 %copy-start.6 = (bf16[1,64,7168]{2,1,0:T(8,128)(2,1)S(1)}, bf16[1,64,7168]{2,1,0:T(8,128)(2,1)}, u32[]{:S(2)}) copy-start(bf16[1,64,7168]{2,1,0:T(8,128)(2,1)} %param.16) | copy-start | bytes 2752516
  7.2 137.6 %all-gather.13.cloned.1.call-start = ((), (), s32[]{:S(2)}) async-start(), calls=%async_computation.2 | async-start | bytes 2293760 | tf_op jit(solution)/shard_map/all_gather | solution.py:249
  9.6 156.6 %all-gather.11.cloned.1.call-start = ((), (), s32[]{:S(2)}) async-start(), calls=%async_computation.1 | async-start | bytes 2293760 | tf_op jit(solution)/shard_map/all_gather | solution.py:249
  10.3 122.6 %copy-start.10 = (s32[1,64,1]{1,2,0:T(1,128)S(1)}, s32[1,64,1]{1,2,0:T(1,128)}, u32[]{:S(2)}) copy-start(s32[1,64,1]{1,2,0:T(1,128)} %param.14) | copy-start | bytes 772
  10.3 122.6 %copy-start.11 = (s32[1,64,1]{1,2,0:T(1,128)S(1)}, s32[1,64,1]{1,2,0:T(1,128)}, u32[]{:S(2)}) copy-start(s32[1,64,1]{1,2,0:T(1,128)} %param.11) | copy-start | bytes 772
  10.3 224.8 %all-gather.15.cloned.1.call-start = ((), (), s32[]{:S(2)}) async-start(), calls=%async_computation.3 | async-start | bytes 4587520 | tf_op jit(solution)/shard_map/all_gather | solution.py:249
  11.1 133.6 %copy-start.9 = (f32[1,64]{1,0:T(1,128)S(1)}, f32[1,64]{1,0:T(1,128)}, u32[]{:S(2)}) copy-start(f32[1,64]{1,0:T(1,128)} %param.12) | copy-start | bytes 772
  11.1 263.2 %all-gather.9.cloned.1.call-start = ((), (), s32[]{:S(2)}) async-start(), calls=%async_computation | async-start | bytes 4587520 | tf_op jit(solution)/shard_map/all_gather | solution.py:249
  11.2 43.1 %collective-permute-start.1 = (bf16[7168,128]{1,0:T(8,128)(2,1)S(1)}, bf16[7168,128]{1,0:T(8,128)(2,1)}, u32[]{:S(2)}, u32[]{:S(2)}) collective-permute-start(bf16[7168,128]{1,0:T(8,128)(2,1)S(1)} %bitcast.37), channel_id=1, source_target_pairs={{0,8},{4,12},{8,0},{12,4},{1,9},{5,13},{9,1},{13,5},{2,10},{6,14},... | collective-permute-start | bytes 5505032 | tf_op jit(solution)/shard_map/ppermute | solution.py:22
  12.7 80.8 %collective-permute-start.4 = (bf16[7168,128]{1,0:T(8,128)(2,1)}, bf16[7168,128]{1,0:T(8,128)(2,1)}, u32[]{:S(2)}, u32[]{:S(2)}) collective-permute-start(bf16[7168,128]{1,0:T(8,128)(2,1)} %bitcast.39), channel_id=1, source_target_pairs={{0,8},{4,12},{8,0},{12,4},{1,9},{5,13},{9,1},{13,5},{2,10},{6,14},... | collective-permute-start | bytes 5505032 | tf_op jit(solution)/shard_map/ppermute | solution.py:22
  13.2 80.3 %collective-permute-start = (bf16[7168,128]{1,0:T(8,128)(2,1)S(1)}, bf16[7168,128]{1,0:T(8,128)(2,1)S(1)}, u32[]{:S(2)}, u32[]{:S(2)}) collective-permute-start(bf16[7168,128]{1,0:T(8,128)(2,1)S(1)} %bitcast.38), channel_id=1, source_target_pairs={{0,4},{4,0},{8,12},{12,8},{1,5},{5,1},{9,13},{13,9},{2,6},{6,2},{1... | collective-permute-start | bytes 5505032 | tf_op jit(solution)/shard_map/ppermute | solution.py:22
  13.2 118.5 %collective-permute-start.7 = (bf16[128,7168]{1,0:T(8,128)(2,1)}, bf16[128,7168]{1,0:T(8,128)(2,1)}, u32[]{:S(2)}, u32[]{:S(2)}) collective-permute-start(bf16[128,7168]{1,0:T(8,128)(2,1)} %bitcast.45), channel_id=1, source_target_pairs={{0,8},{4,12},{8,0},{12,4},{1,9},{5,13},{9,1},{13,5},{2,10},{6,14},... | collective-permute-start | bytes 5505032 | tf_op jit(solution)/shard_map/ppermute | solution.py:22
  14.7 130.0 %collective-permute-start.3 = (bf16[7168,128]{1,0:T(8,128)(2,1)}, bf16[7168,128]{1,0:T(8,128)(2,1)}, u32[]{:S(2)}, u32[]{:S(2)}) collective-permute-start(bf16[7168,128]{1,0:T(8,128)(2,1)} %bitcast.40), channel_id=1, source_target_pairs={{0,4},{4,0},{8,12},{12,8},{1,5},{5,1},{9,13},{13,9},{2,6},{6,2},{1... | collective-permute-start | bytes 5505032 | tf_op jit(solution)/shard_map/ppermute | solution.py:22
  54.2 90.5 %collective-permute-start.6 = (bf16[128,7168]{1,0:T(8,128)(2,1)}, bf16[128,7168]{1,0:T(8,128)(2,1)}, u32[]{:S(2)}, u32[]{:S(2)}) collective-permute-start(bf16[128,7168]{1,0:T(8,128)(2,1)} %bitcast.46), channel_id=1, source_target_pairs={{0,4},{4,0},{8,12},{12,8},{1,5},{5,1},{9,13},{13,9},{2,6},{6,2},{1... | collective-permute-start | bytes 5505032 | tf_op jit(solution)/shard_map/ppermute | solution.py:22
  93.5 51.2 %collective-permute-start.2 = (bf16[7168,128]{1,0:T(8,128)(2,1)}, bf16[7168,128]{1,0:T(8,128)(2,1)}, u32[]{:S(2)}, u32[]{:S(2)}) collective-permute-start(bf16[7168,128]{1,0:T(8,128)(2,1)} %collective-permute-done.1.refs_2_.refs_6_), channel_id=1, source_target_pairs={{0,4},{4,0},{8,12},{12,8},{1,5},{5,1},{9,13},{13,9},{2,6},{6,2},{1... | collective-permute-start | bytes 5505032 | tf_op jit(solution)/shard_map/ppermute | solution.py:22
  93.6 1.3 copy-start.1
  94.9 49.9 %collective-permute-start.5 = (bf16[7168,128]{1,0:T(8,128)(2,1)}, bf16[7168,128]{1,0:T(8,128)(2,1)S(1)}, u32[]{:S(2)}, u32[]{:S(2)}) collective-permute-start(bf16[7168,128]{1,0:T(8,128)(2,1)} %collective-permute-done.4.refs_6_.refs_10_), channel_id=1, source_target_pairs={{0,4},{4,0},{8,12},{12,8},{1,5},{5,1},{9,13},{13,9},{2,6},{6,2},{1... | collective-permute-start | bytes 5505032 | tf_op jit(solution)/shard_map/ppermute | solution.py:22
  131.7 13.1 %collective-permute-start.8 = (bf16[128,7168]{1,0:T(8,128)(2,1)}, bf16[128,7168]{1,0:T(8,128)(2,1)}, u32[]{:S(2)}, u32[]{:S(2)}) collective-permute-start(bf16[128,7168]{1,0:T(8,128)(2,1)} %collective-permute-done.7.refs_10_.refs_2_), channel_id=1, source_target_pairs={{0,4},{4,0},{8,12},{12,8},{1,5},{5,1},{9,13},{13,9},{2,6},{6,2},{1... | collective-permute-start | bytes 5505032 | tf_op jit(solution)/shard_map/ppermute | solution.py:22
  144.8 1.2 copy-start.2
  163.4 22.6 %collective-permute-start.16 = (bf16[32,7168]{1,0:T(8,128)(2,1)}, bf16[32,7168]{1,0:T(8,128)(2,1)}, u32[]{:S(2)}, u32[]{:S(2)}) collective-permute-start(bf16[32,7168]{1,0:T(8,128)(2,1)} %get-tuple-element.16), channel_id=1, source_target_pairs={{0,1},{4,5},{8,9},{12,13},{16,17},{20,21},{24,25},{28,29}} | collective-permute-start | bytes 1376264 | tf_op jit(solution)/shard_map/ppermute | solution.py:222
  164.9 26.8 %collective-permute-start.19 = (bf16[32,7168]{1,0:T(8,128)(2,1)}, bf16[32,7168]{1,0:T(8,128)(2,1)S(1)}, u32[]{:S(2)}, u32[]{:S(2)}) collective-permute-start(bf16[32,7168]{1,0:T(8,128)(2,1)} %get-tuple-element.17), channel_id=1, source_target_pairs={{3,2},{7,6},{11,10},{15,14},{19,18},{23,22},{27,26},{31,30}} | collective-permute-start | bytes 1376264 | tf_op jit(solution)/shard_map/ppermute | solution.py:223
  181.9 4.2 copy-start.4
  184.0 4.5 %collective-permute-start.9 = (bf16[32,7168]{1,0:T(8,128)(2,1)S(1)}, bf16[32,7168]{1,0:T(8,128)(2,1)S(1)}, u32[]{:S(2)}, u32[]{:S(2)}) collective-permute-start(bf16[32,7168]{1,0:T(8,128)(2,1)S(1)} %get-tuple-element.12), channel_id=1, source_target_pairs={{0,1},{4,5},{8,9},{12,13},{16,17},{20,21},{24,25},{28,29}} | collective-permute-start | bytes 1376264 | tf_op jit(solution)/shard_map/ppermute | solution.py:222
  184.7 110.5 %collective-permute-start.12 = (bf16[32,7168]{1,0:T(8,128)(2,1)}, bf16[32,7168]{1,0:T(8,128)(2,1)}, u32[]{:S(2)}, u32[]{:S(2)}) collective-permute-start(bf16[32,7168]{1,0:T(8,128)(2,1)} %get-tuple-element.13), channel_id=1, source_target_pairs={{3,2},{7,6},{11,10},{15,14},{19,18},{23,22},{27,26},{31,30}} | collective-permute-start | bytes 1376264 | tf_op jit(solution)/shard_map/ppermute | solution.py:223
  187.2 30.4 %collective-permute-start.17 = (bf16[32,7168]{1,0:T(8,128)(2,1)S(1)}, bf16[32,7168]{1,0:T(8,128)(2,1)S(1)}, u32[]{:S(2)}, u32[]{:S(2)}) collective-permute-start(bf16[32,7168]{1,0:T(8,128)(2,1)S(1)} %add_convert_fusion.7), channel_id=1, source_target_pairs={{0,1},{1,2},{4,5},{5,6},{8,9},{9,10},{12,13},{13,14},{16,17},{17,1... | collective-permute-start | bytes 1376264 | tf_op jit(solution)/shard_map/ppermute | solution.py:222
  190.4 104.8 %collective-permute-start.10 = (bf16[32,7168]{1,0:T(8,128)(2,1)}, bf16[32,7168]{1,0:T(8,128)(2,1)}, u32[]{:S(2)}, u32[]{:S(2)}) collective-permute-start(bf16[32,7168]{1,0:T(8,128)(2,1)} %add_convert_fusion.11), channel_id=1, source_target_pairs={{0,1},{1,2},{4,5},{5,6},{8,9},{9,10},{12,13},{13,14},{16,17},{17,1... | collective-permute-start | bytes 1376264 | tf_op jit(solution)/shard_map/ppermute | solution.py:222
  191.7 0.8 copy-start.8
  219.6 85.8 %collective-permute-start.20 = (bf16[32,7168]{1,0:T(8,128)(2,1)}, bf16[32,7168]{1,0:T(8,128)(2,1)}, u32[]{:S(2)}, u32[]{:S(2)}) collective-permute-start(bf16[32,7168]{1,0:T(8,128)(2,1)} %get-tuple-element.15), channel_id=1, source_target_pairs={{2,1},{3,2},{6,5},{7,6},{10,9},{11,10},{14,13},{15,14},{18,17},{19... | collective-permute-start | bytes 1376264 | tf_op jit(solution)/shard_map/ppermute | solution.py:223
  233.2 143.0 %collective-permute-start.18 = (bf16[32,7168]{1,0:T(8,128)(2,1)S(1)}, bf16[32,7168]{1,0:T(8,128)(2,1)}, u32[]{:S(2)}, u32[]{:S(2)}) collective-permute-start(bf16[32,7168]{1,0:T(8,128)(2,1)S(1)} %get-tuple-element.14), channel_id=1, source_target_pairs={{0,1},{1,2},{2,3},{4,5},{5,6},{6,7},{8,9},{9,10},{10,11},{12,13},{... | collective-permute-start | bytes 1376264 | tf_op jit(solution)/shard_map/ppermute | solution.py:222
  274.3 20.9 %copy-start.5 = (bf16[128,7168]{1,0:T(8,128)(2,1)S(1)}, bf16[128,7168]{1,0:T(8,128)(2,1)}, u32[]{:S(2)}) copy-start(bf16[128,7168]{1,0:T(8,128)(2,1)} %shard_map.113) | copy-start | bytes 5505028
  292.7 12.4 %copy-start.3 = (bf16[256,7168]{1,0:T(8,128)(2,1)S(1)}, bf16[256,7168]{1,0:T(8,128)(2,1)}, u32[]{:S(2)}) copy-start(bf16[256,7168]{1,0:T(8,128)(2,1)} %shard_map.116) | copy-start | bytes 11010052
  294.5 9.3 %collective-permute-start.23 = (bf16[64,7168]{1,0:T(8,128)(2,1)S(1)}, bf16[64,7168]{1,0:T(8,128)(2,1)S(1)}, u32[]{:S(2)}, u32[]{:S(2)}) collective-permute-start(bf16[64,7168]{1,0:T(8,128)(2,1)S(1)} %get-tuple-element.8), channel_id=1, source_target_pairs={{0,1},{4,5},{8,9},{12,13},{16,17},{20,21},{24,25},{28,29}} | collective-permute-start | bytes 2752520 | tf_op jit(solution)/shard_map/ppermute | solution.py:222
  296.6 56.6 %collective-permute-start.13 = (bf16[32,7168]{1,0:T(8,128)(2,1)S(1)}, bf16[32,7168]{1,0:T(8,128)(2,1)S(1)}, u32[]{:S(2)}, u32[]{:S(2)}) collective-permute-start(bf16[32,7168]{1,0:T(8,128)(2,1)S(1)} %get-tuple-element.11), channel_id=1, source_target_pairs={{2,1},{3,2},{6,5},{7,6},{10,9},{11,10},{14,13},{15,14},{18,17},{19... | collective-permute-start | bytes 1376264 | tf_op jit(solution)/shard_map/ppermute | solution.py:223
  301.9 78.7 %collective-permute-start.11 = (bf16[32,7168]{1,0:T(8,128)(2,1)S(1)}, bf16[32,7168]{1,0:T(8,128)(2,1)S(1)}, u32[]{:S(2)}, u32[]{:S(2)}) collective-permute-start(bf16[32,7168]{1,0:T(8,128)(2,1)S(1)} %get-tuple-element.10), channel_id=1, source_target_pairs={{0,1},{1,2},{2,3},{4,5},{5,6},{6,7},{8,9},{9,10},{10,11},{12,13},{... | collective-permute-start | bytes 1376264 | tf_op jit(solution)/shard_map/ppermute | solution.py:222
  303.8 26.3 %collective-permute-start.26 = (bf16[64,7168]{1,0:T(8,128)(2,1)S(1)}, bf16[64,7168]{1,0:T(8,128)(2,1)S(1)}, u32[]{:S(2)}, u32[]{:S(2)}) collective-permute-start(bf16[64,7168]{1,0:T(8,128)(2,1)S(1)} %get-tuple-element.9), channel_id=1, source_target_pairs={{3,2},{7,6},{11,10},{15,14},{19,18},{23,22},{27,26},{31,30}} | collective-permute-start | bytes 2752520 | tf_op jit(solution)/shard_map/ppermute | solution.py:223
  305.4 38.1 %collective-permute-start.24 = (bf16[64,7168]{1,0:T(8,128)(2,1)S(1)}, bf16[64,7168]{1,0:T(8,128)(2,1)S(1)}, u32[]{:S(2)}, u32[]{:S(2)}) collective-permute-start(bf16[64,7168]{1,0:T(8,128)(2,1)S(1)} %add_convert_fusion.3), channel_id=1, source_target_pairs={{0,1},{1,2},{4,5},{5,6},{8,9},{9,10},{12,13},{13,14},{16,17},{17,1... | collective-permute-start | bytes 2752520 | tf_op jit(solution)/shard_map/ppermute | solution.py:222
  330.1 50.4 %collective-permute-start.21 = (bf16[32,7168]{1,0:T(8,128)(2,1)S(1)}, bf16[32,7168]{1,0:T(8,128)(2,1)S(1)}, u32[]{:S(2)}, u32[]{:S(2)}) collective-permute-start(bf16[32,7168]{1,0:T(8,128)(2,1)S(1)} %add_convert_fusion.4), channel_id=1, source_target_pairs={{1,0},{2,1},{3,2},{5,4},{6,5},{7,6},{9,8},{10,9},{11,10},{13,12},{... | collective-permute-start | bytes 1376264 | tf_op jit(solution)/shard_map/ppermute | solution.py:223
  343.9 39.9 %copy-start.7 = (bf16[1,64,7168]{2,1,0:T(8,128)(2,1)S(1)}, bf16[1,64,7168]{2,1,0:T(8,128)(2,1)}, u32[]{:S(2)}) copy-start(bf16[1,64,7168]{2,1,0:T(8,128)(2,1)} %param.10) | copy-start | bytes 2752516
  343.9 30.0 %collective-permute-start.27 = (bf16[64,7168]{1,0:T(8,128)(2,1)S(1)}, bf16[64,7168]{1,0:T(8,128)(2,1)S(1)}, u32[]{:S(2)}, u32[]{:S(2)}) collective-permute-start(bf16[64,7168]{1,0:T(8,128)(2,1)S(1)} %get-tuple-element.7), channel_id=1, source_target_pairs={{2,1},{3,2},{6,5},{7,6},{10,9},{11,10},{14,13},{15,14},{18,17},{19... | collective-permute-start | bytes 2752520 | tf_op jit(solution)/shard_map/ppermute | solution.py:223
  353.3 30.5 %collective-permute-start.14 = (bf16[32,7168]{1,0:T(8,128)(2,1)S(1)}, bf16[32,7168]{1,0:T(8,128)(2,1)S(1)}, u32[]{:S(2)}, u32[]{:S(2)}) collective-permute-start(bf16[32,7168]{1,0:T(8,128)(2,1)S(1)} %add_convert_fusion.8), channel_id=1, source_target_pairs={{1,0},{2,1},{3,2},{5,4},{6,5},{7,6},{9,8},{10,9},{11,10},{13,12},{... | collective-permute-start | bytes 1376264 | tf_op jit(solution)/shard_map/ppermute | solution.py:223
  374.0 20.8 %collective-permute-start.25 = (bf16[64,7168]{1,0:T(8,128)(2,1)S(1)}, bf16[64,7168]{1,0:T(8,128)(2,1)S(1)}, u32[]{:S(2)}, u32[]{:S(2)}) collective-permute-start(bf16[64,7168]{1,0:T(8,128)(2,1)S(1)} %get-tuple-element.6), channel_id=1, source_target_pairs={{0,1},{1,2},{2,3},{4,5},{5,6},{6,7},{8,9},{9,10},{10,11},{12,13},{... | collective-permute-start | bytes 2752520 | tf_op jit(solution)/shard_map/ppermute | solution.py:222
  376.1 25.2 %collective-permute-start.28 = (bf16[64,7168]{1,0:T(8,128)(2,1)S(1)}, bf16[64,7168]{1,0:T(8,128)(2,1)S(1)}, u32[]{:S(2)}, u32[]{:S(2)}) collective-permute-start(bf16[64,7168]{1,0:T(8,128)(2,1)S(1)} %add_convert_fusion), channel_id=1, source_target_pairs={{1,0},{2,1},{3,2},{5,4},{6,5},{7,6},{9,8},{10,9},{11,10},{13,12},{... | collective-permute-start | bytes 2752520 | tf_op jit(solution)/shard_map/ppermute | solution.py:223
  385.4 17.4 %collective-permute-start.15 = (bf16[32,7168]{1,0:T(8,128)(2,1)S(1)}, bf16[32,7168]{1,0:T(8,128)(2,1)S(1)}, u32[]{:S(2)}, u32[]{:S(2)}) collective-permute-start(bf16[32,7168]{1,0:T(8,128)(2,1)S(1)} %get-tuple-element.18), channel_id=1, source_target_pairs={{16,0},{0,16},{17,1},{1,17},{18,2},{2,18},{19,3},{3,19},{20,4},{4,... | collective-permute-start | bytes 1376264 | tf_op jit(solution)/shard_map/ppermute | solution.py:27
  386.0 18.6 %collective-permute-start.22 = (bf16[32,7168]{1,0:T(8,128)(2,1)S(1)}, bf16[32,7168]{1,0:T(8,128)(2,1)S(1)}, u32[]{:S(2)}, u32[]{:S(2)}) collective-permute-start(bf16[32,7168]{1,0:T(8,128)(2,1)S(1)} %get-tuple-element.19), channel_id=1, source_target_pairs={{16,0},{0,16},{17,1},{1,17},{18,2},{2,18},{19,3},{3,19},{20,4},{4,... | collective-permute-start | bytes 1376264 | tf_op jit(solution)/shard_map/ppermute | solution.py:27
  401.8 21.4 %collective-permute-start.29 = (bf16[64,7168]{1,0:T(8,128)(2,1)S(1)}, bf16[64,7168]{1,0:T(8,128)(2,1)S(1)}, u32[]{:S(2)}, u32[]{:S(2)}) collective-permute-start(bf16[64,7168]{1,0:T(8,128)(2,1)S(1)} %fusion.1), channel_id=1, source_target_pairs={{16,0},{0,16},{17,1},{1,17},{18,2},{2,18},{19,3},{3,19},{20,4},{4,... | collective-permute-start | bytes 2752520 | tf_op jit(solution)/shard_map/ppermute | solution.py:27
Sparse Core Ops, SparseCore 0:
  9.7 41.2 all-gather.12
  53.2 40.2 all-gather.10
  95.0 70.7 all-gather.14
  167.8 106.3 all-gather.8

commit v2 on v1

--- a/solution.py
+++ b/solution.py
@@ -1,4 +1,5 @@
 import functools
+import math
 
 import jax
 import jax.numpy as jnp
@@ -9,6 +10,7 @@
 
 BF16, F32 = jnp.bfloat16, jnp.float32
 VMEM_LIMIT = 56 * 1024 * 1024
+LAST_ROWS = 16
 
 
 def contract_last(left_side, weights):
@@ -44,7 +46,30 @@
     return jnp.concatenate([ref[...] for ref in refs], axis=axis)
 
 
-def gates_kernel(pieces, x_ref, *refs):
+def stacked(refs):
+    return jnp.concatenate([ref[0] for ref in refs], axis=0)
+
+
+def put_blocks(out_refs, total):
+    rows = out_refs[0].shape[0]
+    for index, ref in enumerate(out_refs):
+        ref[...] = total[index * rows : (index + 1) * rows].astype(ref.dtype)
+
+
+def turned_specs(count, begin, rows, chunk, column):
+    unit = math.gcd(begin, rows)
+    return [
+        pl.BlockSpec(
+            (1, unit, chunk),
+            lambda i, at, turn=turn, piece=piece: (lax.rem(at[0] + turn, count), piece, column(i)),
+        )
+        for turn in range(count)
+        for piece in range(begin // unit, (begin + rows) // unit)
+    ]
+
+
+def gates_kernel(inputs, pieces, at_ref, *refs):
+    xs, refs = refs[:inputs], refs[inputs:]
     gates, ups = refs[:pieces], refs[pieces : 2 * pieces]
     c_ref, e_ref = refs[2 * pieces :]
 
@@ -53,35 +78,43 @@
         c_ref[...] = jnp.zeros_like(c_ref)
         e_ref[...] = jnp.zeros_like(e_ref)
 
-    x = x_ref[...]
-    c_ref[...] += jnp.dot(x, joined(gates, 1), preferred_element_type=F32)
-    e_ref[...] += jnp.dot(x, joined(ups, 1), preferred_element_type=F32)
-
-
-def gates_call(x, gates, ups):
-    rows, width = x.shape
+    x = stacked(xs)
+    c = jnp.dot(x, joined(gates, 1), preferred_element_type=F32)
+    e = jnp.dot(x, joined(ups, 1), preferred_element_type=F32)
+    c_ref[...] += c.reshape(c_ref.shape)
+    e_ref[...] += e.reshape(e_ref.shape)
+
+
+def gates_call(at, x, begin, rows, gates, ups):
+    count, _, width = x.shape
     pieces, hid = len(gates), gates[0].shape[1]
-    chunk = chunk_of(width, 1024)
+    chunk = chunk_of(width, 1792)
     hidden = pieces * hid
-    weight_spec = pl.BlockSpec((chunk, hid), lambda i: (i, 0))
+    x_specs = turned_specs(count, begin, rows, chunk, lambda i: i)
+    weight_spec = pl.BlockSpec((chunk, hid), lambda i, at: (i, 0))
     return pl.pallas_call(
-        functools.partial(gates_kernel, pieces),
-        grid=(width // chunk,),
-        in_specs=[pl.BlockSpec((rows, chunk), lambda i: (0, i))] + [weight_spec] * (2 * pieces),
-        out_specs=[pl.BlockSpec((rows, hidden), lambda i: (0, 0))] * 2,
-        out_shape=[jax.ShapeDtypeStruct((rows, hidden), F32)] * 2,
+        functools.partial(gates_kernel, len(x_specs), pieces),
+        grid_spec=pltpu.PrefetchScalarGridSpec(
+            num_scalar_prefetch=1,
+            grid=(width // chunk,),
+            in_specs=x_specs + [weight_spec] * (2 * pieces),
+            out_specs=[pl.BlockSpec((count, rows, hidden), lambda i, at: (0, 0, 0))] * 2,
+        ),
+        out_shape=[jax.ShapeDtypeStruct((count, rows, hidden), F32)] * 2,
         compiler_params=pltpu.CompilerParams(vmem_limit_bytes=VMEM_LIMIT),
         cost_estimate=pl.CostEstimate(
-            flops=4 * rows * width * hidden,
-            bytes_accessed=2 * rows * width + 4 * width * hidden + 8 * rows * hidden,
+            flops=4 * count * rows * width * hidden,
+            bytes_accessed=2 * count * rows * width + 4 * width * hidden,
             transcendentals=0,
         ),
-    )(x, *gates, *ups)
-
-
-def backward_kernel(pieces, steps, mask_ref, s_ref, c_ref, e_ref, *refs):
+    )(at, *[x] * len(x_specs), *gates, *ups)
+
+
+def backward_kernel(count, inputs, pieces, steps, at_ref, mask_ref, c_ref, e_ref, *refs):
+    scaled, refs = refs[:inputs], refs[inputs:]
     downs, gates, ups = refs[:pieces], refs[pieces : 2 * pieces], refs[2 * pieces : 3 * pieces]
-    out_ref, dh_ref, ga_ref, gb_ref = refs[3 * pieces :]
+    outs = refs[3 * pieces : 3 * pieces + count]
+    dh_ref, ga_ref, gb_ref = refs[3 * pieces + count :]
     step = pl.program_id(0)
 
     @pl.when(step == 0)
@@ -90,11 +123,12 @@
 
     @pl.when(step < steps)
     def _():
-        dh_ref[...] += contract_last(s_ref[...], joined(downs, 0))
+        dh_ref[...] += contract_last(stacked(scaled), joined(downs, 0))
 
     @pl.when(step == steps - 1)
     def _():
-        c, e, dh = c_ref[...], e_ref[...], dh_ref[...]
+        dh = dh_ref[...]
+        c, e = c_ref[...].reshape(dh.shape), e_ref[...].reshape(dh.shape)
         s = jax.nn.sigmoid(c)
         silu = c * s
         keep = own_columns(mask_ref[...], c.shape[1])
@@ -105,48 +139,56 @@
     def _():
         total = contract_last(ga_ref[...], joined(gates, 1))
         total += contract_last(gb_ref[...], joined(ups, 1))
-        out_ref[...] = total.astype(BF16)
-
-
-def backward_call(mask, scaled, c, e, downs, gates, ups):
-    rows, width = scaled.shape
+        put_blocks(outs, total)
+
+
+def backward_call(at, mask, scaled, begin, rows, part, c, e, downs, gates, ups):
+    count, _, width = scaled.shape
     pieces, hid = len(gates), gates[0].shape[1]
-    chunk = chunk_of(width, 1024)
+    chunk = chunk_of(width, 1792)
     steps = width // chunk
     hidden = pieces * hid
     first = lambda i: jnp.minimum(i, steps - 1)
     second = lambda i: jnp.maximum(i - steps, 0)
-    whole = lambda i: (0, 0)
+    scaled_specs = turned_specs(count, begin, rows, chunk, first)
+    pre_spec = pl.BlockSpec((count, rows, hidden), lambda i, at: (0, part, 0))
+    out_spec = pl.BlockSpec((rows, chunk), lambda i, at: (0, second(i)))
     return pl.pallas_call(
-        functools.partial(backward_kernel, pieces, steps),
-        grid=(2 * steps,),
-        in_specs=[
-            pl.BlockSpec((rows, 1), whole),
-            pl.BlockSpec((rows, chunk), lambda i: (0, first(i))),
-            pl.BlockSpec((rows, hidden), whole),
-            pl.BlockSpec((rows, hidden), whole),
-        ]
-        + [pl.BlockSpec((hid, chunk), lambda i: (0, first(i)))] * pieces
-        + [pl.BlockSpec((chunk, hid), lambda i: (second(i), 0))] * (2 * pieces),
-        out_specs=pl.BlockSpec((rows, chunk), lambda i: (0, second(i))),
-        out_shape=jax.ShapeDtypeStruct((rows, width), BF16),
-        scratch_shapes=[
-            pltpu.VMEM((rows, hidden), F32),
-            pltpu.VMEM((rows, hidden), BF16),
-            pltpu.VMEM((rows, hidden), BF16),
-        ],
+        functools.partial(backward_kernel, count, len(scaled_specs), pieces, steps),
+        grid_spec=pltpu.PrefetchScalarGridSpec(
+            num_scalar_prefetch=1,
+            grid=(2 * steps,),
+            in_specs=[
+                pl.BlockSpec((count * rows, 1), lambda i, at: (0, 0)),
+                pre_spec,
+                pre_spec,
+            ]
+            + scaled_specs
+            + [pl.BlockSpec((hid, chunk), lambda i, at: (0, first(i)))] * pieces
+            + [pl.BlockSpec((chunk, hid), lambda i, at: (second(i), 0))] * (2 * pieces),
+            out_specs=[out_spec] * count,
+            scratch_shapes=[
+                pltpu.VMEM((count * rows, hidden), F32),
+                pltpu.VMEM((count * rows, hidden), BF16),
+                pltpu.VMEM((count * rows, hidden), BF16),
+            ],
+        ),
+        out_shape=[jax.ShapeDtypeStruct((rows, width), F32)]
+        + [jax.ShapeDtypeStruct((rows, width), BF16)] * (count - 1),
         compiler_params=pltpu.CompilerParams(vmem_limit_bytes=VMEM_LIMIT),
         cost_estimate=pl.CostEstimate(
-            flops=6 * rows * width * hidden,
-            bytes_accessed=4 * rows * width + 6 * width * hidden + 8 * rows * hidden,
-            transcendentals=rows * hidden,
+            flops=6 * count * rows * width * hidden,
+            bytes_accessed=4 * count * rows * width + 6 * width * hidden,
+            transcendentals=count * rows * hidden,
         ),
-    )(mask, scaled, c, e, *downs, *gates, *ups)
-
-
-def forward_kernel(pieces, steps, mask_ref, x_ref, *refs):
+    )(at, mask, c, e, *[scaled] * len(scaled_specs), *downs, *gates, *ups)
+
+
+def forward_kernel(count, pieces, steps, mask_ref, own_ref, *refs):
+    ups_in, downs_in, refs = refs[: count - 1], refs[count - 1 : 2 * count - 2], refs[2 * count - 2 :]
     gates, ups, downs = refs[:pieces], refs[pieces : 2 * pieces], refs[2 * pieces : 3 * pieces]
-    out_ref, a_ref, b_ref, hidden_ref = refs[3 * pieces :]
+    outs = refs[3 * pieces : 3 * pieces + count]
+    a_ref, b_ref, hidden_ref = refs[3 * pieces + count :]
     step = pl.program_id(0)
 
     @pl.when(step == 0)
@@ -156,7 +198,10 @@
 
     @pl.when(step < steps)
     def _():
-        x = x_ref[...]
+        blocks = [own_ref[...]] + [
+            downs_in[away - 1][...] + ups_in[count - away - 1][...] for away in range(1, count)
+        ]
+        x = jnp.concatenate(blocks, axis=0)
         a_ref[...] += jnp.dot(x, joined(gates, 1), preferred_element_type=F32)
         b_ref[...] += jnp.dot(x, joined(ups, 1), preferred_element_type=F32)
 
@@ -168,62 +213,83 @@
 
     @pl.when(step >= steps)
     def _():
-        out_ref[...] = jnp.dot(
-            hidden_ref[...], joined(downs, 0), preferred_element_type=F32
-        ).astype(BF16)
-
-
-def forward_call(mask, x, gates, ups, downs):
-    rows, width = x.shape
+        total = jnp.dot(hidden_ref[...], joined(downs, 0), preferred_element_type=F32)
+        put_blocks(outs, total)
+
+
+def forward_call(mask, own, ups_in, downs_in, gates, ups, downs):
+    rows, width = own.shape
+    count = len(ups_in) + 1
     pieces, hid = len(gates), gates[0].shape[1]
-    chunk = chunk_of(width, 1024)
+    chunk = chunk_of(width, 1792)
     steps = width // chunk
     hidden = pieces * hid
     first = lambda i: jnp.minimum(i, steps - 1)
     second = lambda i: jnp.maximum(i - steps, 0)
+    x_spec = pl.BlockSpec((rows, chunk), lambda i: (0, first(i)))
     return pl.pallas_call(
-        functools.partial(forward_kernel, pieces, steps),
+        functools.partial(forward_kernel, count, pieces, steps),
         grid=(2 * steps,),
-        in_specs=[
-            pl.BlockSpec((rows, 1), lambda i: (0, 0)),
-            pl.BlockSpec((rows, chunk), lambda i: (0, first(i))),
-        ]
+        in_specs=[pl.BlockSpec((count * rows, 1), lambda i: (0, 0))]
+        + [x_spec] * (2 * count - 1)
         + [pl.BlockSpec((chunk, hid), lambda i: (first(i), 0))] * (2 * pieces)
         + [pl.BlockSpec((hid, chunk), lambda i: (0, second(i)))] * pieces,
-        out_specs=pl.BlockSpec((rows, chunk), lambda i: (0, second(i))),
-        out_shape=jax.ShapeDtypeStruct((rows, width), BF16),
+        out_specs=[pl.BlockSpec((rows, chunk), lambda i: (0, second(i)))] * count,
+        out_shape=[jax.ShapeDtypeStruct((rows, width), F32)]
+        + [jax.ShapeDtypeStruct((rows, width), BF16)] * (count - 1),
         scratch_shapes=[
-            pltpu.VMEM((rows, hidden), F32),
-            pltpu.VMEM((rows, hidden), F32),
-            pltpu.VMEM((rows, hidden), BF16),
+            pltpu.VMEM((count * rows, hidden), F32),
+            pltpu.VMEM((count * rows, hidden), F32),
+            pltpu.VMEM((count * rows, hidden), BF16),
         ],
         compiler_params=pltpu.CompilerParams(vmem_limit_bytes=VMEM_LIMIT),
         cost_estimate=pl.CostEstimate(
-            flops=6 * rows * width * hidden,
-            bytes_accessed=4 * rows * width + 6 * width * hidden,
-            transcendentals=rows * hidden,
+            flops=6 * count * rows * width * hidden,
+            bytes_accessed=6 * count * rows * width + 6 * width * hidden,
+            transcendentals=count * rows * hidden,
         ),
-    )(mask, x, *gates, *ups, *downs)
-
-
-def summed_home(partial, axis):
-    count, here = lax.axis_size(axis), lax.axis_index(axis)
-    rows = partial.shape[0] // count
-
-    def block(index):
-        start = jnp.clip(index, 0, count - 1) * rows
-        return lax.dynamic_slice_in_dim(partial, start, rows, 0).astype(F32)
-
+    )(mask, own, *ups_in, *downs_in, *gates, *ups, *downs)
+
+
+def after(value, *earlier):
+    return lax.optimization_barrier((value,) + earlier)[0]
+
+
+def sent_along(block, axis):
+    count = lax.axis_size(axis)
+    from_below, from_above = [block], [block]
+    for step in range(1, count):
+        up = [(i, i + 1) for i in range(step - 1, count - 1)]
+        down = [(i, i - 1) for i in range(1, count - step + 1)]
+        from_below.append(lax.ppermute(from_below[-1], axis, up))
+        from_above.append(lax.ppermute(from_above[-1], axis, down))
+    return from_below[1:], from_above[1:]
+
+
+def steps_home(blocks, axis):
+    count = lax.axis_size(axis)
     up, down = None, None
     for step in range(1, count):
-        to_up, to_down = block(here + count - step), block(here - count + step)
+        to_up, to_down = blocks[count - step], blocks[step]
         if up is not None:
-            to_up, to_down = to_up + up.astype(F32), to_down + down.astype(F32)
-        up = lax.ppermute(to_up.astype(BF16), axis, [(i, i + 1) for i in range(step)])
-        down = lax.ppermute(
-            to_down.astype(BF16), axis, [(i, i - 1) for i in range(count - step, count)]
-        )
-    return block(here) + up.astype(F32) + down.astype(F32)
+            to_up = (to_up.astype(F32) + up.astype(F32)).astype(BF16)
+            to_down = (to_down.astype(F32) + down.astype(F32)).astype(BF16)
+        up = lax.ppermute(to_up, axis, [(i, i + 1) for i in range(step)])
+        down = lax.ppermute(to_down, axis, [(i, i - 1) for i in range(count - step, count)])
+        yield up, down
+
+
+def summed(block, arrived):
+    for part in arrived:
+        block = block + part.astype(F32)
+    return block
+
+
+def sent_home(blocks, axis):
+    total = blocks[0]
+    for away in range(1, len(blocks)):
+        total = total + shifted(blocks[away], axis, away).astype(F32)
+    return total
 
 
 def few_experts(
@@ -240,37 +306,64 @@
 ):
     tokens_here = x_forward.shape[1]
     expert_here = lax.axis_index("expert") // 2
-
-    def with_neighbours(weight):
-        across = flipped(weight, "expert", 2)
+    count = lax.axis_size("dp")
+    at = lax.axis_index("dp").reshape(1).astype(jnp.int32)
+
+    last = min(LAST_ROWS, tokens_here // 2)
+    early = tokens_here - last
+    scaled_grad = (prob_backward[0][:, None] * grad_output[0].astype(F32)).astype(BF16)
+    routes = jnp.concatenate([route_forward[0], route_backward[0]], axis=1)
+    bundle = jnp.concatenate([x_backward[0], scaled_grad[:early]], axis=0)
+    x_fwd, bundle, routes, scaled_last = lax.optimization_barrier(
+        (x_forward[0], bundle, routes, scaled_grad[early:])
+    )
+    bundle = lax.all_gather(bundle, "dp")
+    routes = jnp.stack([routes] + [shifted(routes, "dp", -away) for away in range(1, count)])
+    mine = (routes == expert_here).astype(F32)
+    mask_fwd, mask_bwd = mine[:, :, 0:1], mine[:, :, 1:2]
+
+    def neighbours(weight, across):
         return [weight, flipped(weight, "expert", 1), across, flipped(across, "expert", 1)]
 
-    def gathered(rows):
-        return lax.all_gather(rows, "dp", axis=0, tiled=True)
-
-    routes = jnp.concatenate([route_forward[0], route_backward[0]], axis=1)
-    mine = (gathered(routes) == expert_here).astype(F32)
-    mask_fwd, mask_bwd = mine[:, 0:1], mine[:, 1:2]
-    scaled_grad = (prob_backward[0][:, None] * grad_output[0].astype(F32)).astype(BF16)
-    gates, ups, downs = (with_neighbours(w[0, 0]) for w in (w_gate, w_up, w_down))
-
-    c, e = gates_call(gathered(x_backward[0]), gates, ups)
-    partial_bwd = backward_call(mask_bwd, gathered(scaled_grad), c, e, downs, gates, ups)
-    grad_in = (grad_output[0].astype(F32) + summed_home(partial_bwd, "dp")).astype(BF16)
-    sent_bwd = shifted(grad_in, "pipe", -1)
-
-    parts, sent_fwd = 2, []
-    size = tokens_here // parts
-    count = lax.axis_size("dp")
-    for part in range(parts):
-        rows = slice(part * size, (part + 1) * size)
-        x_part = x_forward[0, rows]
-        mask = mask_fwd.reshape(count, tokens_here, 1)[:, rows].reshape(count * size, 1)
-        partial_fwd = forward_call(mask, gathered(x_part), gates, ups, downs)
-        total = summed_home(partial_fwd, "dp")
-        layer_out = (x_part.astype(F32) + prob_forward[0, rows][:, None] * total).astype(BF16)
-        sent_fwd.append(shifted(layer_out, "pipe", 1))
-    return (jnp.concatenate(sent_fwd, axis=0)[None], sent_bwd[None])
+    gate, up, down = w_gate[0, 0], w_up[0, 0], w_down[0, 0]
+    gate_across, up_across, down_across = (flipped(w, "expert", 2) for w in (gate, up, down))
+    from_below, from_above = sent_along(x_fwd, "dp")
+    gate_across = after(gate_across, from_below[0], from_above[0])
+    up_across = after(up_across, from_below[1], from_above[1])
+    down_across = after(down_across, from_below[2], from_above[2])
+    gates = neighbours(gate, gate_across)
+    ups = neighbours(up, up_across)
+    downs = neighbours(down, down_across)
+
+    partial_fwd = forward_call(
+        mask_fwd.reshape(count * tokens_here, 1), x_fwd, from_below, from_above, gates, ups, downs
+    )
+    home_fwd = list(steps_home(partial_fwd, "dp"))
+    scaled_last = lax.all_gather(after(scaled_last, bundle), "dp")
+    bundle = after(bundle, *home_fwd[0])
+    c, e = gates_call(at, bundle, 0, tokens_here, gates, ups)
+    c = after(c, *home_fwd[1])
+    mask_early = mask_bwd[:, :early].reshape(count * early, 1)
+    blocks_early = backward_call(
+        at, mask_early, bundle, tokens_here, early, 0, c, e, downs, gates, ups
+    )
+    home_early = list(steps_home(blocks_early, "dp"))
+    total_fwd = summed(partial_fwd[0], home_fwd[-1])
+    layer_out = (x_forward[0].astype(F32) + prob_forward[0][:, None] * total_fwd).astype(BF16)
+    sent_fwd = shifted(layer_out, "pipe", 1)
+
+    mask_last = mask_bwd[:, early:].reshape(count * last, 1)
+    scaled_last = after(scaled_last, *home_early[0], *home_fwd[-1])
+    blocks = backward_call(
+        at, mask_last, scaled_last, 0, last, early // last, c, e, downs, gates, ups
+    )
+    total_early = summed(blocks_early[0], home_early[-1])
+    total_last = sent_home(blocks, "dp")
+    sent_bwd = []
+    for rows, total in ((slice(0, early), total_early), (slice(early, None), total_last)):
+        grad_in = (grad_output[0, rows].astype(F32) + total).astype(BF16)
+        sent_bwd.append(shifted(grad_in, "pipe", -1))
+    return (sent_fwd[None], jnp.concatenate(sent_bwd, axis=0)[None])
 
 
 def from_partner(block, axis, stride):

time: 435 us -> 418 us (0.961)
  blocking collectives: 9.13 us -> 28.2 us
  waiting for transfers between devices: 259 us -> 245 us
  local copies, waits for them, and re-layouts: 15.2 us -> 6.99 us
  other arithmetic: 12.7 us -> 8.24 us
    ppermute x18, waiting for transfers between devices: 94.7 us -> 218 us  [the longest x3 131 us: sent_along(): from_below.append(lax.ppermute(from_below[-1], axis, up))]
    ppermute x9, waiting for transfers between devices: 115 us -> 8.09 us  [flipped(): return lax.ppermute(block, axis, route)]
    all_gather x4 -> x1, waiting for transfers between devices: 28.6 us -> 0.01 us  [few_experts(): bundle = lax.all_gather(bundle, 'dp')]
    all_gather x1, blocking collectives: 9.13 us -> 28.2 us  [few_experts(): scaled_last = lax.all_gather(after(scaled_last, bundle), 'dp')]
    ppermute x18, starting transfers between devices: 52.6 us -> 40.1 us  [the longest x6 13.1 us: steps_home(): lax.ppermute(to_down, axis, [(i, i - 1) for i in range(count - step, coun...]
    ppermute x3 -> x9, starting transfers between devices: 2.99 us -> 11.2 us  [shifted(): lax.ppermute(block, axis, [((i - distance) % count, i) for i in range(cou...]
    convert_element_type x12 -> x10, other arithmetic: 10.6 us -> 4.48 us  [the longest x4 3.19 us: steps_home(): to_up = (to_up.astype(F32) + up.astype(F32)).astype(BF16)]
    dynamic_slice x3 -> x0, local copies, waits for them, and re-layouts: 6.02 us -> none  [block(): return lax.dynamic_slice_in_dim(partial, start, rows, 0).astype(F32)]
  transfers between devices with their start and end apart: 34 -> 37, of which waited for: 13 -> 19; matrix products, arithmetic and copies ran while one was open for 5% -> 2% of each run, Pallas kernels for 14% -> 10%
where the time goes in v2:
time: 418 us; the launch traced here: 415 us
  waiting for transfers between devices  245 us (59%)
  starting transfers between devices  56.2 us (13%)
  Pallas kernels  55.9 us (13%)
  blocking collectives  28.2 us (7%)
  between operations  14.6 us (3%)
  other arithmetic  8.24 us (2%)
  local copies, waits for them, and re-layouts  6.99 us (2%)
    ppermute x3, waiting for transfers between devices, sent_along(): from_below.append(lax.ppermute(from_below[-1], axis, up))  131 us
    ppermute x6, waiting for transfers between devices, steps_home(): lax.ppermute(to_down, axis, [(i, i - 1) for i in range(count - step, coun...  70.9 us
    pallas_call x2, Pallas kernels, backward_call(): pl.pallas_call(functools.partial(backward_kernel, count, len(scaled_specs...  30.7 us
    all_gather x1, blocking collectives, few_experts(): scaled_last = lax.all_gather(after(scaled_last, bundle), 'dp')  28.2 us
    ppermute x9, waiting for transfers between devices, shifted(): lax.ppermute(block, axis, [((i - distance) % count, i) for i in range(cou...  18.8 us
    pallas_call x1, Pallas kernels, forward_call(): pl.pallas_call(functools.partial(forward_kernel, count, pieces, steps), g...  15.8 us
    ppermute x6, starting transfers between devices, steps_home(): lax.ppermute(to_down, axis, [(i, i - 1) for i in range(count - step, coun...  13.1 us
    ppermute x9, starting transfers between devices, shifted(): lax.ppermute(block, axis, [((i - distance) % count, i) for i in range(cou...  11.2 us
  transfers between devices with their start and end apart: 37, of which 19 were waited for; matrix products, arithmetic and copies ran while one was open for 2% of the time, Pallas kernels for 10%

profile of v2, /device:TPU:20, one launch (start us, length us, event | category | flops | bytes accessed | tf_op | source)
XLA Modules:
  0.0 415.4 jit_solution(12934779448571866341)
XLA Ops:
  7.2 1.5 fusion.2
  9.6 1.3 pad_maximum_fusion
  11.2 3.5 collective-permute-start.3
  14.7 2.4 collective-permute-start.6
  17.0 1.6 collective-permute-start.10
  18.6 42.3 %collective-permute-done.3.refs_0_ = bf16[64,7168]{1,0:T(8,128)(2,1)S(1)} collective-permute-done((bf16[64,7168]{1,0:T(8,128)(2,1)S(1)}, bf16[64,7168]{1,0:T(8,128)(2,1)S(1)}, u32[]{:S(2)}, u32[]{:S(2)}) %collective-permute-start.3) | collective-permute-done | bytes 917536 | tf_op jit(solution)/shard_map/ppermute | solution.py:264
  60.9 4.4 %collective-permute-start.4 = (bf16[64,7168]{1,0:T(8,128)(2,1)S(1)}, bf16[64,7168]{1,0:T(8,128)(2,1)S(1)}, u32[]{:S(2)}, u32[]{:S(2)}) collective-permute-start(bf16[64,7168]{1,0:T(8,128)(2,1)S(1)} %collective-permute-done.3.refs_0_), channel_id=1, source_target_pairs={{1,2},{2,3},{5,6},{6,7},{9,10},{10,11},{13,14},{14,15},{17,18},{18... | collective-permute-start | bytes 2752520 | tf_op jit(solution)/shard_map/ppermute | solution.py:264
  65.2 1.6 collective-permute-start.13
  67.3 1.4 collective-permute-done.6.refs_3_
  68.7 4.4 %collective-permute-start.7 = (bf16[64,7168]{1,0:T(8,128)(2,1)S(1)}, bf16[64,7168]{1,0:T(8,128)(2,1)S(1)}, u32[]{:S(2)}, u32[]{:S(2)}) collective-permute-start(bf16[64,7168]{1,0:T(8,128)(2,1)S(1)} %collective-permute-done.6.refs_3_), channel_id=1, source_target_pairs={{1,0},{2,1},{5,4},{6,5},{9,8},{10,9},{13,12},{14,13},{17,16},{18,1... | collective-permute-start | bytes 2752520 | tf_op jit(solution)/shard_map/ppermute | solution.py:265
  73.2 62.2 %collective-permute-done.4.refs_1_ = bf16[64,7168]{1,0:T(8,128)(2,1)S(1)} collective-permute-done((bf16[64,7168]{1,0:T(8,128)(2,1)S(1)}, bf16[64,7168]{1,0:T(8,128)(2,1)S(1)}, u32[]{:S(2)}, u32[]{:S(2)}) %collective-permute-start.4) | collective-permute-done | bytes 917536 | tf_op jit(solution)/shard_map/ppermute | solution.py:264
  135.4 8.9 %collective-permute-done.7.refs_4_ = bf16[64,7168]{1,0:T(8,128)(2,1)S(1)} collective-permute-done((bf16[64,7168]{1,0:T(8,128)(2,1)S(1)}, bf16[64,7168]{1,0:T(8,128)(2,1)S(1)}, u32[]{:S(2)}, u32[]{:S(2)}) %collective-permute-start.7) | collective-permute-done | bytes 917536 | tf_op jit(solution)/shard_map/ppermute | solution.py:265
  144.3 1.3 collective-permute-start.5
  146.5 3.9 collective-permute-start.1
  150.4 26.4 %collective-permute-done.5.refs_2_ = bf16[64,7168]{1,0:T(8,128)(2,1)S(1)} collective-permute-done((bf16[64,7168]{1,0:T(8,128)(2,1)S(1)}, bf16[64,7168]{1,0:T(8,128)(2,1)S(1)}, u32[]{:S(2)}, u32[]{:S(2)}) %collective-permute-start.5) | collective-permute-done | bytes 917536 | tf_op jit(solution)/shard_map/ppermute | solution.py:264
  177.5 3.3 collective-permute-done
  180.9 1.2 copy-done.1
  183.7 5.2 %collective-permute-done.11.refs_9_.refs_7_.refs_19_.refs_11_ = bf16[7168,128]{1,0:T(8,128)(2,1)} collective-permute-done((bf16[7168,128]{1,0:T(8,128)(2,1)}, bf16[7168,128]{1,0:T(8,128)(2,1)}, u32[]{:S(2)}, u32[]{:S(2)}) %collective-permute-start.11) | collective-permute-done | bytes 1835040 | tf_op jit(solution)/shard_map/ppermute | solution.py:24
  188.9 2.6 collective-permute-done.14.refs_13_.refs_11_.refs_23_.refs_15_
  191.5 1.3 copy-done.2
  192.8 15.8 %shard_map.113 = (f32[64,7168]{1,0:T(8,128)}, bf16[64,7168]{1,0:T(8,128)(2,1)}, bf16[64,7168]{1,0:T(8,128)(2,1)}, bf16[64,7168]{1,0:T(8,128)(2,1)}) custom-call(f32[256,1]{1,0:T(8,128)} %reshape.33.mask_ref, bf16[64,7168]{1,0:T(8,128)(2,1)} %bitcast.66, bf16[64,7168]{1,0:T(8,128)(2,1)} %copy-done.9, bf16[64,7168]{1,0:T(8,128)(2,1)} %copy-done.11, ...), custom_call_target="tpu_custom_call" | custom-call | flops 5637144576 | bytes 33030144 | tf_op jit(solution)/shard_map/pallas_call | solution.py:230
  209.3 1.3 collective-permute-start.21
  210.6 23.3 %collective-permute-done.21 = bf16[64,7168]{1,0:T(8,128)(2,1)S(1)} collective-permute-done((bf16[64,7168]{1,0:T(8,128)(2,1)}, bf16[64,7168]{1,0:T(8,128)(2,1)S(1)}, u32[]{:S(2)}, u32[]{:S(2)}) %collective-permute-start.21) | collective-permute-done | bytes 917536 | tf_op jit(solution)/shard_map/ppermute | solution.py:278
  233.9 2.5 fusion
  236.4 4.5 %collective-permute-start.22 = (bf16[64,7168]{1,0:T(8,128)(2,1)}, bf16[64,7168]{1,0:T(8,128)(2,1)S(1)}, u32[]{:S(2)}, u32[]{:S(2)}) collective-permute-start(bf16[64,7168]{1,0:T(8,128)(2,1)} %get-tuple-element.53), channel_id=1, source_target_pairs={{2,1},{3,2},{6,5},{7,6},{10,9},{11,10},{14,13},{15,14},{18,17},{19... | collective-permute-start | bytes 2752520 | tf_op jit(solution)/shard_map/ppermute | solution.py:278
  241.0 1.3 collective-permute-start.19
  243.8 9.4 %shard_map.114 = (f32[4,64,512]{2,1,0:T(8,128)}, f32[4,64,512]{2,1,0:T(8,128)}) custom-call(s32[1]{0:T(128)} %bitcast.16.at_ref, bf16[4,112,7168]{2,1,0:T(8,128)(2,1)} %bitcast.29, bf16[4,112,7168]{2,1,0:T(8,128)(2,1)} %bitcast.30, bf16[4,112,7168]{2,1,0:T(8,128)(2,1)} %bitcast.31, bf16[4,112,7168]{2,1,0:T(8,128)(2,1)} %bitcast.32, ...), custom_call_target="tpu_custom_call" | custom-call | flops 3758096384 | bytes 18350080 | tf_op jit(solution)/shard_map/pallas_call | solution.py:95
  253.2 7.2 %collective-permute-done.22 = bf16[64,7168]{1,0:T(8,128)(2,1)S(1)} collective-permute-done((bf16[64,7168]{1,0:T(8,128)(2,1)}, bf16[64,7168]{1,0:T(8,128)(2,1)S(1)}, u32[]{:S(2)}, u32[]{:S(2)}) %collective-permute-start.22) | collective-permute-done | bytes 917536 | tf_op jit(solution)/shard_map/ppermute | solution.py:278
  260.5 3.8 collective-permute-done.19
  264.3 16.3 %shard_map.115 = (f32[48,7168]{1,0:T(8,128)}, bf16[48,7168]{1,0:T(8,128)(2,1)}, bf16[48,7168]{1,0:T(8,128)(2,1)}, bf16[48,7168]{1,0:T(8,128)(2,1)}) custom-call(s32[1]{0:T(128)} %bitcast.16.at_ref, f32[192,1]{1,0:T(8,128)} %reshape.34.mask_ref, f32[4,64,512]{2,1,0:T(8,128)} %get-tuple-element.39.c_ref, f32[4,64,512]{2,1,0:T(8,128)} %get-tuple-element.40.e_ref, ...), custom_call_target="tpu_custom_call" | custom-call | flops 4227858432 | bytes 27525120 | tf_op jit(solution)/shard_map/pallas_call | solution.py:156
  281.4 1.3 collective-permute-start.28
  283.0 2.1 collective-permute-start.23
  285.0 16.9 %collective-permute-done.28 = bf16[48,7168]{1,0:T(8,128)(2,1)S(1)} collective-permute-done((bf16[48,7168]{1,0:T(8,128)(2,1)}, bf16[48,7168]{1,0:T(8,128)(2,1)S(1)}, u32[]{:S(2)}, u32[]{:S(2)}) %collective-permute-start.28) | collective-permute-done | bytes 688160 | tf_op jit(solution)/shard_map/ppermute | solution.py:278
  302.2 2.1 collective-permute-start.29
  304.5 4.0 collective-permute-start.20
  308.5 1.6 collective-permute-start.26
  310.1 23.4 %collective-permute-done.29 = bf16[48,7168]{1,0:T(8,128)(2,1)S(1)} collective-permute-done((bf16[48,7168]{1,0:T(8,128)(2,1)S(1)}, bf16[48,7168]{1,0:T(8,128)(2,1)S(1)}, u32[]{:S(2)}, u32[]{:S(2)}) %collective-permute-start.29) | collective-permute-done | bytes 688160 | tf_op jit(solution)/shard_map/ppermute | solution.py:278
  333.7 1.9 collective-permute-start.30
  335.6 2.6 collective-permute-done.26
  338.4 1.9 collective-permute-start.27
  341.4 28.2 %all-gather.1 = bf16[64,7168]{1,0:T(8,128)(2,1)} all-gather(bf16[16,7168]{1,0:T(8,128)(2,1)S(1)} %slice-done), channel_id=3, replica_groups=mesh['pipe'=2,'expert'=4,'dp'=4] {'dp'}, dimensions={0}, use_global_device_ids=true | all-gather | bytes 1146880 | tf_op jit(solution)/shard_map/all_gather | solution.py:342
  369.7 14.4 %shard_map.116 = (f32[16,7168]{1,0:T(8,128)}, bf16[16,7168]{1,0:T(8,128)(2,1)}, bf16[16,7168]{1,0:T(8,128)(2,1)}, bf16[16,7168]{1,0:T(8,128)(2,1)}) custom-call(s32[1]{0:T(128)} %bitcast.16.at_ref, f32[64,1]{1,0:T(8,128)} %reshape.35.mask_ref, f32[4,64,512]{2,1,0:T(8,128)} %get-tuple-element.39.c_ref, f32[4,64,512]{2,1,0:T(8,128)} %get-tuple-element.40.e_ref, ...), custom_call_target="tpu_custom_call" | custom-call | flops 1409286144 | bytes 23855104 | tf_op jit(solution)/shard_map/pallas_call | solution.py:156
  384.1 2.0 collective-permute-start.34
  386.1 3.6 collective-permute-start.33
  391.5 6.5 %collective-permute-done.33 = bf16[16,7168]{1,0:T(8,128)(2,1)S(1)} collective-permute-done((bf16[16,7168]{1,0:T(8,128)(2,1)}, bf16[16,7168]{1,0:T(8,128)(2,1)S(1)}, u32[]{:S(2)}, u32[]{:S(2)}) %collective-permute-start.33) | collective-permute-done | bytes 229408 | tf_op jit(solution)/shard_map/ppermute | solution.py:29
  397.9 2.5 collective-permute-done.32
  401.1 5.5 %collective-permute-done.35 = bf16[16,7168]{1,0:T(8,128)(2,1)S(1)} collective-permute-done((bf16[16,7168]{1,0:T(8,128)(2,1)S(1)}, bf16[16,7168]{1,0:T(8,128)(2,1)S(1)}, u32[]{:S(2)}, u32[]{:S(2)}) %collective-permute-start.35) | collective-permute-done | bytes 229408 | tf_op jit(solution)/shard_map/ppermute | solution.py:29
  406.7 1.0 maximum_bitcast_fusion
  (106 shorter events, 13.4 us)
Async XLA Ops:
  7.2 236.7 %all-gather.4.cloned.1.call-start = ((), (), s32[]{:S(2)}) async-start(), calls=%async_computation | async-start | bytes 8028160 | tf_op jit(solution)/shard_map/all_gather | solution.py:320
  11.2 49.7 %collective-permute-start.3 = (bf16[64,7168]{1,0:T(8,128)(2,1)S(1)}, bf16[64,7168]{1,0:T(8,128)(2,1)S(1)}, u32[]{:S(2)}, u32[]{:S(2)}) collective-permute-start(bf16[64,7168]{1,0:T(8,128)(2,1)S(1)} %bitcast.67), channel_id=1, source_target_pairs={{0,1},{1,2},{2,3},{4,5},{5,6},{6,7},{8,9},{9,10},{10,11},{12,13},{... | collective-permute-start | bytes 2752520 | tf_op jit(solution)/shard_map/ppermute | solution.py:264
  14.7 54.1 %collective-permute-start.6 = (bf16[64,7168]{1,0:T(8,128)(2,1)S(1)}, bf16[64,7168]{1,0:T(8,128)(2,1)S(1)}, u32[]{:S(2)}, u32[]{:S(2)}) collective-permute-start(bf16[64,7168]{1,0:T(8,128)(2,1)S(1)} %bitcast.68), channel_id=1, source_target_pairs={{1,0},{2,1},{3,2},{5,4},{6,5},{7,6},{9,8},{10,9},{11,10},{13,12},{... | collective-permute-start | bytes 2752520 | tf_op jit(solution)/shard_map/ppermute | solution.py:265
  17.0 128.6 %collective-permute-start.10 = (bf16[7168,128]{1,0:T(8,128)(2,1)S(1)}, bf16[7168,128]{1,0:T(8,128)(2,1)}, u32[]{:S(2)}, u32[]{:S(2)}) collective-permute-start(bf16[7168,128]{1,0:T(8,128)(2,1)S(1)} %bitcast.49), channel_id=1, source_target_pairs={{0,8},{4,12},{8,0},{12,4},{1,9},{5,13},{9,1},{13,5},{2,10},{6,14},... | collective-permute-start | bytes 5505032 | tf_op jit(solution)/shard_map/ppermute | solution.py:24
  60.9 74.5 %collective-permute-start.4 = (bf16[64,7168]{1,0:T(8,128)(2,1)S(1)}, bf16[64,7168]{1,0:T(8,128)(2,1)S(1)}, u32[]{:S(2)}, u32[]{:S(2)}) collective-permute-start(bf16[64,7168]{1,0:T(8,128)(2,1)S(1)} %collective-permute-done.3.refs_0_), channel_id=1, source_target_pairs={{1,2},{2,3},{5,6},{6,7},{9,10},{10,11},{13,14},{14,15},{17,18},{18... | collective-permute-start | bytes 2752520 | tf_op jit(solution)/shard_map/ppermute | solution.py:264
  65.2 81.1 %collective-permute-start.13 = (bf16[7168,128]{1,0:T(8,128)(2,1)}, bf16[7168,128]{1,0:T(8,128)(2,1)}, u32[]{:S(2)}, u32[]{:S(2)}) collective-permute-start(bf16[7168,128]{1,0:T(8,128)(2,1)} %bitcast.51), channel_id=1, source_target_pairs={{0,8},{4,12},{8,0},{12,4},{1,9},{5,13},{9,1},{13,5},{2,10},{6,14},... | collective-permute-start | bytes 5505032 | tf_op jit(solution)/shard_map/ppermute | solution.py:24
  66.8 79.6 %collective-permute-start.16 = (bf16[128,7168]{1,0:T(8,128)(2,1)}, bf16[128,7168]{1,0:T(8,128)(2,1)}, u32[]{:S(2)}, u32[]{:S(2)}) collective-permute-start(bf16[128,7168]{1,0:T(8,128)(2,1)} %bitcast.61), channel_id=1, source_target_pairs={{0,8},{4,12},{8,0},{12,4},{1,9},{5,13},{9,1},{13,5},{2,10},{6,14},... | collective-permute-start | bytes 5505032 | tf_op jit(solution)/shard_map/ppermute | solution.py:24
  68.7 113.9 %copy-start.10 = (bf16[64,7168]{1,0:T(8,128)(2,1)}, bf16[64,7168]{1,0:T(8,128)(2,1)S(1)}, u32[]{:S(2)}) copy-start(bf16[64,7168]{1,0:T(8,128)(2,1)S(1)} %collective-permute-done.6.refs_3_) | copy-start | bytes 2752516
  68.7 75.6 %collective-permute-start.7 = (bf16[64,7168]{1,0:T(8,128)(2,1)S(1)}, bf16[64,7168]{1,0:T(8,128)(2,1)S(1)}, u32[]{:S(2)}, u32[]{:S(2)}) collective-permute-start(bf16[64,7168]{1,0:T(8,128)(2,1)S(1)} %collective-permute-done.6.refs_3_), channel_id=1, source_target_pairs={{1,0},{2,1},{5,4},{6,5},{9,8},{10,9},{13,12},{14,13},{17,16},{18,1... | collective-permute-start | bytes 2752520 | tf_op jit(solution)/shard_map/ppermute | solution.py:265
  135.4 47.2 %copy-start.11 = (bf16[64,7168]{1,0:T(8,128)(2,1)}, bf16[64,7168]{1,0:T(8,128)(2,1)S(1)}, u32[]{:S(2)}) copy-start(bf16[64,7168]{1,0:T(8,128)(2,1)S(1)} %collective-permute-done.4.refs_1_) | copy-start | bytes 2752516
  135.4 45.5 %collective-permute-start.9 = (bf16[7168,128]{1,0:T(8,128)(2,1)S(1)}, bf16[7168,128]{1,0:T(8,128)(2,1)S(1)}, u32[]{:S(2)}, u32[]{:S(2)}) collective-permute-start(bf16[7168,128]{1,0:T(8,128)(2,1)S(1)} %bitcast.50), channel_id=1, source_target_pairs={{0,4},{4,0},{8,12},{12,8},{1,5},{5,1},{9,13},{13,9},{2,6},{6,2},{1... | collective-permute-start | bytes 5505032 | tf_op jit(solution)/shard_map/ppermute | solution.py:24
  144.3 47.2 %copy-start.12 = (bf16[64,7168]{1,0:T(8,128)(2,1)}, bf16[64,7168]{1,0:T(8,128)(2,1)S(1)}, u32[]{:S(2)}) copy-start(bf16[64,7168]{1,0:T(8,128)(2,1)S(1)} %collective-permute-done.7.refs_4_) | copy-start | bytes 2752516
  144.3 32.5 %collective-permute-start.5 = (bf16[64,7168]{1,0:T(8,128)(2,1)S(1)}, bf16[64,7168]{1,0:T(8,128)(2,1)S(1)}, u32[]{:S(2)}, u32[]{:S(2)}) collective-permute-start(bf16[64,7168]{1,0:T(8,128)(2,1)S(1)} %collective-permute-done.4.refs_1_), channel_id=1, source_target_pairs={{2,3},{6,7},{10,11},{14,15},{18,19},{22,23},{26,27},{30,31}} | collective-permute-start | bytes 2752520 | tf_op jit(solution)/shard_map/ppermute | solution.py:264
  145.7 31.2 %collective-permute-start.8 = (bf16[64,7168]{1,0:T(8,128)(2,1)S(1)}, bf16[64,7168]{1,0:T(8,128)(2,1)S(1)}, u32[]{:S(2)}, u32[]{:S(2)}) collective-permute-start(bf16[64,7168]{1,0:T(8,128)(2,1)S(1)} %collective-permute-done.7.refs_4_), channel_id=1, source_target_pairs={{1,0},{5,4},{9,8},{13,12},{17,16},{21,20},{25,24},{29,28}} | collective-permute-start | bytes 2752520 | tf_op jit(solution)/shard_map/ppermute | solution.py:265
  146.4 30.5 %collective-permute-start.2 = (s32[64,2]{0,1:T(2,128)S(1)}, s32[64,2]{0,1:T(2,128)S(1)}, u32[]{:S(2)}, u32[]{:S(2)}) collective-permute-start(s32[64,2]{0,1:T(2,128)S(1)} %pad_add_fusion), channel_id=1, source_target_pairs={{3,0},{0,1},{1,2},{2,3},{7,4},{4,5},{5,6},{6,7},{11,8},{8,9},{9,10... | collective-permute-start | bytes 1544 | tf_op jit(solution)/shard_map/ppermute | solution.py:29
  146.5 31.0 %collective-permute-start.1 = (s32[64,2]{0,1:T(2,128)S(1)}, s32[64,2]{0,1:T(2,128)S(1)}, u32[]{:S(2)}, u32[]{:S(2)}) collective-permute-start(s32[64,2]{0,1:T(2,128)S(1)} %pad_add_fusion), channel_id=1, source_target_pairs={{2,0},{3,1},{0,2},{1,3},{6,4},{7,5},{4,6},{5,7},{10,8},{11,9},{8,1... | collective-permute-start | bytes 1544 | tf_op jit(solution)/shard_map/ppermute | solution.py:29
  176.8 4.0 collective-permute-start
  176.8 6.6 %collective-permute-start.12 = (bf16[7168,128]{1,0:T(8,128)(2,1)}, bf16[7168,128]{1,0:T(8,128)(2,1)}, u32[]{:S(2)}, u32[]{:S(2)}) collective-permute-start(bf16[7168,128]{1,0:T(8,128)(2,1)} %bitcast.52), channel_id=1, source_target_pairs={{0,4},{4,0},{8,12},{12,8},{1,5},{5,1},{9,13},{13,9},{2,6},{6,2},{1... | collective-permute-start | bytes 5505032 | tf_op jit(solution)/shard_map/ppermute | solution.py:24
  176.9 6.7 %collective-permute-start.15 = (bf16[128,7168]{1,0:T(8,128)(2,1)}, bf16[128,7168]{1,0:T(8,128)(2,1)}, u32[]{:S(2)}, u32[]{:S(2)}) collective-permute-start(bf16[128,7168]{1,0:T(8,128)(2,1)} %bitcast.62), channel_id=1, source_target_pairs={{0,4},{4,0},{8,12},{12,8},{1,5},{5,1},{9,13},{13,9},{2,6},{6,2},{1... | collective-permute-start | bytes 5505032 | tf_op jit(solution)/shard_map/ppermute | solution.py:24
  177.4 11.5 %collective-permute-start.11 = (bf16[7168,128]{1,0:T(8,128)(2,1)}, bf16[7168,128]{1,0:T(8,128)(2,1)}, u32[]{:S(2)}, u32[]{:S(2)}) collective-permute-start(bf16[7168,128]{1,0:T(8,128)(2,1)} %collective-permute-done.10.refs_8_.refs_6_.refs_18_.refs_10_), channel_id=1, source_target_pairs={{0,4},{4,0},{8,12},{12,8},{1,5},{5,1},{9,13},{13,9},{2,6},{6,2},{1... | collective-permute-start | bytes 5505032 | tf_op jit(solution)/shard_map/ppermute | solution.py:24
  180.9 10.7 %collective-permute-start.14 = (bf16[7168,128]{1,0:T(8,128)(2,1)}, bf16[7168,128]{1,0:T(8,128)(2,1)}, u32[]{:S(2)}, u32[]{:S(2)}) collective-permute-start(bf16[7168,128]{1,0:T(8,128)(2,1)} %collective-permute-done.13.refs_12_.refs_10_.refs_22_.refs_14_), channel_id=1, source_target_pairs={{0,4},{4,0},{8,12},{12,8},{1,5},{5,1},{9,13},{13,9},{2,6},{6,2},{1... | collective-permute-start | bytes 5505032 | tf_op jit(solution)/shard_map/ppermute | solution.py:24
  182.1 9.4 %collective-permute-start.17 = (bf16[128,7168]{1,0:T(8,128)(2,1)}, bf16[128,7168]{1,0:T(8,128)(2,1)S(1)}, u32[]{:S(2)}, u32[]{:S(2)}) collective-permute-start(bf16[128,7168]{1,0:T(8,128)(2,1)} %collective-permute-done.16.refs_16_.refs_14_.refs_6_), channel_id=1, source_target_pairs={{0,4},{4,0},{8,12},{12,8},{1,5},{5,1},{9,13},{13,9},{2,6},{6,2},{1... | collective-permute-start | bytes 5505032 | tf_op jit(solution)/shard_map/ppermute | solution.py:24
  208.6 2.0 collective-permute-start.18
  209.3 24.6 %collective-permute-start.21 = (bf16[64,7168]{1,0:T(8,128)(2,1)}, bf16[64,7168]{1,0:T(8,128)(2,1)S(1)}, u32[]{:S(2)}, u32[]{:S(2)}) collective-permute-start(bf16[64,7168]{1,0:T(8,128)(2,1)} %get-tuple-element.33), channel_id=1, source_target_pairs={{3,2},{7,6},{11,10},{15,14},{19,18},{23,22},{27,26},{31,30}} | collective-permute-start | bytes 2752520 | tf_op jit(solution)/shard_map/ppermute | solution.py:278
  236.4 24.0 %collective-permute-start.22 = (bf16[64,7168]{1,0:T(8,128)(2,1)}, bf16[64,7168]{1,0:T(8,128)(2,1)S(1)}, u32[]{:S(2)}, u32[]{:S(2)}) collective-permute-start(bf16[64,7168]{1,0:T(8,128)(2,1)} %get-tuple-element.53), channel_id=1, source_target_pairs={{2,1},{3,2},{6,5},{7,6},{10,9},{11,10},{14,13},{15,14},{18,17},{19... | collective-permute-start | bytes 2752520 | tf_op jit(solution)/shard_map/ppermute | solution.py:278
  241.0 23.3 %collective-permute-start.19 = (bf16[64,7168]{1,0:T(8,128)(2,1)S(1)}, bf16[64,7168]{1,0:T(8,128)(2,1)S(1)}, u32[]{:S(2)}, u32[]{:S(2)}) collective-permute-start(bf16[64,7168]{1,0:T(8,128)(2,1)S(1)} %get-tuple-element.52), channel_id=1, source_target_pairs={{0,1},{1,2},{4,5},{5,6},{8,9},{9,10},{12,13},{13,14},{16,17},{17,1... | collective-permute-start | bytes 2752520 | tf_op jit(solution)/shard_map/ppermute | solution.py:277
  280.6 21.3 %copy-start.20 = (bf16[48,7168]{1,0:T(8,128)(2,1)S(1)}, bf16[48,7168]{1,0:T(8,128)(2,1)}, u32[]{:S(2)}) copy-start(bf16[48,7168]{1,0:T(8,128)(2,1)} %get-tuple-element.43) | copy-start | bytes 2064388
  280.6 4.4 %collective-permute-start.25 = (bf16[48,7168]{1,0:T(8,128)(2,1)}, bf16[48,7168]{1,0:T(8,128)(2,1)S(1)}, u32[]{:S(2)}, u32[]{:S(2)}) collective-permute-start(bf16[48,7168]{1,0:T(8,128)(2,1)} %get-tuple-element.44), channel_id=1, source_target_pairs={{0,1},{4,5},{8,9},{12,13},{16,17},{20,21},{24,25},{28,29}} | collective-permute-start | bytes 2064392 | tf_op jit(solution)/shard_map/ppermute | solution.py:277
  281.4 20.5 %collective-permute-start.28 = (bf16[48,7168]{1,0:T(8,128)(2,1)}, bf16[48,7168]{1,0:T(8,128)(2,1)S(1)}, u32[]{:S(2)}, u32[]{:S(2)}) collective-permute-start(bf16[48,7168]{1,0:T(8,128)(2,1)} %get-tuple-element.42), channel_id=1, source_target_pairs={{3,2},{7,6},{11,10},{15,14},{19,18},{23,22},{27,26},{31,30}} | collective-permute-start | bytes 2064392 | tf_op jit(solution)/shard_map/ppermute | solution.py:278
  283.0 21.3 %copy-start.16 = (bf16[64,7168]{1,0:T(8,128)(2,1)S(1)}, bf16[64,7168]{1,0:T(8,128)(2,1)}, u32[]{:S(2)}) copy-start(bf16[64,7168]{1,0:T(8,128)(2,1)} %get-tuple-element.33) | copy-start | bytes 2752516
  283.0 57.4 %collective-permute-start.23 = (bf16[64,7168]{1,0:T(8,128)(2,1)S(1)}, bf16[64,7168]{1,0:T(8,128)(2,1)S(1)}, u32[]{:S(2)}, u32[]{:S(2)}) collective-permute-start(bf16[64,7168]{1,0:T(8,128)(2,1)S(1)} %add_convert_fusion.1), channel_id=1, source_target_pairs={{1,0},{2,1},{3,2},{5,4},{6,5},{7,6},{9,8},{10,9},{11,10},{13,12},{... | collective-permute-start | bytes 2752520 | tf_op jit(solution)/shard_map/ppermute | solution.py:278
  302.2 31.3 %copy-start.19 = (bf16[48,7168]{1,0:T(8,128)(2,1)S(1)}, bf16[48,7168]{1,0:T(8,128)(2,1)}, u32[]{:S(2)}) copy-start(bf16[48,7168]{1,0:T(8,128)(2,1)} %get-tuple-element.44) | copy-start | bytes 2064388
  302.2 36.0 %copy-start.18 = (bf16[48,7168]{1,0:T(8,128)(2,1)S(1)}, bf16[48,7168]{1,0:T(8,128)(2,1)}, u32[]{:S(2)}) copy-start(bf16[48,7168]{1,0:T(8,128)(2,1)} %get-tuple-element.42) | copy-start | bytes 2064388
  302.2 31.3 %collective-permute-start.29 = (bf16[48,7168]{1,0:T(8,128)(2,1)S(1)}, bf16[48,7168]{1,0:T(8,128)(2,1)S(1)}, u32[]{:S(2)}, u32[]{:S(2)}) collective-permute-start(bf16[48,7168]{1,0:T(8,128)(2,1)S(1)} %get-tuple-element.55), channel_id=1, source_target_pairs={{2,1},{3,2},{6,5},{7,6},{10,9},{11,10},{14,13},{15,14},{18,17},{19... | collective-permute-start | bytes 2064392 | tf_op jit(solution)/shard_map/ppermute | solution.py:278
  304.5 35.8 %collective-permute-start.20 = (bf16[64,7168]{1,0:T(8,128)(2,1)S(1)}, bf16[64,7168]{1,0:T(8,128)(2,1)S(1)}, u32[]{:S(2)}, u32[]{:S(2)}) collective-permute-start(bf16[64,7168]{1,0:T(8,128)(2,1)S(1)} %add_convert_fusion.2), channel_id=1, source_target_pairs={{0,1},{1,2},{2,3},{4,5},{5,6},{6,7},{8,9},{9,10},{10,11},{12,13},{... | collective-permute-start | bytes 2752520 | tf_op jit(solution)/shard_map/ppermute | solution.py:277
  308.5 31.9 %copy-start.4 = (bf16[1,64,7168]{2,1,0:T(8,128)(2,1)S(1)}, bf16[1,64,7168]{2,1,0:T(8,128)(2,1)}, u32[]{:S(2)}) copy-start(bf16[1,64,7168]{2,1,0:T(8,128)(2,1)} %param.10) | copy-start | bytes 2752516
  308.5 31.8 %copy-start.7 = (f32[64,7168]{1,0:T(8,128)S(1)}, f32[64,7168]{1,0:T(8,128)}, u32[]{:S(2)}) copy-start(f32[64,7168]{1,0:T(8,128)} %get-tuple-element.32) | copy-start | bytes 5505028
  308.5 31.8 %copy-start.22 = (f32[1,64]{1,0:T(1,128)S(1)}, f32[1,64]{1,0:T(1,128)}, u32[]{:S(2)}) copy-start(f32[1,64]{1,0:T(1,128)} %param.12) | copy-start | bytes 772
  308.5 29.7 %collective-permute-start.26 = (bf16[48,7168]{1,0:T(8,128)(2,1)S(1)}, bf16[48,7168]{1,0:T(8,128)(2,1)S(1)}, u32[]{:S(2)}, u32[]{:S(2)}) collective-permute-start(bf16[48,7168]{1,0:T(8,128)(2,1)S(1)} %get-tuple-element.54), channel_id=1, source_target_pairs={{0,1},{1,2},{4,5},{5,6},{8,9},{9,10},{12,13},{13,14},{16,17},{17,1... | collective-permute-start | bytes 2064392 | tf_op jit(solution)/shard_map/ppermute | solution.py:277
  333.7 55.9 %collective-permute-start.30 = (bf16[48,7168]{1,0:T(8,128)(2,1)S(1)}, bf16[48,7168]{1,0:T(8,128)(2,1)S(1)}, u32[]{:S(2)}, u32[]{:S(2)}) collective-permute-start(bf16[48,7168]{1,0:T(8,128)(2,1)S(1)} %add_convert_fusion.3), channel_id=1, source_target_pairs={{1,0},{2,1},{3,2},{5,4},{6,5},{7,6},{9,8},{10,9},{11,10},{13,12},{... | collective-permute-start | bytes 2064392 | tf_op jit(solution)/shard_map/ppermute | solution.py:278
  338.4 51.3 %collective-permute-start.27 = (bf16[48,7168]{1,0:T(8,128)(2,1)S(1)}, bf16[48,7168]{1,0:T(8,128)(2,1)S(1)}, u32[]{:S(2)}, u32[]{:S(2)}) collective-permute-start(bf16[48,7168]{1,0:T(8,128)(2,1)S(1)} %add_convert_fusion.4), channel_id=1, source_target_pairs={{0,1},{1,2},{2,3},{4,5},{5,6},{6,7},{8,9},{9,10},{10,11},{12,13},{... | collective-permute-start | bytes 2064392 | tf_op jit(solution)/shard_map/ppermute | solution.py:277
  340.9 60.3 %collective-permute-start.24 = (bf16[64,7168]{1,0:T(8,128)(2,1)S(1)}, bf16[64,7168]{1,0:T(8,128)(2,1)S(1)}, u32[]{:S(2)}, u32[]{:S(2)}) collective-permute-start(bf16[64,7168]{1,0:T(8,128)(2,1)S(1)} %add_convert_fusion), channel_id=1, source_target_pairs={{16,0},{0,16},{17,1},{1,17},{18,2},{2,18},{19,3},{3,19},{20,4},{4,... | collective-permute-start | bytes 2752520 | tf_op jit(solution)/shard_map/ppermute | solution.py:29
  369.6 20.0 %copy-start.8 = (f32[48,7168]{1,0:T(8,128)S(1)}, f32[48,7168]{1,0:T(8,128)}, u32[]{:S(2)}) copy-start(f32[48,7168]{1,0:T(8,128)} %get-tuple-element.41) | copy-start | bytes 4128772
  384.1 7.4 %collective-permute-start.34 = (bf16[16,7168]{1,0:T(8,128)(2,1)}, bf16[16,7168]{1,0:T(8,128)(2,1)S(1)}, u32[]{:S(2)}, u32[]{:S(2)}) collective-permute-start(bf16[16,7168]{1,0:T(8,128)(2,1)} %get-tuple-element.51), channel_id=1, source_target_pairs={{1,0},{2,1},{3,2},{0,3},{5,4},{6,5},{7,6},{4,7},{9,8},{10,9},{11,1... | collective-permute-start | bytes 688136 | tf_op jit(solution)/shard_map/ppermute | solution.py:29
  386.1 11.9 %collective-permute-start.33 = (bf16[16,7168]{1,0:T(8,128)(2,1)}, bf16[16,7168]{1,0:T(8,128)(2,1)S(1)}, u32[]{:S(2)}, u32[]{:S(2)}) collective-permute-start(bf16[16,7168]{1,0:T(8,128)(2,1)} %get-tuple-element.50), channel_id=1, source_target_pairs={{2,0},{3,1},{0,2},{1,3},{6,4},{7,5},{4,6},{5,7},{10,8},{11,9},{8,1... | collective-permute-start | bytes 688136 | tf_op jit(solution)/shard_map/ppermute | solution.py:29
  389.6 10.8 %collective-permute-start.32 = (bf16[16,7168]{1,0:T(8,128)(2,1)}, bf16[16,7168]{1,0:T(8,128)(2,1)S(1)}, u32[]{:S(2)}, u32[]{:S(2)}) collective-permute-start(bf16[16,7168]{1,0:T(8,128)(2,1)} %get-tuple-element.49), channel_id=1, source_target_pairs={{3,0},{0,1},{1,2},{2,3},{7,4},{4,5},{5,6},{6,7},{11,8},{8,9},{9,10... | collective-permute-start | bytes 688136 | tf_op jit(solution)/shard_map/ppermute | solution.py:29
  390.0 16.7 %collective-permute-start.31 = (bf16[48,7168]{1,0:T(8,128)(2,1)S(1)}, bf16[48,7168]{1,0:T(8,128)(2,1)S(1)}, u32[]{:S(2)}, u32[]{:S(2)}) collective-permute-start(bf16[48,7168]{1,0:T(8,128)(2,1)S(1)} %fusion.5), channel_id=1, source_target_pairs={{16,0},{0,16},{17,1},{1,17},{18,2},{2,18},{19,3},{3,19},{20,4},{4,... | collective-permute-start | bytes 2064392 | tf_op jit(solution)/shard_map/ppermute | solution.py:29
  400.6 6.1 %collective-permute-start.35 = (bf16[16,7168]{1,0:T(8,128)(2,1)S(1)}, bf16[16,7168]{1,0:T(8,128)(2,1)S(1)}, u32[]{:S(2)}, u32[]{:S(2)}) collective-permute-start(bf16[16,7168]{1,0:T(8,128)(2,1)S(1)} %fusion.6), channel_id=1, source_target_pairs={{16,0},{0,16},{17,1},{1,17},{18,2},{2,18},{19,3},{3,19},{20,4},{4,... | collective-permute-start | bytes 688136 | tf_op jit(solution)/shard_map/ppermute | solution.py:29
  (15 other events, 93.2 us)
Sparse Core Ops, SparseCore 0:
  11.1 148.2 all-gather.3

commit v3 on v2

--- a/solution.py
+++ b/solution.py
@@ -9,8 +9,8 @@
 from jax.sharding import PartitionSpec as P
 
 BF16, F32 = jnp.bfloat16, jnp.float32
-VMEM_LIMIT = 56 * 1024 * 1024
-LAST_ROWS = 16
+VMEM_LIMIT = 20 * 1024 * 1024
+LAST_ROWS = 32
 
 
 def contract_last(left_side, weights):
@@ -88,7 +88,7 @@
 def gates_call(at, x, begin, rows, gates, ups):
     count, _, width = x.shape
     pieces, hid = len(gates), gates[0].shape[1]
-    chunk = chunk_of(width, 1792)
+    chunk = chunk_of(width, 1024)
     hidden = pieces * hid
     x_specs = turned_specs(count, begin, rows, chunk, lambda i: i)
     weight_spec = pl.BlockSpec((chunk, hid), lambda i, at: (i, 0))
@@ -145,7 +145,7 @@
 def backward_call(at, mask, scaled, begin, rows, part, c, e, downs, gates, ups):
     count, _, width = scaled.shape
     pieces, hid = len(gates), gates[0].shape[1]
-    chunk = chunk_of(width, 1792)
+    chunk = chunk_of(width, 1024)
     steps = width // chunk
     hidden = pieces * hid
     first = lambda i: jnp.minimum(i, steps - 1)
@@ -221,7 +221,7 @@
     rows, width = own.shape
     count = len(ups_in) + 1
     pieces, hid = len(gates), gates[0].shape[1]
-    chunk = chunk_of(width, 1792)
+    chunk = chunk_of(width, 1024)
     steps = width // chunk
     hidden = pieces * hid
     first = lambda i: jnp.minimum(i, steps - 1)
@@ -255,28 +255,28 @@
     return lax.optimization_barrier((value,) + earlier)[0]
 
 
-def sent_along(block, axis):
+def hop(below, above, axis, step):
     count = lax.axis_size(axis)
-    from_below, from_above = [block], [block]
-    for step in range(1, count):
-        up = [(i, i + 1) for i in range(step - 1, count - 1)]
-        down = [(i, i - 1) for i in range(1, count - step + 1)]
-        from_below.append(lax.ppermute(from_below[-1], axis, up))
-        from_above.append(lax.ppermute(from_above[-1], axis, down))
-    return from_below[1:], from_above[1:]
+    up = [(i, i + 1) for i in range(step - 1, count - 1)]
+    down = [(i, i - 1) for i in range(1, count - step + 1)]
+    return lax.ppermute(below, axis, up), lax.ppermute(above, axis, down)
 
 
 def steps_home(blocks, axis):
     count = lax.axis_size(axis)
-    up, down = None, None
+    sends, arrivals = [], []
     for step in range(1, count):
-        to_up, to_down = blocks[count - step], blocks[step]
-        if up is not None:
-            to_up = (to_up.astype(F32) + up.astype(F32)).astype(BF16)
-            to_down = (to_down.astype(F32) + down.astype(F32)).astype(BF16)
-        up = lax.ppermute(to_up, axis, [(i, i + 1) for i in range(step)])
-        down = lax.ppermute(to_down, axis, [(i, i - 1) for i in range(count - step, count)])
-        yield up, down
+        pair = (blocks[count - step], blocks[step])
+        if arrivals:
+            pair = tuple(
+                (own.astype(F32) + other.astype(F32)).astype(BF16)
+                for own, other in zip(pair, arrivals[-1])
+            )
+        up = lax.ppermute(pair[0], axis, [(i, i + 1) for i in range(step)])
+        down = lax.ppermute(pair[1], axis, [(i, i - 1) for i in range(count - step, count)])
+        sends.append(pair)
+        arrivals.append((up, down))
+    return sends, arrivals
 
 
 def summed(block, arrived):
@@ -322,42 +322,44 @@
     mine = (routes == expert_here).astype(F32)
     mask_fwd, mask_bwd = mine[:, :, 0:1], mine[:, :, 1:2]
 
-    def neighbours(weight, across):
-        return [weight, flipped(weight, "expert", 1), across, flipped(across, "expert", 1)]
-
-    gate, up, down = w_gate[0, 0], w_up[0, 0], w_down[0, 0]
-    gate_across, up_across, down_across = (flipped(w, "expert", 2) for w in (gate, up, down))
-    from_below, from_above = sent_along(x_fwd, "dp")
-    gate_across = after(gate_across, from_below[0], from_above[0])
-    up_across = after(up_across, from_below[1], from_above[1])
-    down_across = after(down_across, from_below[2], from_above[2])
-    gates = neighbours(gate, gate_across)
-    ups = neighbours(up, up_across)
-    downs = neighbours(down, down_across)
+    own = [w_gate[0, 0], w_up[0, 0], w_down[0, 0]]
+    across = [flipped(weight, "expert", 2) for weight in own]
+    own_flips = [flipped(weight, "expert", 1) for weight in own]
+    x_sent = jnp.where(jnp.min(routes) >= 0, x_fwd, jnp.zeros_like(x_fwd))
+    from_below, from_above = [], []
+    earlier = [[], own_flips, [flipped(across[0], "expert", 1)]]
+    across_flips = [earlier[2][0]] + [flipped(weight, "expert", 1) for weight in across[1:]]
+    below, above = x_sent, x_sent
+    for step in range(1, count):
+        if step > 1:
+            below, above = after(below, *earlier[step - 1]), after(above, *earlier[step - 1])
+        below, above = hop(below, above, "dp", step)
+        from_below.append(below)
+        from_above.append(above)
+    gates, ups, downs = zip(own, own_flips, across, across_flips)
 
     partial_fwd = forward_call(
         mask_fwd.reshape(count * tokens_here, 1), x_fwd, from_below, from_above, gates, ups, downs
     )
-    home_fwd = list(steps_home(partial_fwd, "dp"))
-    scaled_last = lax.all_gather(after(scaled_last, bundle), "dp")
-    bundle = after(bundle, *home_fwd[0])
+    sends_fwd, arrivals_fwd = steps_home(partial_fwd, "dp")
+    scaled_last = lax.all_gather(scaled_last, "dp")
+    bundle = after(bundle, *sends_fwd[1])
     c, e = gates_call(at, bundle, 0, tokens_here, gates, ups)
-    c = after(c, *home_fwd[1])
     mask_early = mask_bwd[:, :early].reshape(count * early, 1)
     blocks_early = backward_call(
         at, mask_early, bundle, tokens_here, early, 0, c, e, downs, gates, ups
     )
-    home_early = list(steps_home(blocks_early, "dp"))
-    total_fwd = summed(partial_fwd[0], home_fwd[-1])
+    sends_early, arrivals_early = steps_home(blocks_early, "dp")
+    total_fwd = summed(partial_fwd[0], arrivals_fwd[-1])
     layer_out = (x_forward[0].astype(F32) + prob_forward[0][:, None] * total_fwd).astype(BF16)
     sent_fwd = shifted(layer_out, "pipe", 1)
 
     mask_last = mask_bwd[:, early:].reshape(count * last, 1)
-    scaled_last = after(scaled_last, *home_early[0], *home_fwd[-1])
+    scaled_last = after(scaled_last, *sends_early[1], *sends_fwd[-1])
     blocks = backward_call(
         at, mask_last, scaled_last, 0, last, early // last, c, e, downs, gates, ups
     )
-    total_early = summed(blocks_early[0], home_early[-1])
+    total_early = summed(blocks_early[0], arrivals_early[-1])
     total_last = sent_home(blocks, "dp")
     sent_bwd = []
     for rows, total in ((slice(0, early), total_early), (slice(early, None), total_last)):

time: 418 us -> 425 us (1.017)
  blocking collectives: 28.2 us -> 0 us
  local copies, waits for them, and re-layouts: 6.99 us -> 29.1 us
  other arithmetic: 8.24 us -> 18.4 us
    ppermute x18, waiting for transfers between devices: 218 us -> 186 us  [the longest x6 118 us: hop(): return (lax.ppermute(below, axis, up), lax.ppermute(above, axis, down))]
    all_gather x1 -> x0, blocking collectives: 28.2 us -> none  [few_experts(): scaled_last = lax.all_gather(after(scaled_last, bundle), 'dp')]
    unnamed x51 -> x91, local copies, waits for them, and re-layouts: 4.58 us -> 27.8 us
    ppermute x9, waiting for transfers between devices: 8.09 us -> 28.2 us  [flipped(): return lax.ppermute(block, axis, route)]
    ppermute x9, waiting for transfers between devices: 18.8 us -> 28.6 us  [shifted(): lax.ppermute(block, axis, [((i - distance) % count, i) for i in range(cou...]
    convert_element_type x6, other arithmetic: 3.56 us -> 9.61 us  [steps_home(): (own.astype(F32) + other.astype(F32)).astype(BF16)]
  transfers between devices with their start and end apart: 37 -> 38, of which waited for: 19 -> 14; matrix products, arithmetic and copies ran while one was open for 2% -> 4% of each run, Pallas kernels for 10% -> 13%
where the time goes in v3:
time: 425 us; the launch traced here: 423 us
  waiting for transfers between devices  243 us (57%)
  starting transfers between devices  58.8 us (14%)
  Pallas kernels  55.5 us (13%)
  local copies, waits for them, and re-layouts  29.1 us (7%)
  other arithmetic  18.4 us (4%)
  between operations  17.3 us (4%)
    ppermute x6, waiting for transfers between devices, hop(): return (lax.ppermute(below, axis, up), lax.ppermute(above, axis, down))  118 us
    ppermute x6, waiting for transfers between devices, steps_home(): lax.ppermute(pair[1], axis, [(i, i - 1) for i in range(count - step, coun...  43.2 us
    pallas_call x2, Pallas kernels, backward_call(): pl.pallas_call(functools.partial(backward_kernel, count, len(scaled_specs...  30.6 us
    ppermute x9, waiting for transfers between devices, shifted(): lax.ppermute(block, axis, [((i - distance) % count, i) for i in range(cou...  28.6 us
    ppermute x9, waiting for transfers between devices, flipped(): return lax.ppermute(block, axis, route)  28.2 us
    unnamed x91, local copies, waits for them, and re-layouts  27.8 us
    ppermute x6, waiting for transfers between devices, steps_home(): up = lax.ppermute(pair[0], axis, [(i, i + 1) for i in range(step)])  25.2 us
    ppermute x6, starting transfers between devices, hop(): return (lax.ppermute(below, axis, up), lax.ppermute(above, axis, down))  18.6 us
  transfers between devices with their start and end apart: 38, of which 14 were waited for; matrix products, arithmetic and copies ran while one was open for 4% of the time, Pallas kernels for 13%

profile of v3, /device:TPU:20, one launch (start us, length us, event | category | flops | bytes accessed | tf_op | source)
XLA Modules:
  0.0 422.5 jit_solution(18431121357919902538)
XLA Ops:
  11.3 1.6 collective-permute-start.2
  12.8 1.9 collective-permute-start.1
  21.8 3.6 collective-permute-start.3
  25.5 63.3 %collective-permute-done.3.refs_0_ = bf16[64,7168]{1,0:T(8,128)(2,1)S(1)} collective-permute-done((bf16[64,7168]{1,0:T(8,128)(2,1)S(1)}, bf16[64,7168]{1,0:T(8,128)(2,1)S(1)}, u32[]{:S(2)}, u32[]{:S(2)}) %collective-permute-start.3) | collective-permute-done | bytes 917536 | tf_op jit(solution)/shard_map/ppermute | solution.py:262
  90.8 1.9 collective-permute-start.11
  94.1 4.0 collective-permute-start.7
  99.0 36.7 %collective-permute-done.11.refs_3_ = bf16[64,7168]{1,0:T(8,128)(2,1)S(1)} collective-permute-done((bf16[64,7168]{1,0:T(8,128)(2,1)S(1)}, bf16[64,7168]{1,0:T(8,128)(2,1)S(1)}, u32[]{:S(2)}, u32[]{:S(2)}) %collective-permute-start.11) | collective-permute-done | bytes 917536 | tf_op jit(solution)/shard_map/ppermute | solution.py:262
  135.7 5.3 %collective-permute-start.12 = (bf16[64,7168]{1,0:T(8,128)(2,1)S(1)}, bf16[64,7168]{1,0:T(8,128)(2,1)}, u32[]{:S(2)}, u32[]{:S(2)}) collective-permute-start(bf16[64,7168]{1,0:T(8,128)(2,1)S(1)} %collective-permute-done.11.refs_3_), channel_id=1, source_target_pairs={{1,0},{2,1},{5,4},{6,5},{9,8},{10,9},{13,12},{14,13},{17,16},{18,1... | collective-permute-start | bytes 2752520 | tf_op jit(solution)/shard_map/ppermute | solution.py:262
  142.0 28.2 %collective-permute-done.16.refs_16_.refs_6_ = bf16[128,7168]{1,0:T(8,128)(2,1)} collective-permute-done((bf16[128,7168]{1,0:T(8,128)(2,1)}, bf16[128,7168]{1,0:T(8,128)(2,1)}, u32[]{:S(2)}, u32[]{:S(2)}) %collective-permute-start.16) | collective-permute-done | bytes 1835040 | tf_op jit(solution)/shard_map/ppermute | solution.py:24
  171.5 2.3 collective-permute-start.10
  173.7 1.6 collective-permute-start.13
  175.5 18.1 %collective-permute-done.10.refs_2_ = bf16[64,7168]{1,0:T(8,128)(2,1)} collective-permute-done((bf16[64,7168]{1,0:T(8,128)(2,1)}, bf16[64,7168]{1,0:T(8,128)(2,1)}, u32[]{:S(2)}, u32[]{:S(2)}) %collective-permute-start.10) | collective-permute-done | bytes 917536 | tf_op jit(solution)/shard_map/ppermute | solution.py:262
  193.6 1.5 copy-done.4
  195.1 1.5 copy-done.9
  202.0 15.1 %shard_map.113 = (f32[64,7168]{1,0:T(8,128)S(1)}, bf16[64,7168]{1,0:T(8,128)(2,1)S(1)}, bf16[64,7168]{1,0:T(8,128)(2,1)S(1)}, bf16[64,7168]{1,0:T(8,128)(2,1)S(1)}) custom-call(f32[256,1]{1,0:T(8,128)S(1)} %reshape.33.mask_ref, bf16[64,7168]{1,0:T(8,128)(2,1)S(1)} %bitcast.59, bf16[64,7168]{1,0:T(8,128)(2,1)S(1)} %copy-done.27, ...), custom_call_target="tpu_custom_call" | custom-call | flops 5637144576 | bytes 33030144 | tf_op jit(solution)/shard_map/pallas_call | solution.py:230
  219.2 22.9 %collective-permute-done.21 = bf16[64,7168]{1,0:T(8,128)(2,1)S(1)} collective-permute-done((bf16[64,7168]{1,0:T(8,128)(2,1)S(1)}, bf16[64,7168]{1,0:T(8,128)(2,1)S(1)}, u32[]{:S(2)}, u32[]{:S(2)}) %collective-permute-start.21) | collective-permute-done | bytes 917536 | tf_op jit(solution)/shard_map/ppermute | solution.py:276
  242.1 1.6 fusion
  243.7 1.9 collective-permute-start.22
  247.3 2.6 copy-done
  249.9 1.5 copy-done.5
  251.4 1.5 copy-done.10
  252.9 9.8 %shard_map.114 = (f32[4,64,512]{2,1,0:T(8,128)S(1)}, f32[4,64,512]{2,1,0:T(8,128)S(1)}) custom-call(s32[1]{0:T(128)} %bitcast.16.at_ref, bf16[4,96,7168]{2,1,0:T(8,128)(2,1)S(1)} %bitcast.29, bf16[4,96,7168]{2,1,0:T(8,128)(2,1)S(1)} %bitcast.30, bf16[4,96,7168]{2,1,0:T(8,128)(2,1)S(1)} %bitcast.31, bf16[4,96,7168]{2,1,0:T(8,128)(2,1)S(1)} %bitcast.32, ...), custom_call_target="tpu_custom_call" | custom-call | flops 3758096384 | bytes 18350080 | tf_op jit(solution)/shard_map/pallas_call | solution.py:95
  262.8 15.4 %shard_map.115 = (f32[32,7168]{1,0:T(8,128)S(1)}, bf16[32,7168]{1,0:T(8,128)(2,1)S(1)}, bf16[32,7168]{1,0:T(8,128)(2,1)S(1)}, bf16[32,7168]{1,0:T(8,128)(2,1)S(1)}) custom-call(s32[1]{0:T(128)} %bitcast.16.at_ref, f32[128,1]{1,0:T(8,128)S(1)} %reshape.34.mask_ref, f32[4,64,512]{2,1,0:T(8,128)S(1)} %get-tuple-element.38.c_ref, ...), custom_call_target="tpu_custom_call" | custom-call | flops 2818572288 | bytes 25690112 | tf_op jit(solution)/shard_map/pallas_call | solution.py:156
  280.2 4.2 collective-permute-done.22
  284.4 2.3 add_convert_fusion.1
  286.7 4.5 %collective-permute-start.23 = (bf16[64,7168]{1,0:T(8,128)(2,1)}, bf16[64,7168]{1,0:T(8,128)(2,1)}, u32[]{:S(2)}, u32[]{:S(2)}) collective-permute-start(bf16[64,7168]{1,0:T(8,128)(2,1)} %add_convert_fusion.1), channel_id=1, source_target_pairs={{1,0},{2,1},{3,2},{5,4},{6,5},{7,6},{9,8},{10,9},{11,10},{13,12},{... | collective-permute-start | bytes 2752520 | tf_op jit(solution)/shard_map/ppermute | solution.py:276
  291.2 12.6 %collective-permute-done.28 = bf16[32,7168]{1,0:T(8,128)(2,1)S(1)} collective-permute-done((bf16[32,7168]{1,0:T(8,128)(2,1)S(1)}, bf16[32,7168]{1,0:T(8,128)(2,1)S(1)}, u32[]{:S(2)}, u32[]{:S(2)}) %collective-permute-start.28) | collective-permute-done | bytes 458784 | tf_op jit(solution)/shard_map/ppermute | solution.py:276
  304.9 3.9 collective-permute-start.29
  308.8 2.3 add_convert_fusion.2
  311.2 2.6 collective-permute-start.20
  316.7 1.5 copy-done.12
  318.2 1.5 copy-done.13
  319.7 1.5 copy-done.16
  321.2 1.5 copy-done.20
  323.7 15.2 %shard_map.116 = (f32[32,7168]{1,0:T(8,128)S(1)}, bf16[32,7168]{1,0:T(8,128)(2,1)S(1)}, bf16[32,7168]{1,0:T(8,128)(2,1)S(1)}, bf16[32,7168]{1,0:T(8,128)(2,1)S(1)}) custom-call(s32[1]{0:T(128)} %bitcast.16.at_ref, f32[128,1]{1,0:T(8,128)S(1)} %reshape.35.mask_ref, f32[4,64,512]{2,1,0:T(8,128)S(1)} %get-tuple-element.38.c_ref, f32[4,64,512]{2,1,0:T(8,128)S(1)} %copy-done.23, ...), custom_call_target="tpu_custom_call" | custom-call | flops 2818572288 | bytes 25690112 | tf_op jit(solution)/shard_map/pallas_call | solution.py:156
  338.9 2.7 collective-permute-start.34
  341.6 1.6 collective-permute-start.33
  344.3 20.6 %collective-permute-done.26 = bf16[32,7168]{1,0:T(8,128)(2,1)} collective-permute-done((bf16[32,7168]{1,0:T(8,128)(2,1)}, bf16[32,7168]{1,0:T(8,128)(2,1)}, u32[]{:S(2)}, u32[]{:S(2)}) %collective-permute-start.26) | collective-permute-done | bytes 458784 | tf_op jit(solution)/shard_map/ppermute | solution.py:275
  366.1 3.9 collective-permute-start.30
  370.0 1.9 collective-permute-start.27
  372.0 2.1 add_convert_fusion
  374.5 7.5 %collective-permute-done.33 = bf16[32,7168]{1,0:T(8,128)(2,1)S(1)} collective-permute-done((bf16[32,7168]{1,0:T(8,128)(2,1)S(1)}, bf16[32,7168]{1,0:T(8,128)(2,1)S(1)}, u32[]{:S(2)}, u32[]{:S(2)}) %collective-permute-start.33) | collective-permute-done | bytes 458784 | tf_op jit(solution)/shard_map/ppermute | solution.py:29
  382.1 2.4 collective-permute-done.32
  384.5 3.6 collective-permute-done.30
  388.1 4.6 %collective-permute-done.27 = bf16[32,7168]{1,0:T(8,128)(2,1)S(1)} collective-permute-done((bf16[32,7168]{1,0:T(8,128)(2,1)S(1)}, bf16[32,7168]{1,0:T(8,128)(2,1)S(1)}, u32[]{:S(2)}, u32[]{:S(2)}) %collective-permute-start.27) | collective-permute-done | bytes 458784 | tf_op jit(solution)/shard_map/ppermute | solution.py:275
  393.5 1.7 collective-permute-start.31
  395.2 11.4 %collective-permute-done.35 = bf16[32,7168]{1,0:T(8,128)(2,1)S(1)} collective-permute-done((bf16[32,7168]{1,0:T(8,128)(2,1)S(1)}, bf16[32,7168]{1,0:T(8,128)(2,1)S(1)}, u32[]{:S(2)}, u32[]{:S(2)}) %collective-permute-start.35) | collective-permute-done | bytes 458784 | tf_op jit(solution)/shard_map/ppermute | solution.py:29
  406.6 7.2 %collective-permute-done.31 = bf16[32,7168]{1,0:T(8,128)(2,1)S(1)} collective-permute-done((bf16[32,7168]{1,0:T(8,128)(2,1)S(1)}, bf16[32,7168]{1,0:T(8,128)(2,1)S(1)}, u32[]{:S(2)}, u32[]{:S(2)}) %collective-permute-start.31) | collective-permute-done | bytes 458784 | tf_op jit(solution)/shard_map/ppermute | solution.py:29
  (149 shorter events, 36.6 us)
Async XLA Ops:
  7.2 240.1 %all-gather.5.cloned.1.call-start = ((), (), s32[]{:S(2)}) async-start(), calls=%async_computation | async-start | bytes 6881280 | tf_op jit(solution)/shard_map/all_gather | solution.py:320
  10.8 6.2 %collective-permute-start = (s32[64,2]{0,1:T(2,128)S(1)}, s32[64,2]{0,1:T(2,128)S(1)}, u32[]{:S(2)}, u32[]{:S(2)}) collective-permute-start(s32[64,2]{0,1:T(2,128)S(1)} %pad_add_fusion), channel_id=1, source_target_pairs={{1,0},{2,1},{3,2},{0,3},{5,4},{6,5},{7,6},{4,7},{9,8},{10,9},{11,1... | collective-permute-start | bytes 1544 | tf_op jit(solution)/shard_map/ppermute | solution.py:29
  11.3 9.2 %collective-permute-start.2 = (s32[64,2]{0,1:T(2,128)S(1)}, s32[64,2]{0,1:T(2,128)S(1)}, u32[]{:S(2)}, u32[]{:S(2)}) collective-permute-start(s32[64,2]{0,1:T(2,128)S(1)} %pad_add_fusion), channel_id=1, source_target_pairs={{3,0},{0,1},{1,2},{2,3},{7,4},{4,5},{5,6},{6,7},{11,8},{8,9},{9,10... | collective-permute-start | bytes 1544 | tf_op jit(solution)/shard_map/ppermute | solution.py:29
  12.8 6.3 %collective-permute-start.1 = (s32[64,2]{0,1:T(2,128)S(1)}, s32[64,2]{0,1:T(2,128)S(1)}, u32[]{:S(2)}, u32[]{:S(2)}) collective-permute-start(s32[64,2]{0,1:T(2,128)S(1)} %pad_add_fusion), channel_id=1, source_target_pairs={{2,0},{3,1},{0,2},{1,3},{6,4},{7,5},{4,6},{5,7},{10,8},{11,9},{8,1... | collective-permute-start | bytes 1544 | tf_op jit(solution)/shard_map/ppermute | solution.py:29
  14.8 75.0 %collective-permute-start.4 = (bf16[7168,128]{1,0:T(8,128)(2,1)S(1)}, bf16[7168,128]{1,0:T(8,128)(2,1)}, u32[]{:S(2)}, u32[]{:S(2)}) collective-permute-start(bf16[7168,128]{1,0:T(8,128)(2,1)S(1)} %bitcast.37), channel_id=1, source_target_pairs={{0,4},{4,0},{8,12},{12,8},{1,5},{5,1},{9,13},{13,9},{2,6},{6,2},{1... | collective-permute-start | bytes 5505032 | tf_op jit(solution)/shard_map/ppermute | solution.py:24
  14.8 78.0 %collective-permute-start.8 = (bf16[7168,128]{1,0:T(8,128)(2,1)S(1)}, bf16[7168,128]{1,0:T(8,128)(2,1)}, u32[]{:S(2)}, u32[]{:S(2)}) collective-permute-start(bf16[7168,128]{1,0:T(8,128)(2,1)S(1)} %bitcast.38), channel_id=1, source_target_pairs={{0,8},{4,12},{8,0},{12,4},{1,9},{5,13},{9,1},{13,5},{2,10},{6,14},... | collective-permute-start | bytes 5505032 | tf_op jit(solution)/shard_map/ppermute | solution.py:24
  16.3 298.9 %all-gather.7.cloned.1.call-start = ((), (), s32[]{:S(2)}) async-start(), calls=%async_computation.1 | async-start | bytes 2293760 | tf_op jit(solution)/shard_map/all_gather | solution.py:345
  17.0 73.9 %collective-permute-start.5 = (bf16[7168,128]{1,0:T(8,128)(2,1)}, bf16[7168,128]{1,0:T(8,128)(2,1)}, u32[]{:S(2)}, u32[]{:S(2)}) collective-permute-start(bf16[7168,128]{1,0:T(8,128)(2,1)} %bitcast.43), channel_id=1, source_target_pairs={{0,4},{4,0},{8,12},{12,8},{1,5},{5,1},{9,13},{13,9},{2,6},{6,2},{1... | collective-permute-start | bytes 5505032 | tf_op jit(solution)/shard_map/ppermute | solution.py:24
  21.7 67.1 %copy-start.3 = (bf16[1,1,7168,128]{3,2,1,0:T(8,128)(2,1)S(1)}, bf16[1,1,7168,128]{3,2,1,0:T(8,128)(2,1)}, u32[]{:S(2)}) copy-start(bf16[1,1,7168,128]{3,2,1,0:T(8,128)(2,1)} %param.18) | copy-start | bytes 5505028
  21.8 67.0 %collective-permute-start.3 = (bf16[64,7168]{1,0:T(8,128)(2,1)S(1)}, bf16[64,7168]{1,0:T(8,128)(2,1)S(1)}, u32[]{:S(2)}, u32[]{:S(2)}) collective-permute-start(bf16[64,7168]{1,0:T(8,128)(2,1)S(1)} %broadcast_select_fusion), channel_id=1, source_target_pairs={{0,1},{1,2},{2,3},{4,5},{5,6},{6,7},{8,9},{9,10},{10,11},{12,13},{... | collective-permute-start | bytes 2752520 | tf_op jit(solution)/shard_map/ppermute | solution.py:262
  25.4 67.4 %collective-permute-start.6 = (bf16[128,7168]{1,0:T(8,128)(2,1)}, bf16[128,7168]{1,0:T(8,128)(2,1)S(1)}, u32[]{:S(2)}, u32[]{:S(2)}) collective-permute-start(bf16[128,7168]{1,0:T(8,128)(2,1)} %bitcast.53), channel_id=1, source_target_pairs={{0,4},{4,0},{8,12},{12,8},{1,5},{5,1},{9,13},{13,9},{2,6},{6,2},{1... | collective-permute-start | bytes 5505032 | tf_op jit(solution)/shard_map/ppermute | solution.py:24
  88.8 53.2 %collective-permute-start.14 = (bf16[7168,128]{1,0:T(8,128)(2,1)S(1)}, bf16[7168,128]{1,0:T(8,128)(2,1)}, u32[]{:S(2)}, u32[]{:S(2)}) collective-permute-start(bf16[7168,128]{1,0:T(8,128)(2,1)S(1)} %bitcast.44), channel_id=1, source_target_pairs={{0,8},{4,12},{8,0},{12,4},{1,9},{5,13},{9,1},{13,5},{2,10},{6,14},... | collective-permute-start | bytes 5505032 | tf_op jit(solution)/shard_map/ppermute | solution.py:24
  89.7 80.4 %collective-permute-start.16 = (bf16[128,7168]{1,0:T(8,128)(2,1)}, bf16[128,7168]{1,0:T(8,128)(2,1)}, u32[]{:S(2)}, u32[]{:S(2)}) collective-permute-start(bf16[128,7168]{1,0:T(8,128)(2,1)} %bitcast.54), channel_id=1, source_target_pairs={{0,8},{4,12},{8,0},{12,4},{1,9},{5,13},{9,1},{13,5},{2,10},{6,14},... | collective-permute-start | bytes 5505032 | tf_op jit(solution)/shard_map/ppermute | solution.py:24
  90.8 44.9 %collective-permute-start.11 = (bf16[64,7168]{1,0:T(8,128)(2,1)S(1)}, bf16[64,7168]{1,0:T(8,128)(2,1)S(1)}, u32[]{:S(2)}, u32[]{:S(2)}) collective-permute-start(bf16[64,7168]{1,0:T(8,128)(2,1)S(1)} %broadcast_select_fusion), channel_id=1, source_target_pairs={{1,0},{2,1},{3,2},{5,4},{6,5},{7,6},{9,8},{10,9},{11,10},{13,12},{... | collective-permute-start | bytes 2752520 | tf_op jit(solution)/shard_map/ppermute | solution.py:262
  92.8 77.4 %collective-permute-start.9 = (bf16[7168,128]{1,0:T(8,128)(2,1)}, bf16[7168,128]{1,0:T(8,128)(2,1)S(1)}, u32[]{:S(2)}, u32[]{:S(2)}) collective-permute-start(bf16[7168,128]{1,0:T(8,128)(2,1)} %collective-permute-done.8.refs_8_.refs_6_.refs_10_), channel_id=1, source_target_pairs={{0,4},{4,0},{8,12},{12,8},{1,5},{5,1},{9,13},{13,9},{2,6},{6,2},{1... | collective-permute-start | bytes 5505032 | tf_op jit(solution)/shard_map/ppermute | solution.py:24
  94.1 76.1 %collective-permute-start.7 = (bf16[64,7168]{1,0:T(8,128)(2,1)S(1)}, bf16[64,7168]{1,0:T(8,128)(2,1)}, u32[]{:S(2)}, u32[]{:S(2)}) collective-permute-start(bf16[64,7168]{1,0:T(8,128)(2,1)S(1)} %collective-permute-done.3.refs_0_), channel_id=1, source_target_pairs={{1,2},{2,3},{5,6},{6,7},{9,10},{10,11},{13,14},{14,15},{17,18},{18... | collective-permute-start | bytes 2752520 | tf_op jit(solution)/shard_map/ppermute | solution.py:262
  135.7 38.0 %collective-permute-start.12 = (bf16[64,7168]{1,0:T(8,128)(2,1)S(1)}, bf16[64,7168]{1,0:T(8,128)(2,1)}, u32[]{:S(2)}, u32[]{:S(2)}) collective-permute-start(bf16[64,7168]{1,0:T(8,128)(2,1)S(1)} %collective-permute-done.11.refs_3_), channel_id=1, source_target_pairs={{1,0},{2,1},{5,4},{6,5},{9,8},{10,9},{13,12},{14,13},{17,16},{18,1... | collective-permute-start | bytes 2752520 | tf_op jit(solution)/shard_map/ppermute | solution.py:262
  142.0 33.5 %collective-permute-start.15 = (bf16[7168,128]{1,0:T(8,128)(2,1)}, bf16[7168,128]{1,0:T(8,128)(2,1)}, u32[]{:S(2)}, u32[]{:S(2)}) collective-permute-start(bf16[7168,128]{1,0:T(8,128)(2,1)} %collective-permute-done.14.refs_12_.refs_10_.refs_14_), channel_id=1, source_target_pairs={{0,4},{4,0},{8,12},{12,8},{1,5},{5,1},{9,13},{13,9},{2,6},{6,2},{1... | collective-permute-start | bytes 5505032 | tf_op jit(solution)/shard_map/ppermute | solution.py:24
  170.2 5.3 %collective-permute-start.17 = (bf16[128,7168]{1,0:T(8,128)(2,1)}, bf16[128,7168]{1,0:T(8,128)(2,1)}, u32[]{:S(2)}, u32[]{:S(2)}) collective-permute-start(bf16[128,7168]{1,0:T(8,128)(2,1)} %collective-permute-done.16.refs_16_.refs_6_), channel_id=1, source_target_pairs={{0,4},{4,0},{8,12},{12,8},{1,5},{5,1},{9,13},{13,9},{2,6},{6,2},{1... | collective-permute-start | bytes 5505032 | tf_op jit(solution)/shard_map/ppermute | solution.py:24
  171.5 22.1 %collective-permute-start.10 = (bf16[64,7168]{1,0:T(8,128)(2,1)}, bf16[64,7168]{1,0:T(8,128)(2,1)}, u32[]{:S(2)}, u32[]{:S(2)}) collective-permute-start(bf16[64,7168]{1,0:T(8,128)(2,1)} %collective-permute-done.7.refs_1_), channel_id=1, source_target_pairs={{2,3},{6,7},{10,11},{14,15},{18,19},{22,23},{26,27},{30,31}} | collective-permute-start | bytes 2752520 | tf_op jit(solution)/shard_map/ppermute | solution.py:262
  173.7 19.9 %collective-permute-start.13 = (bf16[64,7168]{1,0:T(8,128)(2,1)}, bf16[64,7168]{1,0:T(8,128)(2,1)}, u32[]{:S(2)}, u32[]{:S(2)}) collective-permute-start(bf16[64,7168]{1,0:T(8,128)(2,1)} %collective-permute-done.12.refs_4_), channel_id=1, source_target_pairs={{1,0},{5,4},{9,8},{13,12},{17,16},{21,20},{25,24},{29,28}} | collective-permute-start | bytes 2752520 | tf_op jit(solution)/shard_map/ppermute | solution.py:262
  217.1 26.6 %copy-start.24 = (f32[64,7168]{1,0:T(8,128)}, f32[64,7168]{1,0:T(8,128)S(1)}, u32[]{:S(2)}) copy-start(f32[64,7168]{1,0:T(8,128)S(1)} %get-tuple-element.32) | copy-start | bytes 5505028
  217.1 26.6 %copy-start.32 = (bf16[64,7168]{1,0:T(8,128)(2,1)}, bf16[64,7168]{1,0:T(8,128)(2,1)S(1)}, u32[]{:S(2)}) copy-start(bf16[64,7168]{1,0:T(8,128)(2,1)S(1)} %get-tuple-element.33) | copy-start | bytes 2752516
  217.1 26.6 %copy-start.34 = (bf16[64,7168]{1,0:T(8,128)(2,1)}, bf16[64,7168]{1,0:T(8,128)(2,1)S(1)}, u32[]{:S(2)}) copy-start(bf16[64,7168]{1,0:T(8,128)(2,1)S(1)} %get-tuple-element.35) | copy-start | bytes 2752516
  217.2 2.0 collective-permute-start.18
  217.9 24.2 %collective-permute-start.21 = (bf16[64,7168]{1,0:T(8,128)(2,1)S(1)}, bf16[64,7168]{1,0:T(8,128)(2,1)S(1)}, u32[]{:S(2)}, u32[]{:S(2)}) collective-permute-start(bf16[64,7168]{1,0:T(8,128)(2,1)S(1)} %get-tuple-element.33), channel_id=1, source_target_pairs={{3,2},{7,6},{11,10},{15,14},{19,18},{23,22},{27,26},{31,30}} | collective-permute-start | bytes 2752520 | tf_op jit(solution)/shard_map/ppermute | solution.py:276
  243.7 40.7 %collective-permute-start.22 = (bf16[64,7168]{1,0:T(8,128)(2,1)}, bf16[64,7168]{1,0:T(8,128)(2,1)}, u32[]{:S(2)}, u32[]{:S(2)}) collective-permute-start(bf16[64,7168]{1,0:T(8,128)(2,1)} %get-tuple-element.55), channel_id=1, source_target_pairs={{2,1},{3,2},{6,5},{7,6},{10,9},{11,10},{14,13},{15,14},{18,17},{19... | collective-permute-start | bytes 2752520 | tf_op jit(solution)/shard_map/ppermute | solution.py:276
  246.0 62.8 %collective-permute-start.19 = (bf16[64,7168]{1,0:T(8,128)(2,1)}, bf16[64,7168]{1,0:T(8,128)(2,1)}, u32[]{:S(2)}, u32[]{:S(2)}) collective-permute-start(bf16[64,7168]{1,0:T(8,128)(2,1)} %get-tuple-element.54), channel_id=1, source_target_pairs={{0,1},{1,2},{4,5},{5,6},{8,9},{9,10},{12,13},{13,14},{16,17},{17,1... | collective-permute-start | bytes 2752520 | tf_op jit(solution)/shard_map/ppermute | solution.py:275
  278.2 26.7 %copy-start.30 = (f32[32,7168]{1,0:T(8,128)}, f32[32,7168]{1,0:T(8,128)S(1)}, u32[]{:S(2)}) copy-start(f32[32,7168]{1,0:T(8,128)S(1)} %get-tuple-element.40) | copy-start | bytes 2752516
  278.2 26.7 %copy-start.36 = (bf16[32,7168]{1,0:T(8,128)(2,1)}, bf16[32,7168]{1,0:T(8,128)(2,1)S(1)}, u32[]{:S(2)}) copy-start(bf16[32,7168]{1,0:T(8,128)(2,1)S(1)} %get-tuple-element.41) | copy-start | bytes 1376260
  278.2 26.7 %copy-start.38 = (bf16[32,7168]{1,0:T(8,128)(2,1)}, bf16[32,7168]{1,0:T(8,128)(2,1)S(1)}, u32[]{:S(2)}) copy-start(bf16[32,7168]{1,0:T(8,128)(2,1)S(1)} %get-tuple-element.43) | copy-start | bytes 1376260
  278.2 25.6 %collective-permute-start.28 = (bf16[32,7168]{1,0:T(8,128)(2,1)S(1)}, bf16[32,7168]{1,0:T(8,128)(2,1)S(1)}, u32[]{:S(2)}, u32[]{:S(2)}) collective-permute-start(bf16[32,7168]{1,0:T(8,128)(2,1)S(1)} %get-tuple-element.41), channel_id=1, source_target_pairs={{3,2},{7,6},{11,10},{15,14},{19,18},{23,22},{27,26},{31,30}} | collective-permute-start | bytes 1376264 | tf_op jit(solution)/shard_map/ppermute | solution.py:276
  279.5 24.3 %collective-permute-start.25 = (bf16[32,7168]{1,0:T(8,128)(2,1)S(1)}, bf16[32,7168]{1,0:T(8,128)(2,1)S(1)}, u32[]{:S(2)}, u32[]{:S(2)}) collective-permute-start(bf16[32,7168]{1,0:T(8,128)(2,1)S(1)} %get-tuple-element.43), channel_id=1, source_target_pairs={{0,1},{4,5},{8,9},{12,13},{16,17},{20,21},{24,25},{28,29}} | collective-permute-start | bytes 1376264 | tf_op jit(solution)/shard_map/ppermute | solution.py:275
  286.7 79.4 %collective-permute-start.23 = (bf16[64,7168]{1,0:T(8,128)(2,1)}, bf16[64,7168]{1,0:T(8,128)(2,1)}, u32[]{:S(2)}, u32[]{:S(2)}) collective-permute-start(bf16[64,7168]{1,0:T(8,128)(2,1)} %add_convert_fusion.1), channel_id=1, source_target_pairs={{1,0},{2,1},{3,2},{5,4},{6,5},{7,6},{9,8},{10,9},{11,10},{13,12},{... | collective-permute-start | bytes 2752520 | tf_op jit(solution)/shard_map/ppermute | solution.py:276
  304.9 36.7 %collective-permute-start.29 = (bf16[32,7168]{1,0:T(8,128)(2,1)}, bf16[32,7168]{1,0:T(8,128)(2,1)}, u32[]{:S(2)}, u32[]{:S(2)}) collective-permute-start(bf16[32,7168]{1,0:T(8,128)(2,1)} %get-tuple-element.58), channel_id=1, source_target_pairs={{2,1},{3,2},{6,5},{7,6},{10,9},{11,10},{14,13},{15,14},{18,17},{19... | collective-permute-start | bytes 1376264 | tf_op jit(solution)/shard_map/ppermute | solution.py:276
  311.2 58.8 %collective-permute-start.20 = (bf16[64,7168]{1,0:T(8,128)(2,1)}, bf16[64,7168]{1,0:T(8,128)(2,1)}, u32[]{:S(2)}, u32[]{:S(2)}) collective-permute-start(bf16[64,7168]{1,0:T(8,128)(2,1)} %add_convert_fusion.2), channel_id=1, source_target_pairs={{0,1},{1,2},{2,3},{4,5},{5,6},{6,7},{8,9},{9,10},{10,11},{12,13},{... | collective-permute-start | bytes 2752520 | tf_op jit(solution)/shard_map/ppermute | solution.py:275
  313.8 51.1 %collective-permute-start.26 = (bf16[32,7168]{1,0:T(8,128)(2,1)}, bf16[32,7168]{1,0:T(8,128)(2,1)}, u32[]{:S(2)}, u32[]{:S(2)}) collective-permute-start(bf16[32,7168]{1,0:T(8,128)(2,1)} %get-tuple-element.59), channel_id=1, source_target_pairs={{0,1},{1,2},{4,5},{5,6},{8,9},{9,10},{12,13},{13,14},{16,17},{17,1... | collective-permute-start | bytes 1376264 | tf_op jit(solution)/shard_map/ppermute | solution.py:275
  323.7 41.2 %copy-start.37 = (bf16[32,7168]{1,0:T(8,128)(2,1)S(1)}, bf16[32,7168]{1,0:T(8,128)(2,1)}, u32[]{:S(2)}) copy-start(bf16[32,7168]{1,0:T(8,128)(2,1)} %copy-done.36) | copy-start | bytes 1376260
  338.9 33.1 %copy-start.25 = (f32[64,7168]{1,0:T(8,128)S(1)}, f32[64,7168]{1,0:T(8,128)}, u32[]{:S(2)}) copy-start(f32[64,7168]{1,0:T(8,128)} %copy-done.24) | copy-start | bytes 5505028
  338.9 33.1 %copy-start.42 = (f32[1,64]{1,0:T(1,128)S(1)}, f32[1,64]{1,0:T(1,128)}, u32[]{:S(2)}) copy-start(f32[1,64]{1,0:T(1,128)} %param.12) | copy-start | bytes 772
  338.9 35.2 %collective-permute-start.34 = (bf16[32,7168]{1,0:T(8,128)(2,1)S(1)}, bf16[32,7168]{1,0:T(8,128)(2,1)S(1)}, u32[]{:S(2)}, u32[]{:S(2)}) collective-permute-start(bf16[32,7168]{1,0:T(8,128)(2,1)S(1)} %get-tuple-element.49), channel_id=1, source_target_pairs={{1,0},{2,1},{3,2},{0,3},{5,4},{6,5},{7,6},{4,7},{9,8},{10,9},{11,1... | collective-permute-start | bytes 1376264 | tf_op jit(solution)/shard_map/ppermute | solution.py:29
  341.6 40.5 %collective-permute-start.33 = (bf16[32,7168]{1,0:T(8,128)(2,1)S(1)}, bf16[32,7168]{1,0:T(8,128)(2,1)S(1)}, u32[]{:S(2)}, u32[]{:S(2)}) collective-permute-start(bf16[32,7168]{1,0:T(8,128)(2,1)S(1)} %get-tuple-element.48), channel_id=1, source_target_pairs={{2,0},{3,1},{0,2},{1,3},{6,4},{7,5},{4,6},{5,7},{10,8},{11,9},{8,1... | collective-permute-start | bytes 1376264 | tf_op jit(solution)/shard_map/ppermute | solution.py:29
  364.9 19.6 %collective-permute-start.32 = (bf16[32,7168]{1,0:T(8,128)(2,1)S(1)}, bf16[32,7168]{1,0:T(8,128)(2,1)S(1)}, u32[]{:S(2)}, u32[]{:S(2)}) collective-permute-start(bf16[32,7168]{1,0:T(8,128)(2,1)S(1)} %get-tuple-element.47), channel_id=1, source_target_pairs={{3,0},{0,1},{1,2},{2,3},{7,4},{4,5},{5,6},{6,7},{11,8},{8,9},{9,10... | collective-permute-start | bytes 1376264 | tf_op jit(solution)/shard_map/ppermute | solution.py:29
  366.1 22.0 %collective-permute-start.30 = (bf16[32,7168]{1,0:T(8,128)(2,1)S(1)}, bf16[32,7168]{1,0:T(8,128)(2,1)S(1)}, u32[]{:S(2)}, u32[]{:S(2)}) collective-permute-start(bf16[32,7168]{1,0:T(8,128)(2,1)S(1)} %add_convert_fusion.3), channel_id=1, source_target_pairs={{1,0},{2,1},{3,2},{5,4},{6,5},{7,6},{9,8},{10,9},{11,10},{13,12},{... | collective-permute-start | bytes 1376264 | tf_op jit(solution)/shard_map/ppermute | solution.py:276
  370.0 22.6 %collective-permute-start.27 = (bf16[32,7168]{1,0:T(8,128)(2,1)S(1)}, bf16[32,7168]{1,0:T(8,128)(2,1)S(1)}, u32[]{:S(2)}, u32[]{:S(2)}) collective-permute-start(bf16[32,7168]{1,0:T(8,128)(2,1)S(1)} %add_convert_fusion.4), channel_id=1, source_target_pairs={{0,1},{1,2},{2,3},{4,5},{5,6},{6,7},{8,9},{9,10},{10,11},{12,13},{... | collective-permute-start | bytes 1376264 | tf_op jit(solution)/shard_map/ppermute | solution.py:275
  374.1 21.1 %collective-permute-start.24 = (bf16[64,7168]{1,0:T(8,128)(2,1)S(1)}, bf16[64,7168]{1,0:T(8,128)(2,1)S(1)}, u32[]{:S(2)}, u32[]{:S(2)}) collective-permute-start(bf16[64,7168]{1,0:T(8,128)(2,1)S(1)} %add_convert_fusion), channel_id=1, source_target_pairs={{16,0},{0,16},{17,1},{1,17},{18,2},{2,18},{19,3},{3,19},{20,4},{4,... | collective-permute-start | bytes 2752520 | tf_op jit(solution)/shard_map/ppermute | solution.py:29
  393.1 13.5 %collective-permute-start.35 = (bf16[32,7168]{1,0:T(8,128)(2,1)S(1)}, bf16[32,7168]{1,0:T(8,128)(2,1)S(1)}, u32[]{:S(2)}, u32[]{:S(2)}) collective-permute-start(bf16[32,7168]{1,0:T(8,128)(2,1)S(1)} %get-tuple-element.53), channel_id=1, source_target_pairs={{16,0},{0,16},{17,1},{1,17},{18,2},{2,18},{19,3},{3,19},{20,4},{4,... | collective-permute-start | bytes 1376264 | tf_op jit(solution)/shard_map/ppermute | solution.py:29
  393.5 20.3 %collective-permute-start.31 = (bf16[32,7168]{1,0:T(8,128)(2,1)S(1)}, bf16[32,7168]{1,0:T(8,128)(2,1)S(1)}, u32[]{:S(2)}, u32[]{:S(2)}) collective-permute-start(bf16[32,7168]{1,0:T(8,128)(2,1)S(1)} %get-tuple-element.52), channel_id=1, source_target_pairs={{16,0},{0,16},{17,1},{1,17},{18,2},{2,18},{19,3},{3,19},{20,4},{4,... | collective-permute-start | bytes 1376264 | tf_op jit(solution)/shard_map/ppermute | solution.py:29
  (35 other events, 218.2 us)
Sparse Core Ops, SparseCore 0:
  16.4 132.0 all-gather.4
  245.8 65.1 all-gather.6

commit v4 on v3

--- a/solution.py
+++ b/solution.py
@@ -42,12 +42,22 @@
     return (mask > 0) == (column < hidden // 2)
 
 
-def joined(refs, axis):
-    return jnp.concatenate([ref[...] for ref in refs], axis=axis)
-
-
-def stacked(refs):
+def joined(refs, axis, index=None):
+    pick = (lambda ref: ref[...]) if index is None else (lambda ref: ref[index])
+    return jnp.concatenate([pick(ref) for ref in refs], axis=axis)
+
+
+def gathered_rows(refs):
     return jnp.concatenate([ref[0] for ref in refs], axis=0)
+
+
+def chained_rows(refs):
+    others = len(refs) // 2
+    own, below, above = refs[0][...], refs[1 : 1 + others], refs[1 + others :]
+    return jnp.concatenate(
+        [own] + [above[away][...] + below[others - 1 - away][...] for away in range(others)],
+        axis=0,
+    )
 
 
 def put_blocks(out_refs, total):
@@ -56,48 +66,57 @@
         ref[...] = total[index * rows : (index + 1) * rows].astype(ref.dtype)
 
 
-def turned_specs(count, begin, rows, chunk, column):
-    unit = math.gcd(begin, rows)
-    return [
-        pl.BlockSpec(
-            (1, unit, chunk),
-            lambda i, at, turn=turn, piece=piece: (lax.rem(at[0] + turn, count), piece, column(i)),
-        )
-        for turn in range(count)
-        for piece in range(begin // unit, (begin + rows) // unit)
-    ]
-
-
-def gates_kernel(inputs, pieces, at_ref, *refs):
-    xs, refs = refs[:inputs], refs[inputs:]
-    gates, ups = refs[:pieces], refs[pieces : 2 * pieces]
-    c_ref, e_ref = refs[2 * pieces :]
+def gathered_input(x, begin, rows):
+    count, unit = x.shape[0], math.gcd(begin, rows)
+    arrays, specs = [], []
+    for turn in range(count):
+        for piece in range(begin // unit, (begin + rows) // unit):
+            arrays.append(x)
+            specs.append(
+                lambda chunk, column, turn=turn, piece=piece: pl.BlockSpec(
+                    (1, unit, chunk),
+                    lambda i, at: (lax.rem(at[0] + turn, count), piece, column(i)),
+                )
+            )
+    return gathered_rows, arrays, specs, rows
+
+
+def chained_input(own, from_below, from_above):
+    rows = own.shape[0]
+    spec = lambda chunk, column: pl.BlockSpec((rows, chunk), lambda i, at: (0, column(i)))
+    arrays = [own, *from_below, *from_above]
+    return chained_rows, arrays, [spec] * len(arrays), rows
+
+
+def gates_kernel(read, inputs, pieces, at_ref, *refs):
+    xs, gate_ups = refs[:inputs], refs[inputs : inputs + pieces]
+    c_ref, e_ref = refs[inputs + pieces :]
 
     @pl.when(pl.program_id(0) == 0)
     def _():
         c_ref[...] = jnp.zeros_like(c_ref)
         e_ref[...] = jnp.zeros_like(e_ref)
 
-    x = stacked(xs)
-    c = jnp.dot(x, joined(gates, 1), preferred_element_type=F32)
-    e = jnp.dot(x, joined(ups, 1), preferred_element_type=F32)
+    x = read(xs)
+    c = jnp.dot(x, joined(gate_ups, 1, 0), preferred_element_type=F32)
+    e = jnp.dot(x, joined(gate_ups, 1, 1), preferred_element_type=F32)
     c_ref[...] += c.reshape(c_ref.shape)
     e_ref[...] += e.reshape(e_ref.shape)
 
 
-def gates_call(at, x, begin, rows, gates, ups):
-    count, _, width = x.shape
-    pieces, hid = len(gates), gates[0].shape[1]
+def gates_call(at, count, x_input, gate_ups):
+    read, arrays, specs, rows = x_input
+    width = arrays[0].shape[-1]
+    pieces, hid = len(gate_ups), gate_ups[0].shape[2]
     chunk = chunk_of(width, 1024)
     hidden = pieces * hid
-    x_specs = turned_specs(count, begin, rows, chunk, lambda i: i)
-    weight_spec = pl.BlockSpec((chunk, hid), lambda i, at: (i, 0))
+    weight_spec = pl.BlockSpec((2, chunk, hid), lambda i, at: (0, i, 0))
     return pl.pallas_call(
-        functools.partial(gates_kernel, len(x_specs), pieces),
+        functools.partial(gates_kernel, read, len(arrays), pieces),
         grid_spec=pltpu.PrefetchScalarGridSpec(
             num_scalar_prefetch=1,
             grid=(width // chunk,),
-            in_specs=x_specs + [weight_spec] * (2 * pieces),
+            in_specs=[spec(chunk, lambda i: i) for spec in specs] + [weight_spec] * pieces,
             out_specs=[pl.BlockSpec((count, rows, hidden), lambda i, at: (0, 0, 0))] * 2,
         ),
         out_shape=[jax.ShapeDtypeStruct((count, rows, hidden), F32)] * 2,
@@ -107,14 +126,14 @@
             bytes_accessed=2 * count * rows * width + 4 * width * hidden,
             transcendentals=0,
         ),
-    )(at, *[x] * len(x_specs), *gates, *ups)
-
-
-def backward_kernel(count, inputs, pieces, steps, at_ref, mask_ref, c_ref, e_ref, *refs):
+    )(at, *arrays, *gate_ups)
+
+
+def backward_kernel(read, inputs, count, pieces, steps, at_ref, mask_ref, c_ref, e_ref, *refs):
     scaled, refs = refs[:inputs], refs[inputs:]
-    downs, gates, ups = refs[:pieces], refs[pieces : 2 * pieces], refs[2 * pieces : 3 * pieces]
-    outs = refs[3 * pieces : 3 * pieces + count]
-    dh_ref, ga_ref, gb_ref = refs[3 * pieces + count :]
+    downs, gate_ups = refs[:pieces], refs[pieces : 2 * pieces]
+    outs = refs[2 * pieces : 2 * pieces + count]
+    dh_ref, ga_ref, gb_ref = refs[2 * pieces + count :]
     step = pl.program_id(0)
 
     @pl.when(step == 0)
@@ -123,7 +142,7 @@
 
     @pl.when(step < steps)
     def _():
-        dh_ref[...] += contract_last(stacked(scaled), joined(downs, 0))
+        dh_ref[...] += contract_last(read(scaled), joined(downs, 0))
 
     @pl.when(step == steps - 1)
     def _():
@@ -137,24 +156,24 @@
 
     @pl.when(step >= steps)
     def _():
-        total = contract_last(ga_ref[...], joined(gates, 1))
-        total += contract_last(gb_ref[...], joined(ups, 1))
+        total = contract_last(ga_ref[...], joined(gate_ups, 1, 0))
+        total += contract_last(gb_ref[...], joined(gate_ups, 1, 1))
         put_blocks(outs, total)
 
 
-def backward_call(at, mask, scaled, begin, rows, part, c, e, downs, gates, ups):
-    count, _, width = scaled.shape
-    pieces, hid = len(gates), gates[0].shape[1]
+def backward_call(at, count, mask, scaled_input, part, c, e, downs, gate_ups):
+    read, arrays, specs, rows = scaled_input
+    width = arrays[0].shape[-1]
+    pieces, hid = len(downs), downs[0].shape[0]
     chunk = chunk_of(width, 1024)
     steps = width // chunk
     hidden = pieces * hid
     first = lambda i: jnp.minimum(i, steps - 1)
     second = lambda i: jnp.maximum(i - steps, 0)
-    scaled_specs = turned_specs(count, begin, rows, chunk, first)
     pre_spec = pl.BlockSpec((count, rows, hidden), lambda i, at: (0, part, 0))
     out_spec = pl.BlockSpec((rows, chunk), lambda i, at: (0, second(i)))
     return pl.pallas_call(
-        functools.partial(backward_kernel, count, len(scaled_specs), pieces, steps),
+        functools.partial(backward_kernel, read, len(arrays), count, pieces, steps),
         grid_spec=pltpu.PrefetchScalarGridSpec(
             num_scalar_prefetch=1,
             grid=(2 * steps,),
@@ -163,9 +182,9 @@
                 pre_spec,
                 pre_spec,
             ]
-            + scaled_specs
+            + [spec(chunk, first) for spec in specs]
             + [pl.BlockSpec((hid, chunk), lambda i, at: (0, first(i)))] * pieces
-            + [pl.BlockSpec((chunk, hid), lambda i, at: (second(i), 0))] * (2 * pieces),
+            + [pl.BlockSpec((2, chunk, hid), lambda i, at: (0, second(i), 0))] * pieces,
             out_specs=[out_spec] * count,
             scratch_shapes=[
                 pltpu.VMEM((count * rows, hidden), F32),
@@ -181,14 +200,14 @@
             bytes_accessed=4 * count * rows * width + 6 * width * hidden,
             transcendentals=count * rows * hidden,
         ),
-    )(at, mask, c, e, *[scaled] * len(scaled_specs), *downs, *gates, *ups)
-
-
-def forward_kernel(count, pieces, steps, mask_ref, own_ref, *refs):
-    ups_in, downs_in, refs = refs[: count - 1], refs[count - 1 : 2 * count - 2], refs[2 * count - 2 :]
-    gates, ups, downs = refs[:pieces], refs[pieces : 2 * pieces], refs[2 * pieces : 3 * pieces]
-    outs = refs[3 * pieces : 3 * pieces + count]
-    a_ref, b_ref, hidden_ref = refs[3 * pieces + count :]
+    )(at, mask, c, e, *arrays, *downs, *gate_ups)
+
+
+def forward_kernel(read, inputs, count, pieces, steps, at_ref, mask_ref, *refs):
+    xs, refs = refs[:inputs], refs[inputs:]
+    gate_ups, downs = refs[:pieces], refs[pieces : 2 * pieces]
+    outs = refs[2 * pieces : 2 * pieces + count]
+    a_ref, b_ref, hidden_ref = refs[2 * pieces + count :]
     step = pl.program_id(0)
 
     @pl.when(step == 0)
@@ -198,12 +217,9 @@
 
     @pl.when(step < steps)
     def _():
-        blocks = [own_ref[...]] + [
-            downs_in[away - 1][...] + ups_in[count - away - 1][...] for away in range(1, count)
-        ]
-        x = jnp.concatenate(blocks, axis=0)
-        a_ref[...] += jnp.dot(x, joined(gates, 1), preferred_element_type=F32)
-        b_ref[...] += jnp.dot(x, joined(ups, 1), preferred_element_type=F32)
+        x = read(xs)
+        a_ref[...] += jnp.dot(x, joined(gate_ups, 1, 0), preferred_element_type=F32)
+        b_ref[...] += jnp.dot(x, joined(gate_ups, 1, 1), preferred_element_type=F32)
 
     @pl.when(step == steps - 1)
     def _():
@@ -217,42 +233,44 @@
         put_blocks(outs, total)
 
 
-def forward_call(mask, own, ups_in, downs_in, gates, ups, downs):
-    rows, width = own.shape
-    count = len(ups_in) + 1
-    pieces, hid = len(gates), gates[0].shape[1]
+def forward_call(at, count, mask, x_input, gate_ups, downs):
+    read, arrays, specs, rows = x_input
+    width = arrays[0].shape[-1]
+    pieces, hid = len(downs), downs[0].shape[0]
     chunk = chunk_of(width, 1024)
     steps = width // chunk
     hidden = pieces * hid
     first = lambda i: jnp.minimum(i, steps - 1)
     second = lambda i: jnp.maximum(i - steps, 0)
-    x_spec = pl.BlockSpec((rows, chunk), lambda i: (0, first(i)))
     return pl.pallas_call(
-        functools.partial(forward_kernel, count, pieces, steps),
-        grid=(2 * steps,),
-        in_specs=[pl.BlockSpec((count * rows, 1), lambda i: (0, 0))]
-        + [x_spec] * (2 * count - 1)
-        + [pl.BlockSpec((chunk, hid), lambda i: (first(i), 0))] * (2 * pieces)
-        + [pl.BlockSpec((hid, chunk), lambda i: (0, second(i)))] * pieces,
-        out_specs=[pl.BlockSpec((rows, chunk), lambda i: (0, second(i)))] * count,
+        functools.partial(forward_kernel, read, len(arrays), count, pieces, steps),
+        grid_spec=pltpu.PrefetchScalarGridSpec(
+            num_scalar_prefetch=1,
+            grid=(2 * steps,),
+            in_specs=[pl.BlockSpec((count * rows, 1), lambda i, at: (0, 0))]
+            + [spec(chunk, first) for spec in specs]
+            + [pl.BlockSpec((2, chunk, hid), lambda i, at: (0, first(i), 0))] * pieces
+            + [pl.BlockSpec((hid, chunk), lambda i, at: (0, second(i)))] * pieces,
+            out_specs=[pl.BlockSpec((rows, chunk), lambda i, at: (0, second(i)))] * count,
+            scratch_shapes=[
+                pltpu.VMEM((count * rows, hidden), F32),
+                pltpu.VMEM((count * rows, hidden), F32),
+                pltpu.VMEM((count * rows, hidden), BF16),
+            ],
+        ),
         out_shape=[jax.ShapeDtypeStruct((rows, width), F32)]
         + [jax.ShapeDtypeStruct((rows, width), BF16)] * (count - 1),
-        scratch_shapes=[
-            pltpu.VMEM((count * rows, hidden), F32),
-            pltpu.VMEM((count * rows, hidden), F32),
-            pltpu.VMEM((count * rows, hidden), BF16),
-        ],
         compiler_params=pltpu.CompilerParams(vmem_limit_bytes=VMEM_LIMIT),
         cost_estimate=pl.CostEstimate(
             flops=6 * count * rows * width * hidden,
             bytes_accessed=6 * count * rows * width + 6 * width * hidden,
             transcendentals=count * rows * hidden,
         ),
-    )(mask, own, *ups_in, *downs_in, *gates, *ups, *downs)
+    )(at, mask, *arrays, *gate_ups, *downs)
 
 
 def after(value, *earlier):
-    return lax.optimization_barrier((value,) + earlier)[0]
+    return lax.optimization_barrier((value, earlier))[0]
 
 
 def hop(below, above, axis, step):
@@ -262,21 +280,20 @@
     return lax.ppermute(below, axis, up), lax.ppermute(above, axis, down)
 
 
-def steps_home(blocks, axis):
+def summands(blocks, step, arrived):
+    pair = (blocks[len(blocks) - step], blocks[step])
+    if arrived is None:
+        return pair
+    return tuple(
+        (own.astype(F32) + other.astype(F32)).astype(BF16) for own, other in zip(pair, arrived)
+    )
+
+
+def step_home(pair, axis, step):
     count = lax.axis_size(axis)
-    sends, arrivals = [], []
-    for step in range(1, count):
-        pair = (blocks[count - step], blocks[step])
-        if arrivals:
-            pair = tuple(
-                (own.astype(F32) + other.astype(F32)).astype(BF16)
-                for own, other in zip(pair, arrivals[-1])
-            )
-        up = lax.ppermute(pair[0], axis, [(i, i + 1) for i in range(step)])
-        down = lax.ppermute(pair[1], axis, [(i, i - 1) for i in range(count - step, count)])
-        sends.append(pair)
-        arrivals.append((up, down))
-    return sends, arrivals
+    up = lax.ppermute(pair[0], axis, [(i, i + 1) for i in range(step)])
+    down = lax.ppermute(pair[1], axis, [(i, i - 1) for i in range(count - step, count)])
+    return up, down
 
 
 def summed(block, arrived):
@@ -313,54 +330,67 @@
     early = tokens_here - last
     scaled_grad = (prob_backward[0][:, None] * grad_output[0].astype(F32)).astype(BF16)
     routes = jnp.concatenate([route_forward[0], route_backward[0]], axis=1)
+    gate_up, down = jnp.concatenate([w_gate[0], w_up[0]], axis=0), w_down[0, 0]
     bundle = jnp.concatenate([x_backward[0], scaled_grad[:early]], axis=0)
-    x_fwd, bundle, routes, scaled_last = lax.optimization_barrier(
-        (x_forward[0], bundle, routes, scaled_grad[early:])
-    )
+    bundle, routes, scaled_last = lax.optimization_barrier((bundle, routes, scaled_grad[early:]))
     bundle = lax.all_gather(bundle, "dp")
     routes = jnp.stack([routes] + [shifted(routes, "dp", -away) for away in range(1, count)])
     mine = (routes == expert_here).astype(F32)
     mask_fwd, mask_bwd = mine[:, :, 0:1], mine[:, :, 1:2]
 
-    own = [w_gate[0, 0], w_up[0, 0], w_down[0, 0]]
-    across = [flipped(weight, "expert", 2) for weight in own]
-    own_flips = [flipped(weight, "expert", 1) for weight in own]
-    x_sent = jnp.where(jnp.min(routes) >= 0, x_fwd, jnp.zeros_like(x_fwd))
-    from_below, from_above = [], []
-    earlier = [[], own_flips, [flipped(across[0], "expert", 1)]]
-    across_flips = [earlier[2][0]] + [flipped(weight, "expert", 1) for weight in across[1:]]
-    below, above = x_sent, x_sent
+    across_gate_up, across_down = flipped(gate_up, "expert", 2), flipped(down, "expert", 2)
+    x_sent = jnp.where(jnp.min(routes) >= 0, x_forward[0], jnp.zeros_like(x_forward[0]))
+    hops_x = [(x_sent, x_sent)]
     for step in range(1, count):
-        if step > 1:
-            below, above = after(below, *earlier[step - 1]), after(above, *earlier[step - 1])
-        below, above = hop(below, above, "dp", step)
-        from_below.append(below)
-        from_above.append(above)
-    gates, ups, downs = zip(own, own_flips, across, across_flips)
-
+        hops_x.append(hop(*hops_x[-1], "dp", step))
+    gate_ups = [gate_up, flipped(after(gate_up, *hops_x[1]), "expert", 1)]
+    gate_ups += [across_gate_up, flipped(across_gate_up, "expert", 1)]
+    downs = [down, flipped(down, "expert", 1), across_down, flipped(across_down, "expert", 1)]
+    late = after(scaled_last, *hops_x[2])
+    hops_last = [(late, late)]
+    hops_last.append(hop(*hops_last[-1], "dp", 1))
+
+    from_below, from_above = zip(*hops_x[1:])
     partial_fwd = forward_call(
-        mask_fwd.reshape(count * tokens_here, 1), x_fwd, from_below, from_above, gates, ups, downs
-    )
-    sends_fwd, arrivals_fwd = steps_home(partial_fwd, "dp")
-    scaled_last = lax.all_gather(scaled_last, "dp")
-    bundle = after(bundle, *sends_fwd[1])
-    c, e = gates_call(at, bundle, 0, tokens_here, gates, ups)
+        at,
+        count,
+        mask_fwd.reshape(count * tokens_here, 1),
+        chained_input(x_forward[0], from_below, from_above),
+        gate_ups,
+        downs,
+    )
+    late = [after(rows, partial_fwd[1]) for rows in hops_last[-1]]
+    for step in range(2, count):
+        hops_last.append(hop(*(late if step == 2 else hops_last[-1]), "dp", step))
+    arrived_fwd = step_home(summands(partial_fwd, 1, None), "dp", 1)
+    sent_home_fwd = summands(partial_fwd, 2, arrived_fwd)
+    arrived_fwd = step_home(sent_home_fwd, "dp", 2)
+    bundle = after(bundle, sent_home_fwd, hops_last[-1])
+    c, e = gates_call(at, count, gathered_input(bundle, 0, tokens_here), gate_ups)
     mask_early = mask_bwd[:, :early].reshape(count * early, 1)
+    scaled_early = gathered_input(bundle, tokens_here, early)
     blocks_early = backward_call(
-        at, mask_early, bundle, tokens_here, early, 0, c, e, downs, gates, ups
-    )
-    sends_early, arrivals_early = steps_home(blocks_early, "dp")
-    total_fwd = summed(partial_fwd[0], arrivals_fwd[-1])
+        at, count, mask_early, scaled_early, 0, c, e, downs, gate_ups
+    )
+
+    sent_home_fwd = summands(partial_fwd, 3, after(arrived_fwd, blocks_early[1]))
+    arrived_fwd = step_home(sent_home_fwd, "dp", 3)
+    arrived_early = step_home(summands(blocks_early, 1, None), "dp", 1)
+    from_below, from_above = zip(*hops_last[1:])
+    mask_last = after(mask_bwd[:, early:].reshape(count * last, 1), sent_home_fwd)
+    scaled_last = chained_input(scaled_last, from_below, from_above)
+    blocks_last = backward_call(
+        at, count, mask_last, scaled_last, early // last, c, e, downs, gate_ups
+    )
+
+    arrived_early, arrived_fwd = after((arrived_early, arrived_fwd), blocks_last[1])
+    total_fwd = summed(partial_fwd[0], arrived_fwd)
     layer_out = (x_forward[0].astype(F32) + prob_forward[0][:, None] * total_fwd).astype(BF16)
     sent_fwd = shifted(layer_out, "pipe", 1)
-
-    mask_last = mask_bwd[:, early:].reshape(count * last, 1)
-    scaled_last = after(scaled_last, *sends_early[1], *sends_fwd[-1])
-    blocks = backward_call(
-        at, mask_last, scaled_last, 0, last, early // last, c, e, downs, gates, ups
-    )
-    total_early = summed(blocks_early[0], arrivals_early[-1])
-    total_last = sent_home(blocks, "dp")
+    for step in range(2, count):
+        arrived_early = step_home(summands(blocks_early, step, arrived_early), "dp", step)
+    total_early = summed(blocks_early[0], arrived_early)
+    total_last = sent_home(blocks_last, "dp")
     sent_bwd = []
     for rows, total in ((slice(0, early), total_early), (slice(early, None), total_last)):
         grad_in = (grad_output[0, rows].astype(F32) + total).astype(BF16)

time: 425 us -> 416 us (0.979)
  waiting for transfers between devices: 243 us -> 198 us
  starting transfers between devices: 58.8 us -> 96.3 us
  local copies, waits for them, and re-layouts: 29.1 us -> 20.1 us
  Pallas kernels: 55.5 us -> 60.1 us
    ppermute x6 -> x12, starting transfers between devices: 18.6 us -> 54.4 us  [hop(): return (lax.ppermute(below, axis, up), lax.ppermute(above, axis, down))]
    ppermute x6 -> x12, waiting for transfers between devices: 118 us -> 85.3 us  [hop(): return (lax.ppermute(below, axis, up), lax.ppermute(above, axis, down))]
    ppermute x12, waiting for transfers between devices: 68.4 us -> 45.1 us  [the longest x6 39.1 us: step_home(): lax.ppermute(pair[1], axis, [(i, i - 1) for i in range(count - step, coun...]
    unnamed x91 -> x79, local copies, waits for them, and re-layouts: 27.8 us -> 19.5 us
    ppermute x9 -> x6, waiting for transfers between devices: 28.2 us -> 36 us  [flipped(): return lax.ppermute(block, axis, route)]
    pallas_call x4, Pallas kernels: 55.5 us -> 60.1 us  [the longest x2 33.5 us: backward_call(): pl.pallas_call(functools.partial(backward_kernel, read, len(arrays), coun...]
    concatenate x0 -> x1, other arithmetic: none -> 4.33 us  [few_experts(): jnp.concatenate([w_gate[0], w_up[0]], axis=0)]
  transfers between devices with their start and end apart: 38 -> 40, of which waited for: 14 -> 16; matrix products, arithmetic and copies ran while one was open for 4% -> 3% of each run, Pallas kernels for 13% -> 15%
where the time goes in v4:
time: 416 us; the launch traced here: 414 us
  waiting for transfers between devices  198 us (48%)
  starting transfers between devices  96.3 us (23%)
  Pallas kernels  60.1 us (14%)
  other arithmetic  22.1 us (5%)
  local copies, waits for them, and re-layouts  20.1 us (5%)
  between operations  17.3 us (4%)
    ppermute x12, waiting for transfers between devices, hop(): return (lax.ppermute(below, axis, up), lax.ppermute(above, axis, down))  85.3 us
    ppermute x12, starting transfers between devices, hop(): return (lax.ppermute(below, axis, up), lax.ppermute(above, axis, down))  54.4 us
    ppermute x6, waiting for transfers between devices, step_home(): lax.ppermute(pair[1], axis, [(i, i - 1) for i in range(count - step, coun...  39.1 us
    ppermute x6, waiting for transfers between devices, flipped(): return lax.ppermute(block, axis, route)  36 us
    pallas_call x2, Pallas kernels, backward_call(): pl.pallas_call(functools.partial(backward_kernel, read, len(arrays), coun...  33.5 us
    ppermute x9, waiting for transfers between devices, shifted(): lax.ppermute(block, axis, [((i - distance) % count, i) for i in range(cou...  31.4 us
    unnamed x79, local copies, waits for them, and re-layouts  19.5 us
    pallas_call x1, Pallas kernels, forward_call(): pl.pallas_call(functools.partial(forward_kernel, read, len(arrays), count...  16.2 us
  transfers between devices with their start and end apart: 40, of which 16 were waited for; matrix products, arithmetic and copies ran while one was open for 3% of the time, Pallas kernels for 15%

profile of v4, /device:TPU:20, one launch (start us, length us, event | category | flops | bytes accessed | tf_op | source)
XLA Modules:
  0.0 413.8 jit_solution(9299369842642460769)
XLA Ops:
  7.2 4.3 %pad_maximum_fusion.refs_7_.refs_4_.refs_8_.refs_11_ = bf16[2,7168,128]{2,1,0:T(8,128)(2,1)} fusion(bf16[1,7168,128]{2,1,0:T(8,128)(2,1)} %bitcast.43, bf16[1,7168,128]{2,1,0:T(8,128)(2,1)} %bitcast.44), kind=kLoop, calls=%fused_computation | loop fusion | flops 1835008 | bytes 7340032 | tf_op jit(solution)/shard_map/concatenate | solution.py:333
  11.6 1.5 collective-permute-start.10
  16.0 3.5 collective-permute-start.1
  24.7 3.9 collective-permute-start.6
  28.7 2.0 collective-permute-start.3
  31.3 57.6 %collective-permute-done.6.refs_4_ = bf16[64,7168]{1,0:T(8,128)(2,1)S(1)} collective-permute-done((bf16[64,7168]{1,0:T(8,128)(2,1)S(1)}, bf16[64,7168]{1,0:T(8,128)(2,1)S(1)}, u32[]{:S(2)}, u32[]{:S(2)}) %collective-permute-start.6) | collective-permute-done | bytes 917536 | tf_op jit(solution)/shard_map/ppermute | solution.py:280
  88.9 3.2 collective-permute-done.3.refs_1_
  92.1 2.0 collective-permute-done.10.refs_9_.refs_6_.refs_10_.refs_13_
  94.1 3.3 collective-permute-start.7
  98.3 34.0 %collective-permute-done.13.refs_13_.refs_6_.refs_9_ = bf16[128,7168]{1,0:T(8,128)(2,1)} collective-permute-done((bf16[128,7168]{1,0:T(8,128)(2,1)S(1)}, bf16[128,7168]{1,0:T(8,128)(2,1)}, u32[]{:S(2)}, u32[]{:S(2)}) %collective-permute-start.13) | collective-permute-done | bytes 1835040 | tf_op jit(solution)/shard_map/ppermute | solution.py:24
  132.3 3.5 collective-permute-start.4
  137.9 17.2 %collective-permute-done.7.refs_5_ = bf16[64,7168]{1,0:T(8,128)(2,1)} collective-permute-done((bf16[64,7168]{1,0:T(8,128)(2,1)S(1)}, bf16[64,7168]{1,0:T(8,128)(2,1)}, u32[]{:S(2)}, u32[]{:S(2)}) %collective-permute-start.7) | collective-permute-done | bytes 917536 | tf_op jit(solution)/shard_map/ppermute | solution.py:280
  155.1 1.6 collective-permute-start.8
  158.1 4.3 %collective-permute-start.5 = (bf16[64,7168]{1,0:T(8,128)(2,1)}, bf16[64,7168]{1,0:T(8,128)(2,1)}, u32[]{:S(2)}, u32[]{:S(2)}) collective-permute-start(bf16[64,7168]{1,0:T(8,128)(2,1)} %collective-permute-done.4.refs_2_), channel_id=1, source_target_pairs={{2,3},{6,7},{10,11},{14,15},{18,19},{22,23},{26,27},{30,31}} | collective-permute-start | bytes 2752520 | tf_op jit(solution)/shard_map/ppermute | solution.py:280
  162.6 18.2 %collective-permute-start.20 = (bf16[32,7168]{1,0:T(8,128)(2,1)S(1)}, bf16[32,7168]{1,0:T(8,128)(2,1)S(1)}, u32[]{:S(2)}, u32[]{:S(2)}) collective-permute-start(bf16[32,7168]{1,0:T(8,128)(2,1)S(1)} %get-tuple-element.39.refs_0_), channel_id=1, source_target_pairs={{1,0},{2,1},{3,2},{5,4},{6,5},{7,6},{9,8},{10,9},{11,10},{13,12},{... | collective-permute-start | bytes 1376264 | tf_op jit(solution)/shard_map/ppermute | solution.py:280
  181.0 4.4 %collective-permute-start.17 = (bf16[32,7168]{1,0:T(8,128)(2,1)S(1)}, bf16[32,7168]{1,0:T(8,128)(2,1)S(1)}, u32[]{:S(2)}, u32[]{:S(2)}) collective-permute-start(bf16[32,7168]{1,0:T(8,128)(2,1)S(1)} %get-tuple-element.39.refs_0_), channel_id=1, source_target_pairs={{0,1},{1,2},{2,3},{4,5},{5,6},{6,7},{8,9},{9,10},{10,11},{12,13},{... | collective-permute-start | bytes 1376264 | tf_op jit(solution)/shard_map/ppermute | solution.py:280
  185.4 1.5 copy-done.4
  189.2 16.2 %shard_map.113 = (f32[64,7168]{1,0:T(8,128)S(1)}, bf16[64,7168]{1,0:T(8,128)(2,1)S(1)}, bf16[64,7168]{1,0:T(8,128)(2,1)S(1)}, bf16[64,7168]{1,0:T(8,128)(2,1)S(1)}) custom-call(s32[1]{0:T(128)} %bitcast.2.at_ref, f32[256,1]{1,0:T(8,128)S(1)} %reshape.32.mask_ref, bf16[64,7168]{1,0:T(8,128)(2,1)S(1)} %bitcast.42, bf16[64,7168]{1,0:T(8,128)(2,1)S(1)} %copy-done.23, ...), custom_call_target="tpu_custom_call" | custom-call | flops 5637144576 | bytes 33030144 | tf_op jit(solution)/shard_map/pallas_call | solution.py:245
  207.6 4.6 %collective-permute-start.18 = (bf16[32,7168]{1,0:T(8,128)(2,1)S(1)}, bf16[32,7168]{1,0:T(8,128)(2,1)S(1)}, u32[]{:S(2)}, u32[]{:S(2)}) collective-permute-start(bf16[32,7168]{1,0:T(8,128)(2,1)S(1)} %collective-permute-done.17.refs_1_), channel_id=1, source_target_pairs={{1,2},{2,3},{5,6},{6,7},{9,10},{10,11},{13,14},{14,15},{17,18},{18... | collective-permute-start | bytes 1376264 | tf_op jit(solution)/shard_map/ppermute | solution.py:280
  212.2 2.1 collective-permute-start.21
  214.3 5.8 %collective-permute-done.18.refs_2_ = bf16[32,7168]{1,0:T(8,128)(2,1)S(1)} collective-permute-done((bf16[32,7168]{1,0:T(8,128)(2,1)S(1)}, bf16[32,7168]{1,0:T(8,128)(2,1)S(1)}, u32[]{:S(2)}, u32[]{:S(2)}) %collective-permute-start.18) | collective-permute-done | bytes 458784 | tf_op jit(solution)/shard_map/ppermute | solution.py:280
  220.1 5.1 %collective-permute-start.19 = (bf16[32,7168]{1,0:T(8,128)(2,1)S(1)}, bf16[32,7168]{1,0:T(8,128)(2,1)}, u32[]{:S(2)}, u32[]{:S(2)}) collective-permute-start(bf16[32,7168]{1,0:T(8,128)(2,1)S(1)} %collective-permute-done.18.refs_2_), channel_id=1, source_target_pairs={{2,3},{6,7},{10,11},{14,15},{18,19},{22,23},{26,27},{30,31}} | collective-permute-start | bytes 1376264 | tf_op jit(solution)/shard_map/ppermute | solution.py:280
  228.5 1.6 fusion.1
  230.2 1.9 collective-permute-start.26
  233.7 2.6 copy-done
  236.2 10.4 %shard_map.114 = (f32[4,64,512]{2,1,0:T(8,128)S(1)}, f32[4,64,512]{2,1,0:T(8,128)S(1)}) custom-call(s32[1]{0:T(128)} %bitcast.2.at_ref, bf16[4,96,7168]{2,1,0:T(8,128)(2,1)S(1)} %bitcast.29, bf16[4,96,7168]{2,1,0:T(8,128)(2,1)S(1)} %bitcast.30, bf16[4,96,7168]{2,1,0:T(8,128)(2,1)S(1)} %bitcast.31, bf16[4,96,7168]{2,1,0:T(8,128)(2,1)S(1)} %bitcast.32, ...), custom_call_target="tpu_custom_call" | custom-call | flops 3758096384 | bytes 18350080 | tf_op jit(solution)/shard_map/pallas_call | solution.py:114
  246.6 17.2 %shard_map.115 = (f32[32,7168]{1,0:T(8,128)S(1)}, bf16[32,7168]{1,0:T(8,128)(2,1)}, bf16[32,7168]{1,0:T(8,128)(2,1)S(1)}, bf16[32,7168]{1,0:T(8,128)(2,1)}) custom-call(s32[1]{0:T(128)} %bitcast.2.at_ref, f32[128,1]{1,0:T(8,128)S(1)} %reshape.33.mask_ref, f32[4,64,512]{2,1,0:T(8,128)S(1)} %get-tuple-element.43.c_ref, ...), custom_call_target="tpu_custom_call" | custom-call | flops 2818572288 | bytes 25690112 | tf_op jit(solution)/shard_map/pallas_call | solution.py:175
  264.7 2.7 add_convert_fusion.2
  267.3 2.3 add_convert_fusion.1
  269.6 4.5 %collective-permute-start.28 = (bf16[64,7168]{1,0:T(8,128)(2,1)}, bf16[64,7168]{1,0:T(8,128)(2,1)}, u32[]{:S(2)}, u32[]{:S(2)}) collective-permute-start(bf16[64,7168]{1,0:T(8,128)(2,1)} %add_convert_fusion.1), channel_id=1, source_target_pairs={{1,0},{2,1},{3,2},{5,4},{6,5},{7,6},{9,8},{10,9},{11,10},{13,12},{... | collective-permute-start | bytes 2752520 | tf_op jit(solution)/shard_map/ppermute | solution.py:295
  274.2 2.8 collective-permute-start.27
  277.0 1.5 collective-permute-start.23
  280.0 1.5 copy-done.6
  286.6 16.3 %shard_map.116 = (f32[32,7168]{1,0:T(8,128)S(1)}, bf16[32,7168]{1,0:T(8,128)(2,1)S(1)}, bf16[32,7168]{1,0:T(8,128)(2,1)S(1)}, bf16[32,7168]{1,0:T(8,128)(2,1)S(1)}) custom-call(s32[1]{0:T(128)} %bitcast.2.at_ref, f32[128,1]{1,0:T(8,128)S(1)} %copy.16.mask_ref, f32[4,64,512]{2,1,0:T(8,128)S(1)} %get-tuple-element.43.c_ref, f32[4,64,512]{2,1,0:T(8,128)S(1)} %copy-done.9, ...), custom_call_target="tpu_custom_call" | custom-call | flops 2818572288 | bytes 25690112 | tf_op jit(solution)/shard_map/pallas_call | solution.py:175
  305.8 2.9 collective-permute-start.35
  308.6 2.4 collective-permute-start.36
  311.1 2.8 collective-permute-start.37
  313.9 1.9 collective-permute-start.32
  315.8 5.0 %collective-permute-done.30 = bf16[32,7168]{1,0:T(8,128)(2,1)S(1)} collective-permute-done((bf16[32,7168]{1,0:T(8,128)(2,1)S(1)}, bf16[32,7168]{1,0:T(8,128)(2,1)S(1)}, u32[]{:S(2)}, u32[]{:S(2)}) %collective-permute-start.30) | collective-permute-done | bytes 458784 | tf_op jit(solution)/shard_map/ppermute | solution.py:294
  322.0 1.9 collective-permute-start.31
  323.9 32.6 %collective-permute-done.32 = bf16[32,7168]{1,0:T(8,128)(2,1)S(1)} collective-permute-done((bf16[32,7168]{1,0:T(8,128)(2,1)S(1)}, bf16[32,7168]{1,0:T(8,128)(2,1)S(1)}, u32[]{:S(2)}, u32[]{:S(2)}) %collective-permute-start.32) | collective-permute-done | bytes 458784 | tf_op jit(solution)/shard_map/ppermute | solution.py:295
  357.6 4.4 %collective-permute-start.33 = (bf16[32,7168]{1,0:T(8,128)(2,1)S(1)}, bf16[32,7168]{1,0:T(8,128)(2,1)S(1)}, u32[]{:S(2)}, u32[]{:S(2)}) collective-permute-start(bf16[32,7168]{1,0:T(8,128)(2,1)S(1)} %add_convert_fusion.3), channel_id=1, source_target_pairs={{1,0},{2,1},{3,2},{5,4},{6,5},{7,6},{9,8},{10,9},{11,10},{13,12},{... | collective-permute-start | bytes 1376264 | tf_op jit(solution)/shard_map/ppermute | solution.py:295
  362.1 2.1 add_convert_fusion
  365.7 5.4 %collective-permute-done.33 = bf16[32,7168]{1,0:T(8,128)(2,1)S(1)} collective-permute-done((bf16[32,7168]{1,0:T(8,128)(2,1)S(1)}, bf16[32,7168]{1,0:T(8,128)(2,1)S(1)}, u32[]{:S(2)}, u32[]{:S(2)}) %collective-permute-start.33) | collective-permute-done | bytes 458784 | tf_op jit(solution)/shard_map/ppermute | solution.py:295
  372.1 1.5 collective-permute-start.38
  373.6 13.9 %collective-permute-done.29 = bf16[64,7168]{1,0:T(8,128)(2,1)S(1)} collective-permute-done((bf16[64,7168]{1,0:T(8,128)(2,1)S(1)}, bf16[64,7168]{1,0:T(8,128)(2,1)S(1)}, u32[]{:S(2)}, u32[]{:S(2)}) %collective-permute-start.29) | collective-permute-done | bytes 917536 | tf_op jit(solution)/shard_map/ppermute | solution.py:29
  387.5 9.8 %collective-permute-done.34 = bf16[32,7168]{1,0:T(8,128)(2,1)S(1)} collective-permute-done((bf16[32,7168]{1,0:T(8,128)(2,1)S(1)}, bf16[32,7168]{1,0:T(8,128)(2,1)S(1)}, u32[]{:S(2)}, u32[]{:S(2)}) %collective-permute-start.34) | collective-permute-done | bytes 458784 | tf_op jit(solution)/shard_map/ppermute | solution.py:29
  397.4 7.6 %collective-permute-done.38 = bf16[32,7168]{1,0:T(8,128)(2,1)S(1)} collective-permute-done((bf16[32,7168]{1,0:T(8,128)(2,1)S(1)}, bf16[32,7168]{1,0:T(8,128)(2,1)S(1)}, u32[]{:S(2)}, u32[]{:S(2)}) %collective-permute-start.38) | collective-permute-done | bytes 458784 | tf_op jit(solution)/shard_map/ppermute | solution.py:29
  (142 shorter events, 37.1 us)
Async XLA Ops:
  7.2 226.5 %all-gather.3.cloned.1.call-start = ((), (), s32[]{:S(2)}) async-start(), calls=%async_computation | async-start | bytes 6881280 | tf_op jit(solution)/shard_map/all_gather | solution.py:336
  11.6 82.5 %collective-permute-start.10 = (bf16[2,7168,128]{2,1,0:T(8,128)(2,1)}, bf16[2,7168,128]{2,1,0:T(8,128)(2,1)}, u32[]{:S(2)}, u32[]{:S(2)}) collective-permute-start(bf16[2,7168,128]{2,1,0:T(8,128)(2,1)} %pad_maximum_fusion.refs_7_.refs_4_.refs_8_.refs_11_), channel_id=1, source_target_pairs={{0,8},{4,12},{8,0},{12,4},{1,9},{5,13},{9,1},{13,5},{2,10},{6,14},... | collective-permute-start | bytes 11010056 | tf_op jit(solution)/shard_map/ppermute | solution.py:24
  13.4 167.6 %copy-start.12 = (bf16[32,7168]{1,0:T(8,128)(2,1)}, bf16[32,7168]{1,0:T(8,128)(2,1)S(1)}, u32[]{:S(2)}) copy-start(bf16[32,7168]{1,0:T(8,128)(2,1)S(1)} %get-tuple-element.39.refs_0_) | copy-start | bytes 1376260
  15.5 4.6 %collective-permute-start = (s32[64,2]{0,1:T(2,128)S(1)}, s32[64,2]{0,1:T(2,128)S(1)}, u32[]{:S(2)}, u32[]{:S(2)}) collective-permute-start(s32[64,2]{0,1:T(2,128)S(1)} %pad_add_fusion), channel_id=1, source_target_pairs={{1,0},{2,1},{3,2},{0,3},{5,4},{6,5},{7,6},{4,7},{9,8},{10,9},{11,1... | collective-permute-start | bytes 1544 | tf_op jit(solution)/shard_map/ppermute | solution.py:29
  16.0 6.1 %collective-permute-start.1 = (s32[64,2]{0,1:T(2,128)S(1)}, s32[64,2]{0,1:T(2,128)S(1)}, u32[]{:S(2)}, u32[]{:S(2)}) collective-permute-start(s32[64,2]{0,1:T(2,128)S(1)} %pad_add_fusion), channel_id=1, source_target_pairs={{2,0},{3,1},{0,2},{1,3},{6,4},{7,5},{4,6},{5,7},{10,8},{11,9},{8,1... | collective-permute-start | bytes 1544 | tf_op jit(solution)/shard_map/ppermute | solution.py:29
  19.4 3.9 collective-permute-start.2
  24.7 64.1 %collective-permute-start.6 = (bf16[64,7168]{1,0:T(8,128)(2,1)S(1)}, bf16[64,7168]{1,0:T(8,128)(2,1)S(1)}, u32[]{:S(2)}, u32[]{:S(2)}) collective-permute-start(bf16[64,7168]{1,0:T(8,128)(2,1)S(1)} %broadcast_select_fusion), channel_id=1, source_target_pairs={{1,0},{2,1},{3,2},{5,4},{6,5},{7,6},{9,8},{10,9},{11,10},{13,12},{... | collective-permute-start | bytes 2752520 | tf_op jit(solution)/shard_map/ppermute | solution.py:280
  28.7 63.4 %collective-permute-start.3 = (bf16[64,7168]{1,0:T(8,128)(2,1)S(1)}, bf16[64,7168]{1,0:T(8,128)(2,1)S(1)}, u32[]{:S(2)}, u32[]{:S(2)}) collective-permute-start(bf16[64,7168]{1,0:T(8,128)(2,1)S(1)} %broadcast_select_fusion), channel_id=1, source_target_pairs={{0,1},{1,2},{2,3},{4,5},{5,6},{6,7},{8,9},{9,10},{10,11},{12,13},{... | collective-permute-start | bytes 2752520 | tf_op jit(solution)/shard_map/ppermute | solution.py:280
  30.6 101.6 %collective-permute-start.13 = (bf16[128,7168]{1,0:T(8,128)(2,1)S(1)}, bf16[128,7168]{1,0:T(8,128)(2,1)}, u32[]{:S(2)}, u32[]{:S(2)}) collective-permute-start(bf16[128,7168]{1,0:T(8,128)(2,1)S(1)} %bitcast.37), channel_id=1, source_target_pairs={{0,8},{4,12},{8,0},{12,4},{1,9},{5,13},{9,1},{13,5},{2,10},{6,14},... | collective-permute-start | bytes 5505032 | tf_op jit(solution)/shard_map/ppermute | solution.py:24
  31.2 105.4 %collective-permute-start.12 = (bf16[128,7168]{1,0:T(8,128)(2,1)S(1)}, bf16[128,7168]{1,0:T(8,128)(2,1)S(1)}, u32[]{:S(2)}, u32[]{:S(2)}) collective-permute-start(bf16[128,7168]{1,0:T(8,128)(2,1)S(1)} %bitcast.38), channel_id=1, source_target_pairs={{0,4},{4,0},{8,12},{12,8},{1,5},{5,1},{9,13},{13,9},{2,6},{6,2},{1... | collective-permute-start | bytes 5505032 | tf_op jit(solution)/shard_map/ppermute | solution.py:24
  92.1 93.3 %collective-permute-start.9 = (bf16[2,7168,128]{2,1,0:T(8,128)(2,1)}, bf16[2,7168,128]{2,1,0:T(8,128)(2,1)}, u32[]{:S(2)}, u32[]{:S(2)}) collective-permute-start(bf16[2,7168,128]{2,1,0:T(8,128)(2,1)} %pad_maximum_fusion.refs_7_.refs_4_.refs_8_.refs_11_), channel_id=1, source_target_pairs={{0,4},{4,0},{8,12},{12,8},{1,5},{5,1},{9,13},{13,9},{2,6},{6,2},{1... | collective-permute-start | bytes 11010056 | tf_op jit(solution)/shard_map/ppermute | solution.py:24
  94.1 91.3 %collective-permute-start.11 = (bf16[2,7168,128]{2,1,0:T(8,128)(2,1)}, bf16[2,7168,128]{2,1,0:T(8,128)(2,1)}, u32[]{:S(2)}, u32[]{:S(2)}) collective-permute-start(bf16[2,7168,128]{2,1,0:T(8,128)(2,1)} %collective-permute-done.10.refs_9_.refs_6_.refs_10_.refs_13_), channel_id=1, source_target_pairs={{0,4},{4,0},{8,12},{12,8},{1,5},{5,1},{9,13},{13,9},{2,6},{6,2},{1... | collective-permute-start | bytes 11010056 | tf_op jit(solution)/shard_map/ppermute | solution.py:24
  94.1 61.0 %collective-permute-start.7 = (bf16[64,7168]{1,0:T(8,128)(2,1)S(1)}, bf16[64,7168]{1,0:T(8,128)(2,1)}, u32[]{:S(2)}, u32[]{:S(2)}) collective-permute-start(bf16[64,7168]{1,0:T(8,128)(2,1)S(1)} %collective-permute-done.6.refs_4_), channel_id=1, source_target_pairs={{1,0},{2,1},{5,4},{6,5},{9,8},{10,9},{13,12},{14,13},{17,16},{18,1... | collective-permute-start | bytes 2752520 | tf_op jit(solution)/shard_map/ppermute | solution.py:280
  132.3 25.8 %collective-permute-start.4 = (bf16[64,7168]{1,0:T(8,128)(2,1)S(1)}, bf16[64,7168]{1,0:T(8,128)(2,1)}, u32[]{:S(2)}, u32[]{:S(2)}) collective-permute-start(bf16[64,7168]{1,0:T(8,128)(2,1)S(1)} %collective-permute-done.3.refs_1_), channel_id=1, source_target_pairs={{1,2},{2,3},{5,6},{6,7},{9,10},{10,11},{13,14},{14,15},{17,18},{18... | collective-permute-start | bytes 2752520 | tf_op jit(solution)/shard_map/ppermute | solution.py:280
  137.9 47.4 %collective-permute-start.14 = (bf16[128,7168]{1,0:T(8,128)(2,1)}, bf16[128,7168]{1,0:T(8,128)(2,1)}, u32[]{:S(2)}, u32[]{:S(2)}) collective-permute-start(bf16[128,7168]{1,0:T(8,128)(2,1)} %collective-permute-done.13.refs_13_.refs_6_.refs_9_), channel_id=1, source_target_pairs={{0,4},{4,0},{8,12},{12,8},{1,5},{5,1},{9,13},{13,9},{2,6},{6,2},{1... | collective-permute-start | bytes 5505032 | tf_op jit(solution)/shard_map/ppermute | solution.py:24
  155.1 7.6 %collective-permute-start.8 = (bf16[64,7168]{1,0:T(8,128)(2,1)}, bf16[64,7168]{1,0:T(8,128)(2,1)}, u32[]{:S(2)}, u32[]{:S(2)}) collective-permute-start(bf16[64,7168]{1,0:T(8,128)(2,1)} %collective-permute-done.7.refs_5_), channel_id=1, source_target_pairs={{1,0},{5,4},{9,8},{13,12},{17,16},{21,20},{25,24},{29,28}} | collective-permute-start | bytes 2752520 | tf_op jit(solution)/shard_map/ppermute | solution.py:280
  158.1 22.8 %collective-permute-start.5 = (bf16[64,7168]{1,0:T(8,128)(2,1)}, bf16[64,7168]{1,0:T(8,128)(2,1)}, u32[]{:S(2)}, u32[]{:S(2)}) collective-permute-start(bf16[64,7168]{1,0:T(8,128)(2,1)} %collective-permute-done.4.refs_2_), channel_id=1, source_target_pairs={{2,3},{6,7},{10,11},{14,15},{18,19},{22,23},{26,27},{30,31}} | collective-permute-start | bytes 2752520 | tf_op jit(solution)/shard_map/ppermute | solution.py:280
  162.6 44.9 %collective-permute-start.20 = (bf16[32,7168]{1,0:T(8,128)(2,1)S(1)}, bf16[32,7168]{1,0:T(8,128)(2,1)S(1)}, u32[]{:S(2)}, u32[]{:S(2)}) collective-permute-start(bf16[32,7168]{1,0:T(8,128)(2,1)S(1)} %get-tuple-element.39.refs_0_), channel_id=1, source_target_pairs={{1,0},{2,1},{3,2},{5,4},{6,5},{7,6},{9,8},{10,9},{11,10},{13,12},{... | collective-permute-start | bytes 1376264 | tf_op jit(solution)/shard_map/ppermute | solution.py:280
  181.0 26.6 %collective-permute-start.17 = (bf16[32,7168]{1,0:T(8,128)(2,1)S(1)}, bf16[32,7168]{1,0:T(8,128)(2,1)S(1)}, u32[]{:S(2)}, u32[]{:S(2)}) collective-permute-start(bf16[32,7168]{1,0:T(8,128)(2,1)S(1)} %get-tuple-element.39.refs_0_), channel_id=1, source_target_pairs={{0,1},{1,2},{2,3},{4,5},{5,6},{6,7},{8,9},{9,10},{10,11},{12,13},{... | collective-permute-start | bytes 1376264 | tf_op jit(solution)/shard_map/ppermute | solution.py:280
  205.5 24.7 %copy-start.10 = (f32[64,7168]{1,0:T(8,128)}, f32[64,7168]{1,0:T(8,128)S(1)}, u32[]{:S(2)}) copy-start(f32[64,7168]{1,0:T(8,128)S(1)} %get-tuple-element.33) | copy-start | bytes 5505028
  205.5 24.7 %copy-start.16 = (bf16[64,7168]{1,0:T(8,128)(2,1)}, bf16[64,7168]{1,0:T(8,128)(2,1)S(1)}, u32[]{:S(2)}) copy-start(bf16[64,7168]{1,0:T(8,128)(2,1)S(1)} %get-tuple-element.36) | copy-start | bytes 2752516
  205.5 24.7 %copy-start.18 = (bf16[64,7168]{1,0:T(8,128)(2,1)}, bf16[64,7168]{1,0:T(8,128)(2,1)S(1)}, u32[]{:S(2)}) copy-start(bf16[64,7168]{1,0:T(8,128)(2,1)S(1)} %get-tuple-element.37) | copy-start | bytes 2752516
  205.5 21.9 %collective-permute-start.15 = (bf16[64,7168]{1,0:T(8,128)(2,1)S(1)}, bf16[64,7168]{1,0:T(8,128)(2,1)S(1)}, u32[]{:S(2)}, u32[]{:S(2)}) collective-permute-start(bf16[64,7168]{1,0:T(8,128)(2,1)S(1)} %get-tuple-element.36), channel_id=1, source_target_pairs={{0,1},{4,5},{8,9},{12,13},{16,17},{20,21},{24,25},{28,29}} | collective-permute-start | bytes 2752520 | tf_op jit(solution)/shard_map/ppermute | solution.py:294
  206.2 22.3 %collective-permute-start.16 = (bf16[64,7168]{1,0:T(8,128)(2,1)S(1)}, bf16[64,7168]{1,0:T(8,128)(2,1)S(1)}, u32[]{:S(2)}, u32[]{:S(2)}) collective-permute-start(bf16[64,7168]{1,0:T(8,128)(2,1)S(1)} %get-tuple-element.37), channel_id=1, source_target_pairs={{3,2},{7,6},{11,10},{15,14},{19,18},{23,22},{27,26},{31,30}} | collective-permute-start | bytes 2752520 | tf_op jit(solution)/shard_map/ppermute | solution.py:295
  207.6 22.6 %copy-start.24 = (bf16[32,7168]{1,0:T(8,128)(2,1)}, bf16[32,7168]{1,0:T(8,128)(2,1)S(1)}, u32[]{:S(2)}) copy-start(bf16[32,7168]{1,0:T(8,128)(2,1)S(1)} %collective-permute-done.20.refs_4_) | copy-start | bytes 1376260
  207.6 22.6 %copy-start.26 = (bf16[32,7168]{1,0:T(8,128)(2,1)}, bf16[32,7168]{1,0:T(8,128)(2,1)S(1)}, u32[]{:S(2)}) copy-start(bf16[32,7168]{1,0:T(8,128)(2,1)S(1)} %collective-permute-done.17.refs_1_) | copy-start | bytes 1376260
  207.6 12.5 %collective-permute-start.18 = (bf16[32,7168]{1,0:T(8,128)(2,1)S(1)}, bf16[32,7168]{1,0:T(8,128)(2,1)S(1)}, u32[]{:S(2)}, u32[]{:S(2)}) collective-permute-start(bf16[32,7168]{1,0:T(8,128)(2,1)S(1)} %collective-permute-done.17.refs_1_), channel_id=1, source_target_pairs={{1,2},{2,3},{5,6},{6,7},{9,10},{10,11},{13,14},{14,15},{17,18},{18... | collective-permute-start | bytes 1376264 | tf_op jit(solution)/shard_map/ppermute | solution.py:280
  212.2 13.7 %collective-permute-start.21 = (bf16[32,7168]{1,0:T(8,128)(2,1)S(1)}, bf16[32,7168]{1,0:T(8,128)(2,1)}, u32[]{:S(2)}, u32[]{:S(2)}) collective-permute-start(bf16[32,7168]{1,0:T(8,128)(2,1)S(1)} %collective-permute-done.20.refs_4_), channel_id=1, source_target_pairs={{1,0},{2,1},{5,4},{6,5},{9,8},{10,9},{13,12},{14,13},{17,16},{18,1... | collective-permute-start | bytes 1376264 | tf_op jit(solution)/shard_map/ppermute | solution.py:280
  220.1 13.6 %collective-permute-start.19 = (bf16[32,7168]{1,0:T(8,128)(2,1)S(1)}, bf16[32,7168]{1,0:T(8,128)(2,1)}, u32[]{:S(2)}, u32[]{:S(2)}) collective-permute-start(bf16[32,7168]{1,0:T(8,128)(2,1)S(1)} %collective-permute-done.18.refs_2_), channel_id=1, source_target_pairs={{2,3},{6,7},{10,11},{14,15},{18,19},{22,23},{26,27},{30,31}} | collective-permute-start | bytes 1376264 | tf_op jit(solution)/shard_map/ppermute | solution.py:280
  225.9 7.7 %collective-permute-start.22 = (bf16[32,7168]{1,0:T(8,128)(2,1)}, bf16[32,7168]{1,0:T(8,128)(2,1)}, u32[]{:S(2)}, u32[]{:S(2)}) collective-permute-start(bf16[32,7168]{1,0:T(8,128)(2,1)} %collective-permute-done.21.refs_5_), channel_id=1, source_target_pairs={{1,0},{5,4},{9,8},{13,12},{17,16},{21,20},{25,24},{29,28}} | collective-permute-start | bytes 1376264 | tf_op jit(solution)/shard_map/ppermute | solution.py:280
  230.2 34.5 %collective-permute-start.26 = (bf16[64,7168]{1,0:T(8,128)(2,1)}, bf16[64,7168]{1,0:T(8,128)(2,1)}, u32[]{:S(2)}, u32[]{:S(2)}) collective-permute-start(bf16[64,7168]{1,0:T(8,128)(2,1)} %get-tuple-element.64), channel_id=1, source_target_pairs={{2,1},{3,2},{6,5},{7,6},{10,9},{11,10},{14,13},{15,14},{18,17},{19... | collective-permute-start | bytes 2752520 | tf_op jit(solution)/shard_map/ppermute | solution.py:295
  232.1 32.5 %collective-permute-start.25 = (bf16[64,7168]{1,0:T(8,128)(2,1)}, bf16[64,7168]{1,0:T(8,128)(2,1)}, u32[]{:S(2)}, u32[]{:S(2)}) collective-permute-start(bf16[64,7168]{1,0:T(8,128)(2,1)} %get-tuple-element.65), channel_id=1, source_target_pairs={{0,1},{1,2},{4,5},{5,6},{8,9},{9,10},{12,13},{13,14},{16,17},{17,1... | collective-permute-start | bytes 2752520 | tf_op jit(solution)/shard_map/ppermute | solution.py:294
  269.6 33.3 %collective-permute-start.28 = (bf16[64,7168]{1,0:T(8,128)(2,1)}, bf16[64,7168]{1,0:T(8,128)(2,1)}, u32[]{:S(2)}, u32[]{:S(2)}) collective-permute-start(bf16[64,7168]{1,0:T(8,128)(2,1)} %add_convert_fusion.1), channel_id=1, source_target_pairs={{1,0},{2,1},{3,2},{5,4},{6,5},{7,6},{9,8},{10,9},{11,10},{13,12},{... | collective-permute-start | bytes 2752520 | tf_op jit(solution)/shard_map/ppermute | solution.py:295
  274.2 28.8 %collective-permute-start.27 = (bf16[64,7168]{1,0:T(8,128)(2,1)}, bf16[64,7168]{1,0:T(8,128)(2,1)}, u32[]{:S(2)}, u32[]{:S(2)}) collective-permute-start(bf16[64,7168]{1,0:T(8,128)(2,1)} %add_convert_fusion.2), channel_id=1, source_target_pairs={{0,1},{1,2},{2,3},{4,5},{5,6},{6,7},{8,9},{9,10},{10,11},{12,13},{... | collective-permute-start | bytes 2752520 | tf_op jit(solution)/shard_map/ppermute | solution.py:294
  277.0 25.9 %collective-permute-start.23 = (bf16[32,7168]{1,0:T(8,128)(2,1)}, bf16[32,7168]{1,0:T(8,128)(2,1)}, u32[]{:S(2)}, u32[]{:S(2)}) collective-permute-start(bf16[32,7168]{1,0:T(8,128)(2,1)} %get-tuple-element.45), channel_id=1, source_target_pairs={{0,1},{4,5},{8,9},{12,13},{16,17},{20,21},{24,25},{28,29}} | collective-permute-start | bytes 1376264 | tf_op jit(solution)/shard_map/ppermute | solution.py:294
  278.5 24.4 %collective-permute-start.24 = (bf16[32,7168]{1,0:T(8,128)(2,1)}, bf16[32,7168]{1,0:T(8,128)(2,1)}, u32[]{:S(2)}, u32[]{:S(2)}) collective-permute-start(bf16[32,7168]{1,0:T(8,128)(2,1)} %get-tuple-element.46), channel_id=1, source_target_pairs={{3,2},{7,6},{11,10},{15,14},{19,18},{23,22},{27,26},{31,30}} | collective-permute-start | bytes 1376264 | tf_op jit(solution)/shard_map/ppermute | solution.py:295
  304.3 57.7 %copy-start.11 = (f32[64,7168]{1,0:T(8,128)S(1)}, f32[64,7168]{1,0:T(8,128)}, u32[]{:S(2)}) copy-start(f32[64,7168]{1,0:T(8,128)} %copy-done.10) | copy-start | bytes 5505028
  304.3 57.7 %copy-start.35 = (f32[1,64]{1,0:T(1,128)S(1)}, f32[1,64]{1,0:T(1,128)}, u32[]{:S(2)}) copy-start(f32[1,64]{1,0:T(1,128)} %param.12) | copy-start | bytes 772
  304.3 16.5 %collective-permute-start.30 = (bf16[32,7168]{1,0:T(8,128)(2,1)S(1)}, bf16[32,7168]{1,0:T(8,128)(2,1)S(1)}, u32[]{:S(2)}, u32[]{:S(2)}) collective-permute-start(bf16[32,7168]{1,0:T(8,128)(2,1)S(1)} %get-tuple-element.68), channel_id=1, source_target_pairs={{0,1},{1,2},{4,5},{5,6},{8,9},{9,10},{12,13},{13,14},{16,17},{17,1... | collective-permute-start | bytes 1376264 | tf_op jit(solution)/shard_map/ppermute | solution.py:294
  305.8 59.0 %collective-permute-start.35 = (bf16[32,7168]{1,0:T(8,128)(2,1)S(1)}, bf16[32,7168]{1,0:T(8,128)(2,1)S(1)}, u32[]{:S(2)}, u32[]{:S(2)}) collective-permute-start(bf16[32,7168]{1,0:T(8,128)(2,1)S(1)} %get-tuple-element.50), channel_id=1, source_target_pairs={{3,0},{0,1},{1,2},{2,3},{7,4},{4,5},{5,6},{6,7},{11,8},{8,9},{9,10... | collective-permute-start | bytes 1376264 | tf_op jit(solution)/shard_map/ppermute | solution.py:29
  308.6 55.5 %collective-permute-start.36 = (bf16[32,7168]{1,0:T(8,128)(2,1)S(1)}, bf16[32,7168]{1,0:T(8,128)(2,1)S(1)}, u32[]{:S(2)}, u32[]{:S(2)}) collective-permute-start(bf16[32,7168]{1,0:T(8,128)(2,1)S(1)} %get-tuple-element.58), channel_id=1, source_target_pairs={{2,0},{3,1},{0,2},{1,3},{6,4},{7,5},{4,6},{5,7},{10,8},{11,9},{8,1... | collective-permute-start | bytes 1376264 | tf_op jit(solution)/shard_map/ppermute | solution.py:29
  311.1 53.7 %collective-permute-start.37 = (bf16[32,7168]{1,0:T(8,128)(2,1)S(1)}, bf16[32,7168]{1,0:T(8,128)(2,1)S(1)}, u32[]{:S(2)}, u32[]{:S(2)}) collective-permute-start(bf16[32,7168]{1,0:T(8,128)(2,1)S(1)} %get-tuple-element.59), channel_id=1, source_target_pairs={{1,0},{2,1},{3,2},{0,3},{5,4},{6,5},{7,6},{4,7},{9,8},{10,9},{11,1... | collective-permute-start | bytes 1376264 | tf_op jit(solution)/shard_map/ppermute | solution.py:29
  313.9 42.6 %collective-permute-start.32 = (bf16[32,7168]{1,0:T(8,128)(2,1)S(1)}, bf16[32,7168]{1,0:T(8,128)(2,1)S(1)}, u32[]{:S(2)}, u32[]{:S(2)}) collective-permute-start(bf16[32,7168]{1,0:T(8,128)(2,1)S(1)} %get-tuple-element.69), channel_id=1, source_target_pairs={{2,1},{3,2},{6,5},{7,6},{10,9},{11,10},{14,13},{15,14},{18,17},{19... | collective-permute-start | bytes 1376264 | tf_op jit(solution)/shard_map/ppermute | solution.py:295
  322.0 43.7 %collective-permute-start.31 = (bf16[32,7168]{1,0:T(8,128)(2,1)S(1)}, bf16[32,7168]{1,0:T(8,128)(2,1)S(1)}, u32[]{:S(2)}, u32[]{:S(2)}) collective-permute-start(bf16[32,7168]{1,0:T(8,128)(2,1)S(1)} %add_convert_fusion.4), channel_id=1, source_target_pairs={{0,1},{1,2},{2,3},{4,5},{5,6},{6,7},{8,9},{9,10},{10,11},{12,13},{... | collective-permute-start | bytes 1376264 | tf_op jit(solution)/shard_map/ppermute | solution.py:294
  357.6 13.4 %collective-permute-start.33 = (bf16[32,7168]{1,0:T(8,128)(2,1)S(1)}, bf16[32,7168]{1,0:T(8,128)(2,1)S(1)}, u32[]{:S(2)}, u32[]{:S(2)}) collective-permute-start(bf16[32,7168]{1,0:T(8,128)(2,1)S(1)} %add_convert_fusion.3), channel_id=1, source_target_pairs={{1,0},{2,1},{3,2},{5,4},{6,5},{7,6},{9,8},{10,9},{11,10},{13,12},{... | collective-permute-start | bytes 1376264 | tf_op jit(solution)/shard_map/ppermute | solution.py:295
  364.2 23.4 %collective-permute-start.29 = (bf16[64,7168]{1,0:T(8,128)(2,1)S(1)}, bf16[64,7168]{1,0:T(8,128)(2,1)S(1)}, u32[]{:S(2)}, u32[]{:S(2)}) collective-permute-start(bf16[64,7168]{1,0:T(8,128)(2,1)S(1)} %add_convert_fusion), channel_id=1, source_target_pairs={{16,0},{0,16},{17,1},{1,17},{18,2},{2,18},{19,3},{3,19},{20,4},{4,... | collective-permute-start | bytes 2752520 | tf_op jit(solution)/shard_map/ppermute | solution.py:29
  371.5 25.8 %collective-permute-start.34 = (bf16[32,7168]{1,0:T(8,128)(2,1)S(1)}, bf16[32,7168]{1,0:T(8,128)(2,1)S(1)}, u32[]{:S(2)}, u32[]{:S(2)}) collective-permute-start(bf16[32,7168]{1,0:T(8,128)(2,1)S(1)} %get-tuple-element.62), channel_id=1, source_target_pairs={{16,0},{0,16},{17,1},{1,17},{18,2},{2,18},{19,3},{3,19},{20,4},{4,... | collective-permute-start | bytes 1376264 | tf_op jit(solution)/shard_map/ppermute | solution.py:29
  372.1 32.9 %collective-permute-start.38 = (bf16[32,7168]{1,0:T(8,128)(2,1)S(1)}, bf16[32,7168]{1,0:T(8,128)(2,1)S(1)}, u32[]{:S(2)}, u32[]{:S(2)}) collective-permute-start(bf16[32,7168]{1,0:T(8,128)(2,1)S(1)} %get-tuple-element.63), channel_id=1, source_target_pairs={{16,0},{0,16},{17,1},{1,17},{18,2},{2,18},{19,3},{3,19},{20,4},{4,... | collective-permute-start | bytes 1376264 | tf_op jit(solution)/shard_map/ppermute | solution.py:29
  (31 other events, 155.5 us)
Sparse Core Ops, SparseCore 0:
  19.6 135.8 all-gather.2

commit v5 on v4

--- a/solution.py
+++ b/solution.py
@@ -9,7 +9,7 @@
 from jax.sharding import PartitionSpec as P
 
 BF16, F32 = jnp.bfloat16, jnp.float32
-VMEM_LIMIT = 20 * 1024 * 1024
+VMEM_LIMIT = 56 * 1024 * 1024
 LAST_ROWS = 32
 
 
@@ -108,7 +108,7 @@
     read, arrays, specs, rows = x_input
     width = arrays[0].shape[-1]
     pieces, hid = len(gate_ups), gate_ups[0].shape[2]
-    chunk = chunk_of(width, 1024)
+    chunk = chunk_of(width, 1792)
     hidden = pieces * hid
     weight_spec = pl.BlockSpec((2, chunk, hid), lambda i, at: (0, i, 0))
     return pl.pallas_call(
@@ -165,7 +165,7 @@
     read, arrays, specs, rows = scaled_input
     width = arrays[0].shape[-1]
     pieces, hid = len(downs), downs[0].shape[0]
-    chunk = chunk_of(width, 1024)
+    chunk = chunk_of(width, 1792)
     steps = width // chunk
     hidden = pieces * hid
     first = lambda i: jnp.minimum(i, steps - 1)
@@ -237,7 +237,7 @@
     read, arrays, specs, rows = x_input
     width = arrays[0].shape[-1]
     pieces, hid = len(downs), downs[0].shape[0]
-    chunk = chunk_of(width, 1024)
+    chunk = chunk_of(width, 1792)
     steps = width // chunk
     hidden = pieces * hid
     first = lambda i: jnp.minimum(i, steps - 1)
@@ -302,13 +302,6 @@
     return block
 
 
-def sent_home(blocks, axis):
-    total = blocks[0]
-    for away in range(1, len(blocks)):
-        total = total + shifted(blocks[away], axis, away).astype(F32)
-    return total
-
-
 def few_experts(
     x_forward,
     route_forward,
@@ -333,69 +326,72 @@
     gate_up, down = jnp.concatenate([w_gate[0], w_up[0]], axis=0), w_down[0, 0]
     bundle = jnp.concatenate([x_backward[0], scaled_grad[:early]], axis=0)
     bundle, routes, scaled_last = lax.optimization_barrier((bundle, routes, scaled_grad[early:]))
-    bundle = lax.all_gather(bundle, "dp")
-    routes = jnp.stack([routes] + [shifted(routes, "dp", -away) for away in range(1, count)])
-    mine = (routes == expert_here).astype(F32)
+    x_gathered = lax.all_gather(x_forward[0], "dp")
+    bundle = lax.all_gather(after(bundle, x_gathered), "dp")
+    other_routes = [shifted(routes, "dp", -away) for away in range(1, count)]
+    mine = (jnp.stack([routes] + other_routes) == expert_here).astype(F32)
     mask_fwd, mask_bwd = mine[:, :, 0:1], mine[:, :, 1:2]
 
-    across_gate_up, across_down = flipped(gate_up, "expert", 2), flipped(down, "expert", 2)
-    x_sent = jnp.where(jnp.min(routes) >= 0, x_forward[0], jnp.zeros_like(x_forward[0]))
-    hops_x = [(x_sent, x_sent)]
-    for step in range(1, count):
-        hops_x.append(hop(*hops_x[-1], "dp", step))
-    gate_ups = [gate_up, flipped(after(gate_up, *hops_x[1]), "expert", 1)]
-    gate_ups += [across_gate_up, flipped(across_gate_up, "expert", 1)]
-    downs = [down, flipped(down, "expert", 1), across_down, flipped(across_down, "expert", 1)]
-    late = after(scaled_last, *hops_x[2])
-    hops_last = [(late, late)]
-    hops_last.append(hop(*hops_last[-1], "dp", 1))
-
-    from_below, from_above = zip(*hops_x[1:])
+    own = [after(gate_up, other_routes), down]
+    own_flips = [flipped(weight, "expert", 1) for weight in own]
+    across = [flipped(weight, "expert", 2) for weight in (gate_up, down)]
+    across_first = after(across[0], x_gathered, own_flips, other_routes)
+    across_flips = [flipped(weight, "expert", 1) for weight in (across_first, across[1])]
+    gate_ups, downs = zip((gate_up, down), own_flips, across, across_flips)
+    hops_last = [(scaled_last, scaled_last)]
+    hops_last.append(hop(*hops_last[0], "dp", 1))
+
     partial_fwd = forward_call(
         at,
         count,
-        mask_fwd.reshape(count * tokens_here, 1),
-        chained_input(x_forward[0], from_below, from_above),
+        after(mask_fwd.reshape(count * tokens_here, 1), hops_last[1]),
+        gathered_input(x_gathered, 0, tokens_here),
         gate_ups,
         downs,
     )
-    late = [after(rows, partial_fwd[1]) for rows in hops_last[-1]]
+    hops_last[1] = after(hops_last[1], partial_fwd[1])
     for step in range(2, count):
-        hops_last.append(hop(*(late if step == 2 else hops_last[-1]), "dp", step))
+        hops_last.append(hop(*hops_last[-1], "dp", step))
     arrived_fwd = step_home(summands(partial_fwd, 1, None), "dp", 1)
-    sent_home_fwd = summands(partial_fwd, 2, arrived_fwd)
-    arrived_fwd = step_home(sent_home_fwd, "dp", 2)
-    bundle = after(bundle, sent_home_fwd, hops_last[-1])
+    sends_fwd = summands(partial_fwd, 2, arrived_fwd)
+    arrived_fwd = step_home(sends_fwd, "dp", 2)
+    bundle = after(bundle, sends_fwd, hops_last[-1])
     c, e = gates_call(at, count, gathered_input(bundle, 0, tokens_here), gate_ups)
-    mask_early = mask_bwd[:, :early].reshape(count * early, 1)
+
+    sends_fwd = summands(partial_fwd, 3, after(arrived_fwd, c))
+    arrived_fwd = step_home(sends_fwd, "dp", 3)
+    mask_early = after(mask_bwd[:, :early].reshape(count * early, 1), sends_fwd)
     scaled_early = gathered_input(bundle, tokens_here, early)
     blocks_early = backward_call(
         at, count, mask_early, scaled_early, 0, c, e, downs, gate_ups
     )
 
-    sent_home_fwd = summands(partial_fwd, 3, after(arrived_fwd, blocks_early[1]))
-    arrived_fwd = step_home(sent_home_fwd, "dp", 3)
     arrived_early = step_home(summands(blocks_early, 1, None), "dp", 1)
+    total_fwd = summed(partial_fwd[0], after(arrived_fwd, blocks_early[1]))
+    layer_out = (x_forward[0].astype(F32) + prob_forward[0][:, None] * total_fwd).astype(BF16)
+    sent_fwd = shifted(layer_out, "pipe", 1)
     from_below, from_above = zip(*hops_last[1:])
-    mask_last = after(mask_bwd[:, early:].reshape(count * last, 1), sent_home_fwd)
+    mask_last = after(mask_bwd[:, early:].reshape(count * last, 1), layer_out)
     scaled_last = chained_input(scaled_last, from_below, from_above)
     blocks_last = backward_call(
         at, count, mask_last, scaled_last, early // last, c, e, downs, gate_ups
     )
 
-    arrived_early, arrived_fwd = after((arrived_early, arrived_fwd), blocks_last[1])
-    total_fwd = summed(partial_fwd[0], arrived_fwd)
-    layer_out = (x_forward[0].astype(F32) + prob_forward[0][:, None] * total_fwd).astype(BF16)
-    sent_fwd = shifted(layer_out, "pipe", 1)
+    arrived_early, arrived_last = after(arrived_early, blocks_last[1]), None
     for step in range(2, count):
+        if step > 2:
+            arrived_early = after(arrived_early, sent_fwd)
         arrived_early = step_home(summands(blocks_early, step, arrived_early), "dp", step)
-    total_early = summed(blocks_early[0], arrived_early)
-    total_last = sent_home(blocks_last, "dp")
-    sent_bwd = []
-    for rows, total in ((slice(0, early), total_early), (slice(early, None), total_last)):
-        grad_in = (grad_output[0, rows].astype(F32) + total).astype(BF16)
-        sent_bwd.append(shifted(grad_in, "pipe", -1))
-    return (sent_fwd[None], jnp.concatenate(sent_bwd, axis=0)[None])
+        arrived_last = step_home(summands(blocks_last, step - 1, arrived_last), "dp", step - 1)
+
+    def sent_back(rows, block, arrived):
+        grad_in = (grad_output[0, rows].astype(F32) + summed(block, arrived)).astype(BF16)
+        return shifted(grad_in, "pipe", -1)
+
+    sent_early = sent_back(slice(0, early), blocks_early[0], arrived_early)
+    arrived_last = step_home(summands(blocks_last, count - 1, arrived_last), "dp", count - 1)
+    sent_last = sent_back(slice(early, None), blocks_last[0], after(arrived_last, sent_early))
+    return (sent_fwd[None], jnp.concatenate([sent_early, sent_last], axis=0)[None])
 
 
 def from_partner(block, axis, stride):

time: 416 us -> 376 us (0.904)
  starting transfers between devices: 96.3 us -> 64 us
  waiting for transfers between devices: 198 us -> 217 us
  local copies, waits for them, and re-layouts: 20.1 us -> 5.82 us
  other arithmetic: 22.1 us -> 16.8 us
  Pallas kernels: 60.1 us -> 55.7 us
    all_gather x1 -> x2, waiting for transfers between devices: 0.02 us -> 60.8 us  [the longest x1 60.8 us: few_experts(): x_gathered = lax.all_gather(x_forward[0], 'dp')]
    ppermute x12 -> x6, waiting for transfers between devices: 85.3 us -> 38.3 us  [hop(): return (lax.ppermute(below, axis, up), lax.ppermute(above, axis, down))]
    ppermute x12 -> x6, starting transfers between devices: 54.4 us -> 14.5 us  [hop(): return (lax.ppermute(below, axis, up), lax.ppermute(above, axis, down))]
    ppermute x6, waiting for transfers between devices: 36 us -> 55.5 us  [flipped(): return lax.ppermute(block, axis, route)]
    unnamed x79 -> x47, local copies, waits for them, and re-layouts: 19.5 us -> 3.12 us
    ppermute x9 -> x6, waiting for transfers between devices: 31.4 us -> 15.1 us  [shifted(): lax.ppermute(block, axis, [((i - distance) % count, i) for i in range(cou...]
    ppermute x6 -> x9, starting transfers between devices: 15.3 us -> 26.2 us  [step_home(): lax.ppermute(pair[1], axis, [(i, i - 1) for i in range(count - step, coun...]
    ppermute x9 -> x6, starting transfers between devices: 14.8 us -> 4.73 us  [shifted(): lax.ppermute(block, axis, [((i - distance) % count, i) for i in range(cou...]
  transfers between devices with their start and end apart: 40 -> 38, of which waited for: 16 -> 16; matrix products, arithmetic and copies ran while one was open for 3% -> 5% of each run, Pallas kernels for 15% -> 15%
where the time goes in v5:
time: 376 us; the launch traced here: 373 us
  waiting for transfers between devices  217 us (58%)
  starting transfers between devices  64 us (17%)
  Pallas kernels  55.7 us (15%)
  other arithmetic  16.8 us (4%)
  between operations  14.6 us (4%)
  local copies, waits for them, and re-layouts  5.82 us (2%)
    all_gather x1, waiting for transfers between devices, few_experts(): x_gathered = lax.all_gather(x_forward[0], 'dp')  60.8 us
    ppermute x6, waiting for transfers between devices, flipped(): return lax.ppermute(block, axis, route)  55.5 us
    ppermute x6, waiting for transfers between devices, hop(): return (lax.ppermute(below, axis, up), lax.ppermute(above, axis, down))  38.3 us
    ppermute x9, waiting for transfers between devices, step_home(): lax.ppermute(pair[1], axis, [(i, i - 1) for i in range(count - step, coun...  34.1 us
    pallas_call x2, Pallas kernels, backward_call(): pl.pallas_call(functools.partial(backward_kernel, read, len(arrays), coun...  30.7 us
    ppermute x9, starting transfers between devices, step_home(): lax.ppermute(pair[1], axis, [(i, i - 1) for i in range(count - step, coun...  26.2 us
    pallas_call x1, Pallas kernels, forward_call(): pl.pallas_call(functools.partial(forward_kernel, read, len(arrays), count...  15.3 us
    ppermute x6, waiting for transfers between devices, shifted(): lax.ppermute(block, axis, [((i - distance) % count, i) for i in range(cou...  15.1 us
  transfers between devices with their start and end apart: 38, of which 16 were waited for; matrix products, arithmetic and copies ran while one was open for 5% of the time, Pallas kernels for 15%

profile of v5, /device:TPU:20, one launch (start us, length us, event | category | flops | bytes accessed | tf_op | source)
XLA Modules:
  0.0 373.5 jit_solution(1644362152236309816)
XLA Ops:
  8.0 1.5 fusion.2
  10.8 1.6 collective-permute-start.2
  12.7 1.3 collective-permute-start
  14.1 4.4 %pad_maximum_fusion.refs_4_.refs_8_.refs_11_ = bf16[2,7168,128]{2,1,0:T(8,128)(2,1)} fusion(bf16[1,7168,128]{2,1,0:T(8,128)(2,1)} %bitcast.42, bf16[1,7168,128]{2,1,0:T(8,128)(2,1)} %bitcast.43), kind=kLoop, calls=%fused_computation | loop fusion | flops 1835008 | bytes 7340032 | tf_op jit(solution)/shard_map/concatenate | solution.py:326
  18.5 1.5 collective-permute-start.6
  20.6 60.8 %all-gather.4.cloned.1.call-done.refs_0_.refs_1_.refs_2_.refs_3_ = bf16[4,64,7168]{2,1,0:T(8,128)(2,1)} async-done(((bf16[1,64,7168]{2,1,0:T(8,128)(2,1)}), bf16[4,64,7168]{2,1,0:T(8,128)(2,1)}) %all-gather.4.cloned.1.call-update) | async-done | bytes 3670032 | tf_op jit(solution)/shard_map/all_gather | solution.py:329
  81.4 1.5 collective-permute-start.9
  82.9 18.1 %collective-permute-done.6.refs_6_.refs_10_.refs_13_ = bf16[2,7168,128]{2,1,0:T(8,128)(2,1)} collective-permute-done((bf16[2,7168,128]{2,1,0:T(8,128)(2,1)}, bf16[2,7168,128]{2,1,0:T(8,128)(2,1)}, u32[]{:S(2)}, u32[]{:S(2)}) %collective-permute-start.6) | collective-permute-done | bytes 3670048 | tf_op jit(solution)/shard_map/ppermute | solution.py:24
  101.1 37.3 %collective-permute-done.9.refs_10_.refs_6_.refs_9_ = bf16[128,7168]{1,0:T(8,128)(2,1)} collective-permute-done((bf16[128,7168]{1,0:T(8,128)(2,1)S(1)}, bf16[128,7168]{1,0:T(8,128)(2,1)}, u32[]{:S(2)}, u32[]{:S(2)}) %collective-permute-start.9) | collective-permute-done | bytes 1835040 | tf_op jit(solution)/shard_map/ppermute | solution.py:24
  138.4 2.5 collective-permute-start.3
  141.0 3.3 collective-permute-start.4
  144.4 30.0 %collective-permute-done.3.refs_1_ = bf16[32,7168]{1,0:T(8,128)(2,1)S(1)} collective-permute-done((bf16[32,7168]{1,0:T(8,128)(2,1)S(1)}, bf16[32,7168]{1,0:T(8,128)(2,1)S(1)}, u32[]{:S(2)}, u32[]{:S(2)}) %collective-permute-start.3) | collective-permute-done | bytes 458784 | tf_op jit(solution)/shard_map/ppermute | solution.py:280
  174.4 1.3 collective-permute-done.4.refs_4_
  176.6 1.3 copy-done.1
  177.9 15.3 %shard_map.113 = (f32[64,7168]{1,0:T(8,128)}, bf16[64,7168]{1,0:T(8,128)(2,1)}, bf16[64,7168]{1,0:T(8,128)(2,1)}, bf16[64,7168]{1,0:T(8,128)(2,1)}) custom-call(s32[1]{0:T(128)} %bitcast.2.at_ref, f32[256,1]{1,0:T(8,128)} %copy.17.mask_ref, bf16[4,64,7168]{2,1,0:T(8,128)(2,1)} %all-gather.4.cloned.1.call-done.refs_0_.refs_1_.refs_2_.refs_3_, ...), custom_call_target="tpu_custom_call" | custom-call | flops 5637144576 | bytes 33030144 | tf_op jit(solution)/shard_map/pallas_call | solution.py:245
  193.2 1.3 collective-permute-start.13
  195.2 4.6 %collective-permute-start.15 = (bf16[32,7168]{1,0:T(8,128)(2,1)S(1)}, bf16[32,7168]{1,0:T(8,128)(2,1)S(1)}, u32[]{:S(2)}, u32[]{:S(2)}) collective-permute-start(bf16[32,7168]{1,0:T(8,128)(2,1)S(1)} %collective-permute-done.3.refs_1_), channel_id=1, source_target_pairs={{1,2},{2,3},{5,6},{6,7},{9,10},{10,11},{13,14},{14,15},{17,18},{18... | collective-permute-start | bytes 1376264 | tf_op jit(solution)/shard_map/ppermute | solution.py:280
  199.9 1.3 collective-permute-start.17
  201.2 15.8 %collective-permute-done.13 = bf16[64,7168]{1,0:T(8,128)(2,1)S(1)} collective-permute-done((bf16[64,7168]{1,0:T(8,128)(2,1)}, bf16[64,7168]{1,0:T(8,128)(2,1)S(1)}, u32[]{:S(2)}, u32[]{:S(2)}) %collective-permute-start.13) | collective-permute-done | bytes 917536 | tf_op jit(solution)/shard_map/ppermute | solution.py:295
  217.0 2.5 fusion.1
  219.5 1.3 collective-permute-start.12
  220.8 5.8 %collective-permute-start.14 = (bf16[64,7168]{1,0:T(8,128)(2,1)S(1)}, bf16[64,7168]{1,0:T(8,128)(2,1)S(1)}, u32[]{:S(2)}, u32[]{:S(2)}) collective-permute-start(bf16[64,7168]{1,0:T(8,128)(2,1)S(1)} %get-tuple-element.76), channel_id=1, source_target_pairs={{2,1},{3,2},{6,5},{7,6},{10,9},{11,10},{14,13},{15,14},{18,17},{19... | collective-permute-start | bytes 2752520 | tf_op jit(solution)/shard_map/ppermute | solution.py:295
  227.5 1.3 collective-permute-start.16
  228.8 1.4 collective-permute-start.18
  230.3 7.0 %collective-permute-done.16.refs_3_ = bf16[32,7168]{1,0:T(8,128)(2,1)S(1)} collective-permute-done((bf16[32,7168]{1,0:T(8,128)(2,1)S(1)}, bf16[32,7168]{1,0:T(8,128)(2,1)S(1)}, u32[]{:S(2)}, u32[]{:S(2)}) %collective-permute-start.16) | collective-permute-done | bytes 458784 | tf_op jit(solution)/shard_map/ppermute | solution.py:280
  237.2 9.7 %shard_map.114 = (f32[4,64,512]{2,1,0:T(8,128)}, f32[4,64,512]{2,1,0:T(8,128)}) custom-call(s32[1]{0:T(128)} %bitcast.2.at_ref, bf16[4,96,7168]{2,1,0:T(8,128)(2,1)} %bitcast.29, bf16[4,96,7168]{2,1,0:T(8,128)(2,1)} %bitcast.30, bf16[4,96,7168]{2,1,0:T(8,128)(2,1)} %bitcast.31, bf16[4,96,7168]{2,1,0:T(8,128)(2,1)} %bitcast.32, ...), custom_call_target="tpu_custom_call" | custom-call | flops 3758096384 | bytes 18350080 | tf_op jit(solution)/shard_map/pallas_call | solution.py:114
  248.1 4.4 %collective-permute-start.19 = (bf16[64,7168]{1,0:T(8,128)(2,1)}, bf16[64,7168]{1,0:T(8,128)(2,1)S(1)}, u32[]{:S(2)}, u32[]{:S(2)}) collective-permute-start(bf16[64,7168]{1,0:T(8,128)(2,1)} %add_convert_fusion.1), channel_id=1, source_target_pairs={{0,1},{1,2},{2,3},{4,5},{5,6},{6,7},{8,9},{9,10},{10,11},{12,13},{... | collective-permute-start | bytes 2752520 | tf_op jit(solution)/shard_map/ppermute | solution.py:294
  253.6 1.9 collective-permute-start.20
  256.6 15.4 %shard_map.115 = (f32[32,7168]{1,0:T(8,128)}, bf16[32,7168]{1,0:T(8,128)(2,1)}, bf16[32,7168]{1,0:T(8,128)(2,1)}, bf16[32,7168]{1,0:T(8,128)(2,1)}) custom-call(s32[1]{0:T(128)} %bitcast.2.at_ref, f32[128,1]{1,0:T(8,128)} %copy.18.mask_ref, f32[4,64,512]{2,1,0:T(8,128)} %get-tuple-element.52.c_ref, f32[4,64,512]{2,1,0:T(8,128)} %get-tuple-element.56.e_ref, ...), custom_call_target="tpu_custom_call" | custom-call | flops 2818572288 | bytes 25690112 | tf_op jit(solution)/shard_map/pallas_call | solution.py:175
  272.6 1.3 collective-permute-start.23
  273.9 2.0 collective-permute-done.20
  277.1 15.4 %shard_map.116 = (f32[32,7168]{1,0:T(8,128)}, bf16[32,7168]{1,0:T(8,128)(2,1)}, bf16[32,7168]{1,0:T(8,128)(2,1)}, bf16[32,7168]{1,0:T(8,128)(2,1)}) custom-call(s32[1]{0:T(128)} %bitcast.2.at_ref, f32[128,1]{1,0:T(8,128)} %copy.19.mask_ref, f32[4,64,512]{2,1,0:T(8,128)} %get-tuple-element.52.c_ref, f32[4,64,512]{2,1,0:T(8,128)} %get-tuple-element.56.e_ref, ...), custom_call_target="tpu_custom_call" | custom-call | flops 2818572288 | bytes 25690112 | tf_op jit(solution)/shard_map/pallas_call | solution.py:175
  292.5 1.4 collective-permute-start.32
  295.1 8.2 %collective-permute-done.32 = bf16[32,7168]{1,0:T(8,128)(2,1)S(1)} collective-permute-done((bf16[32,7168]{1,0:T(8,128)(2,1)}, bf16[32,7168]{1,0:T(8,128)(2,1)S(1)}, u32[]{:S(2)}, u32[]{:S(2)}) %collective-permute-start.32) | collective-permute-done | bytes 458784 | tf_op jit(solution)/shard_map/ppermute | solution.py:295
  304.6 1.3 collective-permute-start.30
  307.2 1.4 collective-permute-start.24
  308.6 5.2 %collective-permute-start.25 = (bf16[32,7168]{1,0:T(8,128)(2,1)S(1)}, bf16[32,7168]{1,0:T(8,128)(2,1)S(1)}, u32[]{:S(2)}, u32[]{:S(2)}) collective-permute-start(bf16[32,7168]{1,0:T(8,128)(2,1)S(1)} %get-tuple-element.80), channel_id=1, source_target_pairs={{2,1},{3,2},{6,5},{7,6},{10,9},{11,10},{14,13},{15,14},{18,17},{19... | collective-permute-start | bytes 1376264 | tf_op jit(solution)/shard_map/ppermute | solution.py:295
  313.8 2.1 collective-permute-start.33
  315.9 4.1 %collective-permute-done.30 = bf16[32,7168]{1,0:T(8,128)(2,1)S(1)} collective-permute-done((bf16[32,7168]{1,0:T(8,128)(2,1)S(1)}, bf16[32,7168]{1,0:T(8,128)(2,1)S(1)}, u32[]{:S(2)}, u32[]{:S(2)}) %collective-permute-start.30) | collective-permute-done | bytes 458784 | tf_op jit(solution)/shard_map/ppermute | solution.py:294
  320.1 2.1 collective-permute-start.31
  322.2 7.6 %collective-permute-done.24 = bf16[32,7168]{1,0:T(8,128)(2,1)S(1)} collective-permute-done((bf16[32,7168]{1,0:T(8,128)(2,1)S(1)}, bf16[32,7168]{1,0:T(8,128)(2,1)S(1)}, u32[]{:S(2)}, u32[]{:S(2)}) %collective-permute-start.24) | collective-permute-done | bytes 458784 | tf_op jit(solution)/shard_map/ppermute | solution.py:294
  329.9 3.6 collective-permute-start.27
  333.7 2.4 collective-permute-start.26
  336.2 3.6 collective-permute-start.34
  339.8 4.2 %collective-permute-done.27 = bf16[32,7168]{1,0:T(8,128)(2,1)S(1)} collective-permute-done((bf16[32,7168]{1,0:T(8,128)(2,1)S(1)}, bf16[32,7168]{1,0:T(8,128)(2,1)S(1)}, u32[]{:S(2)}, u32[]{:S(2)}) %collective-permute-start.27) | collective-permute-done | bytes 458784 | tf_op jit(solution)/shard_map/ppermute | solution.py:295
  345.1 3.8 %collective-permute-done.34 = bf16[32,7168]{1,0:T(8,128)(2,1)S(1)} collective-permute-done((bf16[32,7168]{1,0:T(8,128)(2,1)S(1)}, bf16[32,7168]{1,0:T(8,128)(2,1)S(1)}, u32[]{:S(2)}, u32[]{:S(2)}) %collective-permute-start.34) | collective-permute-done | bytes 458784 | tf_op jit(solution)/shard_map/ppermute | solution.py:295
  349.0 7.0 %collective-permute-done.28 = bf16[32,7168]{1,0:T(8,128)(2,1)S(1)} collective-permute-done((bf16[32,7168]{1,0:T(8,128)(2,1)S(1)}, bf16[32,7168]{1,0:T(8,128)(2,1)S(1)}, u32[]{:S(2)}, u32[]{:S(2)}) %collective-permute-start.28) | collective-permute-done | bytes 458784 | tf_op jit(solution)/shard_map/ppermute | solution.py:29
  356.7 8.0 %collective-permute-done.35 = bf16[32,7168]{1,0:T(8,128)(2,1)S(1)} collective-permute-done((bf16[32,7168]{1,0:T(8,128)(2,1)S(1)}, bf16[32,7168]{1,0:T(8,128)(2,1)S(1)}, u32[]{:S(2)}, u32[]{:S(2)}) %collective-permute-start.35) | collective-permute-done | bytes 458784 | tf_op jit(solution)/shard_map/ppermute | solution.py:29
  (108 shorter events, 18.5 us)
Async XLA Ops:
  7.2 74.2 %all-gather.4.cloned.1.call-start = ((), (), s32[]{:S(2)}) async-start(), calls=%async_computation | async-start | bytes 4587520 | tf_op jit(solution)/shard_map/all_gather | solution.py:329
  7.9 229.3 %all-gather.6.cloned.1.call-start = ((), (), s32[]{:S(2)}) async-start(), calls=%async_computation.1 | async-start | bytes 6881280 | tf_op jit(solution)/shard_map/all_gather | solution.py:330
  9.6 131.4 %copy-start.5 = (bf16[32,7168]{1,0:T(8,128)(2,1)}, bf16[32,7168]{1,0:T(8,128)(2,1)S(1)}, u32[]{:S(2)}) copy-start(bf16[32,7168]{1,0:T(8,128)(2,1)S(1)} %get-tuple-element.39.refs_0_) | copy-start | bytes 1376260
  10.8 9.1 %collective-permute-start.2 = (s32[64,2]{0,1:T(2,128)S(1)}, s32[64,2]{0,1:T(2,128)S(1)}, u32[]{:S(2)}, u32[]{:S(2)}) collective-permute-start(s32[64,2]{0,1:T(2,128)S(1)} %pad_add_fusion), channel_id=1, source_target_pairs={{3,0},{0,1},{1,2},{2,3},{7,4},{4,5},{5,6},{6,7},{11,8},{8,9},{9,10... | collective-permute-start | bytes 1544 | tf_op jit(solution)/shard_map/ppermute | solution.py:29
  12.4 7.6 %collective-permute-start.1 = (s32[64,2]{0,1:T(2,128)S(1)}, s32[64,2]{0,1:T(2,128)S(1)}, u32[]{:S(2)}, u32[]{:S(2)}) collective-permute-start(s32[64,2]{0,1:T(2,128)S(1)} %pad_add_fusion), channel_id=1, source_target_pairs={{2,0},{3,1},{0,2},{1,3},{6,4},{7,5},{4,6},{5,7},{10,8},{11,9},{8,1... | collective-permute-start | bytes 1544 | tf_op jit(solution)/shard_map/ppermute | solution.py:29
  12.7 7.2 %collective-permute-start = (s32[64,2]{0,1:T(2,128)S(1)}, s32[64,2]{0,1:T(2,128)S(1)}, u32[]{:S(2)}, u32[]{:S(2)}) collective-permute-start(s32[64,2]{0,1:T(2,128)S(1)} %pad_add_fusion), channel_id=1, source_target_pairs={{1,0},{2,1},{3,2},{0,3},{5,4},{6,5},{7,6},{4,7},{9,8},{10,9},{11,1... | collective-permute-start | bytes 1544 | tf_op jit(solution)/shard_map/ppermute | solution.py:29
  18.5 82.6 %collective-permute-start.6 = (bf16[2,7168,128]{2,1,0:T(8,128)(2,1)}, bf16[2,7168,128]{2,1,0:T(8,128)(2,1)}, u32[]{:S(2)}, u32[]{:S(2)}) collective-permute-start(bf16[2,7168,128]{2,1,0:T(8,128)(2,1)} %pad_maximum_fusion.refs_4_.refs_8_.refs_11_), channel_id=1, source_target_pairs={{0,8},{4,12},{8,0},{12,4},{1,9},{5,13},{9,1},{13,5},{2,10},{6,14},... | collective-permute-start | bytes 11010056 | tf_op jit(solution)/shard_map/ppermute | solution.py:24
  20.0 81.1 %collective-permute-start.5 = (bf16[2,7168,128]{2,1,0:T(8,128)(2,1)}, bf16[2,7168,128]{2,1,0:T(8,128)(2,1)}, u32[]{:S(2)}, u32[]{:S(2)}) collective-permute-start(bf16[2,7168,128]{2,1,0:T(8,128)(2,1)} %pad_maximum_fusion.refs_4_.refs_8_.refs_11_), channel_id=1, source_target_pairs={{0,4},{4,0},{8,12},{12,8},{1,5},{5,1},{9,13},{13,9},{2,6},{6,2},{1... | collective-permute-start | bytes 11010056 | tf_op jit(solution)/shard_map/ppermute | solution.py:24
  20.1 62.9 %collective-permute-start.7 = (bf16[128,7168]{1,0:T(8,128)(2,1)S(1)}, bf16[128,7168]{1,0:T(8,128)(2,1)}, u32[]{:S(2)}, u32[]{:S(2)}) collective-permute-start(bf16[128,7168]{1,0:T(8,128)(2,1)S(1)} %bitcast.40), channel_id=1, source_target_pairs={{0,4},{4,0},{8,12},{12,8},{1,5},{5,1},{9,13},{13,9},{2,6},{6,2},{1... | collective-permute-start | bytes 5505032 | tf_op jit(solution)/shard_map/ppermute | solution.py:24
  81.4 57.0 %collective-permute-start.9 = (bf16[128,7168]{1,0:T(8,128)(2,1)S(1)}, bf16[128,7168]{1,0:T(8,128)(2,1)}, u32[]{:S(2)}, u32[]{:S(2)}) collective-permute-start(bf16[128,7168]{1,0:T(8,128)(2,1)S(1)} %bitcast.41), channel_id=1, source_target_pairs={{0,8},{4,12},{8,0},{12,4},{1,9},{5,13},{9,1},{13,5},{2,10},{6,14},... | collective-permute-start | bytes 5505032 | tf_op jit(solution)/shard_map/ppermute | solution.py:24
  101.1 75.5 %collective-permute-start.8 = (bf16[2,7168,128]{2,1,0:T(8,128)(2,1)}, bf16[2,7168,128]{2,1,0:T(8,128)(2,1)}, u32[]{:S(2)}, u32[]{:S(2)}) collective-permute-start(bf16[2,7168,128]{2,1,0:T(8,128)(2,1)} %collective-permute-done.6.refs_6_.refs_10_.refs_13_), channel_id=1, source_target_pairs={{0,4},{4,0},{8,12},{12,8},{1,5},{5,1},{9,13},{13,9},{2,6},{6,2},{1... | collective-permute-start | bytes 11010056 | tf_op jit(solution)/shard_map/ppermute | solution.py:24
  138.4 38.1 %collective-permute-start.10 = (bf16[128,7168]{1,0:T(8,128)(2,1)}, bf16[128,7168]{1,0:T(8,128)(2,1)S(1)}, u32[]{:S(2)}, u32[]{:S(2)}) collective-permute-start(bf16[128,7168]{1,0:T(8,128)(2,1)} %collective-permute-done.9.refs_10_.refs_6_.refs_9_), channel_id=1, source_target_pairs={{0,4},{4,0},{8,12},{12,8},{1,5},{5,1},{9,13},{13,9},{2,6},{6,2},{1... | collective-permute-start | bytes 5505032 | tf_op jit(solution)/shard_map/ppermute | solution.py:24
  138.4 36.0 %collective-permute-start.3 = (bf16[32,7168]{1,0:T(8,128)(2,1)S(1)}, bf16[32,7168]{1,0:T(8,128)(2,1)S(1)}, u32[]{:S(2)}, u32[]{:S(2)}) collective-permute-start(bf16[32,7168]{1,0:T(8,128)(2,1)S(1)} %get-tuple-element.39.refs_0_), channel_id=1, source_target_pairs={{0,1},{1,2},{2,3},{4,5},{5,6},{6,7},{8,9},{9,10},{10,11},{12,13},{... | collective-permute-start | bytes 1376264 | tf_op jit(solution)/shard_map/ppermute | solution.py:280
  141.0 34.8 %collective-permute-start.4 = (bf16[32,7168]{1,0:T(8,128)(2,1)S(1)}, bf16[32,7168]{1,0:T(8,128)(2,1)}, u32[]{:S(2)}, u32[]{:S(2)}) collective-permute-start(bf16[32,7168]{1,0:T(8,128)(2,1)S(1)} %get-tuple-element.39.refs_0_), channel_id=1, source_target_pairs={{1,0},{2,1},{3,2},{5,4},{6,5},{7,6},{9,8},{10,9},{11,10},{13,12},{... | collective-permute-start | bytes 1376264 | tf_op jit(solution)/shard_map/ppermute | solution.py:280
  174.4 20.8 %copy-start.11 = (bf16[32,7168]{1,0:T(8,128)(2,1)}, bf16[32,7168]{1,0:T(8,128)(2,1)S(1)}, u32[]{:S(2)}) copy-start(bf16[32,7168]{1,0:T(8,128)(2,1)S(1)} %collective-permute-done.3.refs_1_) | copy-start | bytes 1376260
  193.2 23.8 %collective-permute-start.13 = (bf16[64,7168]{1,0:T(8,128)(2,1)}, bf16[64,7168]{1,0:T(8,128)(2,1)S(1)}, u32[]{:S(2)}, u32[]{:S(2)}) collective-permute-start(bf16[64,7168]{1,0:T(8,128)(2,1)} %get-tuple-element.44), channel_id=1, source_target_pairs={{3,2},{7,6},{11,10},{15,14},{19,18},{23,22},{27,26},{31,30}} | collective-permute-start | bytes 2752520 | tf_op jit(solution)/shard_map/ppermute | solution.py:295
  194.5 22.5 %collective-permute-start.11 = (bf16[64,7168]{1,0:T(8,128)(2,1)}, bf16[64,7168]{1,0:T(8,128)(2,1)S(1)}, u32[]{:S(2)}, u32[]{:S(2)}) collective-permute-start(bf16[64,7168]{1,0:T(8,128)(2,1)} %get-tuple-element.46), channel_id=1, source_target_pairs={{0,1},{4,5},{8,9},{12,13},{16,17},{20,21},{24,25},{28,29}} | collective-permute-start | bytes 2752520 | tf_op jit(solution)/shard_map/ppermute | solution.py:294
  195.2 31.4 %collective-permute-start.15 = (bf16[32,7168]{1,0:T(8,128)(2,1)S(1)}, bf16[32,7168]{1,0:T(8,128)(2,1)S(1)}, u32[]{:S(2)}, u32[]{:S(2)}) collective-permute-start(bf16[32,7168]{1,0:T(8,128)(2,1)S(1)} %collective-permute-done.3.refs_1_), channel_id=1, source_target_pairs={{1,2},{2,3},{5,6},{6,7},{9,10},{10,11},{13,14},{14,15},{17,18},{18... | collective-permute-start | bytes 1376264 | tf_op jit(solution)/shard_map/ppermute | solution.py:280
  199.9 28.9 %collective-permute-start.17 = (bf16[32,7168]{1,0:T(8,128)(2,1)}, bf16[32,7168]{1,0:T(8,128)(2,1)S(1)}, u32[]{:S(2)}, u32[]{:S(2)}) collective-permute-start(bf16[32,7168]{1,0:T(8,128)(2,1)} %collective-permute-done.4.refs_4_), channel_id=1, source_target_pairs={{1,0},{2,1},{5,4},{6,5},{9,8},{10,9},{13,12},{14,13},{17,16},{18,1... | collective-permute-start | bytes 1376264 | tf_op jit(solution)/shard_map/ppermute | solution.py:280
  219.5 27.4 %collective-permute-start.12 = (bf16[64,7168]{1,0:T(8,128)(2,1)}, bf16[64,7168]{1,0:T(8,128)(2,1)S(1)}, u32[]{:S(2)}, u32[]{:S(2)}) collective-permute-start(bf16[64,7168]{1,0:T(8,128)(2,1)} %get-tuple-element.77), channel_id=1, source_target_pairs={{0,1},{1,2},{4,5},{5,6},{8,9},{9,10},{12,13},{13,14},{16,17},{17,1... | collective-permute-start | bytes 2752520 | tf_op jit(solution)/shard_map/ppermute | solution.py:294
  220.8 26.1 %collective-permute-start.14 = (bf16[64,7168]{1,0:T(8,128)(2,1)S(1)}, bf16[64,7168]{1,0:T(8,128)(2,1)S(1)}, u32[]{:S(2)}, u32[]{:S(2)}) collective-permute-start(bf16[64,7168]{1,0:T(8,128)(2,1)S(1)} %get-tuple-element.76), channel_id=1, source_target_pairs={{2,1},{3,2},{6,5},{7,6},{10,9},{11,10},{14,13},{15,14},{18,17},{19... | collective-permute-start | bytes 2752520 | tf_op jit(solution)/shard_map/ppermute | solution.py:295
  227.5 9.7 %collective-permute-start.16 = (bf16[32,7168]{1,0:T(8,128)(2,1)S(1)}, bf16[32,7168]{1,0:T(8,128)(2,1)S(1)}, u32[]{:S(2)}, u32[]{:S(2)}) collective-permute-start(bf16[32,7168]{1,0:T(8,128)(2,1)S(1)} %collective-permute-done.15.refs_2_), channel_id=1, source_target_pairs={{2,3},{6,7},{10,11},{14,15},{18,19},{22,23},{26,27},{30,31}} | collective-permute-start | bytes 1376264 | tf_op jit(solution)/shard_map/ppermute | solution.py:280
  228.8 8.4 %collective-permute-start.18 = (bf16[32,7168]{1,0:T(8,128)(2,1)S(1)}, bf16[32,7168]{1,0:T(8,128)(2,1)}, u32[]{:S(2)}, u32[]{:S(2)}) collective-permute-start(bf16[32,7168]{1,0:T(8,128)(2,1)S(1)} %collective-permute-done.17.refs_5_), channel_id=1, source_target_pairs={{1,0},{5,4},{9,8},{13,12},{17,16},{21,20},{25,24},{29,28}} | collective-permute-start | bytes 1376264 | tf_op jit(solution)/shard_map/ppermute | solution.py:280
  248.1 25.8 %collective-permute-start.19 = (bf16[64,7168]{1,0:T(8,128)(2,1)}, bf16[64,7168]{1,0:T(8,128)(2,1)S(1)}, u32[]{:S(2)}, u32[]{:S(2)}) collective-permute-start(bf16[64,7168]{1,0:T(8,128)(2,1)} %add_convert_fusion.1), channel_id=1, source_target_pairs={{0,1},{1,2},{2,3},{4,5},{5,6},{6,7},{8,9},{9,10},{10,11},{12,13},{... | collective-permute-start | bytes 2752520 | tf_op jit(solution)/shard_map/ppermute | solution.py:294
  253.6 22.3 %collective-permute-start.20 = (bf16[64,7168]{1,0:T(8,128)(2,1)}, bf16[64,7168]{1,0:T(8,128)(2,1)S(1)}, u32[]{:S(2)}, u32[]{:S(2)}) collective-permute-start(bf16[64,7168]{1,0:T(8,128)(2,1)} %add_convert_fusion), channel_id=1, source_target_pairs={{1,0},{2,1},{3,2},{5,4},{6,5},{7,6},{9,8},{10,9},{11,10},{13,12},{... | collective-permute-start | bytes 2752520 | tf_op jit(solution)/shard_map/ppermute | solution.py:295
  256.5 19.3 %copy-start.4 = (f32[64,7168]{1,0:T(8,128)S(1)}, f32[64,7168]{1,0:T(8,128)}, u32[]{:S(2)}) copy-start(f32[64,7168]{1,0:T(8,128)} %get-tuple-element.43) | copy-start | bytes 5505028
  256.6 19.3 %copy-start.20 = (f32[1,64]{1,0:T(1,128)S(1)}, f32[1,64]{1,0:T(1,128)}, u32[]{:S(2)}) copy-start(f32[1,64]{1,0:T(1,128)} %param.12) | copy-start | bytes 772
  271.9 23.2 %collective-permute-start.22 = (bf16[32,7168]{1,0:T(8,128)(2,1)}, bf16[32,7168]{1,0:T(8,128)(2,1)S(1)}, u32[]{:S(2)}, u32[]{:S(2)}) collective-permute-start(bf16[32,7168]{1,0:T(8,128)(2,1)} %get-tuple-element.62), channel_id=1, source_target_pairs={{0,1},{4,5},{8,9},{12,13},{16,17},{20,21},{24,25},{28,29}} | collective-permute-start | bytes 1376264 | tf_op jit(solution)/shard_map/ppermute | solution.py:294
  272.6 22.5 %collective-permute-start.23 = (bf16[32,7168]{1,0:T(8,128)(2,1)}, bf16[32,7168]{1,0:T(8,128)(2,1)}, u32[]{:S(2)}, u32[]{:S(2)}) collective-permute-start(bf16[32,7168]{1,0:T(8,128)(2,1)} %get-tuple-element.57), channel_id=1, source_target_pairs={{3,2},{7,6},{11,10},{15,14},{19,18},{23,22},{27,26},{31,30}} | collective-permute-start | bytes 1376264 | tf_op jit(solution)/shard_map/ppermute | solution.py:295
  292.5 10.8 %collective-permute-start.32 = (bf16[32,7168]{1,0:T(8,128)(2,1)}, bf16[32,7168]{1,0:T(8,128)(2,1)S(1)}, u32[]{:S(2)}, u32[]{:S(2)}) collective-permute-start(bf16[32,7168]{1,0:T(8,128)(2,1)} %get-tuple-element.64), channel_id=1, source_target_pairs={{3,2},{7,6},{11,10},{15,14},{19,18},{23,22},{27,26},{31,30}} | collective-permute-start | bytes 1376264 | tf_op jit(solution)/shard_map/ppermute | solution.py:295
  293.9 9.4 %collective-permute-start.29 = (bf16[32,7168]{1,0:T(8,128)(2,1)}, bf16[32,7168]{1,0:T(8,128)(2,1)S(1)}, u32[]{:S(2)}, u32[]{:S(2)}) collective-permute-start(bf16[32,7168]{1,0:T(8,128)(2,1)} %get-tuple-element.71), channel_id=1, source_target_pairs={{0,1},{4,5},{8,9},{12,13},{16,17},{20,21},{24,25},{28,29}} | collective-permute-start | bytes 1376264 | tf_op jit(solution)/shard_map/ppermute | solution.py:294
  294.6 35.2 %collective-permute-start.21 = (bf16[64,7168]{1,0:T(8,128)(2,1)S(1)}, bf16[64,7168]{1,0:T(8,128)(2,1)S(1)}, u32[]{:S(2)}, u32[]{:S(2)}) collective-permute-start(bf16[64,7168]{1,0:T(8,128)(2,1)S(1)} %fusion.3), channel_id=1, source_target_pairs={{16,0},{0,16},{17,1},{1,17},{18,2},{2,18},{19,3},{3,19},{20,4},{4,... | collective-permute-start | bytes 2752520 | tf_op jit(solution)/shard_map/ppermute | solution.py:29
  304.6 15.4 %collective-permute-start.30 = (bf16[32,7168]{1,0:T(8,128)(2,1)S(1)}, bf16[32,7168]{1,0:T(8,128)(2,1)S(1)}, u32[]{:S(2)}, u32[]{:S(2)}) collective-permute-start(bf16[32,7168]{1,0:T(8,128)(2,1)S(1)} %get-tuple-element.83), channel_id=1, source_target_pairs={{0,1},{1,2},{4,5},{5,6},{8,9},{9,10},{12,13},{13,14},{16,17},{17,1... | collective-permute-start | bytes 1376264 | tf_op jit(solution)/shard_map/ppermute | solution.py:294
  305.9 23.9 %copy-start.15 = (bf16[32,7168]{1,0:T(8,128)(2,1)S(1)}, bf16[32,7168]{1,0:T(8,128)(2,1)}, u32[]{:S(2)}) copy-start(bf16[32,7168]{1,0:T(8,128)(2,1)} %get-tuple-element.62) | copy-start | bytes 1376260
  307.2 26.4 %copy-start.12 = (bf16[32,7168]{1,0:T(8,128)(2,1)S(1)}, bf16[32,7168]{1,0:T(8,128)(2,1)}, u32[]{:S(2)}) copy-start(bf16[32,7168]{1,0:T(8,128)(2,1)} %get-tuple-element.57) | copy-start | bytes 1376260
  307.2 22.6 %collective-permute-start.24 = (bf16[32,7168]{1,0:T(8,128)(2,1)S(1)}, bf16[32,7168]{1,0:T(8,128)(2,1)S(1)}, u32[]{:S(2)}, u32[]{:S(2)}) collective-permute-start(bf16[32,7168]{1,0:T(8,128)(2,1)S(1)} %get-tuple-element.81), channel_id=1, source_target_pairs={{0,1},{1,2},{4,5},{5,6},{8,9},{9,10},{12,13},{13,14},{16,17},{17,1... | collective-permute-start | bytes 1376264 | tf_op jit(solution)/shard_map/ppermute | solution.py:294
  308.6 21.2 %collective-permute-start.25 = (bf16[32,7168]{1,0:T(8,128)(2,1)S(1)}, bf16[32,7168]{1,0:T(8,128)(2,1)S(1)}, u32[]{:S(2)}, u32[]{:S(2)}) collective-permute-start(bf16[32,7168]{1,0:T(8,128)(2,1)S(1)} %get-tuple-element.80), channel_id=1, source_target_pairs={{2,1},{3,2},{6,5},{7,6},{10,9},{11,10},{14,13},{15,14},{18,17},{19... | collective-permute-start | bytes 1376264 | tf_op jit(solution)/shard_map/ppermute | solution.py:295
  313.8 22.3 %copy-start.16 = (bf16[32,7168]{1,0:T(8,128)(2,1)S(1)}, bf16[32,7168]{1,0:T(8,128)(2,1)}, u32[]{:S(2)}) copy-start(bf16[32,7168]{1,0:T(8,128)(2,1)} %get-tuple-element.71) | copy-start | bytes 1376260
  313.8 22.3 %collective-permute-start.33 = (bf16[32,7168]{1,0:T(8,128)(2,1)S(1)}, bf16[32,7168]{1,0:T(8,128)(2,1)S(1)}, u32[]{:S(2)}, u32[]{:S(2)}) collective-permute-start(bf16[32,7168]{1,0:T(8,128)(2,1)S(1)} %get-tuple-element.82), channel_id=1, source_target_pairs={{2,1},{3,2},{6,5},{7,6},{10,9},{11,10},{14,13},{15,14},{18,17},{19... | collective-permute-start | bytes 1376264 | tf_op jit(solution)/shard_map/ppermute | solution.py:295
  320.1 24.4 %copy-start.3 = (bf16[1,64,7168]{2,1,0:T(8,128)(2,1)S(1)}, bf16[1,64,7168]{2,1,0:T(8,128)(2,1)}, u32[]{:S(2)}) copy-start(bf16[1,64,7168]{2,1,0:T(8,128)(2,1)} %param.16) | copy-start | bytes 2752516
  320.1 24.4 %copy-start.7 = (f32[32,7168]{1,0:T(8,128)S(1)}, f32[32,7168]{1,0:T(8,128)}, u32[]{:S(2)}) copy-start(f32[32,7168]{1,0:T(8,128)} %get-tuple-element.60) | copy-start | bytes 2752516
  320.1 25.0 %collective-permute-start.31 = (bf16[32,7168]{1,0:T(8,128)(2,1)S(1)}, bf16[32,7168]{1,0:T(8,128)(2,1)S(1)}, u32[]{:S(2)}, u32[]{:S(2)}) collective-permute-start(bf16[32,7168]{1,0:T(8,128)(2,1)S(1)} %add_convert_fusion.3), channel_id=1, source_target_pairs={{0,1},{1,2},{2,3},{4,5},{5,6},{6,7},{8,9},{9,10},{10,11},{12,13},{... | collective-permute-start | bytes 1376264 | tf_op jit(solution)/shard_map/ppermute | solution.py:294
  329.9 14.1 %collective-permute-start.27 = (bf16[32,7168]{1,0:T(8,128)(2,1)S(1)}, bf16[32,7168]{1,0:T(8,128)(2,1)S(1)}, u32[]{:S(2)}, u32[]{:S(2)}) collective-permute-start(bf16[32,7168]{1,0:T(8,128)(2,1)S(1)} %add_convert_fusion.4), channel_id=1, source_target_pairs={{1,0},{2,1},{3,2},{5,4},{6,5},{7,6},{9,8},{10,9},{11,10},{13,12},{... | collective-permute-start | bytes 1376264 | tf_op jit(solution)/shard_map/ppermute | solution.py:295
  333.7 22.3 %copy-start.8 = (f32[32,7168]{1,0:T(8,128)S(1)}, f32[32,7168]{1,0:T(8,128)}, u32[]{:S(2)}) copy-start(f32[32,7168]{1,0:T(8,128)} %get-tuple-element.69) | copy-start | bytes 2752516
  333.7 10.8 %collective-permute-start.26 = (bf16[32,7168]{1,0:T(8,128)(2,1)S(1)}, bf16[32,7168]{1,0:T(8,128)(2,1)S(1)}, u32[]{:S(2)}, u32[]{:S(2)}) collective-permute-start(bf16[32,7168]{1,0:T(8,128)(2,1)S(1)} %add_convert_fusion.5), channel_id=1, source_target_pairs={{0,1},{1,2},{2,3},{4,5},{5,6},{6,7},{8,9},{9,10},{10,11},{12,13},{... | collective-permute-start | bytes 1376264 | tf_op jit(solution)/shard_map/ppermute | solution.py:294
  336.2 12.8 %collective-permute-start.34 = (bf16[32,7168]{1,0:T(8,128)(2,1)S(1)}, bf16[32,7168]{1,0:T(8,128)(2,1)S(1)}, u32[]{:S(2)}, u32[]{:S(2)}) collective-permute-start(bf16[32,7168]{1,0:T(8,128)(2,1)S(1)} %add_convert_fusion.2), channel_id=1, source_target_pairs={{1,0},{2,1},{3,2},{5,4},{6,5},{7,6},{9,8},{10,9},{11,10},{13,12},{... | collective-permute-start | bytes 1376264 | tf_op jit(solution)/shard_map/ppermute | solution.py:295
  344.6 11.4 %collective-permute-start.28 = (bf16[32,7168]{1,0:T(8,128)(2,1)S(1)}, bf16[32,7168]{1,0:T(8,128)(2,1)S(1)}, u32[]{:S(2)}, u32[]{:S(2)}) collective-permute-start(bf16[32,7168]{1,0:T(8,128)(2,1)S(1)} %fusion.9), channel_id=1, source_target_pairs={{16,0},{0,16},{17,1},{1,17},{18,2},{2,18},{19,3},{3,19},{20,4},{4,... | collective-permute-start | bytes 1376264 | tf_op jit(solution)/shard_map/ppermute | solution.py:29
  356.2 8.5 %collective-permute-start.35 = (bf16[32,7168]{1,0:T(8,128)(2,1)S(1)}, bf16[32,7168]{1,0:T(8,128)(2,1)S(1)}, u32[]{:S(2)}, u32[]{:S(2)}) collective-permute-start(bf16[32,7168]{1,0:T(8,128)(2,1)S(1)} %fusion.8), channel_id=1, source_target_pairs={{16,0},{0,16},{17,1},{1,17},{18,2},{2,18},{19,3},{3,19},{20,4},{4,... | collective-permute-start | bytes 1376264 | tf_op jit(solution)/shard_map/ppermute | solution.py:29
  (13 other events, 97.1 us)
Sparse Core Ops, SparseCore 0:
  9.6 71.7 all-gather.3
  82.9 110.4 all-gather.5

commit v6 on v0

--- a/solution.py
+++ b/solution.py
@@ -1,7 +1,354 @@
+import functools
+import math
+
 import jax
 import jax.numpy as jnp
 from jax import lax
+from jax.experimental import pallas as pl
+from jax.experimental.pallas import tpu as pltpu
 from jax.sharding import PartitionSpec as P
+
+BF16, F32 = jnp.bfloat16, jnp.float32
+VMEM_LIMIT = 56 * 1024 * 1024
+LEAD_ROWS = 16
+TAG_COLUMNS = 128
+
+
+def contract_last(left_side, weights):
+    return lax.dot_general(
+        left_side, weights, (((1,), (1,)), ((), ())), preferred_element_type=F32
+    )
+
+
+def flipped(block, axis, stride):
+    route = [(i, i ^ stride) for i in range(lax.axis_size(axis))]
+    return lax.ppermute(block, axis, route)
+
+
+def shifted(block, axis, distance):
+    count = lax.axis_size(axis)
+    return lax.ppermute(block, axis, [((i - distance) % count, i) for i in range(count)])
+
+
+def chunk_of(width, most):
+    best = 128
+    for size in range(128, most + 1, 128):
+        if width % size == 0:
+            best = size
+    return best
+
+
+def gathered_rows(refs):
+    return jnp.concatenate([ref[0] for ref in refs], axis=0)
+
+
+def chained_rows(refs):
+    others = len(refs) // 2
+    own, below, above = refs[0][...], refs[1 : 1 + others], refs[1 + others :]
+    return jnp.concatenate(
+        [own] + [above[away][...] + below[others - 1 - away][...] for away in range(others)],
+        axis=0,
+    )
+
+
+def gathered_input(x, begin, rows):
+    count, unit = x.shape[0], math.gcd(begin, rows)
+    arrays, specs = [], []
+    for turn in range(count):
+        for piece in range(begin // unit, (begin + rows) // unit):
+            arrays.append(x)
+            specs.append(
+                lambda chunk, column, turn=turn, piece=piece: pl.BlockSpec(
+                    (1, unit, chunk),
+                    lambda i, at: (lax.rem(at[0] + turn, count), piece, column(i)),
+                )
+            )
+    return gathered_rows, arrays, specs
+
+
+def chained_input(hops, begin, rows):
+    (own, _), *others = hops
+    from_below, from_above = zip(*others)
+    spec = lambda chunk, column: pl.BlockSpec(
+        (rows, chunk), lambda i, at: (begin // rows, column(i))
+    )
+    arrays = [own, *from_below, *from_above]
+    return chained_rows, arrays, [spec] * len(arrays)
+
+
+def weight_copies(chunk, steps, gate_ups, downs, gate_up_held, down_held, sems):
+    by_chunk = []
+    for step in range(steps):
+        part = pl.ds(step * chunk, chunk)
+        by_chunk.append(
+            (
+                [
+                    pltpu.make_async_copy(
+                        ref.at[:, part, :], gate_up_held.at[i, :, part, :], sems.at[0, step, i]
+                    )
+                    for i, ref in enumerate(gate_ups)
+                ],
+                [
+                    pltpu.make_async_copy(
+                        ref.at[:, part], down_held.at[i, :, part], sems.at[1, step, i]
+                    )
+                    for i, ref in enumerate(downs)
+                ],
+            )
+        )
+    return by_chunk
+
+
+def own_hidden(at_ref, tags, column, hidden):
+    mine = tags[:, column : column + 1].astype(jnp.int32) == at_ref[1]
+    unit = lax.broadcasted_iota(jnp.int32, (tags.shape[0], hidden), 1)
+    return mine == (unit < hidden // 2)
+
+
+def expert_kernel(backward, reads, inputs, count, pieces, chunk, steps, at_ref, *refs):
+    groups = []
+    for number in (*inputs, pieces, pieces, count):
+        groups.append(refs[:number])
+        refs = refs[number:]
+    *rows_in, gate_ups, downs, outs = groups
+    (*totals, hidden_refs, gate_up_held, down_held, sems) = (
+        refs[: 3 if backward else 2] + (refs[3 if backward else 2 : -3],) + refs[-3:]
+    )
+    step = pl.program_id(0)
+    hidden = totals[0].shape[1]
+    copies = weight_copies(chunk, steps, gate_ups, downs, gate_up_held, down_held, sems)
+
+    @pl.when(step == 0)
+    def _():
+        for kind in range(2):
+            for by_kind in copies:
+                for copy in by_kind[kind]:
+                    copy.start()
+        for total in totals:
+            total[...] = jnp.zeros_like(total)
+
+    for number in range(steps):
+
+        @pl.when(step == number)
+        def _(number=number):
+            for copy in copies[number][0] + (copies[number][1] if backward else []):
+                copy.wait()
+
+        if not backward:
+
+            @pl.when(step == steps + number)
+            def _(number=number):
+                for copy in copies[number][1]:
+                    copy.wait()
+
+    at_chunk = pl.ds(pl.multiple_of(lax.rem(step, steps) * chunk, chunk), chunk)
+
+    def gate_or_up(which):
+        return jnp.concatenate(
+            [gate_up_held[i, which, at_chunk, :] for i in range(pieces)], axis=1
+        )
+
+    def down():
+        return jnp.concatenate([down_held[i, :, at_chunk] for i in range(pieces)], axis=0)
+
+    @pl.when(step < steps)
+    def _():
+        x = reads[1](rows_in[1])
+        totals[0][...] += jnp.dot(x, gate_or_up(0), preferred_element_type=F32)
+        totals[1][...] += jnp.dot(x, gate_or_up(1), preferred_element_type=F32)
+        if backward:
+            totals[2][...] += contract_last(reads[2](rows_in[2]), down())
+
+    @pl.when(step == steps - 1)
+    def _():
+        tags = reads[0](rows_in[0])
+        keep = own_hidden(at_ref, tags, TAG_COLUMNS // 2 if backward else 0, hidden)
+        gate, up = totals[0][...], totals[1][...]
+        s = jax.nn.sigmoid(gate)
+        silu = gate * s
+        if backward:
+            grad = totals[2][...]
+            grad_gate = grad * up * (s + silu * (1.0 - s))
+            hidden_refs[0][...] = jnp.where(keep, grad_gate, 0.0).astype(BF16)
+            hidden_refs[1][...] = jnp.where(keep, grad * silu, 0.0).astype(BF16)
+        else:
+            hidden_refs[0][...] = jnp.where(keep, silu * up, 0.0).astype(BF16)
+
+    @pl.when(step >= steps)
+    def _():
+        if backward:
+            total = contract_last(hidden_refs[0][...], gate_or_up(0))
+            total += contract_last(hidden_refs[1][...], gate_or_up(1))
+        else:
+            total = jnp.dot(hidden_refs[0][...], down(), preferred_element_type=F32)
+        rows = outs[0].shape[0]
+        for index, ref in enumerate(outs):
+            ref[...] = total[index * rows : (index + 1) * rows].astype(ref.dtype)
+
+
+def expert_call(at, count, rows, width, tags, inputs, gate_ups, downs):
+    backward = len(inputs) == 2
+    pieces, hid = len(downs), downs[0].shape[0]
+    chunk = chunk_of(width, 1792)
+    steps, hidden, many = width // chunk, pieces * hid, count * rows
+    first = lambda i: jnp.minimum(i, steps - 1)
+    second = lambda i: jnp.maximum(i - steps, 0)
+    all_inputs = [tags, *inputs]
+    arrays = [array for _, some, _ in all_inputs for array in some]
+    in_specs = [spec(TAG_COLUMNS, lambda i: width // TAG_COLUMNS) for spec in tags[2]]
+    in_specs += [spec(chunk, first) for _, _, specs in inputs for spec in specs]
+    in_specs += [pl.BlockSpec(memory_space=pl.ANY)] * (2 * pieces)
+    kernel = functools.partial(
+        expert_kernel,
+        backward,
+        [read for read, _, _ in all_inputs],
+        [len(some) for _, some, _ in all_inputs],
+        count,
+        pieces,
+        chunk,
+        steps,
+    )
+    return pl.pallas_call(
+        kernel,
+        grid_spec=pltpu.PrefetchScalarGridSpec(
+            num_scalar_prefetch=1,
+            grid=(2 * steps,),
+            in_specs=in_specs,
+            out_specs=[pl.BlockSpec((rows, chunk), lambda i, at: (0, second(i)))] * count,
+            scratch_shapes=[pltpu.VMEM((many, hidden), F32)] * (3 if backward else 2)
+            + [pltpu.VMEM((many, hidden), BF16)] * (2 if backward else 1)
+            + [
+                pltpu.VMEM((pieces, 2, width, hid), BF16),
+                pltpu.VMEM((pieces, hid, width), BF16),
+                pltpu.SemaphoreType.DMA((2, steps, pieces)),
+            ],
+        ),
+        out_shape=[jax.ShapeDtypeStruct((rows, width), F32)]
+        + [jax.ShapeDtypeStruct((rows, width), BF16)] * (count - 1),
+        compiler_params=pltpu.CompilerParams(vmem_limit_bytes=VMEM_LIMIT),
+        cost_estimate=pl.CostEstimate(
+            flops=(10 if backward else 6) * many * width * hidden,
+            bytes_accessed=6 * many * width + 6 * width * hidden,
+            transcendentals=many * hidden,
+        ),
+    )(at, *arrays, *gate_ups, *downs)
+
+
+def after(value, *earlier):
+    return lax.optimization_barrier((value, earlier))[0]
+
+
+def hop(below, above, axis, step):
+    count = lax.axis_size(axis)
+    up = [(i, i + 1) for i in range(step - 1, count - 1)]
+    down = [(i, i - 1) for i in range(1, count - step + 1)]
+    return lax.ppermute(below, axis, up), lax.ppermute(above, axis, down)
+
+
+def summands(blocks, step, arrived):
+    pair = (blocks[len(blocks) - step], blocks[step])
+    if arrived is None:
+        return pair
+    return tuple(
+        (own.astype(F32) + other.astype(F32)).astype(BF16) for own, other in zip(pair, arrived)
+    )
+
+
+def step_home(pair, axis, step):
+    count = lax.axis_size(axis)
+    up = lax.ppermute(pair[0], axis, [(i, i + 1) for i in range(step)])
+    down = lax.ppermute(pair[1], axis, [(i, i - 1) for i in range(count - step, count)])
+    return up, down
+
+
+def summed(block, arrived):
+    for part in arrived:
+        block = block + part.astype(F32)
+    return block
+
+
+def few_experts(
+    x_forward,
+    route_forward,
+    prob_forward,
+    x_backward,
+    route_backward,
+    prob_backward,
+    grad_output,
+    w_gate,
+    w_up,
+    w_down,
+):
+    tokens_here, width = x_forward.shape[1:]
+    expert_here = lax.axis_index("expert") // 2
+    count = lax.axis_size("dp")
+    at = jnp.stack([lax.axis_index("dp"), expert_here]).astype(jnp.int32)
+    lead = min(LEAD_ROWS, tokens_here // 2)
+    main = tokens_here - lead
+    ends = (slice(0, main), slice(main, tokens_here))
+
+    half_tag = (tokens_here, TAG_COLUMNS // 2)
+    tagged = jnp.concatenate(
+        [x_forward[0]]
+        + [jnp.broadcast_to(r[0].astype(BF16), half_tag) for r in (route_forward, route_backward)],
+        axis=1,
+    )
+    scaled_grad = (prob_backward[0][:, None] * grad_output[0].astype(F32)).astype(BF16)
+    main_rows, lead_rows = (
+        jnp.concatenate([x_backward[0, rows], scaled_grad[rows]], axis=0) for rows in ends
+    )
+    gate_up, down = jnp.concatenate([w_gate[0], w_up[0]], axis=0), w_down[0, 0]
+
+    x_gathered = lax.all_gather(tagged, "dp")
+    main_gathered = lax.all_gather(after(main_rows, x_gathered), "dp")
+    across_down = flipped(down, "expert", 2)
+    across_gate_up = flipped(gate_up, "expert", 2)
+    hops = [(lead_rows, lead_rows)]
+    hops.append(hop(*hops[-1], "dp", 1))
+    hops[1] = after(hops[1], x_gathered)
+    for step in range(2, count):
+        hops.append(hop(*hops[-1], "dp", step))
+    gate_ups = [gate_up, flipped(gate_up, "expert", 1), across_gate_up]
+    downs = [down, flipped(down, "expert", 1), across_down, flipped(across_down, "expert", 1)]
+    gate_ups.append(flipped(after(across_gate_up, hops[-1], gate_ups[1], downs[3]), "expert", 1))
+
+    def call(tags_from, rows, inputs):
+        tags = gathered_input(x_gathered, tags_from, rows)
+        return expert_call(at, count, rows, width, tags, inputs, gate_ups, downs)
+
+    partial_fwd = call(0, tokens_here, [gathered_input(x_gathered, 0, tokens_here)])
+
+    arrived_fwd = step_home(summands(partial_fwd, 1, None), "dp", 1)
+    hops[0] = after(hops[0], partial_fwd[1])
+    partial_lead = call(main, lead, [chained_input(hops, begin, lead) for begin in (0, lead)])
+
+    arrived_fwd = step_home(summands(partial_fwd, 2, after(arrived_fwd, partial_lead[1])), "dp", 2)
+    arrived_lead = step_home(summands(partial_lead, 1, None), "dp", 1)
+    sends_fwd = summands(partial_fwd, 3, arrived_fwd)
+    sends_lead = summands(partial_lead, 2, arrived_lead)
+    arrived_fwd = step_home(sends_fwd, "dp", 3)
+    arrived_lead = step_home(sends_lead, "dp", 2)
+    main_gathered = after(main_gathered, sends_fwd, sends_lead)
+    partial_main = call(0, main, [gathered_input(main_gathered, b, main) for b in (0, main)])
+
+    arrived_fwd, arrived_lead = after((arrived_fwd, arrived_lead), partial_main[1])
+    sends_main = after(summands(partial_main, 1, None), arrived_fwd, arrived_lead)
+    arrived_main = step_home(sends_main, "dp", 1)
+    total_fwd = summed(partial_fwd[0], arrived_fwd)
+    layer_out = (x_forward[0].astype(F32) + prob_forward[0][:, None] * total_fwd).astype(BF16)
+    sent_fwd = shifted(layer_out, "pipe", 1)
+    arrived_lead = step_home(summands(partial_lead, 3, arrived_lead), "dp", 3)
+
+    def sent_back(rows, block, arrived):
+        grad_in = (grad_output[0, rows].astype(F32) + summed(block, arrived)).astype(BF16)
+        return shifted(grad_in, "pipe", -1)
+
+    arrived_main = step_home(summands(partial_main, 2, arrived_main), "dp", 2)
+    sent_lead = sent_back(ends[1], partial_lead[0], arrived_lead)
+    arrived_main = after(arrived_main, sent_fwd, sent_lead)
+    arrived_main = step_home(summands(partial_main, 3, arrived_main), "dp", 3)
+    sent_main = sent_back(ends[0], partial_main[0], arrived_main)
+    return (sent_fwd[None], jnp.concatenate([sent_main, sent_lead], axis=0)[None])
 
 
 def from_partner(block, axis, stride):
@@ -14,21 +361,9 @@
     return lax.ppermute(block, axis, route)
 
 
-def shifted(block, axis, distance):
-    devices = range(lax.axis_size(axis))
-    route = [((i - distance) % len(devices), i) for i in devices]
-    return lax.ppermute(block, axis, route)
-
-
 def silu_parts(pre_gate):
     sigma_gate = jax.nn.sigmoid(pre_gate)
     return (pre_gate * sigma_gate, sigma_gate)
-
-
-def contract_last(left_side, weights):
-    return lax.dot_general(
-        left_side, weights, (((1,), (1,)), ((), ())), preferred_element_type=jnp.float32
-    )
 
 
 def expert_pass(forward_rows, backward_rows, scaled_rows, gate_weight, up_weight, down_weight):
@@ -66,7 +401,7 @@
     return jnp.dot(selector, values, preferred_element_type=jnp.float32).astype(jnp.bfloat16)
 
 
-def on_device(
+def many_experts(
     x_forward,
     route_forward,
     prob_forward,
@@ -142,8 +477,9 @@
 
 
 def solution(mesh):
+    few = mesh.shape["expert"] == 4
     return jax.shard_map(
-        on_device,
+        few_experts if few else many_experts,
         mesh=mesh,
         in_specs=(
             P("pipe", ("expert", "dp"), None),

time: 594 us -> 481 us (0.81)
  waiting for transfers between devices: 411 us -> 311 us
  starting transfers between devices: 7.51 us -> 69.2 us
  Pallas kernels: 0 us -> 59.4 us
  matrix products: 49.1 us -> 0 us
  blocking collectives: 43.5 us -> 0 us
  local copies, waits for them, and re-layouts: 49.5 us -> 6.88 us
    all_gather x3 -> x2, waiting for transfers between devices: 312 us -> 60.3 us  [the longest x1 60.3 us: few_experts(): main_gathered = lax.all_gather(after(main_rows, x_gathered), 'dp')]
    ppermute x4 -> x33, waiting for transfers between devices: 45.5 us -> 251 us  [the longest x6 124 us: flipped(): return lax.ppermute(block, axis, route)]
    ppermute x4 -> x33, starting transfers between devices: 2.19 us -> 69.2 us  [the longest x9 35.8 us: step_home(): lax.ppermute(pair[1], axis, [(i, i - 1) for i in range(count - step, coun...]
    pallas_call x0 -> x3, Pallas kernels: none -> 59.4 us  [expert_call(): pl.pallas_call(kernel, grid_spec=pltpu.PrefetchScalarGridSpec(num_scalar_...]
    all_to_all x1 -> x0, waiting for transfers between devices: 52.1 us -> none  [on_device(): lax.all_to_all(finished, 'expert', split_axis=1, concat_axis=1, tiled=True)]
    dot_general x9 -> x0, matrix products: 49.1 us -> none  [the longest x3 26.6 us: contract_last(): lax.dot_general(left_side, weights, (((1,), (1,)), ((), ())), preferred_e...]
    all_to_all x1 -> x0, blocking collectives: 43.5 us -> none  [on_device(): lax.all_to_all(split_rows, 'expert', split_axis=1, concat_axis=1, tiled=T...]
    another operation x9 -> x0, local copies, waits for them, and re-layouts: 23.2 us -> none  [the longest x3 15 us: on_device(): jnp.stack([expert_out, grad_rows])]
  transfers between devices with their start and end apart: 8 -> 35, of which waited for: 8 -> 17; matrix products, arithmetic and copies ran while one was open for 7% -> 3% of each run, Pallas kernels for 0% -> 9%
where the time goes in v6:
time: 481 us; the launch traced here: 475 us
  waiting for transfers between devices  311 us (65%)
  starting transfers between devices  69.2 us (14%)
  Pallas kernels  59.4 us (12%)
  between operations  14.7 us (3%)
  other arithmetic  14.1 us (3%)
  local copies, waits for them, and re-layouts  6.88 us (1%)
    ppermute x6, waiting for transfers between devices, flipped(): return lax.ppermute(block, axis, route)  124 us
    ppermute x9, waiting for transfers between devices, step_home(): lax.ppermute(pair[1], axis, [(i, i - 1) for i in range(count - step, coun...  63.5 us
    all_gather x1, waiting for transfers between devices, few_experts(): main_gathered = lax.all_gather(after(main_rows, x_gathered), 'dp')  60.3 us
    pallas_call x3, Pallas kernels, expert_call(): pl.pallas_call(kernel, grid_spec=pltpu.PrefetchScalarGridSpec(num_scalar_...  59.4 us
    ppermute x9, starting transfers between devices, step_home(): lax.ppermute(pair[1], axis, [(i, i - 1) for i in range(count - step, coun...  35.8 us
    ppermute x6, waiting for transfers between devices, hop(): return (lax.ppermute(below, axis, up), lax.ppermute(above, axis, down))  27.5 us
    ppermute x3, waiting for transfers between devices, shifted(): lax.ppermute(block, axis, [((i - distance) % count, i) for i in range(cou...  21.3 us
    ppermute x6, starting transfers between devices, hop(): return (lax.ppermute(below, axis, up), lax.ppermute(above, axis, down))  14.6 us
  transfers between devices with their start and end apart: 35, of which 17 were waited for; matrix products, arithmetic and copies ran while one was open for 3% of the time, Pallas kernels for 9%

profile of v6, /device:TPU:20, one launch (start us, length us, event | category | flops | bytes accessed | tf_op | source)
XLA Modules:
  0.0 475.3 jit_solution(12238621949598073626)
XLA Ops:
  8.7 2.1 concatenate.15
  10.8 4.5 pad_maximum_fusion.refs_8_.refs_18_.refs_12_
  15.3 1.5 collective-permute-start.1
  17.6 1.2 slice_bitcast_fusion.1
  18.9 117.9 %collective-permute-done.8.refs_14_.refs_24_.refs_18_ = bf16[128,7168]{1,0:T(8,128)(2,1)} collective-permute-done((bf16[128,7168]{1,0:T(8,128)(2,1)S(1)}, bf16[128,7168]{1,0:T(8,128)(2,1)}, u32[]{:S(2)}, u32[]{:S(2)}) %collective-permute-start.8) | collective-permute-done | bytes 1835040 | tf_op jit(solution)/shard_map/ppermute | solution.py:25
  136.8 3.5 collective-permute-start.2
  140.2 2.4 collective-permute-start.3
  142.6 9.0 %collective-permute-done.2.refs_5_.refs_12_ = bf16[32,7168]{1,0:T(8,128)(2,1)S(1)} collective-permute-done((bf16[32,7168]{1,0:T(8,128)(2,1)S(1)}, bf16[32,7168]{1,0:T(8,128)(2,1)S(1)}, u32[]{:S(2)}, u32[]{:S(2)}) %collective-permute-start.2) | collective-permute-done | bytes 458784 | tf_op jit(solution)/shard_map/ppermute | solution.py:245
  152.4 2.5 collective-permute-done.3.refs_8_.refs_15_
  154.9 1.9 collective-permute-start.4
  156.8 4.0 collective-permute-start.6
  160.8 8.0 %collective-permute-done.4.refs_6_.refs_13_ = bf16[32,7168]{1,0:T(8,128)(2,1)S(1)} collective-permute-done((bf16[32,7168]{1,0:T(8,128)(2,1)}, bf16[32,7168]{1,0:T(8,128)(2,1)S(1)}, u32[]{:S(2)}, u32[]{:S(2)}) %collective-permute-start.4) | collective-permute-done | bytes 458784 | tf_op jit(solution)/shard_map/ppermute | solution.py:245
  168.8 2.2 collective-permute-start.5
  171.8 7.9 %collective-permute-done.5.refs_7_.refs_14_ = bf16[32,7168]{1,0:T(8,128)(2,1)S(1)} collective-permute-done((bf16[32,7168]{1,0:T(8,128)(2,1)S(1)}, bf16[32,7168]{1,0:T(8,128)(2,1)S(1)}, u32[]{:S(2)}, u32[]{:S(2)}) %collective-permute-start.5) | collective-permute-done | bytes 458784 | tf_op jit(solution)/shard_map/ppermute | solution.py:245
  181.3 1.1 slice_bitcast_fusion
  182.5 6.1 %collective-permute-done.11.refs_13_.refs_23_.refs_17_ = bf16[128,7168]{1,0:T(8,128)(2,1)} collective-permute-done((bf16[128,7168]{1,0:T(8,128)(2,1)S(1)}, bf16[128,7168]{1,0:T(8,128)(2,1)}, u32[]{:S(2)}, u32[]{:S(2)}) %collective-permute-start.11) | collective-permute-done | bytes 1835040 | tf_op jit(solution)/shard_map/ppermute | solution.py:25
  189.1 16.9 %shard_map.113 = (f32[64,7168]{1,0:T(8,128)}, bf16[64,7168]{1,0:T(8,128)(2,1)}, bf16[64,7168]{1,0:T(8,128)(2,1)}, bf16[64,7168]{1,0:T(8,128)(2,1)}) custom-call(s32[2]{0:T(128)} %pad_add_fusion.at_ref, bf16[4,64,7296]{2,1,0:T(8,128)(2,1)} %bitcast.31, bf16[4,64,7296]{2,1,0:T(8,128)(2,1)} %bitcast.32, bf16[4,64,7296]{2,1,0:T(8,128)(2,1)} %bitcast.33, ...), custom_call_target="tpu_custom_call" | custom-call | flops 5637144576 | bytes 33030144 | tf_op jit(solution)/shard_map/pallas_call | solution.py:211
  206.8 1.3 collective-permute-start.13
  208.1 1.2 pad_maximum_fusion.1
  209.3 20.0 %shard_map.114 = (f32[16,7168]{1,0:T(8,128)}, bf16[16,7168]{1,0:T(8,128)(2,1)}, bf16[16,7168]{1,0:T(8,128)(2,1)}, bf16[16,7168]{1,0:T(8,128)(2,1)}) custom-call(s32[2]{0:T(128)} %pad_add_fusion.at_ref, bf16[4,64,7296]{2,1,0:T(8,128)(2,1)} %bitcast.39, bf16[4,64,7296]{2,1,0:T(8,128)(2,1)} %bitcast.40, bf16[4,64,7296]{2,1,0:T(8,128)(2,1)} %bitcast.41, ...), custom_call_target="tpu_custom_call" | custom-call | flops 2348810240 | bytes 24772608 | tf_op jit(solution)/shard_map/pallas_call | solution.py:211
  229.3 10.1 %collective-permute-done.13 = bf16[64,7168]{1,0:T(8,128)(2,1)S(1)} collective-permute-done((bf16[64,7168]{1,0:T(8,128)(2,1)}, bf16[64,7168]{1,0:T(8,128)(2,1)S(1)}, u32[]{:S(2)}, u32[]{:S(2)}) %collective-permute-start.13) | collective-permute-done | bytes 917536 | tf_op jit(solution)/shard_map/ppermute | solution.py:260
  239.9 7.7 %collective-permute-start.16 = (bf16[64,7168]{1,0:T(8,128)(2,1)S(1)}, bf16[64,7168]{1,0:T(8,128)(2,1)S(1)}, u32[]{:S(2)}, u32[]{:S(2)}) collective-permute-start(bf16[64,7168]{1,0:T(8,128)(2,1)S(1)} %get-tuple-element.58), channel_id=1, source_target_pairs={{2,1},{3,2},{6,5},{7,6},{10,9},{11,10},{14,13},{15,14},{18,17},{19... | collective-permute-start | bytes 2752520 | tf_op jit(solution)/shard_map/ppermute | solution.py:260
  247.6 1.3 collective-permute-start.20
  249.6 1.3 collective-permute-start.14
  250.9 39.6 %collective-permute-done.16 = bf16[64,7168]{1,0:T(8,128)(2,1)S(1)} collective-permute-done((bf16[64,7168]{1,0:T(8,128)(2,1)S(1)}, bf16[64,7168]{1,0:T(8,128)(2,1)S(1)}, u32[]{:S(2)}, u32[]{:S(2)}) %collective-permute-start.16) | collective-permute-done | bytes 917536 | tf_op jit(solution)/shard_map/ppermute | solution.py:260
  290.7 4.5 collective-permute-start.17
  295.2 1.2 add_convert_fusion.2
  296.4 1.9 collective-permute-start.15
  299.2 1.3 collective-permute-start.19
  300.5 8.6 %collective-permute-start.21 = (bf16[16,7168]{1,0:T(8,128)(2,1)}, bf16[16,7168]{1,0:T(8,128)(2,1)}, u32[]{:S(2)}, u32[]{:S(2)}) collective-permute-start(bf16[16,7168]{1,0:T(8,128)(2,1)} %get-tuple-element.62), channel_id=1, source_target_pairs={{2,1},{3,2},{6,5},{7,6},{10,9},{11,10},{14,13},{15,14},{18,17},{19... | collective-permute-start | bytes 688136 | tf_op jit(solution)/shard_map/ppermute | solution.py:260
  309.2 60.3 %all-gather.7.cloned.1.call-done = bf16[384,7168]{1,0:T(8,128)(2,1)} async-done(((bf16[96,7168]{1,0:T(8,128)(2,1)}), bf16[384,7168]{1,0:T(8,128)(2,1)}) %all-gather.7.cloned.1.call-update) | async-done | bytes 5505040 | tf_op jit(solution)/shard_map/all_gather | solution.py:303
  369.4 22.5 %shard_map.115 = (f32[48,7168]{1,0:T(8,128)}, bf16[48,7168]{1,0:T(8,128)(2,1)}, bf16[48,7168]{1,0:T(8,128)(2,1)}, bf16[48,7168]{1,0:T(8,128)(2,1)}) custom-call(s32[2]{0:T(128)} %pad_add_fusion.at_ref, bf16[4,64,7296]{2,1,0:T(8,128)(2,1)} %bitcast.43, bf16[4,64,7296]{2,1,0:T(8,128)(2,1)} %bitcast.44, bf16[4,64,7296]{2,1,0:T(8,128)(2,1)} %bitcast.45, ...), custom_call_target="tpu_custom_call" | custom-call | flops 7046430720 | bytes 30277632 | tf_op jit(solution)/shard_map/pallas_call | solution.py:211
  392.1 1.1 add_convert_fusion.5
  393.8 1.3 collective-permute-start.25
  395.1 4.6 collective-permute-start.27
  399.7 2.1 collective-permute-start.28
  403.0 11.2 %collective-permute-done.25 = bf16[48,7168]{1,0:T(8,128)(2,1)S(1)} collective-permute-done((bf16[48,7168]{1,0:T(8,128)(2,1)}, bf16[48,7168]{1,0:T(8,128)(2,1)S(1)}, u32[]{:S(2)}, u32[]{:S(2)}) %collective-permute-start.25) | collective-permute-done | bytes 688160 | tf_op jit(solution)/shard_map/ppermute | solution.py:260
  414.5 1.4 collective-permute-start.24
  416.0 4.6 collective-permute-start.26
  421.3 8.1 %collective-permute-done.29 = bf16[16,7168]{1,0:T(8,128)(2,1)S(1)} collective-permute-done((bf16[16,7168]{1,0:T(8,128)(2,1)S(1)}, bf16[16,7168]{1,0:T(8,128)(2,1)S(1)}, u32[]{:S(2)}, u32[]{:S(2)}) %collective-permute-start.29) | collective-permute-done | bytes 229408 | tf_op jit(solution)/shard_map/ppermute | solution.py:30
  429.4 3.0 collective-permute-done.24
  432.4 1.2 collective-permute-done.26
  433.8 1.9 collective-permute-start.30
  435.9 4.4 collective-permute-start.31
  440.3 10.8 %collective-permute-done.30 = bf16[48,7168]{1,0:T(8,128)(2,1)S(1)} collective-permute-done((bf16[48,7168]{1,0:T(8,128)(2,1)S(1)}, bf16[48,7168]{1,0:T(8,128)(2,1)S(1)}, u32[]{:S(2)}, u32[]{:S(2)}) %collective-permute-start.30) | collective-permute-done | bytes 688160 | tf_op jit(solution)/shard_map/ppermute | solution.py:259
  451.1 1.4 collective-permute-done.31
  453.3 13.2 %collective-permute-done.32 = bf16[48,7168]{1,0:T(8,128)(2,1)S(1)} collective-permute-done((bf16[48,7168]{1,0:T(8,128)(2,1)S(1)}, bf16[48,7168]{1,0:T(8,128)(2,1)S(1)}, u32[]{:S(2)}, u32[]{:S(2)}) %collective-permute-start.32) | collective-permute-done | bytes 688160 | tf_op jit(solution)/shard_map/ppermute | solution.py:30
  466.5 1.0 maximum_bitcast_fusion
  (106 shorter events, 14.0 us)
Async XLA Ops:
  7.2 147.7 %all-gather.5.cloned.1.call-start = ((), (), s32[]{:S(2)}) async-start(), calls=%async_computation | async-start | bytes 4669440 | tf_op jit(solution)/shard_map/all_gather | solution.py:302
  10.8 358.7 %all-gather.7.cloned.1.call-start = ((), (), s32[]{:S(2)}) async-start(), calls=%async_computation.1 | async-start | bytes 6881280 | tf_op jit(solution)/shard_map/all_gather | solution.py:303
  15.3 156.5 %collective-permute-start = (bf16[2,7168,128]{2,1,0:T(8,128)(2,1)}, bf16[2,7168,128]{2,1,0:T(8,128)(2,1)}, u32[]{:S(2)}, u32[]{:S(2)}) collective-permute-start(bf16[2,7168,128]{2,1,0:T(8,128)(2,1)} %pad_maximum_fusion.refs_8_.refs_18_.refs_12_), channel_id=1, source_target_pairs={{0,4},{4,0},{8,12},{12,8},{1,5},{5,1},{9,13},{13,9},{2,6},{6,2},{1... | collective-permute-start | bytes 11010056 | tf_op jit(solution)/shard_map/ppermute | solution.py:25
  15.3 156.5 %collective-permute-start.1 = (bf16[2,7168,128]{2,1,0:T(8,128)(2,1)}, bf16[2,7168,128]{2,1,0:T(8,128)(2,1)}, u32[]{:S(2)}, u32[]{:S(2)}) collective-permute-start(bf16[2,7168,128]{2,1,0:T(8,128)(2,1)} %pad_maximum_fusion.refs_8_.refs_18_.refs_12_), channel_id=1, source_target_pairs={{0,8},{4,12},{8,0},{12,4},{1,9},{5,13},{9,1},{13,5},{2,10},{6,14},... | collective-permute-start | bytes 11010056 | tf_op jit(solution)/shard_map/ppermute | solution.py:25
  16.8 119.9 %collective-permute-start.8 = (bf16[128,7168]{1,0:T(8,128)(2,1)S(1)}, bf16[128,7168]{1,0:T(8,128)(2,1)}, u32[]{:S(2)}, u32[]{:S(2)}) collective-permute-start(bf16[128,7168]{1,0:T(8,128)(2,1)S(1)} %bitcast.58), channel_id=1, source_target_pairs={{0,8},{4,12},{8,0},{12,4},{1,9},{5,13},{9,1},{13,5},{2,10},{6,14},... | collective-permute-start | bytes 5505032 | tf_op jit(solution)/shard_map/ppermute | solution.py:25
  17.6 164.9 %copy-start.2 = (bf16[64,7168]{1,0:T(8,128)(2,1)}, bf16[64,7168]{1,0:T(8,128)(2,1)S(1)}, u32[]{:S(2)}) copy-start(bf16[64,7168]{1,0:T(8,128)(2,1)S(1)} %fusion.2) | copy-start | bytes 2752516
  136.7 35.1 %collective-permute-start.9 = (bf16[128,7168]{1,0:T(8,128)(2,1)}, bf16[128,7168]{1,0:T(8,128)(2,1)}, u32[]{:S(2)}, u32[]{:S(2)}) collective-permute-start(bf16[128,7168]{1,0:T(8,128)(2,1)} %collective-permute-done.8.refs_14_.refs_24_.refs_18_), channel_id=1, source_target_pairs={{0,4},{4,0},{8,12},{12,8},{1,5},{5,1},{9,13},{13,9},{2,6},{6,2},{1... | collective-permute-start | bytes 5505032 | tf_op jit(solution)/shard_map/ppermute | solution.py:25
  136.7 69.3 %copy-start.1 = (bf16[32,7168]{1,0:T(8,128)(2,1)}, bf16[32,7168]{1,0:T(8,128)(2,1)S(1)}, u32[]{:S(2)}) copy-start(bf16[32,7168]{1,0:T(8,128)(2,1)S(1)} %pad_maximum_fusion.2.refs_4_.refs_11_) | copy-start | bytes 1376260
  136.8 14.8 %collective-permute-start.2 = (bf16[32,7168]{1,0:T(8,128)(2,1)S(1)}, bf16[32,7168]{1,0:T(8,128)(2,1)S(1)}, u32[]{:S(2)}, u32[]{:S(2)}) collective-permute-start(bf16[32,7168]{1,0:T(8,128)(2,1)S(1)} %pad_maximum_fusion.2.refs_4_.refs_11_), channel_id=1, source_target_pairs={{0,1},{1,2},{2,3},{4,5},{5,6},{6,7},{8,9},{9,10},{10,11},{12,13},{... | collective-permute-start | bytes 1376264 | tf_op jit(solution)/shard_map/ppermute | solution.py:245
  140.2 14.7 %collective-permute-start.3 = (bf16[32,7168]{1,0:T(8,128)(2,1)S(1)}, bf16[32,7168]{1,0:T(8,128)(2,1)}, u32[]{:S(2)}, u32[]{:S(2)}) collective-permute-start(bf16[32,7168]{1,0:T(8,128)(2,1)S(1)} %pad_maximum_fusion.2.refs_4_.refs_11_), channel_id=1, source_target_pairs={{1,0},{2,1},{3,2},{5,4},{6,5},{7,6},{9,8},{10,9},{11,10},{13,12},{... | collective-permute-start | bytes 1376264 | tf_op jit(solution)/shard_map/ppermute | solution.py:245
  154.9 13.9 %collective-permute-start.4 = (bf16[32,7168]{1,0:T(8,128)(2,1)}, bf16[32,7168]{1,0:T(8,128)(2,1)S(1)}, u32[]{:S(2)}, u32[]{:S(2)}) collective-permute-start(bf16[32,7168]{1,0:T(8,128)(2,1)} %copy-done.6), channel_id=1, source_target_pairs={{1,2},{2,3},{5,6},{6,7},{9,10},{10,11},{13,14},{14,15},{17,18},{18... | collective-permute-start | bytes 1376264 | tf_op jit(solution)/shard_map/ppermute | solution.py:245
  156.8 14.2 %collective-permute-start.6 = (bf16[32,7168]{1,0:T(8,128)(2,1)}, bf16[32,7168]{1,0:T(8,128)(2,1)S(1)}, u32[]{:S(2)}, u32[]{:S(2)}) collective-permute-start(bf16[32,7168]{1,0:T(8,128)(2,1)} %collective-permute-done.3.refs_8_.refs_15_), channel_id=1, source_target_pairs={{1,0},{2,1},{5,4},{6,5},{9,8},{10,9},{13,12},{14,13},{17,16},{18,1... | collective-permute-start | bytes 1376264 | tf_op jit(solution)/shard_map/ppermute | solution.py:245
  168.8 10.9 %collective-permute-start.5 = (bf16[32,7168]{1,0:T(8,128)(2,1)S(1)}, bf16[32,7168]{1,0:T(8,128)(2,1)S(1)}, u32[]{:S(2)}, u32[]{:S(2)}) collective-permute-start(bf16[32,7168]{1,0:T(8,128)(2,1)S(1)} %collective-permute-done.4.refs_6_.refs_13_), channel_id=1, source_target_pairs={{2,3},{6,7},{10,11},{14,15},{18,19},{22,23},{26,27},{30,31}} | collective-permute-start | bytes 1376264 | tf_op jit(solution)/shard_map/ppermute | solution.py:245
  171.1 8.7 %collective-permute-start.7 = (bf16[32,7168]{1,0:T(8,128)(2,1)S(1)}, bf16[32,7168]{1,0:T(8,128)(2,1)S(1)}, u32[]{:S(2)}, u32[]{:S(2)}) collective-permute-start(bf16[32,7168]{1,0:T(8,128)(2,1)S(1)} %collective-permute-done.6.refs_9_.refs_16_), channel_id=1, source_target_pairs={{1,0},{5,4},{9,8},{13,12},{17,16},{21,20},{25,24},{29,28}} | collective-permute-start | bytes 1376264 | tf_op jit(solution)/shard_map/ppermute | solution.py:245
  179.7 9.4 %collective-permute-start.10 = (bf16[2,7168,128]{2,1,0:T(8,128)(2,1)}, bf16[2,7168,128]{2,1,0:T(8,128)(2,1)}, u32[]{:S(2)}, u32[]{:S(2)}) collective-permute-start(bf16[2,7168,128]{2,1,0:T(8,128)(2,1)} %collective-permute-done.1.refs_10_.refs_20_.refs_14_), channel_id=1, source_target_pairs={{0,4},{4,0},{8,12},{12,8},{1,5},{5,1},{9,13},{13,9},{2,6},{6,2},{1... | collective-permute-start | bytes 11010056 | tf_op jit(solution)/shard_map/ppermute | solution.py:25
  179.8 8.8 %collective-permute-start.11 = (bf16[128,7168]{1,0:T(8,128)(2,1)S(1)}, bf16[128,7168]{1,0:T(8,128)(2,1)}, u32[]{:S(2)}, u32[]{:S(2)}) collective-permute-start(bf16[128,7168]{1,0:T(8,128)(2,1)S(1)} %bitcast.59), channel_id=1, source_target_pairs={{0,4},{4,0},{8,12},{12,8},{1,5},{5,1},{9,13},{13,9},{2,6},{6,2},{1... | collective-permute-start | bytes 5505032 | tf_op jit(solution)/shard_map/ppermute | solution.py:25
  188.5 19.5 %slice-start = ((bf16[64,7168]{1,0:T(8,128)(2,1)}), bf16[48,7168]{1,0:T(8,128)(2,1)S(1)}, s32[]{:S(2)}) async-start(bf16[64,7168]{1,0:T(8,128)(2,1)} %copy-done.2), calls=%async_computation.2 | async-start | bytes 1376256 | tf_op jit(solution)/shard_map/slice | solution.py:298
  206.0 23.2 %collective-permute-start.12 = (bf16[64,7168]{1,0:T(8,128)(2,1)}, bf16[64,7168]{1,0:T(8,128)(2,1)S(1)}, u32[]{:S(2)}, u32[]{:S(2)}) collective-permute-start(bf16[64,7168]{1,0:T(8,128)(2,1)} %get-tuple-element.36), channel_id=1, source_target_pairs={{0,1},{4,5},{8,9},{12,13},{16,17},{20,21},{24,25},{28,29}} | collective-permute-start | bytes 2752520 | tf_op jit(solution)/shard_map/ppermute | solution.py:259
  206.8 32.7 %collective-permute-start.13 = (bf16[64,7168]{1,0:T(8,128)(2,1)}, bf16[64,7168]{1,0:T(8,128)(2,1)S(1)}, u32[]{:S(2)}, u32[]{:S(2)}) collective-permute-start(bf16[64,7168]{1,0:T(8,128)(2,1)} %get-tuple-element.34), channel_id=1, source_target_pairs={{3,2},{7,6},{11,10},{15,14},{19,18},{23,22},{27,26},{31,30}} | collective-permute-start | bytes 2752520 | tf_op jit(solution)/shard_map/ppermute | solution.py:260
  209.3 30.1 %copy-start.15 = (bf16[64,7168]{1,0:T(8,128)(2,1)S(1)}, bf16[64,7168]{1,0:T(8,128)(2,1)}, u32[]{:S(2)}) copy-start(bf16[64,7168]{1,0:T(8,128)(2,1)} %get-tuple-element.35) | copy-start | bytes 2752516
  239.4 51.0 %copy-start.14 = (bf16[64,7168]{1,0:T(8,128)(2,1)S(1)}, bf16[64,7168]{1,0:T(8,128)(2,1)}, u32[]{:S(2)}) copy-start(bf16[64,7168]{1,0:T(8,128)(2,1)} %get-tuple-element.36) | copy-start | bytes 2752516
  239.9 55.4 %copy-start.13 = (bf16[64,7168]{1,0:T(8,128)(2,1)S(1)}, bf16[64,7168]{1,0:T(8,128)(2,1)}, u32[]{:S(2)}) copy-start(bf16[64,7168]{1,0:T(8,128)(2,1)} %get-tuple-element.34) | copy-start | bytes 2752516
  239.9 50.6 %collective-permute-start.16 = (bf16[64,7168]{1,0:T(8,128)(2,1)S(1)}, bf16[64,7168]{1,0:T(8,128)(2,1)S(1)}, u32[]{:S(2)}, u32[]{:S(2)}) collective-permute-start(bf16[64,7168]{1,0:T(8,128)(2,1)S(1)} %get-tuple-element.58), channel_id=1, source_target_pairs={{2,1},{3,2},{6,5},{7,6},{10,9},{11,10},{14,13},{15,14},{18,17},{19... | collective-permute-start | bytes 2752520 | tf_op jit(solution)/shard_map/ppermute | solution.py:260
  247.6 50.7 %collective-permute-start.20 = (bf16[16,7168]{1,0:T(8,128)(2,1)S(1)}, bf16[16,7168]{1,0:T(8,128)(2,1)S(1)}, u32[]{:S(2)}, u32[]{:S(2)}) collective-permute-start(bf16[16,7168]{1,0:T(8,128)(2,1)S(1)} %copy-done.21), channel_id=1, source_target_pairs={{3,2},{7,6},{11,10},{15,14},{19,18},{23,22},{27,26},{31,30}} | collective-permute-start | bytes 688136 | tf_op jit(solution)/shard_map/ppermute | solution.py:260
  248.9 49.4 %collective-permute-start.18 = (bf16[16,7168]{1,0:T(8,128)(2,1)S(1)}, bf16[16,7168]{1,0:T(8,128)(2,1)S(1)}, u32[]{:S(2)}, u32[]{:S(2)}) collective-permute-start(bf16[16,7168]{1,0:T(8,128)(2,1)S(1)} %copy-done.20), channel_id=1, source_target_pairs={{0,1},{4,5},{8,9},{12,13},{16,17},{20,21},{24,25},{28,29}} | collective-permute-start | bytes 688136 | tf_op jit(solution)/shard_map/ppermute | solution.py:259
  249.6 45.6 %collective-permute-start.14 = (bf16[64,7168]{1,0:T(8,128)(2,1)S(1)}, bf16[64,7168]{1,0:T(8,128)(2,1)S(1)}, u32[]{:S(2)}, u32[]{:S(2)}) collective-permute-start(bf16[64,7168]{1,0:T(8,128)(2,1)S(1)} %get-tuple-element.59), channel_id=1, source_target_pairs={{0,1},{1,2},{4,5},{5,6},{8,9},{9,10},{12,13},{13,14},{16,17},{17,1... | collective-permute-start | bytes 2752520 | tf_op jit(solution)/shard_map/ppermute | solution.py:259
  290.7 101.3 %collective-permute-start.17 = (bf16[64,7168]{1,0:T(8,128)(2,1)S(1)}, bf16[64,7168]{1,0:T(8,128)(2,1)S(1)}, u32[]{:S(2)}, u32[]{:S(2)}) collective-permute-start(bf16[64,7168]{1,0:T(8,128)(2,1)S(1)} %add_convert_fusion.1), channel_id=1, source_target_pairs={{1,0},{2,1},{3,2},{5,4},{6,5},{7,6},{9,8},{10,9},{11,10},{13,12},{... | collective-permute-start | bytes 2752520 | tf_op jit(solution)/shard_map/ppermute | solution.py:260
  296.4 95.6 %collective-permute-start.15 = (bf16[64,7168]{1,0:T(8,128)(2,1)}, bf16[64,7168]{1,0:T(8,128)(2,1)S(1)}, u32[]{:S(2)}, u32[]{:S(2)}) collective-permute-start(bf16[64,7168]{1,0:T(8,128)(2,1)} %add_convert_fusion.2), channel_id=1, source_target_pairs={{0,1},{1,2},{2,3},{4,5},{5,6},{6,7},{8,9},{9,10},{10,11},{12,13},{... | collective-permute-start | bytes 2752520 | tf_op jit(solution)/shard_map/ppermute | solution.py:259
  299.2 92.7 %collective-permute-start.19 = (bf16[16,7168]{1,0:T(8,128)(2,1)}, bf16[16,7168]{1,0:T(8,128)(2,1)S(1)}, u32[]{:S(2)}, u32[]{:S(2)}) collective-permute-start(bf16[16,7168]{1,0:T(8,128)(2,1)} %get-tuple-element.63), channel_id=1, source_target_pairs={{0,1},{1,2},{4,5},{5,6},{8,9},{9,10},{12,13},{13,14},{16,17},{17,1... | collective-permute-start | bytes 688136 | tf_op jit(solution)/shard_map/ppermute | solution.py:259
  300.5 91.5 %collective-permute-start.21 = (bf16[16,7168]{1,0:T(8,128)(2,1)}, bf16[16,7168]{1,0:T(8,128)(2,1)}, u32[]{:S(2)}, u32[]{:S(2)}) collective-permute-start(bf16[16,7168]{1,0:T(8,128)(2,1)} %get-tuple-element.62), channel_id=1, source_target_pairs={{2,1},{3,2},{6,5},{7,6},{10,9},{11,10},{14,13},{15,14},{18,17},{19... | collective-permute-start | bytes 688136 | tf_op jit(solution)/shard_map/ppermute | solution.py:260
  369.4 32.4 %copy-start.11 = (f32[64,7168]{1,0:T(8,128)S(1)}, f32[64,7168]{1,0:T(8,128)}, u32[]{:S(2)}) copy-start(f32[64,7168]{1,0:T(8,128)} %get-tuple-element.33) | copy-start | bytes 5505028
  369.4 32.4 %copy-start.23 = (f32[1,64]{1,0:T(1,128)S(1)}, f32[1,64]{1,0:T(1,128)}, u32[]{:S(2)}) copy-start(f32[1,64]{1,0:T(1,128)} %param.12) | copy-start | bytes 772
  393.1 9.9 %collective-permute-start.23 = (bf16[48,7168]{1,0:T(8,128)(2,1)}, bf16[48,7168]{1,0:T(8,128)(2,1)S(1)}, u32[]{:S(2)}, u32[]{:S(2)}) collective-permute-start(bf16[48,7168]{1,0:T(8,128)(2,1)} %get-tuple-element.53), channel_id=1, source_target_pairs={{0,1},{4,5},{8,9},{12,13},{16,17},{20,21},{24,25},{28,29}} | collective-permute-start | bytes 2064392 | tf_op jit(solution)/shard_map/ppermute | solution.py:259
  393.8 20.4 %collective-permute-start.25 = (bf16[48,7168]{1,0:T(8,128)(2,1)}, bf16[48,7168]{1,0:T(8,128)(2,1)S(1)}, u32[]{:S(2)}, u32[]{:S(2)}) collective-permute-start(bf16[48,7168]{1,0:T(8,128)(2,1)} %get-tuple-element.54), channel_id=1, source_target_pairs={{3,2},{7,6},{11,10},{15,14},{19,18},{23,22},{27,26},{31,30}} | collective-permute-start | bytes 2064392 | tf_op jit(solution)/shard_map/ppermute | solution.py:260
  395.1 25.4 %collective-permute-start.27 = (bf16[16,7168]{1,0:T(8,128)(2,1)S(1)}, bf16[16,7168]{1,0:T(8,128)(2,1)S(1)}, u32[]{:S(2)}, u32[]{:S(2)}) collective-permute-start(bf16[16,7168]{1,0:T(8,128)(2,1)S(1)} %add_convert_fusion.6), channel_id=1, source_target_pairs={{0,1},{1,2},{2,3},{4,5},{5,6},{6,7},{8,9},{9,10},{10,11},{12,13},{... | collective-permute-start | bytes 688136 | tf_op jit(solution)/shard_map/ppermute | solution.py:259
  399.7 20.8 %collective-permute-start.28 = (bf16[16,7168]{1,0:T(8,128)(2,1)S(1)}, bf16[16,7168]{1,0:T(8,128)(2,1)S(1)}, u32[]{:S(2)}, u32[]{:S(2)}) collective-permute-start(bf16[16,7168]{1,0:T(8,128)(2,1)S(1)} %add_convert_fusion.5), channel_id=1, source_target_pairs={{1,0},{2,1},{3,2},{5,4},{6,5},{7,6},{9,8},{10,9},{11,10},{13,12},{... | collective-permute-start | bytes 688136 | tf_op jit(solution)/shard_map/ppermute | solution.py:260
  402.4 18.2 %copy-start.5 = (bf16[1,64,7168]{2,1,0:T(8,128)(2,1)S(1)}, bf16[1,64,7168]{2,1,0:T(8,128)(2,1)}, u32[]{:S(2)}) copy-start(bf16[1,64,7168]{2,1,0:T(8,128)(2,1)} %param.16) | copy-start | bytes 2752516
  402.4 18.2 %copy-start.19 = (f32[16,7168]{1,0:T(8,128)S(1)}, f32[16,7168]{1,0:T(8,128)}, u32[]{:S(2)}) copy-start(f32[16,7168]{1,0:T(8,128)} %get-tuple-element.55) | copy-start | bytes 1376260
  402.4 27.0 %collective-permute-start.22 = (bf16[64,7168]{1,0:T(8,128)(2,1)S(1)}, bf16[64,7168]{1,0:T(8,128)(2,1)S(1)}, u32[]{:S(2)}, u32[]{:S(2)}) collective-permute-start(bf16[64,7168]{1,0:T(8,128)(2,1)S(1)} %add_convert_fusion), channel_id=1, source_target_pairs={{16,0},{0,16},{17,1},{1,17},{18,2},{2,18},{19,3},{3,19},{20,4},{4,... | collective-permute-start | bytes 2752520 | tf_op jit(solution)/shard_map/ppermute | solution.py:30
  414.2 19.4 %copy-start.17 = (bf16[48,7168]{1,0:T(8,128)(2,1)S(1)}, bf16[48,7168]{1,0:T(8,128)(2,1)}, u32[]{:S(2)}) copy-start(bf16[48,7168]{1,0:T(8,128)(2,1)} %get-tuple-element.54) | copy-start | bytes 2064388
  414.5 21.2 %copy-start.16 = (bf16[48,7168]{1,0:T(8,128)(2,1)S(1)}, bf16[48,7168]{1,0:T(8,128)(2,1)}, u32[]{:S(2)}) copy-start(bf16[48,7168]{1,0:T(8,128)(2,1)} %get-tuple-element.53) | copy-start | bytes 2064388
  414.5 17.9 %collective-permute-start.24 = (bf16[48,7168]{1,0:T(8,128)(2,1)S(1)}, bf16[48,7168]{1,0:T(8,128)(2,1)S(1)}, u32[]{:S(2)}, u32[]{:S(2)}) collective-permute-start(bf16[48,7168]{1,0:T(8,128)(2,1)S(1)} %get-tuple-element.61), channel_id=1, source_target_pairs={{0,1},{1,2},{4,5},{5,6},{8,9},{9,10},{12,13},{13,14},{16,17},{17,1... | collective-permute-start | bytes 2064392 | tf_op jit(solution)/shard_map/ppermute | solution.py:259
  416.0 17.6 %collective-permute-start.26 = (bf16[48,7168]{1,0:T(8,128)(2,1)S(1)}, bf16[48,7168]{1,0:T(8,128)(2,1)S(1)}, u32[]{:S(2)}, u32[]{:S(2)}) collective-permute-start(bf16[48,7168]{1,0:T(8,128)(2,1)S(1)} %get-tuple-element.60), channel_id=1, source_target_pairs={{2,1},{3,2},{6,5},{7,6},{10,9},{11,10},{14,13},{15,14},{18,17},{19... | collective-permute-start | bytes 2064392 | tf_op jit(solution)/shard_map/ppermute | solution.py:260
  420.7 31.8 %copy-start.12 = (f32[48,7168]{1,0:T(8,128)S(1)}, f32[48,7168]{1,0:T(8,128)}, u32[]{:S(2)}) copy-start(f32[48,7168]{1,0:T(8,128)} %get-tuple-element.48) | copy-start | bytes 4128772
  420.7 8.7 %collective-permute-start.29 = (bf16[16,7168]{1,0:T(8,128)(2,1)S(1)}, bf16[16,7168]{1,0:T(8,128)(2,1)S(1)}, u32[]{:S(2)}, u32[]{:S(2)}) collective-permute-start(bf16[16,7168]{1,0:T(8,128)(2,1)S(1)} %fusion.8), channel_id=1, source_target_pairs={{16,0},{0,16},{17,1},{1,17},{18,2},{2,18},{19,3},{3,19},{20,4},{4,... | collective-permute-start | bytes 688136 | tf_op jit(solution)/shard_map/ppermute | solution.py:30
  433.8 17.3 %collective-permute-start.30 = (bf16[48,7168]{1,0:T(8,128)(2,1)S(1)}, bf16[48,7168]{1,0:T(8,128)(2,1)S(1)}, u32[]{:S(2)}, u32[]{:S(2)}) collective-permute-start(bf16[48,7168]{1,0:T(8,128)(2,1)S(1)} %add_convert_fusion.4), channel_id=1, source_target_pairs={{0,1},{1,2},{2,3},{4,5},{5,6},{6,7},{8,9},{9,10},{10,11},{12,13},{... | collective-permute-start | bytes 2064392 | tf_op jit(solution)/shard_map/ppermute | solution.py:259
  435.9 16.6 %collective-permute-start.31 = (bf16[48,7168]{1,0:T(8,128)(2,1)S(1)}, bf16[48,7168]{1,0:T(8,128)(2,1)S(1)}, u32[]{:S(2)}, u32[]{:S(2)}) collective-permute-start(bf16[48,7168]{1,0:T(8,128)(2,1)S(1)} %add_convert_fusion.3), channel_id=1, source_target_pairs={{1,0},{2,1},{3,2},{5,4},{6,5},{7,6},{9,8},{10,9},{11,10},{13,12},{... | collective-permute-start | bytes 2064392 | tf_op jit(solution)/shard_map/ppermute | solution.py:260
  452.7 13.8 %collective-permute-start.32 = (bf16[48,7168]{1,0:T(8,128)(2,1)S(1)}, bf16[48,7168]{1,0:T(8,128)(2,1)S(1)}, u32[]{:S(2)}, u32[]{:S(2)}) collective-permute-start(bf16[48,7168]{1,0:T(8,128)(2,1)S(1)} %fusion.5), channel_id=1, source_target_pairs={{16,0},{0,16},{17,1},{1,17},{18,2},{2,18},{19,3},{3,19},{20,4},{4,... | collective-permute-start | bytes 2064392 | tf_op jit(solution)/shard_map/ppermute | solution.py:30
  (13 other events, 89.8 us)
Sparse Core Ops, SparseCore 0:
  10.9 72.8 all-gather.4
  209.4 159.9 all-gather.6

commit v7 on v6

--- a/solution.py
+++ b/solution.py
@@ -105,41 +105,118 @@
     return mine == (unit < hidden // 2)
 
 
-def expert_kernel(backward, reads, inputs, count, pieces, chunk, steps, at_ref, *refs):
-    groups = []
-    for number in (*inputs, pieces, pieces, count):
-        groups.append(refs[:number])
-        refs = refs[number:]
-    *rows_in, gate_ups, downs, outs = groups
-    (*totals, hidden_refs, gate_up_held, down_held, sems) = (
-        refs[: 3 if backward else 2] + (refs[3 if backward else 2 : -3],) + refs[-3:]
-    )
+def joined(refs, axis, index=None):
+    pick = (lambda ref: ref[...]) if index is None else (lambda ref: ref[index])
+    return jnp.concatenate([pick(ref) for ref in refs], axis=axis)
+
+
+def put_blocks(outs, total):
+    rows = outs[0].shape[0]
+    for index, ref in enumerate(outs):
+        ref[...] = total[index * rows : (index + 1) * rows].astype(ref.dtype)
+
+
+def compiler_params():
+    return pltpu.CompilerParams(vmem_limit_bytes=VMEM_LIMIT)
+
+
+def small_cost(many, hidden):
+    return pl.CostEstimate(flops=many * hidden, bytes_accessed=many, transcendentals=0)
+
+
+def home_shapes(count, rows, width):
+    own, others = (jax.ShapeDtypeStruct((rows, width), kind) for kind in (F32, BF16))
+    return [own] + [others] * (count - 1)
+
+
+def hidden_kernel(count, pieces, steps, at_ref, *refs):
+    tags, rows_in, gate_ups = refs[:count], refs[count : 2 * count], refs[2 * count : -3]
+    out_ref, gate_ref, up_ref = refs[-3:]
     step = pl.program_id(0)
-    hidden = totals[0].shape[1]
-    copies = weight_copies(chunk, steps, gate_ups, downs, gate_up_held, down_held, sems)
 
     @pl.when(step == 0)
     def _():
-        for kind in range(2):
-            for by_kind in copies:
-                for copy in by_kind[kind]:
-                    copy.start()
-        for total in totals:
+        gate_ref[...] = jnp.zeros_like(gate_ref)
+        up_ref[...] = jnp.zeros_like(up_ref)
+
+    x = gathered_rows(rows_in)
+    gate_ref[...] += jnp.dot(x, joined(gate_ups, 1, 0), preferred_element_type=F32)
+    up_ref[...] += jnp.dot(x, joined(gate_ups, 1, 1), preferred_element_type=F32)
+
+    @pl.when(step == steps - 1)
+    def _():
+        gate, up = gate_ref[...], up_ref[...]
+        keep = own_hidden(at_ref, gathered_rows(tags), 0, gate.shape[1])
+        out_ref[...] = jnp.where(keep, gate * jax.nn.sigmoid(gate) * up, 0.0).astype(BF16)
+
+
+def hidden_call(at, x_gathered, rows, width, gate_ups):
+    count, pieces, hid = x_gathered.shape[0], len(gate_ups), gate_ups[0].shape[2]
+    chunk = chunk_of(width, 1792)
+    steps, hidden, many = width // chunk, pieces * hid, count * rows
+    _, arrays, specs = gathered_input(x_gathered, 0, rows)
+    return pl.pallas_call(
+        functools.partial(hidden_kernel, count, pieces, steps),
+        grid_spec=pltpu.PrefetchScalarGridSpec(
+            num_scalar_prefetch=1,
+            grid=(steps,),
+            in_specs=[spec(TAG_COLUMNS, lambda i: width // TAG_COLUMNS) for spec in specs]
+            + [spec(chunk, lambda i: i) for spec in specs]
+            + [pl.BlockSpec((2, chunk, hid), lambda i, at: (0, i, 0))] * pieces,
+            out_specs=pl.BlockSpec((many, hidden), lambda i, at: (0, 0)),
+            scratch_shapes=[pltpu.VMEM((many, hidden), F32)] * 2,
+        ),
+        out_shape=jax.ShapeDtypeStruct((many, hidden), BF16),
+        compiler_params=compiler_params(),
+        cost_estimate=small_cost(many, hidden),
+    )(at, *arrays, *arrays, *gate_ups)
+
+
+def down_kernel(pieces, hidden_ref, *refs):
+    downs, outs = refs[:pieces], refs[pieces:]
+    total = jnp.dot(hidden_ref[...], joined(downs, 0), preferred_element_type=F32)
+    put_blocks(outs, total)
+
+
+def down_call(hidden_rows, count, downs):
+    many, hidden = hidden_rows.shape
+    pieces, (hid, width), rows = len(downs), downs[0].shape, many // count
+    chunk = chunk_of(width, 1792)
+    return pl.pallas_call(
+        functools.partial(down_kernel, pieces),
+        grid=(width // chunk,),
+        in_specs=[pl.BlockSpec((many, hidden), lambda i: (0, 0))]
+        + [pl.BlockSpec((hid, chunk), lambda i: (0, i))] * pieces,
+        out_specs=[pl.BlockSpec((rows, chunk), lambda i: (0, i))] * count,
+        out_shape=home_shapes(count, rows, width),
+        compiler_params=compiler_params(),
+        cost_estimate=small_cost(many, hidden),
+    )(hidden_rows, *downs)
+
+
+def backward_kernel(inputs, count, pieces, chunk, steps, at_ref, *refs):
+    tags, refs = refs[:count], refs[count:]
+    rows_in, scaled_in, refs = refs[:inputs], refs[inputs : 2 * inputs], refs[2 * inputs :]
+    gate_ups, downs, outs = refs[:pieces], refs[pieces : 2 * pieces], refs[2 * pieces : -8]
+    gate_ref, up_ref, grad_ref, grad_gate_ref, grad_up_ref = refs[-8:-3]
+    gate_up_held, down_held, sems = refs[-3:]
+    step = pl.program_id(0)
+    copies = weight_copies(chunk, steps, gate_ups, downs, gate_up_held, down_held, sems)
+
+    @pl.when(step == 0)
+    def _():
+        for of_gate_up, of_down in copies:
+            for copy in of_gate_up + of_down:
+                copy.start()
+        for total in (gate_ref, up_ref, grad_ref):
             total[...] = jnp.zeros_like(total)
 
-    for number in range(steps):
+    for number, (of_gate_up, of_down) in enumerate(copies):
 
         @pl.when(step == number)
-        def _(number=number):
-            for copy in copies[number][0] + (copies[number][1] if backward else []):
+        def _(waited=of_gate_up + of_down):
+            for copy in waited:
                 copy.wait()
-
-        if not backward:
-
-            @pl.when(step == steps + number)
-            def _(number=number):
-                for copy in copies[number][1]:
-                    copy.wait()
 
     at_chunk = pl.ds(pl.multiple_of(lax.rem(step, steps) * chunk, chunk), chunk)
 
@@ -148,90 +225,62 @@
             [gate_up_held[i, which, at_chunk, :] for i in range(pieces)], axis=1
         )
 
-    def down():
-        return jnp.concatenate([down_held[i, :, at_chunk] for i in range(pieces)], axis=0)
-
     @pl.when(step < steps)
     def _():
-        x = reads[1](rows_in[1])
-        totals[0][...] += jnp.dot(x, gate_or_up(0), preferred_element_type=F32)
-        totals[1][...] += jnp.dot(x, gate_or_up(1), preferred_element_type=F32)
-        if backward:
-            totals[2][...] += contract_last(reads[2](rows_in[2]), down())
+        x = chained_rows(rows_in)
+        gate_ref[...] += jnp.dot(x, gate_or_up(0), preferred_element_type=F32)
+        up_ref[...] += jnp.dot(x, gate_or_up(1), preferred_element_type=F32)
+        down = jnp.concatenate([down_held[i, :, at_chunk] for i in range(pieces)], axis=0)
+        grad_ref[...] += contract_last(chained_rows(scaled_in), down)
 
     @pl.when(step == steps - 1)
     def _():
-        tags = reads[0](rows_in[0])
-        keep = own_hidden(at_ref, tags, TAG_COLUMNS // 2 if backward else 0, hidden)
-        gate, up = totals[0][...], totals[1][...]
+        gate, up, grad = gate_ref[...], up_ref[...], grad_ref[...]
+        keep = own_hidden(at_ref, gathered_rows(tags), TAG_COLUMNS // 2, gate.shape[1])
         s = jax.nn.sigmoid(gate)
         silu = gate * s
-        if backward:
-            grad = totals[2][...]
-            grad_gate = grad * up * (s + silu * (1.0 - s))
-            hidden_refs[0][...] = jnp.where(keep, grad_gate, 0.0).astype(BF16)
-            hidden_refs[1][...] = jnp.where(keep, grad * silu, 0.0).astype(BF16)
-        else:
-            hidden_refs[0][...] = jnp.where(keep, silu * up, 0.0).astype(BF16)
+        grad_gate = grad * up * (s + silu * (1.0 - s))
+        grad_gate_ref[...] = jnp.where(keep, grad_gate, 0.0).astype(BF16)
+        grad_up_ref[...] = jnp.where(keep, grad * silu, 0.0).astype(BF16)
 
     @pl.when(step >= steps)
     def _():
-        if backward:
-            total = contract_last(hidden_refs[0][...], gate_or_up(0))
-            total += contract_last(hidden_refs[1][...], gate_or_up(1))
-        else:
-            total = jnp.dot(hidden_refs[0][...], down(), preferred_element_type=F32)
-        rows = outs[0].shape[0]
-        for index, ref in enumerate(outs):
-            ref[...] = total[index * rows : (index + 1) * rows].astype(ref.dtype)
-
-
-def expert_call(at, count, rows, width, tags, inputs, gate_ups, downs):
-    backward = len(inputs) == 2
+        total = contract_last(grad_gate_ref[...], gate_or_up(0))
+        total += contract_last(grad_up_ref[...], gate_or_up(1))
+        put_blocks(outs, total)
+
+
+def backward_call(at, x_gathered, begin, rows, hops, gate_ups, downs):
+    count, width = x_gathered.shape[0], hops[0][0].shape[1]
     pieces, hid = len(downs), downs[0].shape[0]
     chunk = chunk_of(width, 1792)
     steps, hidden, many = width // chunk, pieces * hid, count * rows
     first = lambda i: jnp.minimum(i, steps - 1)
     second = lambda i: jnp.maximum(i - steps, 0)
-    all_inputs = [tags, *inputs]
-    arrays = [array for _, some, _ in all_inputs for array in some]
-    in_specs = [spec(TAG_COLUMNS, lambda i: width // TAG_COLUMNS) for spec in tags[2]]
-    in_specs += [spec(chunk, first) for _, _, specs in inputs for spec in specs]
-    in_specs += [pl.BlockSpec(memory_space=pl.ANY)] * (2 * pieces)
-    kernel = functools.partial(
-        expert_kernel,
-        backward,
-        [read for read, _, _ in all_inputs],
-        [len(some) for _, some, _ in all_inputs],
-        count,
-        pieces,
-        chunk,
-        steps,
-    )
+    _, tags, tag_specs = gathered_input(x_gathered, begin, rows)
+    _, rows_in, row_specs = chained_input(hops, 0, rows)
+    _, _, scaled_specs = chained_input(hops, rows, rows)
     return pl.pallas_call(
-        kernel,
+        functools.partial(backward_kernel, len(rows_in), count, pieces, chunk, steps),
         grid_spec=pltpu.PrefetchScalarGridSpec(
             num_scalar_prefetch=1,
             grid=(2 * steps,),
-            in_specs=in_specs,
+            in_specs=[spec(TAG_COLUMNS, lambda i: width // TAG_COLUMNS) for spec in tag_specs]
+            + [spec(chunk, first) for spec in row_specs + scaled_specs]
+            + [pl.BlockSpec(memory_space=pl.ANY)] * (2 * pieces),
             out_specs=[pl.BlockSpec((rows, chunk), lambda i, at: (0, second(i)))] * count,
-            scratch_shapes=[pltpu.VMEM((many, hidden), F32)] * (3 if backward else 2)
-            + [pltpu.VMEM((many, hidden), BF16)] * (2 if backward else 1)
+            scratch_shapes=[pltpu.VMEM((many, hidden), F32)] * 3
+            + [pltpu.VMEM((many, hidden), BF16)] * 2
             + [
                 pltpu.VMEM((pieces, 2, width, hid), BF16),
                 pltpu.VMEM((pieces, hid, width), BF16),
                 pltpu.SemaphoreType.DMA((2, steps, pieces)),
             ],
         ),
-        out_shape=[jax.ShapeDtypeStruct((rows, width), F32)]
-        + [jax.ShapeDtypeStruct((rows, width), BF16)] * (count - 1),
-        compiler_params=pltpu.CompilerParams(vmem_limit_bytes=VMEM_LIMIT),
-        cost_estimate=pl.CostEstimate(
-            flops=(10 if backward else 6) * many * width * hidden,
-            bytes_accessed=6 * many * width + 6 * width * hidden,
-            transcendentals=many * hidden,
-        ),
-    )(at, *arrays, *gate_ups, *downs)
+        out_shape=home_shapes(count, rows, width),
+        compiler_params=compiler_params(),
+        cost_estimate=small_cost(many, hidden),
+    )(at, *tags, *rows_in, *rows_in, *gate_ups, *downs)
 
 
 def after(value, *earlier):
@@ -300,54 +349,52 @@
     gate_up, down = jnp.concatenate([w_gate[0], w_up[0]], axis=0), w_down[0, 0]
 
     x_gathered = lax.all_gather(tagged, "dp")
-    main_gathered = lax.all_gather(after(main_rows, x_gathered), "dp")
+    across_gate_up = flipped(gate_up, "expert", 2)
     across_down = flipped(down, "expert", 2)
-    across_gate_up = flipped(gate_up, "expert", 2)
-    hops = [(lead_rows, lead_rows)]
-    hops.append(hop(*hops[-1], "dp", 1))
-    hops[1] = after(hops[1], x_gathered)
+    hops_main = [(main_rows, main_rows)]
+    for step in range(1, count):
+        hops_main.append(hop(*hops_main[-1], "dp", step))
+    gate_ups = [gate_up, flipped(gate_up, "expert", 1), across_gate_up]
+    downs = [down, flipped(down, "expert", 1), across_down]
+    waits = (x_gathered, hops_main[1], gate_ups[1], downs[1])
+    gate_ups.append(flipped(after(across_gate_up, waits), "expert", 1))
+    hidden_fwd = hidden_call(at, x_gathered, tokens_here, width, gate_ups)
+    downs.append(flipped(after(across_down, hops_main[2], hidden_fwd), "expert", 1))
+    partial_fwd = down_call(hidden_fwd, count, downs)
+
+    arrived_fwd = step_home(summands(partial_fwd, 1, None), "dp", 1)
+    lead_rows = after(lead_rows, hops_main[3])
+    hops_lead = [(lead_rows, lead_rows)]
+    hops_lead.append(hop(*hops_lead[-1], "dp", 1))
+    sends_fwd = summands(partial_fwd, 2, arrived_fwd)
+    arrived_fwd = step_home(sends_fwd, "dp", 2)
+    main_in = after(hops_main[:1], sends_fwd) + hops_main[1:]
+    partial_main = backward_call(at, x_gathered, 0, main, main_in, gate_ups, downs)
+
+    arrived_fwd, hops_lead[1] = after((arrived_fwd, hops_lead[1]), partial_main[1])
+    arrived_fwd = step_home(summands(partial_fwd, 3, arrived_fwd), "dp", 3)
+    arrived_main = step_home(summands(partial_main, 1, None), "dp", 1)
     for step in range(2, count):
-        hops.append(hop(*hops[-1], "dp", step))
-    gate_ups = [gate_up, flipped(gate_up, "expert", 1), across_gate_up]
-    downs = [down, flipped(down, "expert", 1), across_down, flipped(across_down, "expert", 1)]
-    gate_ups.append(flipped(after(across_gate_up, hops[-1], gate_ups[1], downs[3]), "expert", 1))
-
-    def call(tags_from, rows, inputs):
-        tags = gathered_input(x_gathered, tags_from, rows)
-        return expert_call(at, count, rows, width, tags, inputs, gate_ups, downs)
-
-    partial_fwd = call(0, tokens_here, [gathered_input(x_gathered, 0, tokens_here)])
-
-    arrived_fwd = step_home(summands(partial_fwd, 1, None), "dp", 1)
-    hops[0] = after(hops[0], partial_fwd[1])
-    partial_lead = call(main, lead, [chained_input(hops, begin, lead) for begin in (0, lead)])
-
-    arrived_fwd = step_home(summands(partial_fwd, 2, after(arrived_fwd, partial_lead[1])), "dp", 2)
+        hops_lead.append(hop(*hops_lead[-1], "dp", step))
+    partial_lead = backward_call(at, x_gathered, main, lead, hops_lead, gate_ups, downs)
+
+    arrived_fwd, arrived_main = after((arrived_fwd, arrived_main), partial_lead[1])
+    arrived_main = step_home(summands(partial_main, 2, arrived_main), "dp", 2)
     arrived_lead = step_home(summands(partial_lead, 1, None), "dp", 1)
-    sends_fwd = summands(partial_fwd, 3, arrived_fwd)
-    sends_lead = summands(partial_lead, 2, arrived_lead)
-    arrived_fwd = step_home(sends_fwd, "dp", 3)
-    arrived_lead = step_home(sends_lead, "dp", 2)
-    main_gathered = after(main_gathered, sends_fwd, sends_lead)
-    partial_main = call(0, main, [gathered_input(main_gathered, b, main) for b in (0, main)])
-
-    arrived_fwd, arrived_lead = after((arrived_fwd, arrived_lead), partial_main[1])
-    sends_main = after(summands(partial_main, 1, None), arrived_fwd, arrived_lead)
-    arrived_main = step_home(sends_main, "dp", 1)
     total_fwd = summed(partial_fwd[0], arrived_fwd)
     layer_out = (x_forward[0].astype(F32) + prob_forward[0][:, None] * total_fwd).astype(BF16)
     sent_fwd = shifted(layer_out, "pipe", 1)
-    arrived_lead = step_home(summands(partial_lead, 3, arrived_lead), "dp", 3)
 
     def sent_back(rows, block, arrived):
         grad_in = (grad_output[0, rows].astype(F32) + summed(block, arrived)).astype(BF16)
         return shifted(grad_in, "pipe", -1)
 
-    arrived_main = step_home(summands(partial_main, 2, arrived_main), "dp", 2)
-    sent_lead = sent_back(ends[1], partial_lead[0], arrived_lead)
-    arrived_main = after(arrived_main, sent_fwd, sent_lead)
+    arrived_main = after(arrived_main, sent_fwd)
     arrived_main = step_home(summands(partial_main, 3, arrived_main), "dp", 3)
+    arrived_lead = step_home(summands(partial_lead, 2, arrived_lead), "dp", 2)
     sent_main = sent_back(ends[0], partial_main[0], arrived_main)
+    arrived_lead = step_home(summands(partial_lead, 3, arrived_lead), "dp", 3)
+    sent_lead = sent_back(ends[1], partial_lead[0], after(arrived_lead, sent_main))
     return (sent_fwd[None], jnp.concatenate([sent_main, sent_lead], axis=0)[None])
 
 

time: 481 us -> 382 us (0.79)
  waiting for transfers between devices: 311 us -> 188 us
  starting transfers between devices: 69.2 us -> 93 us
    ppermute x6, waiting for transfers between devices: 124 us -> 26.3 us  [flipped(): return lax.ppermute(block, axis, route)]
    ppermute x6 -> x12, waiting for transfers between devices: 27.5 us -> 103 us  [hop(): return (lax.ppermute(below, axis, up), lax.ppermute(above, axis, down))]
    all_gather x1 -> x0, waiting for transfers between devices: 60.3 us -> none  [few_experts(): main_gathered = lax.all_gather(after(main_rows, x_gathered), 'dp')]
    ppermute x9, waiting for transfers between devices: 63.5 us -> 23.6 us  [step_home(): lax.ppermute(pair[1], axis, [(i, i - 1) for i in range(count - step, coun...]
    ppermute x6 -> x12, starting transfers between devices: 14.6 us -> 35.9 us  [hop(): return (lax.ppermute(below, axis, up), lax.ppermute(above, axis, down))]
    ppermute x9, waiting for transfers between devices: 13.8 us -> 20.3 us  [step_home(): up = lax.ppermute(pair[0], axis, [(i, i + 1) for i in range(step)])]
    ppermute x3, waiting for transfers between devices: 21.3 us -> 15.6 us  [shifted(): lax.ppermute(block, axis, [((i - distance) % count, i) for i in range(cou...]
    unnamed x51 -> x67, local copies, waits for them, and re-layouts: 2.28 us -> 7.53 us
  transfers between devices with their start and end apart: 35 -> 40, of which waited for: 17 -> 16; matrix products, arithmetic and copies ran while one was open for 3% -> 3% of each run, Pallas kernels for 9% -> 13%
where the time goes in v7:
time: 382 us; the launch traced here: 378 us
  waiting for transfers between devices  188 us (49%)
  starting transfers between devices  93 us (24%)
  Pallas kernels  57 us (15%)
  between operations  14.8 us (4%)
  other arithmetic  13.8 us (4%)
  local copies, waits for them, and re-layouts  10.8 us (3%)
    ppermute x12, waiting for transfers between devices, hop(): return (lax.ppermute(below, axis, up), lax.ppermute(above, axis, down))  103 us
    pallas_call x2, Pallas kernels, backward_call(): pl.pallas_call(functools.partial(backward_kernel, len(rows_in), count, pi...  39.9 us
    ppermute x9, starting transfers between devices, step_home(): lax.ppermute(pair[1], axis, [(i, i - 1) for i in range(count - step, coun...  39 us
    ppermute x12, starting transfers between devices, hop(): return (lax.ppermute(below, axis, up), lax.ppermute(above, axis, down))  35.9 us
    ppermute x6, waiting for transfers between devices, flipped(): return lax.ppermute(block, axis, route)  26.3 us
    ppermute x9, waiting for transfers between devices, step_home(): lax.ppermute(pair[1], axis, [(i, i - 1) for i in range(count - step, coun...  23.6 us
    ppermute x9, waiting for transfers between devices, step_home(): up = lax.ppermute(pair[0], axis, [(i, i + 1) for i in range(step)])  20.3 us
    ppermute x3, waiting for transfers between devices, shifted(): lax.ppermute(block, axis, [((i - distance) % count, i) for i in range(cou...  15.6 us
  transfers between devices with their start and end apart: 40, of which 16 were waited for; matrix products, arithmetic and copies ran while one was open for 3% of the time, Pallas kernels for 13%

profile of v7, /device:TPU:20, one launch (start us, length us, event | category | flops | bytes accessed | tf_op | source)
XLA Modules:
  0.0 377.9 jit_solution(2421077747031579919)
XLA Ops:
  8.7 2.1 concatenate.15
  10.8 2.5 pad_maximum_fusion.refs_8_.refs_18_
  13.4 1.6 collective-permute-start.1
  16.5 3.5 collective-permute-start.2
  20.0 2.4 collective-permute-start.3
  22.4 87.7 %collective-permute-done.2.refs_5_.refs_12_ = bf16[96,7168]{1,0:T(8,128)(2,1)S(1)} collective-permute-done((bf16[96,7168]{1,0:T(8,128)(2,1)S(1)}, bf16[96,7168]{1,0:T(8,128)(2,1)S(1)}, u32[]{:S(2)}, u32[]{:S(2)}) %collective-permute-start.2) | collective-permute-done | bytes 1376288 | tf_op jit(solution)/shard_map/ppermute | solution.py:294
  112.3 1.8 copy-done.1
  115.5 1.9 collective-permute-start.7
  117.4 6.1 %collective-permute-start.8 = (bf16[96,7168]{1,0:T(8,128)(2,1)}, bf16[96,7168]{1,0:T(8,128)(2,1)}, u32[]{:S(2)}, u32[]{:S(2)}) collective-permute-start(bf16[96,7168]{1,0:T(8,128)(2,1)} %copy-done.7), channel_id=1, source_target_pairs={{1,0},{2,1},{5,4},{6,5},{9,8},{10,9},{13,12},{14,13},{17,16},{18,1... | collective-permute-start | bytes 4128776 | tf_op jit(solution)/shard_map/ppermute | solution.py:294
  124.1 10.2 %shard_map.113.hidden_ref = bf16[256,512]{1,0:T(8,128)(2,1)} custom-call(s32[2]{0:T(128)} %pad_add_fusion.at_ref, bf16[4,64,7296]{2,1,0:T(8,128)(2,1)} %bitcast.30, bf16[4,64,7296]{2,1,0:T(8,128)(2,1)} %bitcast.31, bf16[4,64,7296]{2,1,0:T(8,128)(2,1)} %bitcast.32, bf16[4,64,7296]{2,1,0:T(8,128)(2,1)} %bitcast.33, bf16[4,64,7296]{2,1,0:T(8,128)(2,1)} %bitcast.34, ...), custom_call_target="tpu_custom_call" | custom-call | flops 131072 | bytes 256 | tf_op jit(solution)/shard_map/pallas_call | solution.py:158
  134.4 22.3 %collective-permute-done.6.refs_2_.refs_24_ = bf16[128,7168]{1,0:T(8,128)(2,1)} collective-permute-done((bf16[128,7168]{1,0:T(8,128)(2,1)S(1)}, bf16[128,7168]{1,0:T(8,128)(2,1)}, u32[]{:S(2)}, u32[]{:S(2)}) %collective-permute-start.6) | collective-permute-done | bytes 1835040 | tf_op jit(solution)/shard_map/ppermute | solution.py:25
  156.7 4.0 %collective-permute-done.9.refs_3_.refs_25_ = bf16[128,7168]{1,0:T(8,128)(2,1)S(1)} collective-permute-done((bf16[128,7168]{1,0:T(8,128)(2,1)}, bf16[128,7168]{1,0:T(8,128)(2,1)S(1)}, u32[]{:S(2)}, u32[]{:S(2)}) %collective-permute-start.9) | collective-permute-done | bytes 1835040 | tf_op jit(solution)/shard_map/ppermute | solution.py:25
  162.0 6.8 %shard_map.114 = (f32[64,7168]{1,0:T(8,128)}, bf16[64,7168]{1,0:T(8,128)(2,1)}, bf16[64,7168]{1,0:T(8,128)(2,1)}, bf16[64,7168]{1,0:T(8,128)(2,1)}) custom-call(bf16[256,512]{1,0:T(8,128)(2,1)} %shard_map.113.hidden_ref, bf16[128,7168]{1,0:T(8,128)(2,1)} %bitcast.46, bf16[128,7168]{1,0:T(8,128)(2,1)} %copy-done.3, ...), custom_call_target="tpu_custom_call" | custom-call | flops 131072 | bytes 256 | tf_op jit(solution)/shard_map/pallas_call | solution.py:185
  169.5 1.3 collective-permute-start.12
  171.8 4.7 %collective-permute-start.14 = (bf16[96,7168]{1,0:T(8,128)(2,1)}, bf16[96,7168]{1,0:T(8,128)(2,1)S(1)}, u32[]{:S(2)}, u32[]{:S(2)}) collective-permute-start(bf16[96,7168]{1,0:T(8,128)(2,1)} %collective-permute-done.7.refs_6_.refs_13_), channel_id=1, source_target_pairs={{2,3},{6,7},{10,11},{14,15},{18,19},{22,23},{26,27},{30,31}} | collective-permute-start | bytes 4128776 | tf_op jit(solution)/shard_map/ppermute | solution.py:294
  177.3 16.8 %collective-permute-done.12 = bf16[64,7168]{1,0:T(8,128)(2,1)S(1)} collective-permute-done((bf16[64,7168]{1,0:T(8,128)(2,1)}, bf16[64,7168]{1,0:T(8,128)(2,1)S(1)}, u32[]{:S(2)}, u32[]{:S(2)}) %collective-permute-start.12) | collective-permute-done | bytes 917536 | tf_op jit(solution)/shard_map/ppermute | solution.py:309
  194.0 2.6 fusion.1
  197.9 4.5 %collective-permute-start.13 = (bf16[64,7168]{1,0:T(8,128)(2,1)S(1)}, bf16[64,7168]{1,0:T(8,128)(2,1)S(1)}, u32[]{:S(2)}, u32[]{:S(2)}) collective-permute-start(bf16[64,7168]{1,0:T(8,128)(2,1)S(1)} %get-tuple-element.58), channel_id=1, source_target_pairs={{2,1},{3,2},{6,5},{7,6},{10,9},{11,10},{14,13},{15,14},{18,17},{19... | collective-permute-start | bytes 2752520 | tf_op jit(solution)/shard_map/ppermute | solution.py:309
  202.5 3.7 collective-permute-done.14.refs_7_.refs_14_
  206.2 4.3 %collective-permute-start.16 = (bf16[32,7168]{1,0:T(8,128)(2,1)S(1)}, bf16[32,7168]{1,0:T(8,128)(2,1)S(1)}, u32[]{:S(2)}, u32[]{:S(2)}) collective-permute-start(bf16[32,7168]{1,0:T(8,128)(2,1)S(1)} %pad_maximum_fusion.2.refs_4_.refs_11_), channel_id=1, source_target_pairs={{0,1},{1,2},{2,3},{4,5},{5,6},{6,7},{8,9},{9,10},{10,11},{12,13},{... | collective-permute-start | bytes 1376264 | tf_op jit(solution)/shard_map/ppermute | solution.py:294
  210.5 2.8 collective-permute-start.17
  213.3 21.1 %shard_map.115 = (f32[48,7168]{1,0:T(8,128)}, bf16[48,7168]{1,0:T(8,128)(2,1)}, bf16[48,7168]{1,0:T(8,128)(2,1)}, bf16[48,7168]{1,0:T(8,128)(2,1)}) custom-call(s32[2]{0:T(128)} %pad_add_fusion.at_ref, bf16[4,64,7296]{2,1,0:T(8,128)(2,1)} %bitcast.38, bf16[4,64,7296]{2,1,0:T(8,128)(2,1)} %bitcast.39, bf16[4,64,7296]{2,1,0:T(8,128)(2,1)} %bitcast.40, ...), custom_call_target="tpu_custom_call" | custom-call | flops 98304 | bytes 192 | tf_op jit(solution)/shard_map/pallas_call | solution.py:263
  234.5 3.2 collective-permute-start.22
  237.7 2.8 collective-permute-start.24
  240.7 1.9 collective-permute-start.19
  242.7 5.0 %collective-permute-done.22.refs_6_.refs_13_ = bf16[32,7168]{1,0:T(8,128)(2,1)S(1)} collective-permute-done((bf16[32,7168]{1,0:T(8,128)(2,1)S(1)}, bf16[32,7168]{1,0:T(8,128)(2,1)S(1)}, u32[]{:S(2)}, u32[]{:S(2)}) %collective-permute-start.22) | collective-permute-done | bytes 458784 | tf_op jit(solution)/shard_map/ppermute | solution.py:294
  247.6 2.8 collective-permute-start.23
  250.7 1.9 collective-permute-start.18
  252.6 1.6 collective-permute-start.20
  255.6 5.8 %collective-permute-done.23.refs_7_.refs_14_ = bf16[32,7168]{1,0:T(8,128)(2,1)S(1)} collective-permute-done((bf16[32,7168]{1,0:T(8,128)(2,1)S(1)}, bf16[32,7168]{1,0:T(8,128)(2,1)S(1)}, u32[]{:S(2)}, u32[]{:S(2)}) %collective-permute-start.23) | collective-permute-done | bytes 458784 | tf_op jit(solution)/shard_map/ppermute | solution.py:294
  262.9 18.8 %shard_map.116 = (f32[16,7168]{1,0:T(8,128)}, bf16[16,7168]{1,0:T(8,128)(2,1)}, bf16[16,7168]{1,0:T(8,128)(2,1)}, bf16[16,7168]{1,0:T(8,128)(2,1)}) custom-call(s32[2]{0:T(128)} %pad_add_fusion.at_ref, bf16[4,64,7296]{2,1,0:T(8,128)(2,1)} %bitcast.42, bf16[4,64,7296]{2,1,0:T(8,128)(2,1)} %bitcast.43, bf16[4,64,7296]{2,1,0:T(8,128)(2,1)} %bitcast.44, ...), custom_call_target="tpu_custom_call" | custom-call | flops 32768 | bytes 64 | tf_op jit(solution)/shard_map/pallas_call | solution.py:263
  282.6 1.5 collective-permute-start.35
  284.1 1.4 fusion.4
  285.5 1.3 collective-permute-start.27
  286.8 19.1 %collective-permute-start.28 = (bf16[48,7168]{1,0:T(8,128)(2,1)S(1)}, bf16[48,7168]{1,0:T(8,128)(2,1)S(1)}, u32[]{:S(2)}, u32[]{:S(2)}) collective-permute-start(bf16[48,7168]{1,0:T(8,128)(2,1)S(1)} %get-tuple-element.60), channel_id=1, source_target_pairs={{2,1},{3,2},{6,5},{7,6},{10,9},{11,10},{14,13},{15,14},{18,17},{19... | collective-permute-start | bytes 2064392 | tf_op jit(solution)/shard_map/ppermute | solution.py:309
  307.2 3.5 collective-permute-start.36
  310.8 1.4 collective-permute-start.33
  312.2 7.6 %collective-permute-done.27 = bf16[48,7168]{1,0:T(8,128)(2,1)S(1)} collective-permute-done((bf16[48,7168]{1,0:T(8,128)(2,1)S(1)}, bf16[48,7168]{1,0:T(8,128)(2,1)S(1)}, u32[]{:S(2)}, u32[]{:S(2)}) %collective-permute-start.27) | collective-permute-done | bytes 688160 | tf_op jit(solution)/shard_map/ppermute | solution.py:308
  321.0 5.3 %collective-permute-done.26 = bf16[64,7168]{1,0:T(8,128)(2,1)S(1)} collective-permute-done((bf16[64,7168]{1,0:T(8,128)(2,1)S(1)}, bf16[64,7168]{1,0:T(8,128)(2,1)S(1)}, u32[]{:S(2)}, u32[]{:S(2)}) %collective-permute-start.26) | collective-permute-done | bytes 917536 | tf_op jit(solution)/shard_map/ppermute | solution.py:30
  327.6 2.1 collective-permute-start.29
  330.9 3.9 %collective-permute-start.30 = (bf16[48,7168]{1,0:T(8,128)(2,1)S(1)}, bf16[48,7168]{1,0:T(8,128)(2,1)S(1)}, u32[]{:S(2)}, u32[]{:S(2)}) collective-permute-start(bf16[48,7168]{1,0:T(8,128)(2,1)S(1)} %add_convert_fusion.3), channel_id=1, source_target_pairs={{1,0},{2,1},{3,2},{5,4},{6,5},{7,6},{9,8},{10,9},{11,10},{13,12},{... | collective-permute-start | bytes 2064392 | tf_op jit(solution)/shard_map/ppermute | solution.py:309
  335.0 1.9 collective-permute-start.37
  336.9 6.7 %collective-permute-done.29 = bf16[48,7168]{1,0:T(8,128)(2,1)S(1)} collective-permute-done((bf16[48,7168]{1,0:T(8,128)(2,1)S(1)}, bf16[48,7168]{1,0:T(8,128)(2,1)S(1)}, u32[]{:S(2)}, u32[]{:S(2)}) %collective-permute-start.29) | collective-permute-done | bytes 688160 | tf_op jit(solution)/shard_map/ppermute | solution.py:308
  343.6 5.7 %collective-permute-done.30 = bf16[48,7168]{1,0:T(8,128)(2,1)S(1)} collective-permute-done((bf16[48,7168]{1,0:T(8,128)(2,1)S(1)}, bf16[48,7168]{1,0:T(8,128)(2,1)S(1)}, u32[]{:S(2)}, u32[]{:S(2)}) %collective-permute-start.30) | collective-permute-done | bytes 688160 | tf_op jit(solution)/shard_map/ppermute | solution.py:309
  350.2 1.9 collective-permute-start.34
  352.2 6.0 %collective-permute-done.34 = bf16[16,7168]{1,0:T(8,128)(2,1)S(1)} collective-permute-done((bf16[16,7168]{1,0:T(8,128)(2,1)S(1)}, bf16[16,7168]{1,0:T(8,128)(2,1)S(1)}, u32[]{:S(2)}, u32[]{:S(2)}) %collective-permute-start.34) | collective-permute-done | bytes 229408 | tf_op jit(solution)/shard_map/ppermute | solution.py:308
  358.1 4.8 %collective-permute-done.31 = bf16[48,7168]{1,0:T(8,128)(2,1)S(1)} collective-permute-done((bf16[48,7168]{1,0:T(8,128)(2,1)S(1)}, bf16[48,7168]{1,0:T(8,128)(2,1)S(1)}, u32[]{:S(2)}, u32[]{:S(2)}) %collective-permute-start.31) | collective-permute-done | bytes 688160 | tf_op jit(solution)/shard_map/ppermute | solution.py:30
  363.7 5.4 %collective-permute-done.38 = bf16[16,7168]{1,0:T(8,128)(2,1)S(1)} collective-permute-done((bf16[16,7168]{1,0:T(8,128)(2,1)S(1)}, bf16[16,7168]{1,0:T(8,128)(2,1)S(1)}, u32[]{:S(2)}, u32[]{:S(2)}) %collective-permute-start.38) | collective-permute-done | bytes 229408 | tf_op jit(solution)/shard_map/ppermute | solution.py:30
  (132 shorter events, 25.0 us)
Async XLA Ops:
  7.2 107.0 %all-gather.3.cloned.1.call-start = ((), (), s32[]{:S(2)}) async-start(), calls=%async_computation | async-start | bytes 4669440 | tf_op jit(solution)/shard_map/all_gather | solution.py:351
  13.4 97.3 %collective-permute-start = (bf16[2,7168,128]{2,1,0:T(8,128)(2,1)S(1)}, bf16[2,7168,128]{2,1,0:T(8,128)(2,1)S(1)}, u32[]{:S(2)}, u32[]{:S(2)}) collective-permute-start(bf16[2,7168,128]{2,1,0:T(8,128)(2,1)S(1)} %pad_maximum_fusion.refs_8_.refs_18_), channel_id=1, source_target_pairs={{0,4},{4,0},{8,12},{12,8},{1,5},{5,1},{9,13},{13,9},{2,6},{6,2},{1... | collective-permute-start | bytes 11010056 | tf_op jit(solution)/shard_map/ppermute | solution.py:25
  13.4 100.7 %collective-permute-start.1 = (bf16[2,7168,128]{2,1,0:T(8,128)(2,1)S(1)}, bf16[2,7168,128]{2,1,0:T(8,128)(2,1)}, u32[]{:S(2)}, u32[]{:S(2)}) collective-permute-start(bf16[2,7168,128]{2,1,0:T(8,128)(2,1)S(1)} %pad_maximum_fusion.refs_8_.refs_18_), channel_id=1, source_target_pairs={{0,8},{4,12},{8,0},{12,4},{1,9},{5,13},{9,1},{13,5},{2,10},{6,14},... | collective-permute-start | bytes 11010056 | tf_op jit(solution)/shard_map/ppermute | solution.py:25
  15.0 95.6 %collective-permute-start.4 = (bf16[128,7168]{1,0:T(8,128)(2,1)S(1)}, bf16[128,7168]{1,0:T(8,128)(2,1)S(1)}, u32[]{:S(2)}, u32[]{:S(2)}) collective-permute-start(bf16[128,7168]{1,0:T(8,128)(2,1)S(1)} %bitcast.49), channel_id=1, source_target_pairs={{0,4},{4,0},{8,12},{12,8},{1,5},{5,1},{9,13},{13,9},{2,6},{6,2},{1... | collective-permute-start | bytes 5505032 | tf_op jit(solution)/shard_map/ppermute | solution.py:25
  16.5 117.9 %copy-start.5 = (bf16[96,7168]{1,0:T(8,128)(2,1)}, bf16[96,7168]{1,0:T(8,128)(2,1)S(1)}, u32[]{:S(2)}) copy-start(bf16[96,7168]{1,0:T(8,128)(2,1)S(1)} %pad_maximum_fusion.1.refs_4_.refs_11_) | copy-start | bytes 4128772
  16.5 93.6 %collective-permute-start.2 = (bf16[96,7168]{1,0:T(8,128)(2,1)S(1)}, bf16[96,7168]{1,0:T(8,128)(2,1)S(1)}, u32[]{:S(2)}, u32[]{:S(2)}) collective-permute-start(bf16[96,7168]{1,0:T(8,128)(2,1)S(1)} %pad_maximum_fusion.1.refs_4_.refs_11_), channel_id=1, source_target_pairs={{0,1},{1,2},{2,3},{4,5},{5,6},{6,7},{8,9},{9,10},{10,11},{12,13},{... | collective-permute-start | bytes 4128776 | tf_op jit(solution)/shard_map/ppermute | solution.py:294
  20.0 90.6 %collective-permute-start.3 = (bf16[96,7168]{1,0:T(8,128)(2,1)S(1)}, bf16[96,7168]{1,0:T(8,128)(2,1)S(1)}, u32[]{:S(2)}, u32[]{:S(2)}) collective-permute-start(bf16[96,7168]{1,0:T(8,128)(2,1)S(1)} %pad_maximum_fusion.1.refs_4_.refs_11_), channel_id=1, source_target_pairs={{1,0},{2,1},{3,2},{5,4},{6,5},{7,6},{9,8},{10,9},{11,10},{13,12},{... | collective-permute-start | bytes 4128776 | tf_op jit(solution)/shard_map/ppermute | solution.py:294
  114.2 10.0 %collective-permute-start.5 = (bf16[2,7168,128]{2,1,0:T(8,128)(2,1)}, bf16[2,7168,128]{2,1,0:T(8,128)(2,1)}, u32[]{:S(2)}, u32[]{:S(2)}) collective-permute-start(bf16[2,7168,128]{2,1,0:T(8,128)(2,1)} %collective-permute-done.1.refs_10_.refs_20_), channel_id=1, source_target_pairs={{0,4},{4,0},{8,12},{12,8},{1,5},{5,1},{9,13},{13,9},{2,6},{6,2},{1... | collective-permute-start | bytes 11010056 | tf_op jit(solution)/shard_map/ppermute | solution.py:25
  114.3 42.4 %collective-permute-start.6 = (bf16[128,7168]{1,0:T(8,128)(2,1)S(1)}, bf16[128,7168]{1,0:T(8,128)(2,1)}, u32[]{:S(2)}, u32[]{:S(2)}) collective-permute-start(bf16[128,7168]{1,0:T(8,128)(2,1)S(1)} %bitcast.50), channel_id=1, source_target_pairs={{0,8},{4,12},{8,0},{12,4},{1,9},{5,13},{9,1},{13,5},{2,10},{6,14},... | collective-permute-start | bytes 5505032 | tf_op jit(solution)/shard_map/ppermute | solution.py:25
  115.5 41.2 %collective-permute-start.7 = (bf16[96,7168]{1,0:T(8,128)(2,1)}, bf16[96,7168]{1,0:T(8,128)(2,1)}, u32[]{:S(2)}, u32[]{:S(2)}) collective-permute-start(bf16[96,7168]{1,0:T(8,128)(2,1)} %copy-done.6), channel_id=1, source_target_pairs={{1,2},{2,3},{5,6},{6,7},{9,10},{10,11},{13,14},{14,15},{17,18},{18... | collective-permute-start | bytes 4128776 | tf_op jit(solution)/shard_map/ppermute | solution.py:294
  117.4 39.3 %collective-permute-start.8 = (bf16[96,7168]{1,0:T(8,128)(2,1)}, bf16[96,7168]{1,0:T(8,128)(2,1)}, u32[]{:S(2)}, u32[]{:S(2)}) collective-permute-start(bf16[96,7168]{1,0:T(8,128)(2,1)} %copy-done.7), channel_id=1, source_target_pairs={{1,0},{2,1},{5,4},{6,5},{9,8},{10,9},{13,12},{14,13},{17,16},{18,1... | collective-permute-start | bytes 4128776 | tf_op jit(solution)/shard_map/ppermute | solution.py:294
  156.7 4.0 %collective-permute-start.9 = (bf16[128,7168]{1,0:T(8,128)(2,1)}, bf16[128,7168]{1,0:T(8,128)(2,1)S(1)}, u32[]{:S(2)}, u32[]{:S(2)}) collective-permute-start(bf16[128,7168]{1,0:T(8,128)(2,1)} %collective-permute-done.6.refs_2_.refs_24_), channel_id=1, source_target_pairs={{0,4},{4,0},{8,12},{12,8},{1,5},{5,1},{9,13},{13,9},{2,6},{6,2},{1... | collective-permute-start | bytes 5505032 | tf_op jit(solution)/shard_map/ppermute | solution.py:25
  168.8 8.4 %collective-permute-start.10 = (bf16[64,7168]{1,0:T(8,128)(2,1)}, bf16[64,7168]{1,0:T(8,128)(2,1)S(1)}, u32[]{:S(2)}, u32[]{:S(2)}) collective-permute-start(bf16[64,7168]{1,0:T(8,128)(2,1)} %get-tuple-element.35), channel_id=1, source_target_pairs={{0,1},{4,5},{8,9},{12,13},{16,17},{20,21},{24,25},{28,29}} | collective-permute-start | bytes 2752520 | tf_op jit(solution)/shard_map/ppermute | solution.py:308
  169.5 24.5 %collective-permute-start.12 = (bf16[64,7168]{1,0:T(8,128)(2,1)}, bf16[64,7168]{1,0:T(8,128)(2,1)S(1)}, u32[]{:S(2)}, u32[]{:S(2)}) collective-permute-start(bf16[64,7168]{1,0:T(8,128)(2,1)} %get-tuple-element.33), channel_id=1, source_target_pairs={{3,2},{7,6},{11,10},{15,14},{19,18},{23,22},{27,26},{31,30}} | collective-permute-start | bytes 2752520 | tf_op jit(solution)/shard_map/ppermute | solution.py:309
  171.8 34.4 %collective-permute-start.14 = (bf16[96,7168]{1,0:T(8,128)(2,1)}, bf16[96,7168]{1,0:T(8,128)(2,1)S(1)}, u32[]{:S(2)}, u32[]{:S(2)}) collective-permute-start(bf16[96,7168]{1,0:T(8,128)(2,1)} %collective-permute-done.7.refs_6_.refs_13_), channel_id=1, source_target_pairs={{2,3},{6,7},{10,11},{14,15},{18,19},{22,23},{26,27},{30,31}} | collective-permute-start | bytes 4128776 | tf_op jit(solution)/shard_map/ppermute | solution.py:294
  176.5 29.7 %collective-permute-start.15 = (bf16[96,7168]{1,0:T(8,128)(2,1)}, bf16[96,7168]{1,0:T(8,128)(2,1)S(1)}, u32[]{:S(2)}, u32[]{:S(2)}) collective-permute-start(bf16[96,7168]{1,0:T(8,128)(2,1)} %collective-permute-done.8.refs_9_.refs_16_), channel_id=1, source_target_pairs={{1,0},{5,4},{9,8},{13,12},{17,16},{21,20},{25,24},{29,28}} | collective-permute-start | bytes 4128776 | tf_op jit(solution)/shard_map/ppermute | solution.py:294
  196.6 37.9 %collective-permute-start.11 = (bf16[64,7168]{1,0:T(8,128)(2,1)}, bf16[64,7168]{1,0:T(8,128)(2,1)S(1)}, u32[]{:S(2)}, u32[]{:S(2)}) collective-permute-start(bf16[64,7168]{1,0:T(8,128)(2,1)} %get-tuple-element.59), channel_id=1, source_target_pairs={{0,1},{1,2},{4,5},{5,6},{8,9},{9,10},{12,13},{13,14},{16,17},{17,1... | collective-permute-start | bytes 2752520 | tf_op jit(solution)/shard_map/ppermute | solution.py:308
  197.9 36.6 %collective-permute-start.13 = (bf16[64,7168]{1,0:T(8,128)(2,1)S(1)}, bf16[64,7168]{1,0:T(8,128)(2,1)S(1)}, u32[]{:S(2)}, u32[]{:S(2)}) collective-permute-start(bf16[64,7168]{1,0:T(8,128)(2,1)S(1)} %get-tuple-element.58), channel_id=1, source_target_pairs={{2,1},{3,2},{6,5},{7,6},{10,9},{11,10},{14,13},{15,14},{18,17},{19... | collective-permute-start | bytes 2752520 | tf_op jit(solution)/shard_map/ppermute | solution.py:309
  202.5 31.9 %copy-start.10 = (bf16[32,7168]{1,0:T(8,128)(2,1)}, bf16[32,7168]{1,0:T(8,128)(2,1)S(1)}, u32[]{:S(2)}) copy-start(bf16[32,7168]{1,0:T(8,128)(2,1)S(1)} %pad_maximum_fusion.2.refs_4_.refs_11_) | copy-start | bytes 1376260
  202.5 38.0 %copy-start.25 = (bf16[64,7168]{1,0:T(8,128)(2,1)S(1)}, bf16[64,7168]{1,0:T(8,128)(2,1)}, u32[]{:S(2)}) copy-start(bf16[64,7168]{1,0:T(8,128)(2,1)} %get-tuple-element.35) | copy-start | bytes 2752516
  206.2 28.2 %collective-permute-start.16 = (bf16[32,7168]{1,0:T(8,128)(2,1)S(1)}, bf16[32,7168]{1,0:T(8,128)(2,1)S(1)}, u32[]{:S(2)}, u32[]{:S(2)}) collective-permute-start(bf16[32,7168]{1,0:T(8,128)(2,1)S(1)} %pad_maximum_fusion.2.refs_4_.refs_11_), channel_id=1, source_target_pairs={{0,1},{1,2},{2,3},{4,5},{5,6},{6,7},{8,9},{9,10},{10,11},{12,13},{... | collective-permute-start | bytes 1376264 | tf_op jit(solution)/shard_map/ppermute | solution.py:294
  210.5 24.0 %collective-permute-start.17 = (bf16[32,7168]{1,0:T(8,128)(2,1)S(1)}, bf16[32,7168]{1,0:T(8,128)(2,1)S(1)}, u32[]{:S(2)}, u32[]{:S(2)}) collective-permute-start(bf16[32,7168]{1,0:T(8,128)(2,1)S(1)} %pad_maximum_fusion.2.refs_4_.refs_11_), channel_id=1, source_target_pairs={{1,0},{2,1},{3,2},{5,4},{6,5},{7,6},{9,8},{10,9},{11,10},{13,12},{... | collective-permute-start | bytes 1376264 | tf_op jit(solution)/shard_map/ppermute | solution.py:294
  234.5 13.1 %collective-permute-start.22 = (bf16[32,7168]{1,0:T(8,128)(2,1)S(1)}, bf16[32,7168]{1,0:T(8,128)(2,1)S(1)}, u32[]{:S(2)}, u32[]{:S(2)}) collective-permute-start(bf16[32,7168]{1,0:T(8,128)(2,1)S(1)} %collective-permute-done.16.refs_5_.refs_12_), channel_id=1, source_target_pairs={{1,2},{2,3},{5,6},{6,7},{9,10},{10,11},{13,14},{14,15},{17,18},{18... | collective-permute-start | bytes 1376264 | tf_op jit(solution)/shard_map/ppermute | solution.py:294
  237.7 16.6 %collective-permute-start.24 = (bf16[32,7168]{1,0:T(8,128)(2,1)S(1)}, bf16[32,7168]{1,0:T(8,128)(2,1)S(1)}, u32[]{:S(2)}, u32[]{:S(2)}) collective-permute-start(bf16[32,7168]{1,0:T(8,128)(2,1)S(1)} %collective-permute-done.17.refs_8_.refs_15_), channel_id=1, source_target_pairs={{1,0},{2,1},{5,4},{6,5},{9,8},{10,9},{13,12},{14,13},{17,16},{18,1... | collective-permute-start | bytes 1376264 | tf_op jit(solution)/shard_map/ppermute | solution.py:294
  240.7 43.3 %collective-permute-start.19 = (bf16[64,7168]{1,0:T(8,128)(2,1)S(1)}, bf16[64,7168]{1,0:T(8,128)(2,1)S(1)}, u32[]{:S(2)}, u32[]{:S(2)}) collective-permute-start(bf16[64,7168]{1,0:T(8,128)(2,1)S(1)} %add_convert_fusion.1), channel_id=1, source_target_pairs={{1,0},{2,1},{3,2},{5,4},{6,5},{7,6},{9,8},{10,9},{11,10},{13,12},{... | collective-permute-start | bytes 2752520 | tf_op jit(solution)/shard_map/ppermute | solution.py:309
  247.6 13.8 %collective-permute-start.23 = (bf16[32,7168]{1,0:T(8,128)(2,1)S(1)}, bf16[32,7168]{1,0:T(8,128)(2,1)S(1)}, u32[]{:S(2)}, u32[]{:S(2)}) collective-permute-start(bf16[32,7168]{1,0:T(8,128)(2,1)S(1)} %collective-permute-done.22.refs_6_.refs_13_), channel_id=1, source_target_pairs={{2,3},{6,7},{10,11},{14,15},{18,19},{22,23},{26,27},{30,31}} | collective-permute-start | bytes 1376264 | tf_op jit(solution)/shard_map/ppermute | solution.py:294
  250.7 33.4 %collective-permute-start.18 = (bf16[64,7168]{1,0:T(8,128)(2,1)S(1)}, bf16[64,7168]{1,0:T(8,128)(2,1)S(1)}, u32[]{:S(2)}, u32[]{:S(2)}) collective-permute-start(bf16[64,7168]{1,0:T(8,128)(2,1)S(1)} %add_convert_fusion.2), channel_id=1, source_target_pairs={{0,1},{1,2},{2,3},{4,5},{5,6},{6,7},{8,9},{9,10},{10,11},{12,13},{... | collective-permute-start | bytes 2752520 | tf_op jit(solution)/shard_map/ppermute | solution.py:308
  252.6 31.5 %copy-start.26 = (bf16[48,7168]{1,0:T(8,128)(2,1)S(1)}, bf16[48,7168]{1,0:T(8,128)(2,1)}, u32[]{:S(2)}) copy-start(bf16[48,7168]{1,0:T(8,128)(2,1)} %get-tuple-element.48) | copy-start | bytes 2064388
  252.6 29.9 %collective-permute-start.20 = (bf16[48,7168]{1,0:T(8,128)(2,1)}, bf16[48,7168]{1,0:T(8,128)(2,1)}, u32[]{:S(2)}, u32[]{:S(2)}) collective-permute-start(bf16[48,7168]{1,0:T(8,128)(2,1)} %get-tuple-element.41), channel_id=1, source_target_pairs={{0,1},{4,5},{8,9},{12,13},{16,17},{20,21},{24,25},{28,29}} | collective-permute-start | bytes 2064392 | tf_op jit(solution)/shard_map/ppermute | solution.py:308
  254.3 29.8 %collective-permute-start.21 = (bf16[48,7168]{1,0:T(8,128)(2,1)}, bf16[48,7168]{1,0:T(8,128)(2,1)S(1)}, u32[]{:S(2)}, u32[]{:S(2)}) collective-permute-start(bf16[48,7168]{1,0:T(8,128)(2,1)} %get-tuple-element.38), channel_id=1, source_target_pairs={{3,2},{7,6},{11,10},{15,14},{19,18},{23,22},{27,26},{31,30}} | collective-permute-start | bytes 2064392 | tf_op jit(solution)/shard_map/ppermute | solution.py:309
  261.4 0.7 collective-permute-start.25
  281.7 24.2 %copy-start.12 = (bf16[1,64,7168]{2,1,0:T(8,128)(2,1)S(1)}, bf16[1,64,7168]{2,1,0:T(8,128)(2,1)}, u32[]{:S(2)}) copy-start(bf16[1,64,7168]{2,1,0:T(8,128)(2,1)} %param.10) | copy-start | bytes 2752516
  281.8 24.2 %copy-start.21 = (f32[64,7168]{1,0:T(8,128)S(1)}, f32[64,7168]{1,0:T(8,128)}, u32[]{:S(2)}) copy-start(f32[64,7168]{1,0:T(8,128)} %get-tuple-element.32) | copy-start | bytes 5505028
  281.8 24.2 %copy-start.31 = (f32[1,64]{1,0:T(1,128)S(1)}, f32[1,64]{1,0:T(1,128)}, u32[]{:S(2)}) copy-start(f32[1,64]{1,0:T(1,128)} %param.12) | copy-start | bytes 772
  281.8 25.3 %collective-permute-start.32 = (bf16[16,7168]{1,0:T(8,128)(2,1)}, bf16[16,7168]{1,0:T(8,128)(2,1)S(1)}, u32[]{:S(2)}, u32[]{:S(2)}) collective-permute-start(bf16[16,7168]{1,0:T(8,128)(2,1)} %get-tuple-element.55), channel_id=1, source_target_pairs={{0,1},{4,5},{8,9},{12,13},{16,17},{20,21},{24,25},{28,29}} | collective-permute-start | bytes 688136 | tf_op jit(solution)/shard_map/ppermute | solution.py:308
  282.6 24.5 %collective-permute-start.35 = (bf16[16,7168]{1,0:T(8,128)(2,1)}, bf16[16,7168]{1,0:T(8,128)(2,1)S(1)}, u32[]{:S(2)}, u32[]{:S(2)}) collective-permute-start(bf16[16,7168]{1,0:T(8,128)(2,1)} %get-tuple-element.44), channel_id=1, source_target_pairs={{3,2},{7,6},{11,10},{15,14},{19,18},{23,22},{27,26},{31,30}} | collective-permute-start | bytes 688136 | tf_op jit(solution)/shard_map/ppermute | solution.py:309
  285.5 34.3 %collective-permute-start.27 = (bf16[48,7168]{1,0:T(8,128)(2,1)S(1)}, bf16[48,7168]{1,0:T(8,128)(2,1)S(1)}, u32[]{:S(2)}, u32[]{:S(2)}) collective-permute-start(bf16[48,7168]{1,0:T(8,128)(2,1)S(1)} %get-tuple-element.61), channel_id=1, source_target_pairs={{0,1},{1,2},{4,5},{5,6},{8,9},{9,10},{12,13},{13,14},{16,17},{17,1... | collective-permute-start | bytes 2064392 | tf_op jit(solution)/shard_map/ppermute | solution.py:308
  286.8 34.2 %collective-permute-start.28 = (bf16[48,7168]{1,0:T(8,128)(2,1)S(1)}, bf16[48,7168]{1,0:T(8,128)(2,1)S(1)}, u32[]{:S(2)}, u32[]{:S(2)}) collective-permute-start(bf16[48,7168]{1,0:T(8,128)(2,1)S(1)} %get-tuple-element.60), channel_id=1, source_target_pairs={{2,1},{3,2},{6,5},{7,6},{10,9},{11,10},{14,13},{15,14},{18,17},{19... | collective-permute-start | bytes 2064392 | tf_op jit(solution)/shard_map/ppermute | solution.py:309
  306.5 19.8 %collective-permute-start.26 = (bf16[64,7168]{1,0:T(8,128)(2,1)S(1)}, bf16[64,7168]{1,0:T(8,128)(2,1)S(1)}, u32[]{:S(2)}, u32[]{:S(2)}) collective-permute-start(bf16[64,7168]{1,0:T(8,128)(2,1)S(1)} %add_convert_fusion), channel_id=1, source_target_pairs={{16,0},{0,16},{17,1},{1,17},{18,2},{2,18},{19,3},{3,19},{20,4},{4,... | collective-permute-start | bytes 2752520 | tf_op jit(solution)/shard_map/ppermute | solution.py:30
  307.2 27.6 %collective-permute-start.36 = (bf16[16,7168]{1,0:T(8,128)(2,1)S(1)}, bf16[16,7168]{1,0:T(8,128)(2,1)S(1)}, u32[]{:S(2)}, u32[]{:S(2)}) collective-permute-start(bf16[16,7168]{1,0:T(8,128)(2,1)S(1)} %get-tuple-element.62), channel_id=1, source_target_pairs={{2,1},{3,2},{6,5},{7,6},{10,9},{11,10},{14,13},{15,14},{18,17},{19... | collective-permute-start | bytes 688136 | tf_op jit(solution)/shard_map/ppermute | solution.py:309
  310.8 24.1 %copy-start.29 = (bf16[16,7168]{1,0:T(8,128)(2,1)S(1)}, bf16[16,7168]{1,0:T(8,128)(2,1)}, u32[]{:S(2)}) copy-start(bf16[16,7168]{1,0:T(8,128)(2,1)} %get-tuple-element.55) | copy-start | bytes 688132
  310.8 39.4 %collective-permute-start.33 = (bf16[16,7168]{1,0:T(8,128)(2,1)S(1)}, bf16[16,7168]{1,0:T(8,128)(2,1)S(1)}, u32[]{:S(2)}, u32[]{:S(2)}) collective-permute-start(bf16[16,7168]{1,0:T(8,128)(2,1)S(1)} %get-tuple-element.63), channel_id=1, source_target_pairs={{0,1},{1,2},{4,5},{5,6},{8,9},{9,10},{12,13},{13,14},{16,17},{17,1... | collective-permute-start | bytes 688136 | tf_op jit(solution)/shard_map/ppermute | solution.py:308
  327.6 15.9 %collective-permute-start.29 = (bf16[48,7168]{1,0:T(8,128)(2,1)S(1)}, bf16[48,7168]{1,0:T(8,128)(2,1)S(1)}, u32[]{:S(2)}, u32[]{:S(2)}) collective-permute-start(bf16[48,7168]{1,0:T(8,128)(2,1)S(1)} %add_convert_fusion.4), channel_id=1, source_target_pairs={{0,1},{1,2},{2,3},{4,5},{5,6},{6,7},{8,9},{9,10},{10,11},{12,13},{... | collective-permute-start | bytes 2064392 | tf_op jit(solution)/shard_map/ppermute | solution.py:308
  330.9 18.3 %collective-permute-start.30 = (bf16[48,7168]{1,0:T(8,128)(2,1)S(1)}, bf16[48,7168]{1,0:T(8,128)(2,1)S(1)}, u32[]{:S(2)}, u32[]{:S(2)}) collective-permute-start(bf16[48,7168]{1,0:T(8,128)(2,1)S(1)} %add_convert_fusion.3), channel_id=1, source_target_pairs={{1,0},{2,1},{3,2},{5,4},{6,5},{7,6},{9,8},{10,9},{11,10},{13,12},{... | collective-permute-start | bytes 2064392 | tf_op jit(solution)/shard_map/ppermute | solution.py:309
  335.0 17.2 %collective-permute-start.37 = (bf16[16,7168]{1,0:T(8,128)(2,1)S(1)}, bf16[16,7168]{1,0:T(8,128)(2,1)S(1)}, u32[]{:S(2)}, u32[]{:S(2)}) collective-permute-start(bf16[16,7168]{1,0:T(8,128)(2,1)S(1)} %add_convert_fusion.5), channel_id=1, source_target_pairs={{1,0},{2,1},{3,2},{5,4},{6,5},{7,6},{9,8},{10,9},{11,10},{13,12},{... | collective-permute-start | bytes 688136 | tf_op jit(solution)/shard_map/ppermute | solution.py:309
  349.5 13.5 %collective-permute-start.31 = (bf16[48,7168]{1,0:T(8,128)(2,1)S(1)}, bf16[48,7168]{1,0:T(8,128)(2,1)S(1)}, u32[]{:S(2)}, u32[]{:S(2)}) collective-permute-start(bf16[48,7168]{1,0:T(8,128)(2,1)S(1)} %fusion.5), channel_id=1, source_target_pairs={{16,0},{0,16},{17,1},{1,17},{18,2},{2,18},{19,3},{3,19},{20,4},{4,... | collective-permute-start | bytes 2064392 | tf_op jit(solution)/shard_map/ppermute | solution.py:30
  350.2 7.9 %collective-permute-start.34 = (bf16[16,7168]{1,0:T(8,128)(2,1)S(1)}, bf16[16,7168]{1,0:T(8,128)(2,1)S(1)}, u32[]{:S(2)}, u32[]{:S(2)}) collective-permute-start(bf16[16,7168]{1,0:T(8,128)(2,1)S(1)} %add_convert_fusion.6), channel_id=1, source_target_pairs={{0,1},{1,2},{2,3},{4,5},{5,6},{6,7},{8,9},{9,10},{10,11},{12,13},{... | collective-permute-start | bytes 688136 | tf_op jit(solution)/shard_map/ppermute | solution.py:308
  363.1 6.1 %collective-permute-start.38 = (bf16[16,7168]{1,0:T(8,128)(2,1)S(1)}, bf16[16,7168]{1,0:T(8,128)(2,1)S(1)}, u32[]{:S(2)}, u32[]{:S(2)}) collective-permute-start(bf16[16,7168]{1,0:T(8,128)(2,1)S(1)} %fusion.8), channel_id=1, source_target_pairs={{16,0},{0,16},{17,1},{1,17},{18,2},{2,18},{19,3},{3,19},{20,4},{4,... | collective-permute-start | bytes 688136 | tf_op jit(solution)/shard_map/ppermute | solution.py:30
  (26 other events, 181.1 us)
Sparse Core Ops, SparseCore 0:
  10.9 102.0 all-gather.2

commit v8 on v7

--- a/solution.py
+++ b/solution.py
@@ -10,7 +10,7 @@
 
 BF16, F32 = jnp.bfloat16, jnp.float32
 VMEM_LIMIT = 56 * 1024 * 1024
-LEAD_ROWS = 16
+ROW_PARTS = 2
 TAG_COLUMNS = 128
 
 
@@ -124,9 +124,9 @@
     return pl.CostEstimate(flops=many * hidden, bytes_accessed=many, transcendentals=0)
 
 
-def home_shapes(count, rows, width):
-    own, others = (jax.ShapeDtypeStruct((rows, width), kind) for kind in (F32, BF16))
-    return [own] + [others] * (count - 1)
+def home_shapes(count, rows, width, parts=1):
+    own, others = (jax.ShapeDtypeStruct((rows // parts, width), kind) for kind in (F32, BF16))
+    return [own] * parts + [others] * (parts * (count - 1))
 
 
 def hidden_kernel(count, pieces, steps, at_ref, *refs):
@@ -250,14 +250,14 @@
         put_blocks(outs, total)
 
 
-def backward_call(at, x_gathered, begin, rows, hops, gate_ups, downs):
+def backward_call(at, x_gathered, rows, parts, hops, gate_ups, downs):
     count, width = x_gathered.shape[0], hops[0][0].shape[1]
     pieces, hid = len(downs), downs[0].shape[0]
     chunk = chunk_of(width, 1792)
     steps, hidden, many = width // chunk, pieces * hid, count * rows
     first = lambda i: jnp.minimum(i, steps - 1)
     second = lambda i: jnp.maximum(i - steps, 0)
-    _, tags, tag_specs = gathered_input(x_gathered, begin, rows)
+    _, tags, tag_specs = gathered_input(x_gathered, 0, rows)
     _, rows_in, row_specs = chained_input(hops, 0, rows)
     _, _, scaled_specs = chained_input(hops, rows, rows)
     return pl.pallas_call(
@@ -268,7 +268,8 @@
             in_specs=[spec(TAG_COLUMNS, lambda i: width // TAG_COLUMNS) for spec in tag_specs]
             + [spec(chunk, first) for spec in row_specs + scaled_specs]
             + [pl.BlockSpec(memory_space=pl.ANY)] * (2 * pieces),
-            out_specs=[pl.BlockSpec((rows, chunk), lambda i, at: (0, second(i)))] * count,
+            out_specs=[pl.BlockSpec((rows // parts, chunk), lambda i, at: (0, second(i)))]
+            * (parts * count),
             scratch_shapes=[pltpu.VMEM((many, hidden), F32)] * 3
             + [pltpu.VMEM((many, hidden), BF16)] * 2
             + [
@@ -277,7 +278,7 @@
                 pltpu.SemaphoreType.DMA((2, steps, pieces)),
             ],
         ),
-        out_shape=home_shapes(count, rows, width),
+        out_shape=home_shapes(count, rows, width, parts),
         compiler_params=compiler_params(),
         cost_estimate=small_cost(many, hidden),
     )(at, *tags, *rows_in, *rows_in, *gate_ups, *downs)
@@ -332,10 +333,6 @@
     expert_here = lax.axis_index("expert") // 2
     count = lax.axis_size("dp")
     at = jnp.stack([lax.axis_index("dp"), expert_here]).astype(jnp.int32)
-    lead = min(LEAD_ROWS, tokens_here // 2)
-    main = tokens_here - lead
-    ends = (slice(0, main), slice(main, tokens_here))
-
     half_tag = (tokens_here, TAG_COLUMNS // 2)
     tagged = jnp.concatenate(
         [x_forward[0]]
@@ -343,59 +340,50 @@
         axis=1,
     )
     scaled_grad = (prob_backward[0][:, None] * grad_output[0].astype(F32)).astype(BF16)
-    main_rows, lead_rows = (
-        jnp.concatenate([x_backward[0, rows], scaled_grad[rows]], axis=0) for rows in ends
-    )
+    back_rows = jnp.concatenate([x_backward[0], scaled_grad], axis=0)
     gate_up, down = jnp.concatenate([w_gate[0], w_up[0]], axis=0), w_down[0, 0]
 
     x_gathered = lax.all_gather(tagged, "dp")
+    across_down = flipped(down, "expert", 2)
+    gate_up, back_rows = after((gate_up, back_rows), across_down)
     across_gate_up = flipped(gate_up, "expert", 2)
-    across_down = flipped(down, "expert", 2)
-    hops_main = [(main_rows, main_rows)]
+    hops = [(back_rows, back_rows)]
     for step in range(1, count):
-        hops_main.append(hop(*hops_main[-1], "dp", step))
-    gate_ups = [gate_up, flipped(gate_up, "expert", 1), across_gate_up]
-    downs = [down, flipped(down, "expert", 1), across_down]
-    waits = (x_gathered, hops_main[1], gate_ups[1], downs[1])
-    gate_ups.append(flipped(after(across_gate_up, waits), "expert", 1))
+        hops.append(hop(*hops[-1], "dp", step))
+    gate_ups = [gate_up, flipped(after(gate_up, hops[1]), "expert", 1), across_gate_up]
+    downs = [down, flipped(down, "expert", 1), across_down, flipped(across_down, "expert", 1)]
+    gate_ups.append(flipped(after(across_gate_up, x_gathered, hops[1], downs[1:]), "expert", 1))
     hidden_fwd = hidden_call(at, x_gathered, tokens_here, width, gate_ups)
-    downs.append(flipped(after(across_down, hops_main[2], hidden_fwd), "expert", 1))
     partial_fwd = down_call(hidden_fwd, count, downs)
 
     arrived_fwd = step_home(summands(partial_fwd, 1, None), "dp", 1)
-    lead_rows = after(lead_rows, hops_main[3])
-    hops_lead = [(lead_rows, lead_rows)]
-    hops_lead.append(hop(*hops_lead[-1], "dp", 1))
-    sends_fwd = summands(partial_fwd, 2, arrived_fwd)
-    arrived_fwd = step_home(sends_fwd, "dp", 2)
-    main_in = after(hops_main[:1], sends_fwd) + hops_main[1:]
-    partial_main = backward_call(at, x_gathered, 0, main, main_in, gate_ups, downs)
-
-    arrived_fwd, hops_lead[1] = after((arrived_fwd, hops_lead[1]), partial_main[1])
-    arrived_fwd = step_home(summands(partial_fwd, 3, arrived_fwd), "dp", 3)
-    arrived_main = step_home(summands(partial_main, 1, None), "dp", 1)
-    for step in range(2, count):
-        hops_lead.append(hop(*hops_lead[-1], "dp", step))
-    partial_lead = backward_call(at, x_gathered, main, lead, hops_lead, gate_ups, downs)
-
-    arrived_fwd, arrived_main = after((arrived_fwd, arrived_main), partial_lead[1])
-    arrived_main = step_home(summands(partial_main, 2, arrived_main), "dp", 2)
-    arrived_lead = step_home(summands(partial_lead, 1, None), "dp", 1)
+    arrived_fwd = after(arrived_fwd, hops[2])
+    arrived_fwd = step_home(summands(partial_fwd, 2, arrived_fwd), "dp", 2)
+    sends_fwd = summands(partial_fwd, 3, arrived_fwd)
+    arrived_fwd = step_home(sends_fwd, "dp", 3)
+    hops[0] = after(hops[0], sends_fwd)
+    partial_bwd = backward_call(at, x_gathered, tokens_here, ROW_PARTS, hops, gate_ups, downs)
+
+    arrived_fwd = after(arrived_fwd, partial_bwd[-1])
     total_fwd = summed(partial_fwd[0], arrived_fwd)
     layer_out = (x_forward[0].astype(F32) + prob_forward[0][:, None] * total_fwd).astype(BF16)
     sent_fwd = shifted(layer_out, "pipe", 1)
-
-    def sent_back(rows, block, arrived):
-        grad_in = (grad_output[0, rows].astype(F32) + summed(block, arrived)).astype(BF16)
-        return shifted(grad_in, "pipe", -1)
-
-    arrived_main = after(arrived_main, sent_fwd)
-    arrived_main = step_home(summands(partial_main, 3, arrived_main), "dp", 3)
-    arrived_lead = step_home(summands(partial_lead, 2, arrived_lead), "dp", 2)
-    sent_main = sent_back(ends[0], partial_main[0], arrived_main)
-    arrived_lead = step_home(summands(partial_lead, 3, arrived_lead), "dp", 3)
-    sent_lead = sent_back(ends[1], partial_lead[0], after(arrived_lead, sent_main))
-    return (sent_fwd[None], jnp.concatenate([sent_main, sent_lead], axis=0)[None])
+    size = tokens_here // ROW_PARTS
+    partial_bwd = after(tuple(partial_bwd), arrived_fwd)
+    blocks = [partial_bwd[part::ROW_PARTS] for part in range(ROW_PARTS)]
+    arrived = [None] * ROW_PARTS
+    for step in range(1, count):
+        for part in range(ROW_PARTS):
+            if step == 3 and part == 0:
+                arrived[0] = after(arrived[0], sent_fwd)
+            arrived[part] = step_home(summands(blocks[part], step, arrived[part]), "dp", step)
+    sent_bwd = []
+    for part in range(ROW_PARTS):
+        rows = slice(part * size, (part + 1) * size)
+        total = summed(blocks[part][0], after(arrived[part], sent_bwd))
+        grad_in = (grad_output[0, rows].astype(F32) + total).astype(BF16)
+        sent_bwd.append(shifted(grad_in, "pipe", -1))
+    return (sent_fwd[None], jnp.concatenate(sent_bwd, axis=0)[None])
 
 
 def from_partner(block, axis, stride):

time: 382 us -> 346 us (0.906)
  starting transfers between devices: 93 us -> 56.8 us
  waiting for transfers between devices: 188 us -> 213 us
  Pallas kernels: 57 us -> 38.4 us
    ppermute x9, waiting for transfers between devices: 23.6 us -> 49.3 us  [step_home(): lax.ppermute(pair[1], axis, [(i, i - 1) for i in range(count - step, coun...]
    ppermute x12 -> x6, starting transfers between devices: 35.9 us -> 13.6 us  [hop(): return (lax.ppermute(below, axis, up), lax.ppermute(above, axis, down))]
    pallas_call x2 -> x1, Pallas kernels: 39.9 us -> 21.3 us  [backward_call(): pl.pallas_call(functools.partial(backward_kernel, len(rows_in), count, pi...]
    ppermute x6, waiting for transfers between devices: 26.3 us -> 43.9 us  [flipped(): return lax.ppermute(block, axis, route)]
    ppermute x9, waiting for transfers between devices: 20.3 us -> 5.58 us  [step_home(): up = lax.ppermute(pair[0], axis, [(i, i + 1) for i in range(step)])]
    ppermute x9, starting transfers between devices: 39 us -> 24.7 us  [step_home(): lax.ppermute(pair[1], axis, [(i, i - 1) for i in range(count - step, coun...]
    ppermute x12 -> x6, waiting for transfers between devices: 103 us -> 98.1 us  [hop(): return (lax.ppermute(below, axis, up), lax.ppermute(above, axis, down))]
    unnamed x67 -> x53, local copies, waits for them, and re-layouts: 7.53 us -> 7.78 us
  transfers between devices with their start and end apart: 40 -> 34, of which waited for: 16 -> 18; matrix products, arithmetic and copies ran while one was open for 3% -> 2% of each run, Pallas kernels for 13% -> 11%
where the time goes in v8:
time: 346 us; the launch traced here: 345 us
  waiting for transfers between devices  213 us (62%)
  starting transfers between devices  56.8 us (16%)
  Pallas kernels  38.4 us (11%)
  between operations  14.6 us (4%)
  other arithmetic  12.5 us (4%)
  local copies, waits for them, and re-layouts  10 us (3%)
    ppermute x6, waiting for transfers between devices, hop(): return (lax.ppermute(below, axis, up), lax.ppermute(above, axis, down))  98.1 us
    ppermute x9, waiting for transfers between devices, step_home(): lax.ppermute(pair[1], axis, [(i, i - 1) for i in range(count - step, coun...  49.3 us
    ppermute x6, waiting for transfers between devices, flipped(): return lax.ppermute(block, axis, route)  43.9 us
    ppermute x9, starting transfers between devices, step_home(): lax.ppermute(pair[1], axis, [(i, i - 1) for i in range(count - step, coun...  24.7 us
    pallas_call x1, Pallas kernels, backward_call(): pl.pallas_call(functools.partial(backward_kernel, len(rows_in), count, pi...  21.3 us
    ppermute x3, waiting for transfers between devices, shifted(): lax.ppermute(block, axis, [((i - distance) % count, i) for i in range(cou...  16.1 us
    ppermute x6, starting transfers between devices, hop(): return (lax.ppermute(below, axis, up), lax.ppermute(above, axis, down))  13.6 us
    ppermute x9, starting transfers between devices, step_home(): up = lax.ppermute(pair[0], axis, [(i, i + 1) for i in range(step)])  13.1 us
  transfers between devices with their start and end apart: 34, of which 18 were waited for; matrix products, arithmetic and copies ran while one was open for 2% of the time, Pallas kernels for 11%

profile of v8, /device:TPU:20, one launch (start us, length us, event | category | flops | bytes accessed | tf_op | source)
XLA Modules:
  0.0 345.4 jit_solution(9368606803306276376)
XLA Ops:
  8.8 2.1 concatenate.12
  10.9 1.6 collective-permute-start
  12.8 2.0 copy-done.10
  15.4 2.1 pad_maximum_fusion.refs_8_.refs_18_
  17.5 35.4 %collective-permute-done.refs_2_.refs_24_ = bf16[128,7168]{1,0:T(8,128)(2,1)S(1)} collective-permute-done((bf16[128,7168]{1,0:T(8,128)(2,1)}, bf16[128,7168]{1,0:T(8,128)(2,1)S(1)}, u32[]{:S(2)}, u32[]{:S(2)}) %collective-permute-start) | collective-permute-done | bytes 1835040 | tf_op jit(solution)/shard_map/ppermute | solution.py:25
  52.9 1.5 collective-permute-start.4
  54.4 2.3 collective-permute-start.2
  56.8 3.6 %collective-permute-start.1 = (bf16[128,7168]{1,0:T(8,128)(2,1)S(1)}, bf16[128,7168]{1,0:T(8,128)(2,1)S(1)}, u32[]{:S(2)}, u32[]{:S(2)}) collective-permute-start(bf16[128,7168]{1,0:T(8,128)(2,1)S(1)} %pad_maximum_fusion.1.refs_4_.refs_11_), channel_id=1, source_target_pairs={{0,1},{1,2},{2,3},{4,5},{5,6},{6,7},{8,9},{9,10},{10,11},{12,13},{... | collective-permute-start | bytes 5505032 | tf_op jit(solution)/shard_map/ppermute | solution.py:295
  60.9 61.6 %collective-permute-done.2.refs_8_.refs_15_ = bf16[128,7168]{1,0:T(8,128)(2,1)S(1)} collective-permute-done((bf16[128,7168]{1,0:T(8,128)(2,1)S(1)}, bf16[128,7168]{1,0:T(8,128)(2,1)S(1)}, u32[]{:S(2)}, u32[]{:S(2)}) %collective-permute-start.2) | collective-permute-done | bytes 1835040 | tf_op jit(solution)/shard_map/ppermute | solution.py:295
  122.7 1.1 copy-done.3
  124.4 1.3 copy-done.5
  125.6 7.9 %collective-permute-done.4.refs_10_.refs_20_ = bf16[2,7168,128]{2,1,0:T(8,128)(2,1)} collective-permute-done((bf16[2,7168,128]{2,1,0:T(8,128)(2,1)}, bf16[2,7168,128]{2,1,0:T(8,128)(2,1)}, u32[]{:S(2)}, u32[]{:S(2)}) %collective-permute-start.4) | collective-permute-done | bytes 3670048 | tf_op jit(solution)/shard_map/ppermute | solution.py:25
  133.5 3.6 %collective-permute-start.11 = (bf16[128,7168]{1,0:T(8,128)(2,1)S(1)}, bf16[128,7168]{1,0:T(8,128)(2,1)}, u32[]{:S(2)}, u32[]{:S(2)}) collective-permute-start(bf16[128,7168]{1,0:T(8,128)(2,1)S(1)} %collective-permute-done.2.refs_8_.refs_15_), channel_id=1, source_target_pairs={{1,0},{2,1},{5,4},{6,5},{9,8},{10,9},{13,12},{14,13},{17,16},{18,1... | collective-permute-start | bytes 5505032 | tf_op jit(solution)/shard_map/ppermute | solution.py:295
  137.1 1.9 collective-permute-start.10
  140.3 10.2 %shard_map.113.hidden_ref = bf16[256,512]{1,0:T(8,128)(2,1)} custom-call(s32[2]{0:T(128)} %pad_add_fusion.at_ref, bf16[4,64,7296]{2,1,0:T(8,128)(2,1)} %bitcast.27, bf16[4,64,7296]{2,1,0:T(8,128)(2,1)} %bitcast.28, bf16[4,64,7296]{2,1,0:T(8,128)(2,1)} %bitcast.29, bf16[4,64,7296]{2,1,0:T(8,128)(2,1)} %bitcast.30, bf16[4,64,7296]{2,1,0:T(8,128)(2,1)} %bitcast.31, ...), custom_call_target="tpu_custom_call" | custom-call | flops 131072 | bytes 256 | tf_op jit(solution)/shard_map/pallas_call | solution.py:158
  150.5 6.8 %shard_map.114 = (f32[64,7168]{1,0:T(8,128)}, bf16[64,7168]{1,0:T(8,128)(2,1)}, bf16[64,7168]{1,0:T(8,128)(2,1)}, bf16[64,7168]{1,0:T(8,128)(2,1)}) custom-call(bf16[256,512]{1,0:T(8,128)(2,1)} %shard_map.113.hidden_ref, bf16[128,7168]{1,0:T(8,128)(2,1)} %bitcast.12.refs_0_.refs_22_, bf16[128,7168]{1,0:T(8,128)(2,1)} %copy-done.4, ...), custom_call_target="tpu_custom_call" | custom-call | flops 131072 | bytes 256 | tf_op jit(solution)/shard_map/pallas_call | solution.py:185
  157.4 1.3 collective-permute-start.9
  159.4 16.4 %collective-permute-done.11.refs_9_.refs_16_ = bf16[128,7168]{1,0:T(8,128)(2,1)} collective-permute-done((bf16[128,7168]{1,0:T(8,128)(2,1)S(1)}, bf16[128,7168]{1,0:T(8,128)(2,1)}, u32[]{:S(2)}, u32[]{:S(2)}) %collective-permute-start.11) | collective-permute-done | bytes 1835040 | tf_op jit(solution)/shard_map/ppermute | solution.py:295
  175.8 5.6 %collective-permute-done.10.refs_6_.refs_13_ = bf16[128,7168]{1,0:T(8,128)(2,1)} collective-permute-done((bf16[128,7168]{1,0:T(8,128)(2,1)}, bf16[128,7168]{1,0:T(8,128)(2,1)}, u32[]{:S(2)}, u32[]{:S(2)}) %collective-permute-start.10) | collective-permute-done | bytes 1835040 | tf_op jit(solution)/shard_map/ppermute | solution.py:295
  181.9 1.6 fusion.1
  183.5 5.2 %collective-permute-start.14 = (bf16[64,7168]{1,0:T(8,128)(2,1)S(1)}, bf16[64,7168]{1,0:T(8,128)(2,1)S(1)}, u32[]{:S(2)}, u32[]{:S(2)}) collective-permute-start(bf16[64,7168]{1,0:T(8,128)(2,1)S(1)} %get-tuple-element.72), channel_id=1, source_target_pairs={{2,1},{3,2},{6,5},{7,6},{10,9},{11,10},{14,13},{15,14},{18,17},{19... | collective-permute-start | bytes 2752520 | tf_op jit(solution)/shard_map/ppermute | solution.py:310
  189.4 1.4 collective-permute-start.16
  190.9 1.3 collective-permute-start.12
  192.2 15.3 %collective-permute-done.14 = bf16[64,7168]{1,0:T(8,128)(2,1)S(1)} collective-permute-done((bf16[64,7168]{1,0:T(8,128)(2,1)S(1)}, bf16[64,7168]{1,0:T(8,128)(2,1)S(1)}, u32[]{:S(2)}, u32[]{:S(2)}) %collective-permute-start.14) | collective-permute-done | bytes 917536 | tf_op jit(solution)/shard_map/ppermute | solution.py:310
  208.6 4.4 %collective-permute-start.15 = (bf16[64,7168]{1,0:T(8,128)(2,1)}, bf16[64,7168]{1,0:T(8,128)(2,1)}, u32[]{:S(2)}, u32[]{:S(2)}) collective-permute-start(bf16[64,7168]{1,0:T(8,128)(2,1)} %add_convert_fusion.1), channel_id=1, source_target_pairs={{1,0},{2,1},{3,2},{5,4},{6,5},{7,6},{9,8},{10,9},{11,10},{13,12},{... | collective-permute-start | bytes 2752520 | tf_op jit(solution)/shard_map/ppermute | solution.py:310
  213.8 1.1 add_convert_fusion.2
  215.0 2.2 collective-permute-start.13
  217.2 14.3 %collective-permute-done.16.refs_7_.refs_14_ = bf16[128,7168]{1,0:T(8,128)(2,1)S(1)} collective-permute-done((bf16[128,7168]{1,0:T(8,128)(2,1)}, bf16[128,7168]{1,0:T(8,128)(2,1)S(1)}, u32[]{:S(2)}, u32[]{:S(2)}) %collective-permute-start.16) | collective-permute-done | bytes 1835040 | tf_op jit(solution)/shard_map/ppermute | solution.py:295
  231.5 1.3 copy-done.7
  232.8 21.3 %shard_map.115 = (f32[32,7168]{1,0:T(8,128)}, f32[32,7168]{1,0:T(8,128)}, bf16[32,7168]{1,0:T(8,128)(2,1)}, bf16[32,7168]{1,0:T(8,128)(2,1)}, bf16[32,7168]{1,0:...) custom-call(s32[2]{0:T(128)} %pad_add_fusion.at_ref, ...), custom_call_target="tpu_custom_call" | custom-call | flops 131072 | bytes 256 | tf_op jit(solution)/shard_map/pallas_call | solution.py:263
  254.2 1.3 collective-permute-start.21
  256.2 1.3 collective-permute-start.29
  258.2 2.0 add_convert_fusion
  260.8 14.0 %collective-permute-done.29 = bf16[32,7168]{1,0:T(8,128)(2,1)S(1)} collective-permute-done((bf16[32,7168]{1,0:T(8,128)(2,1)}, bf16[32,7168]{1,0:T(8,128)(2,1)S(1)}, u32[]{:S(2)}, u32[]{:S(2)}) %collective-permute-start.29) | collective-permute-done | bytes 458784 | tf_op jit(solution)/shard_map/ppermute | solution.py:310
  275.0 3.1 collective-permute-start.30
  278.3 2.1 collective-permute-start.22
  280.4 1.3 collective-permute-start.20
  281.7 1.4 collective-permute-start.27
  283.1 7.3 %collective-permute-done.30 = bf16[32,7168]{1,0:T(8,128)(2,1)S(1)} collective-permute-done((bf16[32,7168]{1,0:T(8,128)(2,1)S(1)}, bf16[32,7168]{1,0:T(8,128)(2,1)S(1)}, u32[]{:S(2)}, u32[]{:S(2)}) %collective-permute-start.30) | collective-permute-done | bytes 458784 | tf_op jit(solution)/shard_map/ppermute | solution.py:310
  290.6 3.1 collective-permute-start.31
  293.7 6.6 %collective-permute-done.22 = bf16[32,7168]{1,0:T(8,128)(2,1)S(1)} collective-permute-done((bf16[32,7168]{1,0:T(8,128)(2,1)S(1)}, bf16[32,7168]{1,0:T(8,128)(2,1)S(1)}, u32[]{:S(2)}, u32[]{:S(2)}) %collective-permute-start.22) | collective-permute-done | bytes 458784 | tf_op jit(solution)/shard_map/ppermute | solution.py:310
  300.6 3.1 collective-permute-start.24
  303.7 2.9 collective-permute-start.23
  306.7 1.9 collective-permute-start.28
  308.6 5.6 %collective-permute-done.24 = bf16[32,7168]{1,0:T(8,128)(2,1)S(1)} collective-permute-done((bf16[32,7168]{1,0:T(8,128)(2,1)S(1)}, bf16[32,7168]{1,0:T(8,128)(2,1)S(1)}, u32[]{:S(2)}, u32[]{:S(2)}) %collective-permute-start.24) | collective-permute-done | bytes 458784 | tf_op jit(solution)/shard_map/ppermute | solution.py:310
  315.6 4.2 %collective-permute-done.28 = bf16[32,7168]{1,0:T(8,128)(2,1)S(1)} collective-permute-done((bf16[32,7168]{1,0:T(8,128)(2,1)S(1)}, bf16[32,7168]{1,0:T(8,128)(2,1)S(1)}, u32[]{:S(2)}, u32[]{:S(2)}) %collective-permute-start.28) | collective-permute-done | bytes 458784 | tf_op jit(solution)/shard_map/ppermute | solution.py:309
  319.8 8.1 %collective-permute-done.25 = bf16[32,7168]{1,0:T(8,128)(2,1)S(1)} collective-permute-done((bf16[32,7168]{1,0:T(8,128)(2,1)S(1)}, bf16[32,7168]{1,0:T(8,128)(2,1)S(1)}, u32[]{:S(2)}, u32[]{:S(2)}) %collective-permute-start.25) | collective-permute-done | bytes 458784 | tf_op jit(solution)/shard_map/ppermute | solution.py:30
  328.6 8.0 %collective-permute-done.32 = bf16[32,7168]{1,0:T(8,128)(2,1)S(1)} collective-permute-done((bf16[32,7168]{1,0:T(8,128)(2,1)S(1)}, bf16[32,7168]{1,0:T(8,128)(2,1)S(1)}, u32[]{:S(2)}, u32[]{:S(2)}) %collective-permute-start.32) | collective-permute-done | bytes 458784 | tf_op jit(solution)/shard_map/ppermute | solution.py:30
  (99 shorter events, 15.6 us)
Async XLA Ops:
  7.2 126.3 %all-gather.3.cloned.1.call-start = ((), (), s32[]{:S(2)}) async-start(), calls=%async_computation | async-start | bytes 4669440 | tf_op jit(solution)/shard_map/all_gather | solution.py:346
  10.9 42.0 %collective-permute-start = (bf16[128,7168]{1,0:T(8,128)(2,1)}, bf16[128,7168]{1,0:T(8,128)(2,1)S(1)}, u32[]{:S(2)}, u32[]{:S(2)}) collective-permute-start(bf16[128,7168]{1,0:T(8,128)(2,1)} %bitcast.12.refs_0_.refs_22_), channel_id=1, source_target_pairs={{0,8},{4,12},{8,0},{12,4},{1,9},{5,13},{9,1},{13,5},{2,10},{6,14},... | collective-permute-start | bytes 5505032 | tf_op jit(solution)/shard_map/ppermute | solution.py:25
  12.8 43.9 %copy-start = (bf16[128,7168]{1,0:T(8,128)(2,1)}, bf16[128,7168]{1,0:T(8,128)(2,1)S(1)}, u32[]{:S(2)}) copy-start(bf16[128,7168]{1,0:T(8,128)(2,1)S(1)} %pad_maximum_fusion.1.refs_4_.refs_11_) | copy-start | bytes 5505028
  52.9 69.7 %copy-start.1 = (bf16[128,7168]{1,0:T(8,128)(2,1)}, bf16[128,7168]{1,0:T(8,128)(2,1)S(1)}, u32[]{:S(2)}) copy-start(bf16[128,7168]{1,0:T(8,128)(2,1)S(1)} %collective-permute-done.refs_2_.refs_24_) | copy-start | bytes 5505028
  52.9 80.6 %collective-permute-start.4 = (bf16[2,7168,128]{2,1,0:T(8,128)(2,1)}, bf16[2,7168,128]{2,1,0:T(8,128)(2,1)}, u32[]{:S(2)}, u32[]{:S(2)}) collective-permute-start(bf16[2,7168,128]{2,1,0:T(8,128)(2,1)} %pad_maximum_fusion.refs_8_.refs_18_), channel_id=1, source_target_pairs={{0,8},{4,12},{8,0},{12,4},{1,9},{5,13},{9,1},{13,5},{2,10},{6,14},... | collective-permute-start | bytes 11010056 | tf_op jit(solution)/shard_map/ppermute | solution.py:25
  54.4 68.2 %collective-permute-start.2 = (bf16[128,7168]{1,0:T(8,128)(2,1)S(1)}, bf16[128,7168]{1,0:T(8,128)(2,1)S(1)}, u32[]{:S(2)}, u32[]{:S(2)}) collective-permute-start(bf16[128,7168]{1,0:T(8,128)(2,1)S(1)} %pad_maximum_fusion.1.refs_4_.refs_11_), channel_id=1, source_target_pairs={{1,0},{2,1},{3,2},{5,4},{6,5},{7,6},{9,8},{10,9},{11,10},{13,12},{... | collective-permute-start | bytes 5505032 | tf_op jit(solution)/shard_map/ppermute | solution.py:295
  56.8 65.8 %collective-permute-start.1 = (bf16[128,7168]{1,0:T(8,128)(2,1)S(1)}, bf16[128,7168]{1,0:T(8,128)(2,1)S(1)}, u32[]{:S(2)}, u32[]{:S(2)}) collective-permute-start(bf16[128,7168]{1,0:T(8,128)(2,1)S(1)} %pad_maximum_fusion.1.refs_4_.refs_11_), channel_id=1, source_target_pairs={{0,1},{1,2},{2,3},{4,5},{5,6},{6,7},{8,9},{9,10},{10,11},{12,13},{... | collective-permute-start | bytes 5505032 | tf_op jit(solution)/shard_map/ppermute | solution.py:295
  60.4 62.3 %collective-permute-start.5 = (bf16[128,7168]{1,0:T(8,128)(2,1)}, bf16[128,7168]{1,0:T(8,128)(2,1)S(1)}, u32[]{:S(2)}, u32[]{:S(2)}) collective-permute-start(bf16[128,7168]{1,0:T(8,128)(2,1)} %bitcast.12.refs_0_.refs_22_), channel_id=1, source_target_pairs={{0,4},{4,0},{8,12},{12,8},{1,5},{5,1},{9,13},{13,9},{2,6},{6,2},{1... | collective-permute-start | bytes 5505032 | tf_op jit(solution)/shard_map/ppermute | solution.py:25
  60.4 62.3 %collective-permute-start.6 = (bf16[128,7168]{1,0:T(8,128)(2,1)S(1)}, bf16[128,7168]{1,0:T(8,128)(2,1)S(1)}, u32[]{:S(2)}, u32[]{:S(2)}) collective-permute-start(bf16[128,7168]{1,0:T(8,128)(2,1)S(1)} %collective-permute-done.refs_2_.refs_24_), channel_id=1, source_target_pairs={{0,4},{4,0},{8,12},{12,8},{1,5},{5,1},{9,13},{13,9},{2,6},{6,2},{1... | collective-permute-start | bytes 5505032 | tf_op jit(solution)/shard_map/ppermute | solution.py:25
  122.6 27.9 %copy-start.2 = (bf16[128,7168]{1,0:T(8,128)(2,1)}, bf16[128,7168]{1,0:T(8,128)(2,1)S(1)}, u32[]{:S(2)}) copy-start(bf16[128,7168]{1,0:T(8,128)(2,1)S(1)} %collective-permute-done.2.refs_8_.refs_15_) | copy-start | bytes 5505028
  122.6 17.0 %collective-permute-start.3 = (bf16[2,7168,128]{2,1,0:T(8,128)(2,1)}, bf16[2,7168,128]{2,1,0:T(8,128)(2,1)}, u32[]{:S(2)}, u32[]{:S(2)}) collective-permute-start(bf16[2,7168,128]{2,1,0:T(8,128)(2,1)} %pad_maximum_fusion.refs_8_.refs_18_), channel_id=1, source_target_pairs={{0,4},{4,0},{8,12},{12,8},{1,5},{5,1},{9,13},{13,9},{2,6},{6,2},{1... | collective-permute-start | bytes 11010056 | tf_op jit(solution)/shard_map/ppermute | solution.py:25
  133.5 6.8 %collective-permute-start.7 = (bf16[2,7168,128]{2,1,0:T(8,128)(2,1)}, bf16[2,7168,128]{2,1,0:T(8,128)(2,1)}, u32[]{:S(2)}, u32[]{:S(2)}) collective-permute-start(bf16[2,7168,128]{2,1,0:T(8,128)(2,1)} %collective-permute-done.4.refs_10_.refs_20_), channel_id=1, source_target_pairs={{0,4},{4,0},{8,12},{12,8},{1,5},{5,1},{9,13},{13,9},{2,6},{6,2},{1... | collective-permute-start | bytes 11010056 | tf_op jit(solution)/shard_map/ppermute | solution.py:25
  133.5 42.3 %collective-permute-start.11 = (bf16[128,7168]{1,0:T(8,128)(2,1)S(1)}, bf16[128,7168]{1,0:T(8,128)(2,1)}, u32[]{:S(2)}, u32[]{:S(2)}) collective-permute-start(bf16[128,7168]{1,0:T(8,128)(2,1)S(1)} %collective-permute-done.2.refs_8_.refs_15_), channel_id=1, source_target_pairs={{1,0},{2,1},{5,4},{6,5},{9,8},{10,9},{13,12},{14,13},{17,16},{18,1... | collective-permute-start | bytes 5505032 | tf_op jit(solution)/shard_map/ppermute | solution.py:295
  137.1 44.3 %collective-permute-start.10 = (bf16[128,7168]{1,0:T(8,128)(2,1)}, bf16[128,7168]{1,0:T(8,128)(2,1)}, u32[]{:S(2)}, u32[]{:S(2)}) collective-permute-start(bf16[128,7168]{1,0:T(8,128)(2,1)} %copy-done.3), channel_id=1, source_target_pairs={{1,2},{2,3},{5,6},{6,7},{9,10},{10,11},{13,14},{14,15},{17,18},{18... | collective-permute-start | bytes 5505032 | tf_op jit(solution)/shard_map/ppermute | solution.py:295
  157.4 24.5 %collective-permute-start.9 = (bf16[64,7168]{1,0:T(8,128)(2,1)}, bf16[64,7168]{1,0:T(8,128)(2,1)S(1)}, u32[]{:S(2)}, u32[]{:S(2)}) collective-permute-start(bf16[64,7168]{1,0:T(8,128)(2,1)} %get-tuple-element.42), channel_id=1, source_target_pairs={{3,2},{7,6},{11,10},{15,14},{19,18},{23,22},{27,26},{31,30}} | collective-permute-start | bytes 2752520 | tf_op jit(solution)/shard_map/ppermute | solution.py:310
  158.6 23.2 %collective-permute-start.8 = (bf16[64,7168]{1,0:T(8,128)(2,1)}, bf16[64,7168]{1,0:T(8,128)(2,1)S(1)}, u32[]{:S(2)}, u32[]{:S(2)}) collective-permute-start(bf16[64,7168]{1,0:T(8,128)(2,1)} %get-tuple-element.44), channel_id=1, source_target_pairs={{0,1},{4,5},{8,9},{12,13},{16,17},{20,21},{24,25},{28,29}} | collective-permute-start | bytes 2752520 | tf_op jit(solution)/shard_map/ppermute | solution.py:309
  181.8 25.6 %copy-start.17 = (bf16[64,7168]{1,0:T(8,128)(2,1)S(1)}, bf16[64,7168]{1,0:T(8,128)(2,1)}, u32[]{:S(2)}) copy-start(bf16[64,7168]{1,0:T(8,128)(2,1)} %get-tuple-element.44) | copy-start | bytes 2752516
  183.5 30.3 %copy-start.16 = (bf16[64,7168]{1,0:T(8,128)(2,1)S(1)}, bf16[64,7168]{1,0:T(8,128)(2,1)}, u32[]{:S(2)}) copy-start(bf16[64,7168]{1,0:T(8,128)(2,1)} %get-tuple-element.42) | copy-start | bytes 2752516
  183.5 24.0 %collective-permute-start.14 = (bf16[64,7168]{1,0:T(8,128)(2,1)S(1)}, bf16[64,7168]{1,0:T(8,128)(2,1)S(1)}, u32[]{:S(2)}, u32[]{:S(2)}) collective-permute-start(bf16[64,7168]{1,0:T(8,128)(2,1)S(1)} %get-tuple-element.72), channel_id=1, source_target_pairs={{2,1},{3,2},{6,5},{7,6},{10,9},{11,10},{14,13},{15,14},{18,17},{19... | collective-permute-start | bytes 2752520 | tf_op jit(solution)/shard_map/ppermute | solution.py:310
  188.7 28.5 %collective-permute-start.17 = (bf16[128,7168]{1,0:T(8,128)(2,1)}, bf16[128,7168]{1,0:T(8,128)(2,1)S(1)}, u32[]{:S(2)}, u32[]{:S(2)}) collective-permute-start(bf16[128,7168]{1,0:T(8,128)(2,1)} %collective-permute-done.11.refs_9_.refs_16_), channel_id=1, source_target_pairs={{1,0},{5,4},{9,8},{13,12},{17,16},{21,20},{25,24},{29,28}} | collective-permute-start | bytes 5505032 | tf_op jit(solution)/shard_map/ppermute | solution.py:295
  189.4 42.1 %collective-permute-start.16 = (bf16[128,7168]{1,0:T(8,128)(2,1)}, bf16[128,7168]{1,0:T(8,128)(2,1)S(1)}, u32[]{:S(2)}, u32[]{:S(2)}) collective-permute-start(bf16[128,7168]{1,0:T(8,128)(2,1)} %collective-permute-done.10.refs_6_.refs_13_), channel_id=1, source_target_pairs={{2,3},{6,7},{10,11},{14,15},{18,19},{22,23},{26,27},{30,31}} | collective-permute-start | bytes 5505032 | tf_op jit(solution)/shard_map/ppermute | solution.py:295
  190.9 23.0 %collective-permute-start.12 = (bf16[64,7168]{1,0:T(8,128)(2,1)S(1)}, bf16[64,7168]{1,0:T(8,128)(2,1)S(1)}, u32[]{:S(2)}, u32[]{:S(2)}) collective-permute-start(bf16[64,7168]{1,0:T(8,128)(2,1)S(1)} %get-tuple-element.73), channel_id=1, source_target_pairs={{0,1},{1,2},{4,5},{5,6},{8,9},{9,10},{12,13},{13,14},{16,17},{17,1... | collective-permute-start | bytes 2752520 | tf_op jit(solution)/shard_map/ppermute | solution.py:309
  208.6 45.5 %collective-permute-start.15 = (bf16[64,7168]{1,0:T(8,128)(2,1)}, bf16[64,7168]{1,0:T(8,128)(2,1)}, u32[]{:S(2)}, u32[]{:S(2)}) collective-permute-start(bf16[64,7168]{1,0:T(8,128)(2,1)} %add_convert_fusion.1), channel_id=1, source_target_pairs={{1,0},{2,1},{3,2},{5,4},{6,5},{7,6},{9,8},{10,9},{11,10},{13,12},{... | collective-permute-start | bytes 2752520 | tf_op jit(solution)/shard_map/ppermute | solution.py:310
  214.9 43.2 %copy-start.8 = (bf16[1,64,7168]{2,1,0:T(8,128)(2,1)S(1)}, bf16[1,64,7168]{2,1,0:T(8,128)(2,1)}, u32[]{:S(2)}) copy-start(bf16[1,64,7168]{2,1,0:T(8,128)(2,1)} %param.10) | copy-start | bytes 2752516
  215.0 43.2 %copy-start.12 = (f32[64,7168]{1,0:T(8,128)S(1)}, f32[64,7168]{1,0:T(8,128)}, u32[]{:S(2)}) copy-start(f32[64,7168]{1,0:T(8,128)} %get-tuple-element.41) | copy-start | bytes 5505028
  215.0 43.2 %copy-start.24 = (f32[1,64]{1,0:T(1,128)S(1)}, f32[1,64]{1,0:T(1,128)}, u32[]{:S(2)}) copy-start(f32[1,64]{1,0:T(1,128)} %param.12) | copy-start | bytes 772
  215.0 39.2 %collective-permute-start.13 = (bf16[64,7168]{1,0:T(8,128)(2,1)}, bf16[64,7168]{1,0:T(8,128)(2,1)}, u32[]{:S(2)}, u32[]{:S(2)}) collective-permute-start(bf16[64,7168]{1,0:T(8,128)(2,1)} %add_convert_fusion.2), channel_id=1, source_target_pairs={{0,1},{1,2},{2,3},{4,5},{5,6},{6,7},{8,9},{9,10},{10,11},{12,13},{... | collective-permute-start | bytes 2752520 | tf_op jit(solution)/shard_map/ppermute | solution.py:309
  254.2 23.9 %collective-permute-start.21 = (bf16[32,7168]{1,0:T(8,128)(2,1)}, bf16[32,7168]{1,0:T(8,128)(2,1)S(1)}, u32[]{:S(2)}, u32[]{:S(2)}) collective-permute-start(bf16[32,7168]{1,0:T(8,128)(2,1)} %get-tuple-element.59), channel_id=1, source_target_pairs={{3,2},{7,6},{11,10},{15,14},{19,18},{23,22},{27,26},{31,30}} | collective-permute-start | bytes 1376264 | tf_op jit(solution)/shard_map/ppermute | solution.py:310
  255.5 22.6 %collective-permute-start.19 = (bf16[32,7168]{1,0:T(8,128)(2,1)}, bf16[32,7168]{1,0:T(8,128)(2,1)S(1)}, u32[]{:S(2)}, u32[]{:S(2)}) collective-permute-start(bf16[32,7168]{1,0:T(8,128)(2,1)} %get-tuple-element.61), channel_id=1, source_target_pairs={{0,1},{4,5},{8,9},{12,13},{16,17},{20,21},{24,25},{28,29}} | collective-permute-start | bytes 1376264 | tf_op jit(solution)/shard_map/ppermute | solution.py:309
  256.2 18.6 %collective-permute-start.29 = (bf16[32,7168]{1,0:T(8,128)(2,1)}, bf16[32,7168]{1,0:T(8,128)(2,1)S(1)}, u32[]{:S(2)}, u32[]{:S(2)}) collective-permute-start(bf16[32,7168]{1,0:T(8,128)(2,1)} %get-tuple-element.67), channel_id=1, source_target_pairs={{3,2},{7,6},{11,10},{15,14},{19,18},{23,22},{27,26},{31,30}} | collective-permute-start | bytes 1376264 | tf_op jit(solution)/shard_map/ppermute | solution.py:310
  257.5 17.3 %collective-permute-start.26 = (bf16[32,7168]{1,0:T(8,128)(2,1)}, bf16[32,7168]{1,0:T(8,128)(2,1)S(1)}, u32[]{:S(2)}, u32[]{:S(2)}) collective-permute-start(bf16[32,7168]{1,0:T(8,128)(2,1)} %get-tuple-element.69), channel_id=1, source_target_pairs={{0,1},{4,5},{8,9},{12,13},{16,17},{20,21},{24,25},{28,29}} | collective-permute-start | bytes 1376264 | tf_op jit(solution)/shard_map/ppermute | solution.py:309
  260.2 30.3 %copy-start.21 = (bf16[32,7168]{1,0:T(8,128)(2,1)S(1)}, bf16[32,7168]{1,0:T(8,128)(2,1)}, u32[]{:S(2)}) copy-start(bf16[32,7168]{1,0:T(8,128)(2,1)} %get-tuple-element.69) | copy-start | bytes 1376260
  260.2 40.1 %collective-permute-start.18 = (bf16[64,7168]{1,0:T(8,128)(2,1)S(1)}, bf16[64,7168]{1,0:T(8,128)(2,1)S(1)}, u32[]{:S(2)}, u32[]{:S(2)}) collective-permute-start(bf16[64,7168]{1,0:T(8,128)(2,1)S(1)} %add_convert_fusion), channel_id=1, source_target_pairs={{16,0},{0,16},{17,1},{1,17},{18,2},{2,18},{19,3},{3,19},{20,4},{4,... | collective-permute-start | bytes 2752520 | tf_op jit(solution)/shard_map/ppermute | solution.py:30
  275.0 25.3 %copy-start.20 = (bf16[32,7168]{1,0:T(8,128)(2,1)S(1)}, bf16[32,7168]{1,0:T(8,128)(2,1)}, u32[]{:S(2)}) copy-start(bf16[32,7168]{1,0:T(8,128)(2,1)} %get-tuple-element.59) | copy-start | bytes 1376260
  275.0 15.5 %collective-permute-start.30 = (bf16[32,7168]{1,0:T(8,128)(2,1)S(1)}, bf16[32,7168]{1,0:T(8,128)(2,1)S(1)}, u32[]{:S(2)}, u32[]{:S(2)}) collective-permute-start(bf16[32,7168]{1,0:T(8,128)(2,1)S(1)} %get-tuple-element.76), channel_id=1, source_target_pairs={{2,1},{3,2},{6,5},{7,6},{10,9},{11,10},{14,13},{15,14},{18,17},{19... | collective-permute-start | bytes 1376264 | tf_op jit(solution)/shard_map/ppermute | solution.py:310
  278.3 22.1 %copy-start.19 = (bf16[32,7168]{1,0:T(8,128)(2,1)S(1)}, bf16[32,7168]{1,0:T(8,128)(2,1)}, u32[]{:S(2)}) copy-start(bf16[32,7168]{1,0:T(8,128)(2,1)} %get-tuple-element.61) | copy-start | bytes 1376260
  278.3 22.0 %collective-permute-start.22 = (bf16[32,7168]{1,0:T(8,128)(2,1)S(1)}, bf16[32,7168]{1,0:T(8,128)(2,1)S(1)}, u32[]{:S(2)}, u32[]{:S(2)}) collective-permute-start(bf16[32,7168]{1,0:T(8,128)(2,1)S(1)} %get-tuple-element.74), channel_id=1, source_target_pairs={{2,1},{3,2},{6,5},{7,6},{10,9},{11,10},{14,13},{15,14},{18,17},{19... | collective-permute-start | bytes 1376264 | tf_op jit(solution)/shard_map/ppermute | solution.py:310
  280.4 19.9 %collective-permute-start.20 = (bf16[32,7168]{1,0:T(8,128)(2,1)S(1)}, bf16[32,7168]{1,0:T(8,128)(2,1)S(1)}, u32[]{:S(2)}, u32[]{:S(2)}) collective-permute-start(bf16[32,7168]{1,0:T(8,128)(2,1)S(1)} %get-tuple-element.75), channel_id=1, source_target_pairs={{0,1},{1,2},{4,5},{5,6},{8,9},{9,10},{12,13},{13,14},{16,17},{17,1... | collective-permute-start | bytes 1376264 | tf_op jit(solution)/shard_map/ppermute | solution.py:309
  281.7 24.9 %copy-start.18 = (bf16[32,7168]{1,0:T(8,128)(2,1)S(1)}, bf16[32,7168]{1,0:T(8,128)(2,1)}, u32[]{:S(2)}) copy-start(bf16[32,7168]{1,0:T(8,128)(2,1)} %get-tuple-element.67) | copy-start | bytes 1376260
  281.7 24.9 %collective-permute-start.27 = (bf16[32,7168]{1,0:T(8,128)(2,1)S(1)}, bf16[32,7168]{1,0:T(8,128)(2,1)S(1)}, u32[]{:S(2)}, u32[]{:S(2)}) collective-permute-start(bf16[32,7168]{1,0:T(8,128)(2,1)S(1)} %get-tuple-element.77), channel_id=1, source_target_pairs={{0,1},{1,2},{4,5},{5,6},{8,9},{9,10},{12,13},{13,14},{16,17},{17,1... | collective-permute-start | bytes 1376264 | tf_op jit(solution)/shard_map/ppermute | solution.py:309
  290.6 24.3 %copy-start.15 = (f32[32,7168]{1,0:T(8,128)S(1)}, f32[32,7168]{1,0:T(8,128)}, u32[]{:S(2)}) copy-start(f32[32,7168]{1,0:T(8,128)} %get-tuple-element.58) | copy-start | bytes 2752516
  290.6 25.0 %collective-permute-start.31 = (bf16[32,7168]{1,0:T(8,128)(2,1)S(1)}, bf16[32,7168]{1,0:T(8,128)(2,1)S(1)}, u32[]{:S(2)}, u32[]{:S(2)}) collective-permute-start(bf16[32,7168]{1,0:T(8,128)(2,1)S(1)} %add_convert_fusion.3), channel_id=1, source_target_pairs={{1,0},{2,1},{3,2},{5,4},{6,5},{7,6},{9,8},{10,9},{11,10},{13,12},{... | collective-permute-start | bytes 1376264 | tf_op jit(solution)/shard_map/ppermute | solution.py:310
  300.6 27.3 %copy-start.14 = (f32[32,7168]{1,0:T(8,128)S(1)}, f32[32,7168]{1,0:T(8,128)}, u32[]{:S(2)}) copy-start(f32[32,7168]{1,0:T(8,128)} %get-tuple-element.66) | copy-start | bytes 2752516
  300.6 13.7 %collective-permute-start.24 = (bf16[32,7168]{1,0:T(8,128)(2,1)S(1)}, bf16[32,7168]{1,0:T(8,128)(2,1)S(1)}, u32[]{:S(2)}, u32[]{:S(2)}) collective-permute-start(bf16[32,7168]{1,0:T(8,128)(2,1)S(1)} %add_convert_fusion.5), channel_id=1, source_target_pairs={{1,0},{2,1},{3,2},{5,4},{6,5},{7,6},{9,8},{10,9},{11,10},{13,12},{... | collective-permute-start | bytes 1376264 | tf_op jit(solution)/shard_map/ppermute | solution.py:310
  303.7 11.2 %collective-permute-start.23 = (bf16[32,7168]{1,0:T(8,128)(2,1)S(1)}, bf16[32,7168]{1,0:T(8,128)(2,1)S(1)}, u32[]{:S(2)}, u32[]{:S(2)}) collective-permute-start(bf16[32,7168]{1,0:T(8,128)(2,1)S(1)} %add_convert_fusion.6), channel_id=1, source_target_pairs={{0,1},{1,2},{2,3},{4,5},{5,6},{6,7},{8,9},{9,10},{10,11},{12,13},{... | collective-permute-start | bytes 1376264 | tf_op jit(solution)/shard_map/ppermute | solution.py:309
  306.7 13.1 %collective-permute-start.28 = (bf16[32,7168]{1,0:T(8,128)(2,1)S(1)}, bf16[32,7168]{1,0:T(8,128)(2,1)S(1)}, u32[]{:S(2)}, u32[]{:S(2)}) collective-permute-start(bf16[32,7168]{1,0:T(8,128)(2,1)S(1)} %add_convert_fusion.4), channel_id=1, source_target_pairs={{0,1},{1,2},{2,3},{4,5},{5,6},{6,7},{8,9},{9,10},{10,11},{12,13},{... | collective-permute-start | bytes 1376264 | tf_op jit(solution)/shard_map/ppermute | solution.py:309
  315.1 12.8 %collective-permute-start.25 = (bf16[32,7168]{1,0:T(8,128)(2,1)S(1)}, bf16[32,7168]{1,0:T(8,128)(2,1)S(1)}, u32[]{:S(2)}, u32[]{:S(2)}) collective-permute-start(bf16[32,7168]{1,0:T(8,128)(2,1)S(1)} %fusion.8), channel_id=1, source_target_pairs={{16,0},{0,16},{17,1},{1,17},{18,2},{2,18},{19,3},{3,19},{20,4},{4,... | collective-permute-start | bytes 1376264 | tf_op jit(solution)/shard_map/ppermute | solution.py:30
  328.1 8.5 %collective-permute-start.32 = (bf16[32,7168]{1,0:T(8,128)(2,1)S(1)}, bf16[32,7168]{1,0:T(8,128)(2,1)S(1)}, u32[]{:S(2)}, u32[]{:S(2)}) collective-permute-start(bf16[32,7168]{1,0:T(8,128)(2,1)S(1)} %fusion.7), channel_id=1, source_target_pairs={{16,0},{0,16},{17,1},{1,17},{18,2},{2,18},{19,3},{3,19},{20,4},{4,... | collective-permute-start | bytes 1376264 | tf_op jit(solution)/shard_map/ppermute | solution.py:30
  (12 other events, 71.6 us)
Sparse Core Ops, SparseCore 0:
  11.0 97.7 all-gather.2

commit v9 on v8

--- a/solution.py
+++ b/solution.py
@@ -250,16 +250,16 @@
         put_blocks(outs, total)
 
 
-def backward_call(at, x_gathered, rows, parts, hops, gate_ups, downs):
-    count, width = x_gathered.shape[0], hops[0][0].shape[1]
+def backward_call(at, x_gathered, rows, parts, hops_x, hops_scaled, gate_ups, downs):
+    count, width = x_gathered.shape[0], hops_x[0][0].shape[1]
     pieces, hid = len(downs), downs[0].shape[0]
     chunk = chunk_of(width, 1792)
     steps, hidden, many = width // chunk, pieces * hid, count * rows
     first = lambda i: jnp.minimum(i, steps - 1)
     second = lambda i: jnp.maximum(i - steps, 0)
     _, tags, tag_specs = gathered_input(x_gathered, 0, rows)
-    _, rows_in, row_specs = chained_input(hops, 0, rows)
-    _, _, scaled_specs = chained_input(hops, rows, rows)
+    _, rows_in, row_specs = chained_input(hops_x, 0, rows)
+    _, scaled_in, scaled_specs = chained_input(hops_scaled, 0, rows)
     return pl.pallas_call(
         functools.partial(backward_kernel, len(rows_in), count, pieces, chunk, steps),
         grid_spec=pltpu.PrefetchScalarGridSpec(
@@ -281,7 +281,7 @@
         out_shape=home_shapes(count, rows, width, parts),
         compiler_params=compiler_params(),
         cost_estimate=small_cost(many, hidden),
-    )(at, *tags, *rows_in, *rows_in, *gate_ups, *downs)
+    )(at, *tags, *rows_in, *scaled_in, *gate_ups, *downs)
 
 
 def after(value, *earlier):
@@ -340,29 +340,33 @@
         axis=1,
     )
     scaled_grad = (prob_backward[0][:, None] * grad_output[0].astype(F32)).astype(BF16)
-    back_rows = jnp.concatenate([x_backward[0], scaled_grad], axis=0)
     gate_up, down = jnp.concatenate([w_gate[0], w_up[0]], axis=0), w_down[0, 0]
 
     x_gathered = lax.all_gather(tagged, "dp")
     across_down = flipped(down, "expert", 2)
-    gate_up, back_rows = after((gate_up, back_rows), across_down)
-    across_gate_up = flipped(gate_up, "expert", 2)
-    hops = [(back_rows, back_rows)]
-    for step in range(1, count):
-        hops.append(hop(*hops[-1], "dp", step))
-    gate_ups = [gate_up, flipped(after(gate_up, hops[1]), "expert", 1), across_gate_up]
+    first_scaled = after(scaled_grad, across_down)
+    hops_scaled = [(first_scaled, first_scaled)]
+    own_flip = flipped(gate_up, "expert", 1)
+    across_gate_up = flipped(after(gate_up, across_down, own_flip), "expert", 2)
+    hops_x = [(x_backward[0], x_backward[0])]
+    for hops in (hops_x, hops_scaled):
+        for step in range(1, count):
+            hops.append(hop(*hops[-1], "dp", step))
+    gate_ups = [gate_up, own_flip, across_gate_up]
     downs = [down, flipped(down, "expert", 1), across_down, flipped(across_down, "expert", 1)]
-    gate_ups.append(flipped(after(across_gate_up, x_gathered, hops[1], downs[1:]), "expert", 1))
+    gate_ups.append(flipped(after(across_gate_up, x_gathered, hops_x[2], hops_scaled[1]), "expert", 1))
     hidden_fwd = hidden_call(at, x_gathered, tokens_here, width, gate_ups)
     partial_fwd = down_call(hidden_fwd, count, downs)
 
     arrived_fwd = step_home(summands(partial_fwd, 1, None), "dp", 1)
-    arrived_fwd = after(arrived_fwd, hops[2])
+    arrived_fwd = after(arrived_fwd, hops_x[3], hops_scaled[2])
     arrived_fwd = step_home(summands(partial_fwd, 2, arrived_fwd), "dp", 2)
     sends_fwd = summands(partial_fwd, 3, arrived_fwd)
     arrived_fwd = step_home(sends_fwd, "dp", 3)
-    hops[0] = after(hops[0], sends_fwd)
-    partial_bwd = backward_call(at, x_gathered, tokens_here, ROW_PARTS, hops, gate_ups, downs)
+    hops_scaled[0] = (after(scaled_grad, sends_fwd),) * 2
+    partial_bwd = backward_call(
+        at, x_gathered, tokens_here, ROW_PARTS, hops_x, hops_scaled, gate_ups, downs
+    )
 
     arrived_fwd = after(arrived_fwd, partial_bwd[-1])
     total_fwd = summed(partial_fwd[0], arrived_fwd)

time: 346 us -> 359 us (1.038)
  starting transfers between devices: 56.8 us -> 72.8 us
    ppermute x6 -> x12, starting transfers between devices: 13.6 us -> 27.4 us  [hop(): return (lax.ppermute(below, axis, up), lax.ppermute(above, axis, down))]
    ppermute x6 -> x12, waiting for transfers between devices: 98.1 us -> 86.9 us  [hop(): return (lax.ppermute(below, axis, up), lax.ppermute(above, axis, down))]
    ppermute x9, waiting for transfers between devices: 49.3 us -> 59.1 us  [step_home(): lax.ppermute(pair[1], axis, [(i, i - 1) for i in range(count - step, coun...]
    unnamed x53 -> x61, local copies, waits for them, and re-layouts: 7.78 us -> 5.59 us
  transfers between devices with their start and end apart: 34 -> 40, of which waited for: 18 -> 19; matrix products, arithmetic and copies ran while one was open for 2% -> 2% of each run, Pallas kernels for 11% -> 11%
where the time goes in v9:
time: 359 us; the launch traced here: 358 us
  waiting for transfers between devices  212 us (59%)
  starting transfers between devices  72.8 us (20%)
  Pallas kernels  38.5 us (11%)
  between operations  14.7 us (4%)
  other arithmetic  12.9 us (4%)
  local copies, waits for them, and re-layouts  6.85 us (2%)
    ppermute x12, waiting for transfers between devices, hop(): return (lax.ppermute(below, axis, up), lax.ppermute(above, axis, down))  86.9 us
    ppermute x9, waiting for transfers between devices, step_home(): lax.ppermute(pair[1], axis, [(i, i - 1) for i in range(count - step, coun...  59.1 us
    ppermute x6, waiting for transfers between devices, flipped(): return lax.ppermute(block, axis, route)  44.8 us
    ppermute x9, starting transfers between devices, step_home(): lax.ppermute(pair[1], axis, [(i, i - 1) for i in range(count - step, coun...  28 us
    ppermute x12, starting transfers between devices, hop(): return (lax.ppermute(below, axis, up), lax.ppermute(above, axis, down))  27.4 us
    pallas_call x1, Pallas kernels, backward_call(): pl.pallas_call(functools.partial(backward_kernel, len(rows_in), count, pi...  21.4 us
    ppermute x3, waiting for transfers between devices, shifted(): lax.ppermute(block, axis, [((i - distance) % count, i) for i in range(cou...  14.9 us
    ppermute x9, starting transfers between devices, step_home(): up = lax.ppermute(pair[0], axis, [(i, i + 1) for i in range(step)])  12 us
  transfers between devices with their start and end apart: 40, of which 19 were waited for; matrix products, arithmetic and copies ran while one was open for 2% of the time, Pallas kernels for 11%

profile of v9, /device:TPU:20, one launch (start us, length us, event | category | flops | bytes accessed | tf_op | source)
XLA Modules:
  0.0 357.7 jit_solution(9625761106821851408)
XLA Ops:
  7.2 4.3 %pad_maximum_fusion.refs_8_.refs_18_ = bf16[2,7168,128]{2,1,0:T(8,128)(2,1)} fusion(bf16[1,7168,128]{2,1,0:T(8,128)(2,1)} %bitcast.44, bf16[1,7168,128]{2,1,0:T(8,128)(2,1)} %bitcast.45), kind=kLoop, calls=%fused_computation | loop fusion | flops 1835008 | bytes 7340032 | tf_op jit(solution)/shard_map/concatenate | solution.py:343
  13.4 1.5 collective-permute-start.1
  14.9 40.5 %collective-permute-done.1.refs_2_.refs_24_ = bf16[128,7168]{1,0:T(8,128)(2,1)S(1)} collective-permute-done((bf16[128,7168]{1,0:T(8,128)(2,1)S(1)}, bf16[128,7168]{1,0:T(8,128)(2,1)S(1)}, u32[]{:S(2)}, u32[]{:S(2)}) %collective-permute-start.1) | collective-permute-done | bytes 1835040 | tf_op jit(solution)/shard_map/ppermute | solution.py:25
  56.6 1.5 collective-permute-start.2
  58.1 2.3 collective-permute-start.5
  60.5 3.5 collective-permute-start.3
  64.0 1.4 fusion.2.refs_11_
  65.5 38.3 %collective-permute-done.5.refs_8_ = bf16[64,7168]{1,0:T(8,128)(2,1)S(1)} collective-permute-done((bf16[64,7168]{1,0:T(8,128)(2,1)}, bf16[64,7168]{1,0:T(8,128)(2,1)S(1)}, u32[]{:S(2)}, u32[]{:S(2)}) %collective-permute-start.5) | collective-permute-done | bytes 917536 | tf_op jit(solution)/shard_map/ppermute | solution.py:295
  103.8 4.3 %collective-permute-start.6 = (bf16[64,7168]{1,0:T(8,128)(2,1)S(1)}, bf16[64,7168]{1,0:T(8,128)(2,1)S(1)}, u32[]{:S(2)}, u32[]{:S(2)}) collective-permute-start(bf16[64,7168]{1,0:T(8,128)(2,1)S(1)} %collective-permute-done.5.refs_8_), channel_id=1, source_target_pairs={{1,0},{2,1},{5,4},{6,5},{9,8},{10,9},{13,12},{14,13},{17,16},{18,1... | collective-permute-start | bytes 2752520 | tf_op jit(solution)/shard_map/ppermute | solution.py:295
  108.1 1.9 collective-permute-start.4
  110.1 4.0 %collective-permute-start.8 = (bf16[64,7168]{1,0:T(8,128)(2,1)S(1)}, bf16[64,7168]{1,0:T(8,128)(2,1)S(1)}, u32[]{:S(2)}, u32[]{:S(2)}) collective-permute-start(bf16[64,7168]{1,0:T(8,128)(2,1)S(1)} %fusion.2.refs_11_), channel_id=1, source_target_pairs={{1,0},{2,1},{3,2},{5,4},{6,5},{7,6},{9,8},{10,9},{11,10},{13,12},{... | collective-permute-start | bytes 2752520 | tf_op jit(solution)/shard_map/ppermute | solution.py:295
  114.0 1.9 collective-permute-start.7
  116.0 12.8 %collective-permute-done.6.refs_9_ = bf16[64,7168]{1,0:T(8,128)(2,1)S(1)} collective-permute-done((bf16[64,7168]{1,0:T(8,128)(2,1)S(1)}, bf16[64,7168]{1,0:T(8,128)(2,1)S(1)}, u32[]{:S(2)}, u32[]{:S(2)}) %collective-permute-start.6) | collective-permute-done | bytes 917536 | tf_op jit(solution)/shard_map/ppermute | solution.py:295
  128.7 4.5 %collective-permute-done.4.refs_6_ = bf16[64,7168]{1,0:T(8,128)(2,1)S(1)} collective-permute-done((bf16[64,7168]{1,0:T(8,128)(2,1)S(1)}, bf16[64,7168]{1,0:T(8,128)(2,1)S(1)}, u32[]{:S(2)}, u32[]{:S(2)}) %collective-permute-start.4) | collective-permute-done | bytes 917536 | tf_op jit(solution)/shard_map/ppermute | solution.py:295
  133.3 14.3 %collective-permute-done.8.refs_15_ = bf16[64,7168]{1,0:T(8,128)(2,1)S(1)} collective-permute-done((bf16[64,7168]{1,0:T(8,128)(2,1)S(1)}, bf16[64,7168]{1,0:T(8,128)(2,1)S(1)}, u32[]{:S(2)}, u32[]{:S(2)}) %collective-permute-start.8) | collective-permute-done | bytes 917536 | tf_op jit(solution)/shard_map/ppermute | solution.py:295
  148.6 3.3 collective-permute-done.7.refs_12_
  152.5 1.6 collective-permute-start.15
  154.7 2.2 collective-permute-start.14
  156.9 4.4 %collective-permute-done.9.refs_11_.refs_21_ = bf16[2,7168,128]{2,1,0:T(8,128)(2,1)} collective-permute-done((bf16[2,7168,128]{2,1,0:T(8,128)(2,1)}, bf16[2,7168,128]{2,1,0:T(8,128)(2,1)}, u32[]{:S(2)}, u32[]{:S(2)}) %collective-permute-start.9) | collective-permute-done | bytes 3670048 | tf_op jit(solution)/shard_map/ppermute | solution.py:25
  161.3 1.4 collective-permute-start.17
  162.7 10.3 %shard_map.113.hidden_ref = bf16[256,512]{1,0:T(8,128)(2,1)} custom-call(s32[2]{0:T(128)} %pad_add_fusion.at_ref, bf16[4,64,7296]{2,1,0:T(8,128)(2,1)} %bitcast.27, bf16[4,64,7296]{2,1,0:T(8,128)(2,1)} %bitcast.28, bf16[4,64,7296]{2,1,0:T(8,128)(2,1)} %bitcast.29, bf16[4,64,7296]{2,1,0:T(8,128)(2,1)} %bitcast.30, bf16[4,64,7296]{2,1,0:T(8,128)(2,1)} %bitcast.31, ...), custom_call_target="tpu_custom_call" | custom-call | flops 131072 | bytes 256 | tf_op jit(solution)/shard_map/pallas_call | solution.py:158
  172.9 1.9 collective-permute-start.16
  174.9 6.9 %shard_map.114 = (f32[64,7168]{1,0:T(8,128)}, bf16[64,7168]{1,0:T(8,128)(2,1)}, bf16[64,7168]{1,0:T(8,128)(2,1)}, bf16[64,7168]{1,0:T(8,128)(2,1)}) custom-call(bf16[256,512]{1,0:T(8,128)(2,1)} %shard_map.113.hidden_ref, bf16[128,7168]{1,0:T(8,128)(2,1)} %bitcast.39, bf16[128,7168]{1,0:T(8,128)(2,1)} %collective-permute-done.10.refs_1_.refs_23_, ...), custom_call_target="tpu_custom_call" | custom-call | flops 131072 | bytes 256 | tf_op jit(solution)/shard_map/pallas_call | solution.py:185
  183.8 13.6 %collective-permute-done.16.refs_13_ = bf16[64,7168]{1,0:T(8,128)(2,1)S(1)} collective-permute-done((bf16[64,7168]{1,0:T(8,128)(2,1)}, bf16[64,7168]{1,0:T(8,128)(2,1)S(1)}, u32[]{:S(2)}, u32[]{:S(2)}) %collective-permute-start.16) | collective-permute-done | bytes 917536 | tf_op jit(solution)/shard_map/ppermute | solution.py:295
  197.4 8.8 %collective-permute-done.13 = bf16[64,7168]{1,0:T(8,128)(2,1)S(1)} collective-permute-done((bf16[64,7168]{1,0:T(8,128)(2,1)}, bf16[64,7168]{1,0:T(8,128)(2,1)S(1)}, u32[]{:S(2)}, u32[]{:S(2)}) %collective-permute-start.13) | collective-permute-done | bytes 917536 | tf_op jit(solution)/shard_map/ppermute | solution.py:310
  206.2 1.7 fusion.1
  207.9 4.6 %collective-permute-start.20 = (bf16[64,7168]{1,0:T(8,128)(2,1)S(1)}, bf16[64,7168]{1,0:T(8,128)(2,1)S(1)}, u32[]{:S(2)}, u32[]{:S(2)}) collective-permute-start(bf16[64,7168]{1,0:T(8,128)(2,1)S(1)} %get-tuple-element.70), channel_id=1, source_target_pairs={{2,1},{3,2},{6,5},{7,6},{10,9},{11,10},{14,13},{15,14},{18,17},{19... | collective-permute-start | bytes 2752520 | tf_op jit(solution)/shard_map/ppermute | solution.py:310
  213.2 1.5 collective-permute-start.22
  214.7 1.3 collective-permute-start.18
  216.0 15.4 %collective-permute-done.20 = bf16[64,7168]{1,0:T(8,128)(2,1)S(1)} collective-permute-done((bf16[64,7168]{1,0:T(8,128)(2,1)S(1)}, bf16[64,7168]{1,0:T(8,128)(2,1)S(1)}, u32[]{:S(2)}, u32[]{:S(2)}) %collective-permute-start.20) | collective-permute-done | bytes 917536 | tf_op jit(solution)/shard_map/ppermute | solution.py:310
  232.5 4.1 %collective-permute-start.21 = (bf16[64,7168]{1,0:T(8,128)(2,1)}, bf16[64,7168]{1,0:T(8,128)(2,1)S(1)}, u32[]{:S(2)}, u32[]{:S(2)}) collective-permute-start(bf16[64,7168]{1,0:T(8,128)(2,1)} %add_convert_fusion.1), channel_id=1, source_target_pairs={{1,0},{2,1},{3,2},{5,4},{6,5},{7,6},{9,8},{10,9},{11,10},{13,12},{... | collective-permute-start | bytes 2752520 | tf_op jit(solution)/shard_map/ppermute | solution.py:310
  238.7 2.0 collective-permute-start.19
  242.6 21.4 %shard_map.115 = (f32[32,7168]{1,0:T(8,128)}, f32[32,7168]{1,0:T(8,128)}, bf16[32,7168]{1,0:T(8,128)(2,1)}, bf16[32,7168]{1,0:T(8,128)(2,1)}, bf16[32,7168]{1,0:...) custom-call(s32[2]{0:T(128)} %pad_add_fusion.at_ref, ...), custom_call_target="tpu_custom_call" | custom-call | flops 131072 | bytes 256 | tf_op jit(solution)/shard_map/pallas_call | solution.py:263
  264.0 1.3 collective-permute-start.27
  269.2 17.0 %collective-permute-done.35 = bf16[32,7168]{1,0:T(8,128)(2,1)S(1)} collective-permute-done((bf16[32,7168]{1,0:T(8,128)(2,1)}, bf16[32,7168]{1,0:T(8,128)(2,1)S(1)}, u32[]{:S(2)}, u32[]{:S(2)}) %collective-permute-start.35) | collective-permute-done | bytes 458784 | tf_op jit(solution)/shard_map/ppermute | solution.py:310
  286.3 4.5 %collective-permute-start.36 = (bf16[32,7168]{1,0:T(8,128)(2,1)S(1)}, bf16[32,7168]{1,0:T(8,128)(2,1)S(1)}, u32[]{:S(2)}, u32[]{:S(2)}) collective-permute-start(bf16[32,7168]{1,0:T(8,128)(2,1)S(1)} %get-tuple-element.74), channel_id=1, source_target_pairs={{2,1},{3,2},{6,5},{7,6},{10,9},{11,10},{14,13},{15,14},{18,17},{19... | collective-permute-start | bytes 1376264 | tf_op jit(solution)/shard_map/ppermute | solution.py:310
  291.0 2.1 collective-permute-start.28
  294.4 1.4 collective-permute-start.33
  295.8 6.0 %collective-permute-done.36 = bf16[32,7168]{1,0:T(8,128)(2,1)S(1)} collective-permute-done((bf16[32,7168]{1,0:T(8,128)(2,1)S(1)}, bf16[32,7168]{1,0:T(8,128)(2,1)S(1)}, u32[]{:S(2)}, u32[]{:S(2)}) %collective-permute-start.36) | collective-permute-done | bytes 458784 | tf_op jit(solution)/shard_map/ppermute | solution.py:310
  301.9 4.5 %collective-permute-start.37 = (bf16[32,7168]{1,0:T(8,128)(2,1)S(1)}, bf16[32,7168]{1,0:T(8,128)(2,1)S(1)}, u32[]{:S(2)}, u32[]{:S(2)}) collective-permute-start(bf16[32,7168]{1,0:T(8,128)(2,1)S(1)} %add_convert_fusion.3), channel_id=1, source_target_pairs={{1,0},{2,1},{3,2},{5,4},{6,5},{7,6},{9,8},{10,9},{11,10},{13,12},{... | collective-permute-start | bytes 1376264 | tf_op jit(solution)/shard_map/ppermute | solution.py:310
  306.4 5.2 %collective-permute-done.28 = bf16[32,7168]{1,0:T(8,128)(2,1)S(1)} collective-permute-done((bf16[32,7168]{1,0:T(8,128)(2,1)S(1)}, bf16[32,7168]{1,0:T(8,128)(2,1)S(1)}, u32[]{:S(2)}, u32[]{:S(2)}) %collective-permute-start.28) | collective-permute-done | bytes 458784 | tf_op jit(solution)/shard_map/ppermute | solution.py:310
  311.9 4.5 %collective-permute-start.30 = (bf16[32,7168]{1,0:T(8,128)(2,1)S(1)}, bf16[32,7168]{1,0:T(8,128)(2,1)S(1)}, u32[]{:S(2)}, u32[]{:S(2)}) collective-permute-start(bf16[32,7168]{1,0:T(8,128)(2,1)S(1)} %add_convert_fusion.5), channel_id=1, source_target_pairs={{1,0},{2,1},{3,2},{5,4},{6,5},{7,6},{9,8},{10,9},{11,10},{13,12},{... | collective-permute-start | bytes 1376264 | tf_op jit(solution)/shard_map/ppermute | solution.py:310
  316.4 1.9 collective-permute-start.29
  318.4 1.9 collective-permute-start.34
  320.4 6.7 %collective-permute-done.30 = bf16[32,7168]{1,0:T(8,128)(2,1)S(1)} collective-permute-done((bf16[32,7168]{1,0:T(8,128)(2,1)S(1)}, bf16[32,7168]{1,0:T(8,128)(2,1)S(1)}, u32[]{:S(2)}, u32[]{:S(2)}) %collective-permute-start.30) | collective-permute-done | bytes 458784 | tf_op jit(solution)/shard_map/ppermute | solution.py:310
  329.1 4.1 %collective-permute-done.34 = bf16[32,7168]{1,0:T(8,128)(2,1)S(1)} collective-permute-done((bf16[32,7168]{1,0:T(8,128)(2,1)S(1)}, bf16[32,7168]{1,0:T(8,128)(2,1)S(1)}, u32[]{:S(2)}, u32[]{:S(2)}) %collective-permute-start.34) | collective-permute-done | bytes 458784 | tf_op jit(solution)/shard_map/ppermute | solution.py:309
  333.2 7.0 %collective-permute-done.31 = bf16[32,7168]{1,0:T(8,128)(2,1)S(1)} collective-permute-done((bf16[32,7168]{1,0:T(8,128)(2,1)S(1)}, bf16[32,7168]{1,0:T(8,128)(2,1)S(1)}, u32[]{:S(2)}, u32[]{:S(2)}) %collective-permute-start.31) | collective-permute-done | bytes 458784 | tf_op jit(solution)/shard_map/ppermute | solution.py:30
  341.0 7.9 %collective-permute-done.38 = bf16[32,7168]{1,0:T(8,128)(2,1)S(1)} collective-permute-done((bf16[32,7168]{1,0:T(8,128)(2,1)S(1)}, bf16[32,7168]{1,0:T(8,128)(2,1)S(1)}, u32[]{:S(2)}, u32[]{:S(2)}) %collective-permute-start.38) | collective-permute-done | bytes 458784 | tf_op jit(solution)/shard_map/ppermute | solution.py:30
  (118 shorter events, 23.6 us)
Async XLA Ops:
  7.2 144.7 %all-gather.3.cloned.1.call-start = ((), (), s32[]{:S(2)}) async-start(), calls=%async_computation | async-start | bytes 4669440 | tf_op jit(solution)/shard_map/all_gather | solution.py:345
  11.5 52.5 %copy-start.27 = (f32[1,64]{1,0:T(1,128)S(1)}, f32[1,64]{1,0:T(1,128)}, u32[]{:S(2)}) copy-start(f32[1,64]{1,0:T(1,128)} %param.15) | copy-start | bytes 772
  11.5 45.1 %collective-permute-start = (bf16[2,7168,128]{2,1,0:T(8,128)(2,1)}, bf16[2,7168,128]{2,1,0:T(8,128)(2,1)}, u32[]{:S(2)}, u32[]{:S(2)}) collective-permute-start(bf16[2,7168,128]{2,1,0:T(8,128)(2,1)} %pad_maximum_fusion.refs_8_.refs_18_), channel_id=1, source_target_pairs={{0,4},{4,0},{8,12},{12,8},{1,5},{5,1},{9,13},{13,9},{2,6},{6,2},{1... | collective-permute-start | bytes 11010056 | tf_op jit(solution)/shard_map/ppermute | solution.py:25
  13.4 42.0 %collective-permute-start.1 = (bf16[128,7168]{1,0:T(8,128)(2,1)S(1)}, bf16[128,7168]{1,0:T(8,128)(2,1)S(1)}, u32[]{:S(2)}, u32[]{:S(2)}) collective-permute-start(bf16[128,7168]{1,0:T(8,128)(2,1)S(1)} %bitcast.41), channel_id=1, source_target_pairs={{0,8},{4,12},{8,0},{12,4},{1,9},{5,13},{9,1},{13,5},{2,10},{6,14},... | collective-permute-start | bytes 5505032 | tf_op jit(solution)/shard_map/ppermute | solution.py:25
  56.6 95.3 %collective-permute-start.2 = (bf16[2,7168,128]{2,1,0:T(8,128)(2,1)}, bf16[2,7168,128]{2,1,0:T(8,128)(2,1)}, u32[]{:S(2)}, u32[]{:S(2)}) collective-permute-start(bf16[2,7168,128]{2,1,0:T(8,128)(2,1)} %pad_maximum_fusion.refs_8_.refs_18_), channel_id=1, source_target_pairs={{0,8},{4,12},{8,0},{12,4},{1,9},{5,13},{9,1},{13,5},{2,10},{6,14},... | collective-permute-start | bytes 11010056 | tf_op jit(solution)/shard_map/ppermute | solution.py:25
  58.1 45.6 %collective-permute-start.5 = (bf16[64,7168]{1,0:T(8,128)(2,1)}, bf16[64,7168]{1,0:T(8,128)(2,1)S(1)}, u32[]{:S(2)}, u32[]{:S(2)}) collective-permute-start(bf16[64,7168]{1,0:T(8,128)(2,1)} %bitcast.47), channel_id=1, source_target_pairs={{1,0},{2,1},{3,2},{5,4},{6,5},{7,6},{9,8},{10,9},{11,10},{13,12},{... | collective-permute-start | bytes 2752520 | tf_op jit(solution)/shard_map/ppermute | solution.py:295
  60.5 47.6 %collective-permute-start.3 = (bf16[64,7168]{1,0:T(8,128)(2,1)}, bf16[64,7168]{1,0:T(8,128)(2,1)S(1)}, u32[]{:S(2)}, u32[]{:S(2)}) collective-permute-start(bf16[64,7168]{1,0:T(8,128)(2,1)} %bitcast.48), channel_id=1, source_target_pairs={{0,1},{1,2},{2,3},{4,5},{5,6},{6,7},{8,9},{9,10},{10,11},{12,13},{... | collective-permute-start | bytes 2752520 | tf_op jit(solution)/shard_map/ppermute | solution.py:295
  65.4 48.6 %copy-start.4 = (bf16[64,7168]{1,0:T(8,128)(2,1)}, bf16[64,7168]{1,0:T(8,128)(2,1)S(1)}, u32[]{:S(2)}) copy-start(bf16[64,7168]{1,0:T(8,128)(2,1)S(1)} %fusion.2.refs_11_) | copy-start | bytes 2752516
  103.8 43.8 %copy-start.6 = (bf16[64,7168]{1,0:T(8,128)(2,1)}, bf16[64,7168]{1,0:T(8,128)(2,1)S(1)}, u32[]{:S(2)}) copy-start(bf16[64,7168]{1,0:T(8,128)(2,1)S(1)} %collective-permute-done.5.refs_8_) | copy-start | bytes 2752516
  103.8 25.0 %collective-permute-start.6 = (bf16[64,7168]{1,0:T(8,128)(2,1)S(1)}, bf16[64,7168]{1,0:T(8,128)(2,1)S(1)}, u32[]{:S(2)}, u32[]{:S(2)}) collective-permute-start(bf16[64,7168]{1,0:T(8,128)(2,1)S(1)} %collective-permute-done.5.refs_8_), channel_id=1, source_target_pairs={{1,0},{2,1},{5,4},{6,5},{9,8},{10,9},{13,12},{14,13},{17,16},{18,1... | collective-permute-start | bytes 2752520 | tf_op jit(solution)/shard_map/ppermute | solution.py:295
  108.1 39.5 %copy-start.7 = (bf16[64,7168]{1,0:T(8,128)(2,1)}, bf16[64,7168]{1,0:T(8,128)(2,1)S(1)}, u32[]{:S(2)}) copy-start(bf16[64,7168]{1,0:T(8,128)(2,1)S(1)} %collective-permute-done.3.refs_5_) | copy-start | bytes 2752516
  108.1 25.1 %collective-permute-start.4 = (bf16[64,7168]{1,0:T(8,128)(2,1)S(1)}, bf16[64,7168]{1,0:T(8,128)(2,1)S(1)}, u32[]{:S(2)}, u32[]{:S(2)}) collective-permute-start(bf16[64,7168]{1,0:T(8,128)(2,1)S(1)} %collective-permute-done.3.refs_5_), channel_id=1, source_target_pairs={{1,2},{2,3},{5,6},{6,7},{9,10},{10,11},{13,14},{14,15},{17,18},{18... | collective-permute-start | bytes 2752520 | tf_op jit(solution)/shard_map/ppermute | solution.py:295
  110.1 37.5 %collective-permute-start.8 = (bf16[64,7168]{1,0:T(8,128)(2,1)S(1)}, bf16[64,7168]{1,0:T(8,128)(2,1)S(1)}, u32[]{:S(2)}, u32[]{:S(2)}) collective-permute-start(bf16[64,7168]{1,0:T(8,128)(2,1)S(1)} %fusion.2.refs_11_), channel_id=1, source_target_pairs={{1,0},{2,1},{3,2},{5,4},{6,5},{7,6},{9,8},{10,9},{11,10},{13,12},{... | collective-permute-start | bytes 2752520 | tf_op jit(solution)/shard_map/ppermute | solution.py:295
  114.0 37.8 %collective-permute-start.7 = (bf16[64,7168]{1,0:T(8,128)(2,1)S(1)}, bf16[64,7168]{1,0:T(8,128)(2,1)}, u32[]{:S(2)}, u32[]{:S(2)}) collective-permute-start(bf16[64,7168]{1,0:T(8,128)(2,1)S(1)} %fusion.2.refs_11_), channel_id=1, source_target_pairs={{0,1},{1,2},{2,3},{4,5},{5,6},{6,7},{8,9},{9,10},{10,11},{12,13},{... | collective-permute-start | bytes 2752520 | tf_op jit(solution)/shard_map/ppermute | solution.py:295
  151.9 9.4 %collective-permute-start.9 = (bf16[2,7168,128]{2,1,0:T(8,128)(2,1)}, bf16[2,7168,128]{2,1,0:T(8,128)(2,1)}, u32[]{:S(2)}, u32[]{:S(2)}) collective-permute-start(bf16[2,7168,128]{2,1,0:T(8,128)(2,1)} %collective-permute-done.2.refs_10_.refs_20_), channel_id=1, source_target_pairs={{0,4},{4,0},{8,12},{12,8},{1,5},{5,1},{9,13},{13,9},{2,6},{6,2},{1... | collective-permute-start | bytes 11010056 | tf_op jit(solution)/shard_map/ppermute | solution.py:25
  151.9 21.0 %collective-permute-start.10 = (bf16[128,7168]{1,0:T(8,128)(2,1)S(1)}, bf16[128,7168]{1,0:T(8,128)(2,1)}, u32[]{:S(2)}, u32[]{:S(2)}) collective-permute-start(bf16[128,7168]{1,0:T(8,128)(2,1)S(1)} %bitcast.42), channel_id=1, source_target_pairs={{0,4},{4,0},{8,12},{12,8},{1,5},{5,1},{9,13},{13,9},{2,6},{6,2},{1... | collective-permute-start | bytes 5505032 | tf_op jit(solution)/shard_map/ppermute | solution.py:25
  152.4 22.5 %collective-permute-start.11 = (bf16[128,7168]{1,0:T(8,128)(2,1)}, bf16[128,7168]{1,0:T(8,128)(2,1)}, u32[]{:S(2)}, u32[]{:S(2)}) collective-permute-start(bf16[128,7168]{1,0:T(8,128)(2,1)} %copy-done.1), channel_id=1, source_target_pairs={{0,4},{4,0},{8,12},{12,8},{1,5},{5,1},{9,13},{13,9},{2,6},{6,2},{1... | collective-permute-start | bytes 5505032 | tf_op jit(solution)/shard_map/ppermute | solution.py:25
  152.5 30.5 %collective-permute-start.15 = (bf16[64,7168]{1,0:T(8,128)(2,1)}, bf16[64,7168]{1,0:T(8,128)(2,1)}, u32[]{:S(2)}, u32[]{:S(2)}) collective-permute-start(bf16[64,7168]{1,0:T(8,128)(2,1)} %copy-done.8), channel_id=1, source_target_pairs={{1,0},{5,4},{9,8},{13,12},{17,16},{21,20},{25,24},{29,28}} | collective-permute-start | bytes 2752520 | tf_op jit(solution)/shard_map/ppermute | solution.py:295
  154.7 29.1 %collective-permute-start.14 = (bf16[64,7168]{1,0:T(8,128)(2,1)}, bf16[64,7168]{1,0:T(8,128)(2,1)S(1)}, u32[]{:S(2)}, u32[]{:S(2)}) collective-permute-start(bf16[64,7168]{1,0:T(8,128)(2,1)} %copy-done.9), channel_id=1, source_target_pairs={{2,3},{6,7},{10,11},{14,15},{18,19},{22,23},{26,27},{30,31}} | collective-permute-start | bytes 2752520 | tf_op jit(solution)/shard_map/ppermute | solution.py:295
  161.3 22.5 %collective-permute-start.17 = (bf16[64,7168]{1,0:T(8,128)(2,1)}, bf16[64,7168]{1,0:T(8,128)(2,1)S(1)}, u32[]{:S(2)}, u32[]{:S(2)}) collective-permute-start(bf16[64,7168]{1,0:T(8,128)(2,1)} %copy-done.10), channel_id=1, source_target_pairs={{1,0},{2,1},{5,4},{6,5},{9,8},{10,9},{13,12},{14,13},{17,16},{18,1... | collective-permute-start | bytes 2752520 | tf_op jit(solution)/shard_map/ppermute | solution.py:295
  172.9 24.4 %collective-permute-start.16 = (bf16[64,7168]{1,0:T(8,128)(2,1)}, bf16[64,7168]{1,0:T(8,128)(2,1)S(1)}, u32[]{:S(2)}, u32[]{:S(2)}) collective-permute-start(bf16[64,7168]{1,0:T(8,128)(2,1)} %collective-permute-done.7.refs_12_), channel_id=1, source_target_pairs={{1,2},{2,3},{5,6},{6,7},{9,10},{10,11},{13,14},{14,15},{17,18},{18... | collective-permute-start | bytes 2752520 | tf_op jit(solution)/shard_map/ppermute | solution.py:295
  181.7 24.4 %collective-permute-start.13 = (bf16[64,7168]{1,0:T(8,128)(2,1)}, bf16[64,7168]{1,0:T(8,128)(2,1)S(1)}, u32[]{:S(2)}, u32[]{:S(2)}) collective-permute-start(bf16[64,7168]{1,0:T(8,128)(2,1)} %get-tuple-element.40), channel_id=1, source_target_pairs={{3,2},{7,6},{11,10},{15,14},{19,18},{23,22},{27,26},{31,30}} | collective-permute-start | bytes 2752520 | tf_op jit(solution)/shard_map/ppermute | solution.py:310
  183.0 23.1 %collective-permute-start.12 = (bf16[64,7168]{1,0:T(8,128)(2,1)}, bf16[64,7168]{1,0:T(8,128)(2,1)S(1)}, u32[]{:S(2)}, u32[]{:S(2)}) collective-permute-start(bf16[64,7168]{1,0:T(8,128)(2,1)} %get-tuple-element.42), channel_id=1, source_target_pairs={{0,1},{4,5},{8,9},{12,13},{16,17},{20,21},{24,25},{28,29}} | collective-permute-start | bytes 2752520 | tf_op jit(solution)/shard_map/ppermute | solution.py:309
  207.9 29.7 %copy-start.16 = (bf16[64,7168]{1,0:T(8,128)(2,1)S(1)}, bf16[64,7168]{1,0:T(8,128)(2,1)}, u32[]{:S(2)}) copy-start(bf16[64,7168]{1,0:T(8,128)(2,1)} %get-tuple-element.40) | copy-start | bytes 2752516
  207.9 23.5 %collective-permute-start.20 = (bf16[64,7168]{1,0:T(8,128)(2,1)S(1)}, bf16[64,7168]{1,0:T(8,128)(2,1)S(1)}, u32[]{:S(2)}, u32[]{:S(2)}) collective-permute-start(bf16[64,7168]{1,0:T(8,128)(2,1)S(1)} %get-tuple-element.70), channel_id=1, source_target_pairs={{2,1},{3,2},{6,5},{7,6},{10,9},{11,10},{14,13},{15,14},{18,17},{19... | collective-permute-start | bytes 2752520 | tf_op jit(solution)/shard_map/ppermute | solution.py:310
  212.4 28.3 %collective-permute-start.23 = (bf16[64,7168]{1,0:T(8,128)(2,1)S(1)}, bf16[64,7168]{1,0:T(8,128)(2,1)S(1)}, u32[]{:S(2)}, u32[]{:S(2)}) collective-permute-start(bf16[64,7168]{1,0:T(8,128)(2,1)S(1)} %collective-permute-done.17.refs_16_), channel_id=1, source_target_pairs={{1,0},{5,4},{9,8},{13,12},{17,16},{21,20},{25,24},{29,28}} | collective-permute-start | bytes 2752520 | tf_op jit(solution)/shard_map/ppermute | solution.py:295
  213.2 27.6 %collective-permute-start.22 = (bf16[64,7168]{1,0:T(8,128)(2,1)S(1)}, bf16[64,7168]{1,0:T(8,128)(2,1)S(1)}, u32[]{:S(2)}, u32[]{:S(2)}) collective-permute-start(bf16[64,7168]{1,0:T(8,128)(2,1)S(1)} %collective-permute-done.16.refs_13_), channel_id=1, source_target_pairs={{2,3},{6,7},{10,11},{14,15},{18,19},{22,23},{26,27},{30,31}} | collective-permute-start | bytes 2752520 | tf_op jit(solution)/shard_map/ppermute | solution.py:295
  214.7 22.8 %collective-permute-start.18 = (bf16[64,7168]{1,0:T(8,128)(2,1)S(1)}, bf16[64,7168]{1,0:T(8,128)(2,1)S(1)}, u32[]{:S(2)}, u32[]{:S(2)}) collective-permute-start(bf16[64,7168]{1,0:T(8,128)(2,1)S(1)} %get-tuple-element.71), channel_id=1, source_target_pairs={{0,1},{1,2},{4,5},{5,6},{8,9},{9,10},{12,13},{13,14},{16,17},{17,1... | collective-permute-start | bytes 2752520 | tf_op jit(solution)/shard_map/ppermute | solution.py:309
  232.5 31.5 %collective-permute-start.21 = (bf16[64,7168]{1,0:T(8,128)(2,1)}, bf16[64,7168]{1,0:T(8,128)(2,1)S(1)}, u32[]{:S(2)}, u32[]{:S(2)}) collective-permute-start(bf16[64,7168]{1,0:T(8,128)(2,1)} %add_convert_fusion.1), channel_id=1, source_target_pairs={{1,0},{2,1},{3,2},{5,4},{6,5},{7,6},{9,8},{10,9},{11,10},{13,12},{... | collective-permute-start | bytes 2752520 | tf_op jit(solution)/shard_map/ppermute | solution.py:310
  238.7 29.3 %copy-start.5 = (f32[64,7168]{1,0:T(8,128)S(1)}, f32[64,7168]{1,0:T(8,128)}, u32[]{:S(2)}) copy-start(f32[64,7168]{1,0:T(8,128)} %get-tuple-element.39) | copy-start | bytes 5505028
  238.7 29.3 %copy-start.26 = (f32[1,64]{1,0:T(1,128)S(1)}, f32[1,64]{1,0:T(1,128)}, u32[]{:S(2)}) copy-start(f32[1,64]{1,0:T(1,128)} %param.12) | copy-start | bytes 772
  238.7 25.3 %collective-permute-start.19 = (bf16[64,7168]{1,0:T(8,128)(2,1)}, bf16[64,7168]{1,0:T(8,128)(2,1)S(1)}, u32[]{:S(2)}, u32[]{:S(2)}) collective-permute-start(bf16[64,7168]{1,0:T(8,128)(2,1)} %add_convert_fusion.2), channel_id=1, source_target_pairs={{0,1},{1,2},{2,3},{4,5},{5,6},{6,7},{8,9},{9,10},{10,11},{12,13},{... | collective-permute-start | bytes 2752520 | tf_op jit(solution)/shard_map/ppermute | solution.py:309
  264.0 26.8 %collective-permute-start.27 = (bf16[32,7168]{1,0:T(8,128)(2,1)}, bf16[32,7168]{1,0:T(8,128)(2,1)S(1)}, u32[]{:S(2)}, u32[]{:S(2)}) collective-permute-start(bf16[32,7168]{1,0:T(8,128)(2,1)} %get-tuple-element.57), channel_id=1, source_target_pairs={{3,2},{7,6},{11,10},{15,14},{19,18},{23,22},{27,26},{31,30}} | collective-permute-start | bytes 1376264 | tf_op jit(solution)/shard_map/ppermute | solution.py:310
  265.3 25.5 %collective-permute-start.25 = (bf16[32,7168]{1,0:T(8,128)(2,1)}, bf16[32,7168]{1,0:T(8,128)(2,1)S(1)}, u32[]{:S(2)}, u32[]{:S(2)}) collective-permute-start(bf16[32,7168]{1,0:T(8,128)(2,1)} %get-tuple-element.59), channel_id=1, source_target_pairs={{0,1},{4,5},{8,9},{12,13},{16,17},{20,21},{24,25},{28,29}} | collective-permute-start | bytes 1376264 | tf_op jit(solution)/shard_map/ppermute | solution.py:309
  266.0 20.1 %collective-permute-start.35 = (bf16[32,7168]{1,0:T(8,128)(2,1)}, bf16[32,7168]{1,0:T(8,128)(2,1)S(1)}, u32[]{:S(2)}, u32[]{:S(2)}) collective-permute-start(bf16[32,7168]{1,0:T(8,128)(2,1)} %get-tuple-element.65), channel_id=1, source_target_pairs={{3,2},{7,6},{11,10},{15,14},{19,18},{23,22},{27,26},{31,30}} | collective-permute-start | bytes 1376264 | tf_op jit(solution)/shard_map/ppermute | solution.py:310
  267.3 18.8 %collective-permute-start.32 = (bf16[32,7168]{1,0:T(8,128)(2,1)}, bf16[32,7168]{1,0:T(8,128)(2,1)S(1)}, u32[]{:S(2)}, u32[]{:S(2)}) collective-permute-start(bf16[32,7168]{1,0:T(8,128)(2,1)} %get-tuple-element.67), channel_id=1, source_target_pairs={{0,1},{4,5},{8,9},{12,13},{16,17},{20,21},{24,25},{28,29}} | collective-permute-start | bytes 1376264 | tf_op jit(solution)/shard_map/ppermute | solution.py:309
  268.5 33.3 %copy-start.23 = (bf16[32,7168]{1,0:T(8,128)(2,1)S(1)}, bf16[32,7168]{1,0:T(8,128)(2,1)}, u32[]{:S(2)}) copy-start(bf16[32,7168]{1,0:T(8,128)(2,1)} %get-tuple-element.67) | copy-start | bytes 1376260
  268.5 43.1 %collective-permute-start.24 = (bf16[64,7168]{1,0:T(8,128)(2,1)S(1)}, bf16[64,7168]{1,0:T(8,128)(2,1)S(1)}, u32[]{:S(2)}, u32[]{:S(2)}) collective-permute-start(bf16[64,7168]{1,0:T(8,128)(2,1)S(1)} %add_convert_fusion), channel_id=1, source_target_pairs={{16,0},{0,16},{17,1},{1,17},{18,2},{2,18},{19,3},{3,19},{20,4},{4,... | collective-permute-start | bytes 2752520 | tf_op jit(solution)/shard_map/ppermute | solution.py:30
  286.3 15.5 %collective-permute-start.36 = (bf16[32,7168]{1,0:T(8,128)(2,1)S(1)}, bf16[32,7168]{1,0:T(8,128)(2,1)S(1)}, u32[]{:S(2)}, u32[]{:S(2)}) collective-permute-start(bf16[32,7168]{1,0:T(8,128)(2,1)S(1)} %get-tuple-element.74), channel_id=1, source_target_pairs={{2,1},{3,2},{6,5},{7,6},{10,9},{11,10},{14,13},{15,14},{18,17},{19... | collective-permute-start | bytes 1376264 | tf_op jit(solution)/shard_map/ppermute | solution.py:310
  291.0 20.6 %collective-permute-start.28 = (bf16[32,7168]{1,0:T(8,128)(2,1)S(1)}, bf16[32,7168]{1,0:T(8,128)(2,1)S(1)}, u32[]{:S(2)}, u32[]{:S(2)}) collective-permute-start(bf16[32,7168]{1,0:T(8,128)(2,1)S(1)} %get-tuple-element.72), channel_id=1, source_target_pairs={{2,1},{3,2},{6,5},{7,6},{10,9},{11,10},{14,13},{15,14},{18,17},{19... | collective-permute-start | bytes 1376264 | tf_op jit(solution)/shard_map/ppermute | solution.py:310
  293.1 18.6 %collective-permute-start.26 = (bf16[32,7168]{1,0:T(8,128)(2,1)S(1)}, bf16[32,7168]{1,0:T(8,128)(2,1)S(1)}, u32[]{:S(2)}, u32[]{:S(2)}) collective-permute-start(bf16[32,7168]{1,0:T(8,128)(2,1)S(1)} %get-tuple-element.73), channel_id=1, source_target_pairs={{0,1},{1,2},{4,5},{5,6},{8,9},{9,10},{12,13},{13,14},{16,17},{17,1... | collective-permute-start | bytes 1376264 | tf_op jit(solution)/shard_map/ppermute | solution.py:309
  294.4 23.9 %collective-permute-start.33 = (bf16[32,7168]{1,0:T(8,128)(2,1)S(1)}, bf16[32,7168]{1,0:T(8,128)(2,1)S(1)}, u32[]{:S(2)}, u32[]{:S(2)}) collective-permute-start(bf16[32,7168]{1,0:T(8,128)(2,1)S(1)} %get-tuple-element.75), channel_id=1, source_target_pairs={{0,1},{1,2},{4,5},{5,6},{8,9},{9,10},{12,13},{13,14},{16,17},{17,1... | collective-permute-start | bytes 1376264 | tf_op jit(solution)/shard_map/ppermute | solution.py:309
  301.9 27.1 %collective-permute-start.37 = (bf16[32,7168]{1,0:T(8,128)(2,1)S(1)}, bf16[32,7168]{1,0:T(8,128)(2,1)S(1)}, u32[]{:S(2)}, u32[]{:S(2)}) collective-permute-start(bf16[32,7168]{1,0:T(8,128)(2,1)S(1)} %add_convert_fusion.3), channel_id=1, source_target_pairs={{1,0},{2,1},{3,2},{5,4},{6,5},{7,6},{9,8},{10,9},{11,10},{13,12},{... | collective-permute-start | bytes 1376264 | tf_op jit(solution)/shard_map/ppermute | solution.py:310
  311.9 15.2 %collective-permute-start.30 = (bf16[32,7168]{1,0:T(8,128)(2,1)S(1)}, bf16[32,7168]{1,0:T(8,128)(2,1)S(1)}, u32[]{:S(2)}, u32[]{:S(2)}) collective-permute-start(bf16[32,7168]{1,0:T(8,128)(2,1)S(1)} %add_convert_fusion.5), channel_id=1, source_target_pairs={{1,0},{2,1},{3,2},{5,4},{6,5},{7,6},{9,8},{10,9},{11,10},{13,12},{... | collective-permute-start | bytes 1376264 | tf_op jit(solution)/shard_map/ppermute | solution.py:310
  316.4 11.9 %collective-permute-start.29 = (bf16[32,7168]{1,0:T(8,128)(2,1)S(1)}, bf16[32,7168]{1,0:T(8,128)(2,1)S(1)}, u32[]{:S(2)}, u32[]{:S(2)}) collective-permute-start(bf16[32,7168]{1,0:T(8,128)(2,1)S(1)} %add_convert_fusion.6), channel_id=1, source_target_pairs={{0,1},{1,2},{2,3},{4,5},{5,6},{6,7},{8,9},{9,10},{10,11},{12,13},{... | collective-permute-start | bytes 1376264 | tf_op jit(solution)/shard_map/ppermute | solution.py:309
  318.4 14.7 %collective-permute-start.34 = (bf16[32,7168]{1,0:T(8,128)(2,1)S(1)}, bf16[32,7168]{1,0:T(8,128)(2,1)S(1)}, u32[]{:S(2)}, u32[]{:S(2)}) collective-permute-start(bf16[32,7168]{1,0:T(8,128)(2,1)S(1)} %add_convert_fusion.4), channel_id=1, source_target_pairs={{0,1},{1,2},{2,3},{4,5},{5,6},{6,7},{8,9},{9,10},{10,11},{12,13},{... | collective-permute-start | bytes 1376264 | tf_op jit(solution)/shard_map/ppermute | solution.py:309
  328.5 11.7 %collective-permute-start.31 = (bf16[32,7168]{1,0:T(8,128)(2,1)S(1)}, bf16[32,7168]{1,0:T(8,128)(2,1)S(1)}, u32[]{:S(2)}, u32[]{:S(2)}) collective-permute-start(bf16[32,7168]{1,0:T(8,128)(2,1)S(1)} %fusion.8), channel_id=1, source_target_pairs={{16,0},{0,16},{17,1},{1,17},{18,2},{2,18},{19,3},{3,19},{20,4},{4,... | collective-permute-start | bytes 1376264 | tf_op jit(solution)/shard_map/ppermute | solution.py:30
  340.4 8.5 %collective-permute-start.38 = (bf16[32,7168]{1,0:T(8,128)(2,1)S(1)}, bf16[32,7168]{1,0:T(8,128)(2,1)S(1)}, u32[]{:S(2)}, u32[]{:S(2)}) collective-permute-start(bf16[32,7168]{1,0:T(8,128)(2,1)S(1)} %fusion.7), channel_id=1, source_target_pairs={{16,0},{0,16},{17,1},{1,17},{18,2},{2,18},{19,3},{3,19},{20,4},{4,... | collective-permute-start | bytes 1376264 | tf_op jit(solution)/shard_map/ppermute | solution.py:30
  (22 other events, 337.4 us)
Sparse Core Ops, SparseCore 0:
  13.0 92.4 all-gather.2

commit v10 on v8

--- a/solution.py
+++ b/solution.py
@@ -231,11 +231,11 @@
         gate_ref[...] += jnp.dot(x, gate_or_up(0), preferred_element_type=F32)
         up_ref[...] += jnp.dot(x, gate_or_up(1), preferred_element_type=F32)
         down = jnp.concatenate([down_held[i, :, at_chunk] for i in range(pieces)], axis=0)
-        grad_ref[...] += contract_last(chained_rows(scaled_in), down)
+        grad_ref[...] += contract_last(down, chained_rows(scaled_in))
 
     @pl.when(step == steps - 1)
     def _():
-        gate, up, grad = gate_ref[...], up_ref[...], grad_ref[...]
+        gate, up, grad = gate_ref[...], up_ref[...], grad_ref[...].T
         keep = own_hidden(at_ref, gathered_rows(tags), TAG_COLUMNS // 2, gate.shape[1])
         s = jax.nn.sigmoid(gate)
         silu = gate * s
@@ -245,9 +245,9 @@
 
     @pl.when(step >= steps)
     def _():
-        total = contract_last(grad_gate_ref[...], gate_or_up(0))
-        total += contract_last(grad_up_ref[...], gate_or_up(1))
-        put_blocks(outs, total)
+        total = contract_last(gate_or_up(0), grad_gate_ref[...])
+        total += contract_last(gate_or_up(1), grad_up_ref[...])
+        put_blocks(outs, total.T)
 
 
 def backward_call(at, x_gathered, rows, parts, hops, gate_ups, downs):
@@ -270,7 +270,8 @@
             + [pl.BlockSpec(memory_space=pl.ANY)] * (2 * pieces),
             out_specs=[pl.BlockSpec((rows // parts, chunk), lambda i, at: (0, second(i)))]
             * (parts * count),
-            scratch_shapes=[pltpu.VMEM((many, hidden), F32)] * 3
+            scratch_shapes=[pltpu.VMEM((many, hidden), F32)] * 2
+            + [pltpu.VMEM((hidden, many), F32)]
             + [pltpu.VMEM((many, hidden), BF16)] * 2
             + [
                 pltpu.VMEM((pieces, 2, width, hid), BF16),

time: 346 us -> 347 us (level)
  no operation moved by 1% of the time
where the time goes in v10:
time: 347 us; the launch traced here: 346 us
  waiting for transfers between devices  213 us (61%)
  starting transfers between devices  56.9 us (16%)
  Pallas kernels  38.8 us (11%)
  between operations  14.6 us (4%)
  other arithmetic  12.5 us (4%)
  local copies, waits for them, and re-layouts  10 us (3%)
    ppermute x6, waiting for transfers between devices, hop(): return (lax.ppermute(below, axis, up), lax.ppermute(above, axis, down))  98.1 us
    ppermute x9, waiting for transfers between devices, step_home(): lax.ppermute(pair[1], axis, [(i, i - 1) for i in range(count - step, coun...  49.3 us
    ppermute x6, waiting for transfers between devices, flipped(): return lax.ppermute(block, axis, route)  43.9 us
    ppermute x9, starting transfers between devices, step_home(): lax.ppermute(pair[1], axis, [(i, i - 1) for i in range(count - step, coun...  24.8 us
    pallas_call x1, Pallas kernels, backward_call(): pl.pallas_call(functools.partial(backward_kernel, len(rows_in), count, pi...  21.7 us
    ppermute x3, waiting for transfers between devices, shifted(): lax.ppermute(block, axis, [((i - distance) % count, i) for i in range(cou...  16.1 us
    ppermute x6, starting transfers between devices, hop(): return (lax.ppermute(below, axis, up), lax.ppermute(above, axis, down))  13.6 us
    ppermute x9, starting transfers between devices, step_home(): up = lax.ppermute(pair[0], axis, [(i, i + 1) for i in range(step)])  13.1 us
  transfers between devices with their start and end apart: 34, of which 18 were waited for; matrix products, arithmetic and copies ran while one was open for 2% of the time, Pallas kernels for 11%

profile of v10, /device:TPU:20, one launch (start us, length us, event | category | flops | bytes accessed | tf_op | source)
XLA Modules:
  0.0 345.8 jit_solution(1735773713275481933)
XLA Ops:
  8.8 2.1 concatenate.12
  10.9 1.6 collective-permute-start
  12.8 2.0 copy-done.10
  15.4 2.1 pad_maximum_fusion.refs_8_.refs_18_
  17.5 35.4 %collective-permute-done.refs_2_.refs_24_ = bf16[128,7168]{1,0:T(8,128)(2,1)S(1)} collective-permute-done((bf16[128,7168]{1,0:T(8,128)(2,1)}, bf16[128,7168]{1,0:T(8,128)(2,1)S(1)}, u32[]{:S(2)}, u32[]{:S(2)}) %collective-permute-start) | collective-permute-done | bytes 1835040 | tf_op jit(solution)/shard_map/ppermute | solution.py:25
  52.9 1.5 collective-permute-start.4
  54.4 2.3 collective-permute-start.2
  56.8 3.6 %collective-permute-start.1 = (bf16[128,7168]{1,0:T(8,128)(2,1)S(1)}, bf16[128,7168]{1,0:T(8,128)(2,1)S(1)}, u32[]{:S(2)}, u32[]{:S(2)}) collective-permute-start(bf16[128,7168]{1,0:T(8,128)(2,1)S(1)} %pad_maximum_fusion.1.refs_4_.refs_11_), channel_id=1, source_target_pairs={{0,1},{1,2},{2,3},{4,5},{5,6},{6,7},{8,9},{9,10},{10,11},{12,13},{... | collective-permute-start | bytes 5505032 | tf_op jit(solution)/shard_map/ppermute | solution.py:296
  60.9 61.6 %collective-permute-done.2.refs_8_.refs_15_ = bf16[128,7168]{1,0:T(8,128)(2,1)S(1)} collective-permute-done((bf16[128,7168]{1,0:T(8,128)(2,1)S(1)}, bf16[128,7168]{1,0:T(8,128)(2,1)S(1)}, u32[]{:S(2)}, u32[]{:S(2)}) %collective-permute-start.2) | collective-permute-done | bytes 1835040 | tf_op jit(solution)/shard_map/ppermute | solution.py:296
  122.7 1.1 copy-done.3
  124.4 1.3 copy-done.5
  125.6 7.9 %collective-permute-done.4.refs_10_.refs_20_ = bf16[2,7168,128]{2,1,0:T(8,128)(2,1)} collective-permute-done((bf16[2,7168,128]{2,1,0:T(8,128)(2,1)}, bf16[2,7168,128]{2,1,0:T(8,128)(2,1)}, u32[]{:S(2)}, u32[]{:S(2)}) %collective-permute-start.4) | collective-permute-done | bytes 3670048 | tf_op jit(solution)/shard_map/ppermute | solution.py:25
  133.5 3.6 %collective-permute-start.11 = (bf16[128,7168]{1,0:T(8,128)(2,1)S(1)}, bf16[128,7168]{1,0:T(8,128)(2,1)}, u32[]{:S(2)}, u32[]{:S(2)}) collective-permute-start(bf16[128,7168]{1,0:T(8,128)(2,1)S(1)} %collective-permute-done.2.refs_8_.refs_15_), channel_id=1, source_target_pairs={{1,0},{2,1},{5,4},{6,5},{9,8},{10,9},{13,12},{14,13},{17,16},{18,1... | collective-permute-start | bytes 5505032 | tf_op jit(solution)/shard_map/ppermute | solution.py:296
  137.1 1.9 collective-permute-start.10
  140.3 10.2 %shard_map.113.hidden_ref = bf16[256,512]{1,0:T(8,128)(2,1)} custom-call(s32[2]{0:T(128)} %pad_add_fusion.at_ref, bf16[4,64,7296]{2,1,0:T(8,128)(2,1)} %bitcast.27, bf16[4,64,7296]{2,1,0:T(8,128)(2,1)} %bitcast.28, bf16[4,64,7296]{2,1,0:T(8,128)(2,1)} %bitcast.29, bf16[4,64,7296]{2,1,0:T(8,128)(2,1)} %bitcast.30, bf16[4,64,7296]{2,1,0:T(8,128)(2,1)} %bitcast.31, ...), custom_call_target="tpu_custom_call" | custom-call | flops 131072 | bytes 256 | tf_op jit(solution)/shard_map/pallas_call | solution.py:158
  150.5 6.8 %shard_map.114 = (f32[64,7168]{1,0:T(8,128)}, bf16[64,7168]{1,0:T(8,128)(2,1)}, bf16[64,7168]{1,0:T(8,128)(2,1)}, bf16[64,7168]{1,0:T(8,128)(2,1)}) custom-call(bf16[256,512]{1,0:T(8,128)(2,1)} %shard_map.113.hidden_ref, bf16[128,7168]{1,0:T(8,128)(2,1)} %bitcast.12.refs_0_.refs_22_, bf16[128,7168]{1,0:T(8,128)(2,1)} %copy-done.4, ...), custom_call_target="tpu_custom_call" | custom-call | flops 131072 | bytes 256 | tf_op jit(solution)/shard_map/pallas_call | solution.py:185
  157.4 1.3 collective-permute-start.9
  159.4 16.4 %collective-permute-done.11.refs_9_.refs_16_ = bf16[128,7168]{1,0:T(8,128)(2,1)} collective-permute-done((bf16[128,7168]{1,0:T(8,128)(2,1)S(1)}, bf16[128,7168]{1,0:T(8,128)(2,1)}, u32[]{:S(2)}, u32[]{:S(2)}) %collective-permute-start.11) | collective-permute-done | bytes 1835040 | tf_op jit(solution)/shard_map/ppermute | solution.py:296
  175.8 5.6 %collective-permute-done.10.refs_6_.refs_13_ = bf16[128,7168]{1,0:T(8,128)(2,1)} collective-permute-done((bf16[128,7168]{1,0:T(8,128)(2,1)}, bf16[128,7168]{1,0:T(8,128)(2,1)}, u32[]{:S(2)}, u32[]{:S(2)}) %collective-permute-start.10) | collective-permute-done | bytes 1835040 | tf_op jit(solution)/shard_map/ppermute | solution.py:296
  181.9 1.6 fusion.1
  183.5 5.2 %collective-permute-start.14 = (bf16[64,7168]{1,0:T(8,128)(2,1)S(1)}, bf16[64,7168]{1,0:T(8,128)(2,1)S(1)}, u32[]{:S(2)}, u32[]{:S(2)}) collective-permute-start(bf16[64,7168]{1,0:T(8,128)(2,1)S(1)} %get-tuple-element.72), channel_id=1, source_target_pairs={{2,1},{3,2},{6,5},{7,6},{10,9},{11,10},{14,13},{15,14},{18,17},{19... | collective-permute-start | bytes 2752520 | tf_op jit(solution)/shard_map/ppermute | solution.py:311
  189.4 1.4 collective-permute-start.16
  190.9 1.3 collective-permute-start.12
  192.2 15.3 %collective-permute-done.14 = bf16[64,7168]{1,0:T(8,128)(2,1)S(1)} collective-permute-done((bf16[64,7168]{1,0:T(8,128)(2,1)S(1)}, bf16[64,7168]{1,0:T(8,128)(2,1)S(1)}, u32[]{:S(2)}, u32[]{:S(2)}) %collective-permute-start.14) | collective-permute-done | bytes 917536 | tf_op jit(solution)/shard_map/ppermute | solution.py:311
  208.6 4.4 %collective-permute-start.15 = (bf16[64,7168]{1,0:T(8,128)(2,1)}, bf16[64,7168]{1,0:T(8,128)(2,1)}, u32[]{:S(2)}, u32[]{:S(2)}) collective-permute-start(bf16[64,7168]{1,0:T(8,128)(2,1)} %add_convert_fusion.1), channel_id=1, source_target_pairs={{1,0},{2,1},{3,2},{5,4},{6,5},{7,6},{9,8},{10,9},{11,10},{13,12},{... | collective-permute-start | bytes 2752520 | tf_op jit(solution)/shard_map/ppermute | solution.py:311
  213.8 1.1 add_convert_fusion.2
  215.0 2.2 collective-permute-start.13
  217.2 14.3 %collective-permute-done.16.refs_7_.refs_14_ = bf16[128,7168]{1,0:T(8,128)(2,1)S(1)} collective-permute-done((bf16[128,7168]{1,0:T(8,128)(2,1)}, bf16[128,7168]{1,0:T(8,128)(2,1)S(1)}, u32[]{:S(2)}, u32[]{:S(2)}) %collective-permute-start.16) | collective-permute-done | bytes 1835040 | tf_op jit(solution)/shard_map/ppermute | solution.py:296
  231.5 1.3 copy-done.7
  232.8 21.7 %shard_map.115 = (f32[32,7168]{1,0:T(8,128)}, f32[32,7168]{1,0:T(8,128)}, bf16[32,7168]{1,0:T(8,128)(2,1)}, bf16[32,7168]{1,0:T(8,128)(2,1)}, bf16[32,7168]{1,0:...) custom-call(s32[2]{0:T(128)} %pad_add_fusion.at_ref, ...), custom_call_target="tpu_custom_call" | custom-call | flops 131072 | bytes 256 | tf_op jit(solution)/shard_map/pallas_call | solution.py:263
  254.5 1.3 collective-permute-start.21
  256.5 1.3 collective-permute-start.29
  258.6 2.0 add_convert_fusion
  261.1 14.0 %collective-permute-done.29 = bf16[32,7168]{1,0:T(8,128)(2,1)S(1)} collective-permute-done((bf16[32,7168]{1,0:T(8,128)(2,1)}, bf16[32,7168]{1,0:T(8,128)(2,1)S(1)}, u32[]{:S(2)}, u32[]{:S(2)}) %collective-permute-start.29) | collective-permute-done | bytes 458784 | tf_op jit(solution)/shard_map/ppermute | solution.py:311
  275.3 3.1 collective-permute-start.30
  278.7 2.1 collective-permute-start.22
  280.7 1.3 collective-permute-start.20
  282.1 1.4 collective-permute-start.27
  283.5 7.3 %collective-permute-done.30 = bf16[32,7168]{1,0:T(8,128)(2,1)S(1)} collective-permute-done((bf16[32,7168]{1,0:T(8,128)(2,1)S(1)}, bf16[32,7168]{1,0:T(8,128)(2,1)S(1)}, u32[]{:S(2)}, u32[]{:S(2)}) %collective-permute-start.30) | collective-permute-done | bytes 458784 | tf_op jit(solution)/shard_map/ppermute | solution.py:311
  290.9 3.1 collective-permute-start.31
  294.1 6.6 %collective-permute-done.22 = bf16[32,7168]{1,0:T(8,128)(2,1)S(1)} collective-permute-done((bf16[32,7168]{1,0:T(8,128)(2,1)S(1)}, bf16[32,7168]{1,0:T(8,128)(2,1)S(1)}, u32[]{:S(2)}, u32[]{:S(2)}) %collective-permute-start.22) | collective-permute-done | bytes 458784 | tf_op jit(solution)/shard_map/ppermute | solution.py:311
  300.9 3.1 collective-permute-start.24
  304.0 2.9 collective-permute-start.23
  307.1 1.9 collective-permute-start.28
  309.0 5.6 %collective-permute-done.24 = bf16[32,7168]{1,0:T(8,128)(2,1)S(1)} collective-permute-done((bf16[32,7168]{1,0:T(8,128)(2,1)S(1)}, bf16[32,7168]{1,0:T(8,128)(2,1)S(1)}, u32[]{:S(2)}, u32[]{:S(2)}) %collective-permute-start.24) | collective-permute-done | bytes 458784 | tf_op jit(solution)/shard_map/ppermute | solution.py:311
  316.0 4.1 %collective-permute-done.28 = bf16[32,7168]{1,0:T(8,128)(2,1)S(1)} collective-permute-done((bf16[32,7168]{1,0:T(8,128)(2,1)S(1)}, bf16[32,7168]{1,0:T(8,128)(2,1)S(1)}, u32[]{:S(2)}, u32[]{:S(2)}) %collective-permute-start.28) | collective-permute-done | bytes 458784 | tf_op jit(solution)/shard_map/ppermute | solution.py:310
  320.2 8.1 %collective-permute-done.25 = bf16[32,7168]{1,0:T(8,128)(2,1)S(1)} collective-permute-done((bf16[32,7168]{1,0:T(8,128)(2,1)S(1)}, bf16[32,7168]{1,0:T(8,128)(2,1)S(1)}, u32[]{:S(2)}, u32[]{:S(2)}) %collective-permute-start.25) | collective-permute-done | bytes 458784 | tf_op jit(solution)/shard_map/ppermute | solution.py:30
  329.0 8.0 %collective-permute-done.32 = bf16[32,7168]{1,0:T(8,128)(2,1)S(1)} collective-permute-done((bf16[32,7168]{1,0:T(8,128)(2,1)S(1)}, bf16[32,7168]{1,0:T(8,128)(2,1)S(1)}, u32[]{:S(2)}, u32[]{:S(2)}) %collective-permute-start.32) | collective-permute-done | bytes 458784 | tf_op jit(solution)/shard_map/ppermute | solution.py:30
  (99 shorter events, 15.7 us)
Async XLA Ops:
  7.2 126.3 %all-gather.3.cloned.1.call-start = ((), (), s32[]{:S(2)}) async-start(), calls=%async_computation | async-start | bytes 4669440 | tf_op jit(solution)/shard_map/all_gather | solution.py:347
  10.9 42.0 %collective-permute-start = (bf16[128,7168]{1,0:T(8,128)(2,1)}, bf16[128,7168]{1,0:T(8,128)(2,1)S(1)}, u32[]{:S(2)}, u32[]{:S(2)}) collective-permute-start(bf16[128,7168]{1,0:T(8,128)(2,1)} %bitcast.12.refs_0_.refs_22_), channel_id=1, source_target_pairs={{0,8},{4,12},{8,0},{12,4},{1,9},{5,13},{9,1},{13,5},{2,10},{6,14},... | collective-permute-start | bytes 5505032 | tf_op jit(solution)/shard_map/ppermute | solution.py:25
  12.8 43.9 %copy-start = (bf16[128,7168]{1,0:T(8,128)(2,1)}, bf16[128,7168]{1,0:T(8,128)(2,1)S(1)}, u32[]{:S(2)}) copy-start(bf16[128,7168]{1,0:T(8,128)(2,1)S(1)} %pad_maximum_fusion.1.refs_4_.refs_11_) | copy-start | bytes 5505028
  52.9 69.7 %copy-start.1 = (bf16[128,7168]{1,0:T(8,128)(2,1)}, bf16[128,7168]{1,0:T(8,128)(2,1)S(1)}, u32[]{:S(2)}) copy-start(bf16[128,7168]{1,0:T(8,128)(2,1)S(1)} %collective-permute-done.refs_2_.refs_24_) | copy-start | bytes 5505028
  52.9 80.6 %collective-permute-start.4 = (bf16[2,7168,128]{2,1,0:T(8,128)(2,1)}, bf16[2,7168,128]{2,1,0:T(8,128)(2,1)}, u32[]{:S(2)}, u32[]{:S(2)}) collective-permute-start(bf16[2,7168,128]{2,1,0:T(8,128)(2,1)} %pad_maximum_fusion.refs_8_.refs_18_), channel_id=1, source_target_pairs={{0,8},{4,12},{8,0},{12,4},{1,9},{5,13},{9,1},{13,5},{2,10},{6,14},... | collective-permute-start | bytes 11010056 | tf_op jit(solution)/shard_map/ppermute | solution.py:25
  54.4 68.2 %collective-permute-start.2 = (bf16[128,7168]{1,0:T(8,128)(2,1)S(1)}, bf16[128,7168]{1,0:T(8,128)(2,1)S(1)}, u32[]{:S(2)}, u32[]{:S(2)}) collective-permute-start(bf16[128,7168]{1,0:T(8,128)(2,1)S(1)} %pad_maximum_fusion.1.refs_4_.refs_11_), channel_id=1, source_target_pairs={{1,0},{2,1},{3,2},{5,4},{6,5},{7,6},{9,8},{10,9},{11,10},{13,12},{... | collective-permute-start | bytes 5505032 | tf_op jit(solution)/shard_map/ppermute | solution.py:296
  56.8 65.8 %collective-permute-start.1 = (bf16[128,7168]{1,0:T(8,128)(2,1)S(1)}, bf16[128,7168]{1,0:T(8,128)(2,1)S(1)}, u32[]{:S(2)}, u32[]{:S(2)}) collective-permute-start(bf16[128,7168]{1,0:T(8,128)(2,1)S(1)} %pad_maximum_fusion.1.refs_4_.refs_11_), channel_id=1, source_target_pairs={{0,1},{1,2},{2,3},{4,5},{5,6},{6,7},{8,9},{9,10},{10,11},{12,13},{... | collective-permute-start | bytes 5505032 | tf_op jit(solution)/shard_map/ppermute | solution.py:296
  60.4 62.3 %collective-permute-start.5 = (bf16[128,7168]{1,0:T(8,128)(2,1)}, bf16[128,7168]{1,0:T(8,128)(2,1)S(1)}, u32[]{:S(2)}, u32[]{:S(2)}) collective-permute-start(bf16[128,7168]{1,0:T(8,128)(2,1)} %bitcast.12.refs_0_.refs_22_), channel_id=1, source_target_pairs={{0,4},{4,0},{8,12},{12,8},{1,5},{5,1},{9,13},{13,9},{2,6},{6,2},{1... | collective-permute-start | bytes 5505032 | tf_op jit(solution)/shard_map/ppermute | solution.py:25
  60.4 62.3 %collective-permute-start.6 = (bf16[128,7168]{1,0:T(8,128)(2,1)S(1)}, bf16[128,7168]{1,0:T(8,128)(2,1)S(1)}, u32[]{:S(2)}, u32[]{:S(2)}) collective-permute-start(bf16[128,7168]{1,0:T(8,128)(2,1)S(1)} %collective-permute-done.refs_2_.refs_24_), channel_id=1, source_target_pairs={{0,4},{4,0},{8,12},{12,8},{1,5},{5,1},{9,13},{13,9},{2,6},{6,2},{1... | collective-permute-start | bytes 5505032 | tf_op jit(solution)/shard_map/ppermute | solution.py:25
  122.6 27.9 %copy-start.2 = (bf16[128,7168]{1,0:T(8,128)(2,1)}, bf16[128,7168]{1,0:T(8,128)(2,1)S(1)}, u32[]{:S(2)}) copy-start(bf16[128,7168]{1,0:T(8,128)(2,1)S(1)} %collective-permute-done.2.refs_8_.refs_15_) | copy-start | bytes 5505028
  122.6 17.0 %collective-permute-start.3 = (bf16[2,7168,128]{2,1,0:T(8,128)(2,1)}, bf16[2,7168,128]{2,1,0:T(8,128)(2,1)}, u32[]{:S(2)}, u32[]{:S(2)}) collective-permute-start(bf16[2,7168,128]{2,1,0:T(8,128)(2,1)} %pad_maximum_fusion.refs_8_.refs_18_), channel_id=1, source_target_pairs={{0,4},{4,0},{8,12},{12,8},{1,5},{5,1},{9,13},{13,9},{2,6},{6,2},{1... | collective-permute-start | bytes 11010056 | tf_op jit(solution)/shard_map/ppermute | solution.py:25
  133.5 6.8 %collective-permute-start.7 = (bf16[2,7168,128]{2,1,0:T(8,128)(2,1)}, bf16[2,7168,128]{2,1,0:T(8,128)(2,1)}, u32[]{:S(2)}, u32[]{:S(2)}) collective-permute-start(bf16[2,7168,128]{2,1,0:T(8,128)(2,1)} %collective-permute-done.4.refs_10_.refs_20_), channel_id=1, source_target_pairs={{0,4},{4,0},{8,12},{12,8},{1,5},{5,1},{9,13},{13,9},{2,6},{6,2},{1... | collective-permute-start | bytes 11010056 | tf_op jit(solution)/shard_map/ppermute | solution.py:25
  133.5 42.3 %collective-permute-start.11 = (bf16[128,7168]{1,0:T(8,128)(2,1)S(1)}, bf16[128,7168]{1,0:T(8,128)(2,1)}, u32[]{:S(2)}, u32[]{:S(2)}) collective-permute-start(bf16[128,7168]{1,0:T(8,128)(2,1)S(1)} %collective-permute-done.2.refs_8_.refs_15_), channel_id=1, source_target_pairs={{1,0},{2,1},{5,4},{6,5},{9,8},{10,9},{13,12},{14,13},{17,16},{18,1... | collective-permute-start | bytes 5505032 | tf_op jit(solution)/shard_map/ppermute | solution.py:296
  137.1 44.3 %collective-permute-start.10 = (bf16[128,7168]{1,0:T(8,128)(2,1)}, bf16[128,7168]{1,0:T(8,128)(2,1)}, u32[]{:S(2)}, u32[]{:S(2)}) collective-permute-start(bf16[128,7168]{1,0:T(8,128)(2,1)} %copy-done.3), channel_id=1, source_target_pairs={{1,2},{2,3},{5,6},{6,7},{9,10},{10,11},{13,14},{14,15},{17,18},{18... | collective-permute-start | bytes 5505032 | tf_op jit(solution)/shard_map/ppermute | solution.py:296
  157.4 24.5 %collective-permute-start.9 = (bf16[64,7168]{1,0:T(8,128)(2,1)}, bf16[64,7168]{1,0:T(8,128)(2,1)S(1)}, u32[]{:S(2)}, u32[]{:S(2)}) collective-permute-start(bf16[64,7168]{1,0:T(8,128)(2,1)} %get-tuple-element.42), channel_id=1, source_target_pairs={{3,2},{7,6},{11,10},{15,14},{19,18},{23,22},{27,26},{31,30}} | collective-permute-start | bytes 2752520 | tf_op jit(solution)/shard_map/ppermute | solution.py:311
  158.6 23.2 %collective-permute-start.8 = (bf16[64,7168]{1,0:T(8,128)(2,1)}, bf16[64,7168]{1,0:T(8,128)(2,1)S(1)}, u32[]{:S(2)}, u32[]{:S(2)}) collective-permute-start(bf16[64,7168]{1,0:T(8,128)(2,1)} %get-tuple-element.44), channel_id=1, source_target_pairs={{0,1},{4,5},{8,9},{12,13},{16,17},{20,21},{24,25},{28,29}} | collective-permute-start | bytes 2752520 | tf_op jit(solution)/shard_map/ppermute | solution.py:310
  181.8 25.6 %copy-start.17 = (bf16[64,7168]{1,0:T(8,128)(2,1)S(1)}, bf16[64,7168]{1,0:T(8,128)(2,1)}, u32[]{:S(2)}) copy-start(bf16[64,7168]{1,0:T(8,128)(2,1)} %get-tuple-element.44) | copy-start | bytes 2752516
  183.5 30.3 %copy-start.16 = (bf16[64,7168]{1,0:T(8,128)(2,1)S(1)}, bf16[64,7168]{1,0:T(8,128)(2,1)}, u32[]{:S(2)}) copy-start(bf16[64,7168]{1,0:T(8,128)(2,1)} %get-tuple-element.42) | copy-start | bytes 2752516
  183.5 24.0 %collective-permute-start.14 = (bf16[64,7168]{1,0:T(8,128)(2,1)S(1)}, bf16[64,7168]{1,0:T(8,128)(2,1)S(1)}, u32[]{:S(2)}, u32[]{:S(2)}) collective-permute-start(bf16[64,7168]{1,0:T(8,128)(2,1)S(1)} %get-tuple-element.72), channel_id=1, source_target_pairs={{2,1},{3,2},{6,5},{7,6},{10,9},{11,10},{14,13},{15,14},{18,17},{19... | collective-permute-start | bytes 2752520 | tf_op jit(solution)/shard_map/ppermute | solution.py:311
  188.7 28.5 %collective-permute-start.17 = (bf16[128,7168]{1,0:T(8,128)(2,1)}, bf16[128,7168]{1,0:T(8,128)(2,1)S(1)}, u32[]{:S(2)}, u32[]{:S(2)}) collective-permute-start(bf16[128,7168]{1,0:T(8,128)(2,1)} %collective-permute-done.11.refs_9_.refs_16_), channel_id=1, source_target_pairs={{1,0},{5,4},{9,8},{13,12},{17,16},{21,20},{25,24},{29,28}} | collective-permute-start | bytes 5505032 | tf_op jit(solution)/shard_map/ppermute | solution.py:296
  189.4 42.1 %collective-permute-start.16 = (bf16[128,7168]{1,0:T(8,128)(2,1)}, bf16[128,7168]{1,0:T(8,128)(2,1)S(1)}, u32[]{:S(2)}, u32[]{:S(2)}) collective-permute-start(bf16[128,7168]{1,0:T(8,128)(2,1)} %collective-permute-done.10.refs_6_.refs_13_), channel_id=1, source_target_pairs={{2,3},{6,7},{10,11},{14,15},{18,19},{22,23},{26,27},{30,31}} | collective-permute-start | bytes 5505032 | tf_op jit(solution)/shard_map/ppermute | solution.py:296
  190.9 23.0 %collective-permute-start.12 = (bf16[64,7168]{1,0:T(8,128)(2,1)S(1)}, bf16[64,7168]{1,0:T(8,128)(2,1)S(1)}, u32[]{:S(2)}, u32[]{:S(2)}) collective-permute-start(bf16[64,7168]{1,0:T(8,128)(2,1)S(1)} %get-tuple-element.73), channel_id=1, source_target_pairs={{0,1},{1,2},{4,5},{5,6},{8,9},{9,10},{12,13},{13,14},{16,17},{17,1... | collective-permute-start | bytes 2752520 | tf_op jit(solution)/shard_map/ppermute | solution.py:310
  208.6 45.9 %collective-permute-start.15 = (bf16[64,7168]{1,0:T(8,128)(2,1)}, bf16[64,7168]{1,0:T(8,128)(2,1)}, u32[]{:S(2)}, u32[]{:S(2)}) collective-permute-start(bf16[64,7168]{1,0:T(8,128)(2,1)} %add_convert_fusion.1), channel_id=1, source_target_pairs={{1,0},{2,1},{3,2},{5,4},{6,5},{7,6},{9,8},{10,9},{11,10},{13,12},{... | collective-permute-start | bytes 2752520 | tf_op jit(solution)/shard_map/ppermute | solution.py:311
  214.9 43.6 %copy-start.8 = (bf16[1,64,7168]{2,1,0:T(8,128)(2,1)S(1)}, bf16[1,64,7168]{2,1,0:T(8,128)(2,1)}, u32[]{:S(2)}) copy-start(bf16[1,64,7168]{2,1,0:T(8,128)(2,1)} %param.10) | copy-start | bytes 2752516
  215.0 43.6 %copy-start.12 = (f32[64,7168]{1,0:T(8,128)S(1)}, f32[64,7168]{1,0:T(8,128)}, u32[]{:S(2)}) copy-start(f32[64,7168]{1,0:T(8,128)} %get-tuple-element.41) | copy-start | bytes 5505028
  215.0 43.6 %copy-start.24 = (f32[1,64]{1,0:T(1,128)S(1)}, f32[1,64]{1,0:T(1,128)}, u32[]{:S(2)}) copy-start(f32[1,64]{1,0:T(1,128)} %param.12) | copy-start | bytes 772
  215.0 39.6 %collective-permute-start.13 = (bf16[64,7168]{1,0:T(8,128)(2,1)}, bf16[64,7168]{1,0:T(8,128)(2,1)}, u32[]{:S(2)}, u32[]{:S(2)}) collective-permute-start(bf16[64,7168]{1,0:T(8,128)(2,1)} %add_convert_fusion.2), channel_id=1, source_target_pairs={{0,1},{1,2},{2,3},{4,5},{5,6},{6,7},{8,9},{9,10},{10,11},{12,13},{... | collective-permute-start | bytes 2752520 | tf_op jit(solution)/shard_map/ppermute | solution.py:310
  254.5 23.9 %collective-permute-start.21 = (bf16[32,7168]{1,0:T(8,128)(2,1)}, bf16[32,7168]{1,0:T(8,128)(2,1)S(1)}, u32[]{:S(2)}, u32[]{:S(2)}) collective-permute-start(bf16[32,7168]{1,0:T(8,128)(2,1)} %get-tuple-element.59), channel_id=1, source_target_pairs={{3,2},{7,6},{11,10},{15,14},{19,18},{23,22},{27,26},{31,30}} | collective-permute-start | bytes 1376264 | tf_op jit(solution)/shard_map/ppermute | solution.py:311
  255.8 22.6 %collective-permute-start.19 = (bf16[32,7168]{1,0:T(8,128)(2,1)}, bf16[32,7168]{1,0:T(8,128)(2,1)S(1)}, u32[]{:S(2)}, u32[]{:S(2)}) collective-permute-start(bf16[32,7168]{1,0:T(8,128)(2,1)} %get-tuple-element.61), channel_id=1, source_target_pairs={{0,1},{4,5},{8,9},{12,13},{16,17},{20,21},{24,25},{28,29}} | collective-permute-start | bytes 1376264 | tf_op jit(solution)/shard_map/ppermute | solution.py:310
  256.5 18.6 %collective-permute-start.29 = (bf16[32,7168]{1,0:T(8,128)(2,1)}, bf16[32,7168]{1,0:T(8,128)(2,1)S(1)}, u32[]{:S(2)}, u32[]{:S(2)}) collective-permute-start(bf16[32,7168]{1,0:T(8,128)(2,1)} %get-tuple-element.67), channel_id=1, source_target_pairs={{3,2},{7,6},{11,10},{15,14},{19,18},{23,22},{27,26},{31,30}} | collective-permute-start | bytes 1376264 | tf_op jit(solution)/shard_map/ppermute | solution.py:311
  257.8 17.3 %collective-permute-start.26 = (bf16[32,7168]{1,0:T(8,128)(2,1)}, bf16[32,7168]{1,0:T(8,128)(2,1)S(1)}, u32[]{:S(2)}, u32[]{:S(2)}) collective-permute-start(bf16[32,7168]{1,0:T(8,128)(2,1)} %get-tuple-element.69), channel_id=1, source_target_pairs={{0,1},{4,5},{8,9},{12,13},{16,17},{20,21},{24,25},{28,29}} | collective-permute-start | bytes 1376264 | tf_op jit(solution)/shard_map/ppermute | solution.py:310
  260.6 30.3 %copy-start.21 = (bf16[32,7168]{1,0:T(8,128)(2,1)S(1)}, bf16[32,7168]{1,0:T(8,128)(2,1)}, u32[]{:S(2)}) copy-start(bf16[32,7168]{1,0:T(8,128)(2,1)} %get-tuple-element.69) | copy-start | bytes 1376260
  260.6 40.1 %collective-permute-start.18 = (bf16[64,7168]{1,0:T(8,128)(2,1)S(1)}, bf16[64,7168]{1,0:T(8,128)(2,1)S(1)}, u32[]{:S(2)}, u32[]{:S(2)}) collective-permute-start(bf16[64,7168]{1,0:T(8,128)(2,1)S(1)} %add_convert_fusion), channel_id=1, source_target_pairs={{16,0},{0,16},{17,1},{1,17},{18,2},{2,18},{19,3},{3,19},{20,4},{4,... | collective-permute-start | bytes 2752520 | tf_op jit(solution)/shard_map/ppermute | solution.py:30
  275.3 25.3 %copy-start.20 = (bf16[32,7168]{1,0:T(8,128)(2,1)S(1)}, bf16[32,7168]{1,0:T(8,128)(2,1)}, u32[]{:S(2)}) copy-start(bf16[32,7168]{1,0:T(8,128)(2,1)} %get-tuple-element.59) | copy-start | bytes 1376260
  275.3 15.5 %collective-permute-start.30 = (bf16[32,7168]{1,0:T(8,128)(2,1)S(1)}, bf16[32,7168]{1,0:T(8,128)(2,1)S(1)}, u32[]{:S(2)}, u32[]{:S(2)}) collective-permute-start(bf16[32,7168]{1,0:T(8,128)(2,1)S(1)} %get-tuple-element.76), channel_id=1, source_target_pairs={{2,1},{3,2},{6,5},{7,6},{10,9},{11,10},{14,13},{15,14},{18,17},{19... | collective-permute-start | bytes 1376264 | tf_op jit(solution)/shard_map/ppermute | solution.py:311
  278.7 22.1 %copy-start.19 = (bf16[32,7168]{1,0:T(8,128)(2,1)S(1)}, bf16[32,7168]{1,0:T(8,128)(2,1)}, u32[]{:S(2)}) copy-start(bf16[32,7168]{1,0:T(8,128)(2,1)} %get-tuple-element.61) | copy-start | bytes 1376260
  278.7 22.0 %collective-permute-start.22 = (bf16[32,7168]{1,0:T(8,128)(2,1)S(1)}, bf16[32,7168]{1,0:T(8,128)(2,1)S(1)}, u32[]{:S(2)}, u32[]{:S(2)}) collective-permute-start(bf16[32,7168]{1,0:T(8,128)(2,1)S(1)} %get-tuple-element.74), channel_id=1, source_target_pairs={{2,1},{3,2},{6,5},{7,6},{10,9},{11,10},{14,13},{15,14},{18,17},{19... | collective-permute-start | bytes 1376264 | tf_op jit(solution)/shard_map/ppermute | solution.py:311
  280.7 19.9 %collective-permute-start.20 = (bf16[32,7168]{1,0:T(8,128)(2,1)S(1)}, bf16[32,7168]{1,0:T(8,128)(2,1)S(1)}, u32[]{:S(2)}, u32[]{:S(2)}) collective-permute-start(bf16[32,7168]{1,0:T(8,128)(2,1)S(1)} %get-tuple-element.75), channel_id=1, source_target_pairs={{0,1},{1,2},{4,5},{5,6},{8,9},{9,10},{12,13},{13,14},{16,17},{17,1... | collective-permute-start | bytes 1376264 | tf_op jit(solution)/shard_map/ppermute | solution.py:310
  282.0 24.9 %copy-start.18 = (bf16[32,7168]{1,0:T(8,128)(2,1)S(1)}, bf16[32,7168]{1,0:T(8,128)(2,1)}, u32[]{:S(2)}) copy-start(bf16[32,7168]{1,0:T(8,128)(2,1)} %get-tuple-element.67) | copy-start | bytes 1376260
  282.1 24.9 %collective-permute-start.27 = (bf16[32,7168]{1,0:T(8,128)(2,1)S(1)}, bf16[32,7168]{1,0:T(8,128)(2,1)S(1)}, u32[]{:S(2)}, u32[]{:S(2)}) collective-permute-start(bf16[32,7168]{1,0:T(8,128)(2,1)S(1)} %get-tuple-element.77), channel_id=1, source_target_pairs={{0,1},{1,2},{4,5},{5,6},{8,9},{9,10},{12,13},{13,14},{16,17},{17,1... | collective-permute-start | bytes 1376264 | tf_op jit(solution)/shard_map/ppermute | solution.py:310
  290.9 24.3 %copy-start.15 = (f32[32,7168]{1,0:T(8,128)S(1)}, f32[32,7168]{1,0:T(8,128)}, u32[]{:S(2)}) copy-start(f32[32,7168]{1,0:T(8,128)} %get-tuple-element.58) | copy-start | bytes 2752516
  290.9 25.1 %collective-permute-start.31 = (bf16[32,7168]{1,0:T(8,128)(2,1)S(1)}, bf16[32,7168]{1,0:T(8,128)(2,1)S(1)}, u32[]{:S(2)}, u32[]{:S(2)}) collective-permute-start(bf16[32,7168]{1,0:T(8,128)(2,1)S(1)} %add_convert_fusion.3), channel_id=1, source_target_pairs={{1,0},{2,1},{3,2},{5,4},{6,5},{7,6},{9,8},{10,9},{11,10},{13,12},{... | collective-permute-start | bytes 1376264 | tf_op jit(solution)/shard_map/ppermute | solution.py:311
  300.9 27.4 %copy-start.14 = (f32[32,7168]{1,0:T(8,128)S(1)}, f32[32,7168]{1,0:T(8,128)}, u32[]{:S(2)}) copy-start(f32[32,7168]{1,0:T(8,128)} %get-tuple-element.66) | copy-start | bytes 2752516
  300.9 13.7 %collective-permute-start.24 = (bf16[32,7168]{1,0:T(8,128)(2,1)S(1)}, bf16[32,7168]{1,0:T(8,128)(2,1)S(1)}, u32[]{:S(2)}, u32[]{:S(2)}) collective-permute-start(bf16[32,7168]{1,0:T(8,128)(2,1)S(1)} %add_convert_fusion.5), channel_id=1, source_target_pairs={{1,0},{2,1},{3,2},{5,4},{6,5},{7,6},{9,8},{10,9},{11,10},{13,12},{... | collective-permute-start | bytes 1376264 | tf_op jit(solution)/shard_map/ppermute | solution.py:311
  304.0 11.2 %collective-permute-start.23 = (bf16[32,7168]{1,0:T(8,128)(2,1)S(1)}, bf16[32,7168]{1,0:T(8,128)(2,1)S(1)}, u32[]{:S(2)}, u32[]{:S(2)}) collective-permute-start(bf16[32,7168]{1,0:T(8,128)(2,1)S(1)} %add_convert_fusion.6), channel_id=1, source_target_pairs={{0,1},{1,2},{2,3},{4,5},{5,6},{6,7},{8,9},{9,10},{10,11},{12,13},{... | collective-permute-start | bytes 1376264 | tf_op jit(solution)/shard_map/ppermute | solution.py:310
  307.1 13.1 %collective-permute-start.28 = (bf16[32,7168]{1,0:T(8,128)(2,1)S(1)}, bf16[32,7168]{1,0:T(8,128)(2,1)S(1)}, u32[]{:S(2)}, u32[]{:S(2)}) collective-permute-start(bf16[32,7168]{1,0:T(8,128)(2,1)S(1)} %add_convert_fusion.4), channel_id=1, source_target_pairs={{0,1},{1,2},{2,3},{4,5},{5,6},{6,7},{8,9},{9,10},{10,11},{12,13},{... | collective-permute-start | bytes 1376264 | tf_op jit(solution)/shard_map/ppermute | solution.py:310
  315.5 12.8 %collective-permute-start.25 = (bf16[32,7168]{1,0:T(8,128)(2,1)S(1)}, bf16[32,7168]{1,0:T(8,128)(2,1)S(1)}, u32[]{:S(2)}, u32[]{:S(2)}) collective-permute-start(bf16[32,7168]{1,0:T(8,128)(2,1)S(1)} %fusion.8), channel_id=1, source_target_pairs={{16,0},{0,16},{17,1},{1,17},{18,2},{2,18},{19,3},{3,19},{20,4},{4,... | collective-permute-start | bytes 1376264 | tf_op jit(solution)/shard_map/ppermute | solution.py:30
  328.5 8.5 %collective-permute-start.32 = (bf16[32,7168]{1,0:T(8,128)(2,1)S(1)}, bf16[32,7168]{1,0:T(8,128)(2,1)S(1)}, u32[]{:S(2)}, u32[]{:S(2)}) collective-permute-start(bf16[32,7168]{1,0:T(8,128)(2,1)S(1)} %fusion.7), channel_id=1, source_target_pairs={{16,0},{0,16},{17,1},{1,17},{18,2},{2,18},{19,3},{3,19},{20,4},{4,... | collective-permute-start | bytes 1376264 | tf_op jit(solution)/shard_map/ppermute | solution.py:30
  (12 other events, 71.6 us)
Sparse Core Ops, SparseCore 0:
  11.0 97.7 all-gather.2

commit v11 on v8

--- a/solution.py
+++ b/solution.py
@@ -69,11 +69,16 @@
 def chained_input(hops, begin, rows):
     (own, _), *others = hops
     from_below, from_above = zip(*others)
-    spec = lambda chunk, column: pl.BlockSpec(
-        (rows, chunk), lambda i, at: (begin // rows, column(i))
-    )
     arrays = [own, *from_below, *from_above]
-    return chained_rows, arrays, [spec] * len(arrays)
+    specs = []
+    for array in arrays:
+        block = begin // rows if array.shape[0] > rows else 0
+        specs.append(
+            lambda chunk, column, block=block: pl.BlockSpec(
+                (rows, chunk), lambda i, at: (block, column(i))
+            )
+        )
+    return chained_rows, arrays, specs
 
 
 def weight_copies(chunk, steps, gate_ups, downs, gate_up_held, down_held, sems):
@@ -250,7 +255,7 @@
         put_blocks(outs, total)
 
 
-def backward_call(at, x_gathered, rows, parts, hops, gate_ups, downs):
+def backward_call(at, x_gathered, rows, parts, hops, last_hops, gate_ups, downs):
     count, width = x_gathered.shape[0], hops[0][0].shape[1]
     pieces, hid = len(downs), downs[0].shape[0]
     chunk = chunk_of(width, 1792)
@@ -258,8 +263,8 @@
     first = lambda i: jnp.minimum(i, steps - 1)
     second = lambda i: jnp.maximum(i - steps, 0)
     _, tags, tag_specs = gathered_input(x_gathered, 0, rows)
-    _, rows_in, row_specs = chained_input(hops, 0, rows)
-    _, _, scaled_specs = chained_input(hops, rows, rows)
+    _, rows_in, row_specs = chained_input([*hops, last_hops[0]], 0, rows)
+    _, scaled_in, scaled_specs = chained_input([*hops, last_hops[1]], rows, rows)
     return pl.pallas_call(
         functools.partial(backward_kernel, len(rows_in), count, pieces, chunk, steps),
         grid_spec=pltpu.PrefetchScalarGridSpec(
@@ -281,7 +286,7 @@
         out_shape=home_shapes(count, rows, width, parts),
         compiler_params=compiler_params(),
         cost_estimate=small_cost(many, hidden),
-    )(at, *tags, *rows_in, *rows_in, *gate_ups, *downs)
+    )(at, *tags, *rows_in, *scaled_in, *gate_ups, *downs)
 
 
 def after(value, *earlier):
@@ -348,21 +353,28 @@
     gate_up, back_rows = after((gate_up, back_rows), across_down)
     across_gate_up = flipped(gate_up, "expert", 2)
     hops = [(back_rows, back_rows)]
-    for step in range(1, count):
+    for step in range(1, count - 1):
         hops.append(hop(*hops[-1], "dp", step))
-    gate_ups = [gate_up, flipped(after(gate_up, hops[1]), "expert", 1), across_gate_up]
     downs = [down, flipped(down, "expert", 1), across_down, flipped(across_down, "expert", 1)]
-    gate_ups.append(flipped(after(across_gate_up, x_gathered, hops[1], downs[1:]), "expert", 1))
+    own_flip = flipped(after(gate_up, hops[1], downs[1], downs[3]), "expert", 1)
+    gate_ups = [gate_up, own_flip, across_gate_up]
+    gate_ups.append(flipped(after(across_gate_up, x_gathered, own_flip), "expert", 1))
     hidden_fwd = hidden_call(at, x_gathered, tokens_here, width, gate_ups)
     partial_fwd = down_call(hidden_fwd, count, downs)
+    last_hops, arrived_rows = [], after(hops[-1], partial_fwd[-1])
+    for part in (slice(0, tokens_here), slice(tokens_here, None)):
+        below, above = (rows[part] for rows in arrived_rows)
+        last_hops.append(hop(below, above, "dp", count - 1))
 
     arrived_fwd = step_home(summands(partial_fwd, 1, None), "dp", 1)
-    arrived_fwd = after(arrived_fwd, hops[2])
+    arrived_fwd = after(arrived_fwd, last_hops[0])
     arrived_fwd = step_home(summands(partial_fwd, 2, arrived_fwd), "dp", 2)
     sends_fwd = summands(partial_fwd, 3, arrived_fwd)
     arrived_fwd = step_home(sends_fwd, "dp", 3)
     hops[0] = after(hops[0], sends_fwd)
-    partial_bwd = backward_call(at, x_gathered, tokens_here, ROW_PARTS, hops, gate_ups, downs)
+    partial_bwd = backward_call(
+        at, x_gathered, tokens_here, ROW_PARTS, hops, last_hops, gate_ups, downs
+    )
 
     arrived_fwd = after(arrived_fwd, partial_bwd[-1])
     total_fwd = summed(partial_fwd[0], arrived_fwd)

time: 346 us -> 362 us (1.046)
  waiting for transfers between devices: 213 us -> 221 us
  starting transfers between devices: 56.8 us -> 62.2 us
    ppermute x9, waiting for transfers between devices: 49.3 us -> 59.9 us  [step_home(): lax.ppermute(pair[1], axis, [(i, i - 1) for i in range(count - step, coun...]
    ppermute x6 -> x8, starting transfers between devices: 13.6 us -> 21.6 us  [hop(): return (lax.ppermute(below, axis, up), lax.ppermute(above, axis, down))]
    ppermute x6 -> x8, waiting for transfers between devices: 98.1 us -> 91.6 us  [hop(): return (lax.ppermute(below, axis, up), lax.ppermute(above, axis, down))]
  transfers between devices with their start and end apart: 34 -> 36, of which waited for: 18 -> 18; matrix products, arithmetic and copies ran while one was open for 2% -> 5% of each run, Pallas kernels for 11% -> 11%
where the time goes in v11:
time: 362 us; the launch traced here: 361 us
  waiting for transfers between devices  221 us (61%)
  starting transfers between devices  62.2 us (17%)
  Pallas kernels  38.4 us (11%)
  between operations  14.6 us (4%)
  other arithmetic  13 us (4%)
  local copies, waits for them, and re-layouts  12 us (3%)
    ppermute x8, waiting for transfers between devices, hop(): return (lax.ppermute(below, axis, up), lax.ppermute(above, axis, down))  91.6 us
    ppermute x9, waiting for transfers between devices, step_home(): lax.ppermute(pair[1], axis, [(i, i - 1) for i in range(count - step, coun...  59.9 us
    ppermute x6, waiting for transfers between devices, flipped(): return lax.ppermute(block, axis, route)  45.4 us
    ppermute x9, starting transfers between devices, step_home(): lax.ppermute(pair[1], axis, [(i, i - 1) for i in range(count - step, coun...  23.4 us
    ppermute x8, starting transfers between devices, hop(): return (lax.ppermute(below, axis, up), lax.ppermute(above, axis, down))  21.6 us
    pallas_call x1, Pallas kernels, backward_call(): pl.pallas_call(functools.partial(backward_kernel, len(rows_in), count, pi...  21.4 us
    ppermute x3, waiting for transfers between devices, shifted(): lax.ppermute(block, axis, [((i - distance) % count, i) for i in range(cou...  15.9 us
    ppermute x9, starting transfers between devices, step_home(): up = lax.ppermute(pair[0], axis, [(i, i + 1) for i in range(step)])  12.1 us
  transfers between devices with their start and end apart: 36, of which 18 were waited for; matrix products, arithmetic and copies ran while one was open for 5% of the time, Pallas kernels for 11%

profile of v11, /device:TPU:20, one launch (start us, length us, event | category | flops | bytes accessed | tf_op | source)
XLA Modules:
  0.0 361.3 jit_solution(17058189790978668139)
XLA Ops:
  7.3 1.6 collective-permute-start
  10.3 2.1 concatenate.12
  12.7 1.2 copy-done.6
  13.9 3.7 %pad_maximum_fusion.refs_8_.refs_18_ = bf16[2,7168,128]{2,1,0:T(8,128)(2,1)} fusion(bf16[1,7168,128]{2,1,0:T(8,128)(2,1)S(1)} %bitcast.44, bf16[1,7168,128]{2,1,0:T(8,128)(2,1)} %bitcast.45), kind=kLoop, calls=%fused_computation | loop fusion | flops 1835008 | bytes 7340032 | tf_op jit(solution)/shard_map/concatenate | solution.py:349
  17.8 32.3 %collective-permute-done.refs_2_.refs_24_ = bf16[128,7168]{1,0:T(8,128)(2,1)} collective-permute-done((bf16[128,7168]{1,0:T(8,128)(2,1)}, bf16[128,7168]{1,0:T(8,128)(2,1)}, u32[]{:S(2)}, u32[]{:S(2)}) %collective-permute-start) | collective-permute-done | bytes 1835040 | tf_op jit(solution)/shard_map/ppermute | solution.py:25
  50.1 2.3 collective-permute-start.2
  52.4 3.6 collective-permute-start.1
  56.0 1.6 collective-permute-start.6
  57.6 65.6 %collective-permute-done.2.refs_8_.refs_15_ = bf16[128,7168]{1,0:T(8,128)(2,1)S(1)} collective-permute-done((bf16[128,7168]{1,0:T(8,128)(2,1)S(1)}, bf16[128,7168]{1,0:T(8,128)(2,1)S(1)}, u32[]{:S(2)}, u32[]{:S(2)}) %collective-permute-start.2) | collective-permute-done | bytes 1835040 | tf_op jit(solution)/shard_map/ppermute | solution.py:300
  125.1 12.5 %collective-permute-done.6.refs_10_.refs_20_ = bf16[2,7168,128]{2,1,0:T(8,128)(2,1)} collective-permute-done((bf16[2,7168,128]{2,1,0:T(8,128)(2,1)}, bf16[2,7168,128]{2,1,0:T(8,128)(2,1)}, u32[]{:S(2)}, u32[]{:S(2)}) %collective-permute-start.6) | collective-permute-done | bytes 3670048 | tf_op jit(solution)/shard_map/ppermute | solution.py:25
  137.6 3.5 collective-permute-start.11
  141.1 1.9 collective-permute-start.10
  144.3 10.2 %shard_map.113.hidden_ref = bf16[256,512]{1,0:T(8,128)(2,1)} custom-call(s32[2]{0:T(128)} %pad_add_fusion.at_ref, bf16[4,64,7296]{2,1,0:T(8,128)(2,1)} %bitcast.27, bf16[4,64,7296]{2,1,0:T(8,128)(2,1)} %bitcast.28, bf16[4,64,7296]{2,1,0:T(8,128)(2,1)} %bitcast.29, bf16[4,64,7296]{2,1,0:T(8,128)(2,1)} %bitcast.30, bf16[4,64,7296]{2,1,0:T(8,128)(2,1)} %bitcast.31, ...), custom_call_target="tpu_custom_call" | custom-call | flops 131072 | bytes 256 | tf_op jit(solution)/shard_map/pallas_call | solution.py:163
  154.6 6.8 %shard_map.114 = (f32[64,7168]{1,0:T(8,128)}, bf16[64,7168]{1,0:T(8,128)(2,1)}, bf16[64,7168]{1,0:T(8,128)(2,1)}, bf16[64,7168]{1,0:T(8,128)(2,1)}) custom-call(bf16[256,512]{1,0:T(8,128)(2,1)} %shard_map.113.hidden_ref, bf16[128,7168]{1,0:T(8,128)(2,1)} %bitcast.41, bf16[128,7168]{1,0:T(8,128)(2,1)} %collective-permute-done.3.refs_1_.refs_23_, ...), custom_call_target="tpu_custom_call" | custom-call | flops 131072 | bytes 256 | tf_op jit(solution)/shard_map/pallas_call | solution.py:190
  162.1 18.0 %collective-permute-done.11.refs_9_.refs_16_ = bf16[128,7168]{1,0:T(8,128)(2,1)} collective-permute-done((bf16[128,7168]{1,0:T(8,128)(2,1)}, bf16[128,7168]{1,0:T(8,128)(2,1)}, u32[]{:S(2)}, u32[]{:S(2)}) %collective-permute-start.11) | collective-permute-done | bytes 1835040 | tf_op jit(solution)/shard_map/ppermute | solution.py:300
  180.1 5.3 %collective-permute-done.10.refs_6_.refs_13_ = bf16[128,7168]{1,0:T(8,128)(2,1)} collective-permute-done((bf16[128,7168]{1,0:T(8,128)(2,1)}, bf16[128,7168]{1,0:T(8,128)(2,1)}, u32[]{:S(2)}, u32[]{:S(2)}) %collective-permute-start.10) | collective-permute-done | bytes 1835040 | tf_op jit(solution)/shard_map/ppermute | solution.py:300
  185.4 1.3 collective-permute-start.9
  186.7 1.6 fusion.10
  188.3 4.8 %collective-permute-start.12 = (bf16[64,7168]{1,0:T(8,128)(2,1)S(1)}, bf16[64,7168]{1,0:T(8,128)(2,1)S(1)}, u32[]{:S(2)}, u32[]{:S(2)}) collective-permute-start(bf16[64,7168]{1,0:T(8,128)(2,1)S(1)} %get-tuple-element.79), channel_id=1, source_target_pairs={{2,3},{6,7},{10,11},{14,15},{18,19},{22,23},{26,27},{30,31}} | collective-permute-start | bytes 2752520 | tf_op jit(solution)/shard_map/ppermute | solution.py:300
  193.1 1.6 fusion.9
  195.4 13.8 %collective-permute-done.9 = bf16[64,7168]{1,0:T(8,128)(2,1)S(1)} collective-permute-done((bf16[64,7168]{1,0:T(8,128)(2,1)}, bf16[64,7168]{1,0:T(8,128)(2,1)S(1)}, u32[]{:S(2)}, u32[]{:S(2)}) %collective-permute-start.9) | collective-permute-done | bytes 917536 | tf_op jit(solution)/shard_map/ppermute | solution.py:315
  209.1 2.7 collective-permute-done.12.refs_7_
  213.1 2.0 collective-permute-start.16
  215.2 4.0 %collective-permute-start.18 = (bf16[64,7168]{1,0:T(8,128)(2,1)S(1)}, bf16[64,7168]{1,0:T(8,128)(2,1)S(1)}, u32[]{:S(2)}, u32[]{:S(2)}) collective-permute-start(bf16[64,7168]{1,0:T(8,128)(2,1)S(1)} %get-tuple-element.78), channel_id=1, source_target_pairs={{2,3},{6,7},{10,11},{14,15},{18,19},{22,23},{26,27},{30,31}} | collective-permute-start | bytes 2752520 | tf_op jit(solution)/shard_map/ppermute | solution.py:300
  219.9 1.3 collective-permute-start.14
  221.2 14.5 %collective-permute-done.16 = bf16[64,7168]{1,0:T(8,128)(2,1)S(1)} collective-permute-done((bf16[64,7168]{1,0:T(8,128)(2,1)S(1)}, bf16[64,7168]{1,0:T(8,128)(2,1)S(1)}, u32[]{:S(2)}, u32[]{:S(2)}) %collective-permute-start.16) | collective-permute-done | bytes 917536 | tf_op jit(solution)/shard_map/ppermute | solution.py:315
  236.9 2.1 collective-permute-start.17
  238.9 2.9 collective-permute-done.14
  243.0 2.2 collective-permute-start.15
  247.1 21.4 %shard_map.115 = (f32[32,7168]{1,0:T(8,128)}, f32[32,7168]{1,0:T(8,128)}, bf16[32,7168]{1,0:T(8,128)(2,1)}, bf16[32,7168]{1,0:T(8,128)(2,1)}, bf16[32,7168]{1,0:...) custom-call(s32[2]{0:T(128)} %pad_add_fusion.at_ref, ...), custom_call_target="tpu_custom_call" | custom-call | flops 131072 | bytes 256 | tf_op jit(solution)/shard_map/pallas_call | solution.py:268
  268.5 1.3 collective-permute-start.23
  270.5 1.3 collective-permute-start.31
  272.5 2.0 add_convert_fusion
  275.1 14.6 %collective-permute-done.31 = bf16[32,7168]{1,0:T(8,128)(2,1)S(1)} collective-permute-done((bf16[32,7168]{1,0:T(8,128)(2,1)}, bf16[32,7168]{1,0:T(8,128)(2,1)S(1)}, u32[]{:S(2)}, u32[]{:S(2)}) %collective-permute-start.31) | collective-permute-done | bytes 458784 | tf_op jit(solution)/shard_map/ppermute | solution.py:315
  289.9 4.5 %collective-permute-start.32 = (bf16[32,7168]{1,0:T(8,128)(2,1)S(1)}, bf16[32,7168]{1,0:T(8,128)(2,1)S(1)}, u32[]{:S(2)}, u32[]{:S(2)}) collective-permute-start(bf16[32,7168]{1,0:T(8,128)(2,1)S(1)} %get-tuple-element.84), channel_id=1, source_target_pairs={{2,1},{3,2},{6,5},{7,6},{10,9},{11,10},{14,13},{15,14},{18,17},{19... | collective-permute-start | bytes 1376264 | tf_op jit(solution)/shard_map/ppermute | solution.py:315
  294.6 2.1 collective-permute-start.24
  296.7 1.3 collective-permute-start.22
  298.0 1.4 collective-permute-start.29
  299.4 6.0 %collective-permute-done.32 = bf16[32,7168]{1,0:T(8,128)(2,1)S(1)} collective-permute-done((bf16[32,7168]{1,0:T(8,128)(2,1)S(1)}, bf16[32,7168]{1,0:T(8,128)(2,1)S(1)}, u32[]{:S(2)}, u32[]{:S(2)}) %collective-permute-start.32) | collective-permute-done | bytes 458784 | tf_op jit(solution)/shard_map/ppermute | solution.py:315
  305.5 4.5 %collective-permute-start.33 = (bf16[32,7168]{1,0:T(8,128)(2,1)S(1)}, bf16[32,7168]{1,0:T(8,128)(2,1)S(1)}, u32[]{:S(2)}, u32[]{:S(2)}) collective-permute-start(bf16[32,7168]{1,0:T(8,128)(2,1)S(1)} %add_convert_fusion.3), channel_id=1, source_target_pairs={{1,0},{2,1},{3,2},{5,4},{6,5},{7,6},{9,8},{10,9},{11,10},{13,12},{... | collective-permute-start | bytes 1376264 | tf_op jit(solution)/shard_map/ppermute | solution.py:315
  310.0 5.2 %collective-permute-done.24 = bf16[32,7168]{1,0:T(8,128)(2,1)S(1)} collective-permute-done((bf16[32,7168]{1,0:T(8,128)(2,1)S(1)}, bf16[32,7168]{1,0:T(8,128)(2,1)S(1)}, u32[]{:S(2)}, u32[]{:S(2)}) %collective-permute-start.24) | collective-permute-done | bytes 458784 | tf_op jit(solution)/shard_map/ppermute | solution.py:315
  315.5 4.5 %collective-permute-start.26 = (bf16[32,7168]{1,0:T(8,128)(2,1)S(1)}, bf16[32,7168]{1,0:T(8,128)(2,1)S(1)}, u32[]{:S(2)}, u32[]{:S(2)}) collective-permute-start(bf16[32,7168]{1,0:T(8,128)(2,1)S(1)} %add_convert_fusion.5), channel_id=1, source_target_pairs={{1,0},{2,1},{3,2},{5,4},{6,5},{7,6},{9,8},{10,9},{11,10},{13,12},{... | collective-permute-start | bytes 1376264 | tf_op jit(solution)/shard_map/ppermute | solution.py:315
  319.9 1.9 collective-permute-start.25
  322.0 1.9 collective-permute-start.30
  323.9 5.8 %collective-permute-done.26 = bf16[32,7168]{1,0:T(8,128)(2,1)S(1)} collective-permute-done((bf16[32,7168]{1,0:T(8,128)(2,1)S(1)}, bf16[32,7168]{1,0:T(8,128)(2,1)S(1)}, u32[]{:S(2)}, u32[]{:S(2)}) %collective-permute-start.26) | collective-permute-done | bytes 458784 | tf_op jit(solution)/shard_map/ppermute | solution.py:315
  331.7 4.1 %collective-permute-done.30 = bf16[32,7168]{1,0:T(8,128)(2,1)S(1)} collective-permute-done((bf16[32,7168]{1,0:T(8,128)(2,1)S(1)}, bf16[32,7168]{1,0:T(8,128)(2,1)S(1)}, u32[]{:S(2)}, u32[]{:S(2)}) %collective-permute-start.30) | collective-permute-done | bytes 458784 | tf_op jit(solution)/shard_map/ppermute | solution.py:314
  335.8 8.0 %collective-permute-done.27 = bf16[32,7168]{1,0:T(8,128)(2,1)S(1)} collective-permute-done((bf16[32,7168]{1,0:T(8,128)(2,1)S(1)}, bf16[32,7168]{1,0:T(8,128)(2,1)S(1)}, u32[]{:S(2)}, u32[]{:S(2)}) %collective-permute-start.27) | collective-permute-done | bytes 458784 | tf_op jit(solution)/shard_map/ppermute | solution.py:30
  344.6 7.9 %collective-permute-done.34 = bf16[32,7168]{1,0:T(8,128)(2,1)S(1)} collective-permute-done((bf16[32,7168]{1,0:T(8,128)(2,1)S(1)}, bf16[32,7168]{1,0:T(8,128)(2,1)S(1)}, u32[]{:S(2)}, u32[]{:S(2)}) %collective-permute-start.34) | collective-permute-done | bytes 458784 | tf_op jit(solution)/shard_map/ppermute | solution.py:30
  (105 shorter events, 20.2 us)
Async XLA Ops:
  7.2 130.4 %all-gather.3.cloned.1.call-start = ((), (), s32[]{:S(2)}) async-start(), calls=%async_computation | async-start | bytes 4669440 | tf_op jit(solution)/shard_map/all_gather | solution.py:351
  7.2 50.3 %collective-permute-start.3 = (bf16[128,7168]{1,0:T(8,128)(2,1)}, bf16[128,7168]{1,0:T(8,128)(2,1)}, u32[]{:S(2)}, u32[]{:S(2)}) collective-permute-start(bf16[128,7168]{1,0:T(8,128)(2,1)} %bitcast.39), channel_id=1, source_target_pairs={{0,4},{4,0},{8,12},{12,8},{1,5},{5,1},{9,13},{13,9},{2,6},{6,2},{1... | collective-permute-start | bytes 5505032 | tf_op jit(solution)/shard_map/ppermute | solution.py:25
  7.3 42.7 %collective-permute-start = (bf16[128,7168]{1,0:T(8,128)(2,1)}, bf16[128,7168]{1,0:T(8,128)(2,1)}, u32[]{:S(2)}, u32[]{:S(2)}) collective-permute-start(bf16[128,7168]{1,0:T(8,128)(2,1)} %bitcast.40), channel_id=1, source_target_pairs={{0,8},{4,12},{8,0},{12,4},{1,9},{5,13},{9,1},{13,5},{2,10},{6,14},... | collective-permute-start | bytes 5505032 | tf_op jit(solution)/shard_map/ppermute | solution.py:25
  17.8 136.8 %copy-start = (bf16[128,7168]{1,0:T(8,128)(2,1)}, bf16[128,7168]{1,0:T(8,128)(2,1)S(1)}, u32[]{:S(2)}) copy-start(bf16[128,7168]{1,0:T(8,128)(2,1)S(1)} %pad_maximum_fusion.1.refs_4_.refs_11_) | copy-start | bytes 5505028
  50.1 7.5 %collective-permute-start.4 = (bf16[128,7168]{1,0:T(8,128)(2,1)}, bf16[128,7168]{1,0:T(8,128)(2,1)S(1)}, u32[]{:S(2)}, u32[]{:S(2)}) collective-permute-start(bf16[128,7168]{1,0:T(8,128)(2,1)} %collective-permute-done.refs_2_.refs_24_), channel_id=1, source_target_pairs={{0,4},{4,0},{8,12},{12,8},{1,5},{5,1},{9,13},{13,9},{2,6},{6,2},{1... | collective-permute-start | bytes 5505032 | tf_op jit(solution)/shard_map/ppermute | solution.py:25
  50.1 73.1 %collective-permute-start.2 = (bf16[128,7168]{1,0:T(8,128)(2,1)S(1)}, bf16[128,7168]{1,0:T(8,128)(2,1)S(1)}, u32[]{:S(2)}, u32[]{:S(2)}) collective-permute-start(bf16[128,7168]{1,0:T(8,128)(2,1)S(1)} %pad_maximum_fusion.1.refs_4_.refs_11_), channel_id=1, source_target_pairs={{1,0},{2,1},{3,2},{5,4},{6,5},{7,6},{9,8},{10,9},{11,10},{13,12},{... | collective-permute-start | bytes 5505032 | tf_op jit(solution)/shard_map/ppermute | solution.py:300
  52.4 70.8 %collective-permute-start.1 = (bf16[128,7168]{1,0:T(8,128)(2,1)S(1)}, bf16[128,7168]{1,0:T(8,128)(2,1)S(1)}, u32[]{:S(2)}, u32[]{:S(2)}) collective-permute-start(bf16[128,7168]{1,0:T(8,128)(2,1)S(1)} %pad_maximum_fusion.1.refs_4_.refs_11_), channel_id=1, source_target_pairs={{0,1},{1,2},{2,3},{4,5},{5,6},{6,7},{8,9},{9,10},{10,11},{12,13},{... | collective-permute-start | bytes 5505032 | tf_op jit(solution)/shard_map/ppermute | solution.py:300
  56.0 81.6 %collective-permute-start.6 = (bf16[2,7168,128]{2,1,0:T(8,128)(2,1)}, bf16[2,7168,128]{2,1,0:T(8,128)(2,1)}, u32[]{:S(2)}, u32[]{:S(2)}) collective-permute-start(bf16[2,7168,128]{2,1,0:T(8,128)(2,1)} %pad_maximum_fusion.refs_8_.refs_18_), channel_id=1, source_target_pairs={{0,8},{4,12},{8,0},{12,4},{1,9},{5,13},{9,1},{13,5},{2,10},{6,14},... | collective-permute-start | bytes 11010056 | tf_op jit(solution)/shard_map/ppermute | solution.py:25
  57.6 65.6 %copy-start.1 = (bf16[128,7168]{1,0:T(8,128)(2,1)}, bf16[128,7168]{1,0:T(8,128)(2,1)S(1)}, u32[]{:S(2)}) copy-start(bf16[128,7168]{1,0:T(8,128)(2,1)S(1)} %collective-permute-done.4.refs_3_.refs_25_) | copy-start | bytes 5505028
  123.2 14.4 %collective-permute-start.5 = (bf16[2,7168,128]{2,1,0:T(8,128)(2,1)}, bf16[2,7168,128]{2,1,0:T(8,128)(2,1)}, u32[]{:S(2)}, u32[]{:S(2)}) collective-permute-start(bf16[2,7168,128]{2,1,0:T(8,128)(2,1)} %pad_maximum_fusion.refs_8_.refs_18_), channel_id=1, source_target_pairs={{0,4},{4,0},{8,12},{12,8},{1,5},{5,1},{9,13},{13,9},{2,6},{6,2},{1... | collective-permute-start | bytes 11010056 | tf_op jit(solution)/shard_map/ppermute | solution.py:25
  137.6 6.8 %collective-permute-start.7 = (bf16[2,7168,128]{2,1,0:T(8,128)(2,1)}, bf16[2,7168,128]{2,1,0:T(8,128)(2,1)}, u32[]{:S(2)}, u32[]{:S(2)}) collective-permute-start(bf16[2,7168,128]{2,1,0:T(8,128)(2,1)} %collective-permute-done.6.refs_10_.refs_20_), channel_id=1, source_target_pairs={{0,4},{4,0},{8,12},{12,8},{1,5},{5,1},{9,13},{13,9},{2,6},{6,2},{1... | collective-permute-start | bytes 11010056 | tf_op jit(solution)/shard_map/ppermute | solution.py:25
  137.6 42.5 %collective-permute-start.11 = (bf16[128,7168]{1,0:T(8,128)(2,1)}, bf16[128,7168]{1,0:T(8,128)(2,1)}, u32[]{:S(2)}, u32[]{:S(2)}) collective-permute-start(bf16[128,7168]{1,0:T(8,128)(2,1)} %copy-done.2), channel_id=1, source_target_pairs={{1,0},{2,1},{5,4},{6,5},{9,8},{10,9},{13,12},{14,13},{17,16},{18,1... | collective-permute-start | bytes 5505032 | tf_op jit(solution)/shard_map/ppermute | solution.py:300
  141.1 44.3 %collective-permute-start.10 = (bf16[128,7168]{1,0:T(8,128)(2,1)}, bf16[128,7168]{1,0:T(8,128)(2,1)}, u32[]{:S(2)}, u32[]{:S(2)}) collective-permute-start(bf16[128,7168]{1,0:T(8,128)(2,1)} %copy-done.3), channel_id=1, source_target_pairs={{1,2},{2,3},{5,6},{6,7},{9,10},{10,11},{13,14},{14,15},{17,18},{18... | collective-permute-start | bytes 5505032 | tf_op jit(solution)/shard_map/ppermute | solution.py:300
  161.4 47.7 %collective-permute-start.8 = (bf16[64,7168]{1,0:T(8,128)(2,1)}, bf16[64,7168]{1,0:T(8,128)(2,1)S(1)}, u32[]{:S(2)}, u32[]{:S(2)}) collective-permute-start(bf16[64,7168]{1,0:T(8,128)(2,1)} %get-tuple-element.46), channel_id=1, source_target_pairs={{0,1},{4,5},{8,9},{12,13},{16,17},{20,21},{24,25},{28,29}} | collective-permute-start | bytes 2752520 | tf_op jit(solution)/shard_map/ppermute | solution.py:314
  185.4 23.7 %collective-permute-start.9 = (bf16[64,7168]{1,0:T(8,128)(2,1)}, bf16[64,7168]{1,0:T(8,128)(2,1)S(1)}, u32[]{:S(2)}, u32[]{:S(2)}) collective-permute-start(bf16[64,7168]{1,0:T(8,128)(2,1)} %get-tuple-element.44), channel_id=1, source_target_pairs={{3,2},{7,6},{11,10},{15,14},{19,18},{23,22},{27,26},{31,30}} | collective-permute-start | bytes 2752520 | tf_op jit(solution)/shard_map/ppermute | solution.py:315
  188.3 23.6 %collective-permute-start.12 = (bf16[64,7168]{1,0:T(8,128)(2,1)S(1)}, bf16[64,7168]{1,0:T(8,128)(2,1)S(1)}, u32[]{:S(2)}, u32[]{:S(2)}) collective-permute-start(bf16[64,7168]{1,0:T(8,128)(2,1)S(1)} %get-tuple-element.79), channel_id=1, source_target_pairs={{2,3},{6,7},{10,11},{14,15},{18,19},{22,23},{26,27},{30,31}} | collective-permute-start | bytes 2752520 | tf_op jit(solution)/shard_map/ppermute | solution.py:300
  194.7 17.2 %collective-permute-start.13 = (bf16[64,7168]{1,0:T(8,128)(2,1)S(1)}, bf16[64,7168]{1,0:T(8,128)(2,1)S(1)}, u32[]{:S(2)}, u32[]{:S(2)}) collective-permute-start(bf16[64,7168]{1,0:T(8,128)(2,1)S(1)} %get-tuple-element.77), channel_id=1, source_target_pairs={{1,0},{5,4},{9,8},{13,12},{17,16},{21,20},{25,24},{29,28}} | collective-permute-start | bytes 2752520 | tf_op jit(solution)/shard_map/ppermute | solution.py:300
  211.9 23.8 %copy-start.16 = (bf16[64,7168]{1,0:T(8,128)(2,1)S(1)}, bf16[64,7168]{1,0:T(8,128)(2,1)}, u32[]{:S(2)}) copy-start(bf16[64,7168]{1,0:T(8,128)(2,1)} %get-tuple-element.46) | copy-start | bytes 2752516
  213.1 28.7 %copy-start.15 = (bf16[64,7168]{1,0:T(8,128)(2,1)S(1)}, bf16[64,7168]{1,0:T(8,128)(2,1)}, u32[]{:S(2)}) copy-start(bf16[64,7168]{1,0:T(8,128)(2,1)} %get-tuple-element.44) | copy-start | bytes 2752516
  213.1 22.6 %collective-permute-start.16 = (bf16[64,7168]{1,0:T(8,128)(2,1)S(1)}, bf16[64,7168]{1,0:T(8,128)(2,1)S(1)}, u32[]{:S(2)}, u32[]{:S(2)}) collective-permute-start(bf16[64,7168]{1,0:T(8,128)(2,1)S(1)} %get-tuple-element.80), channel_id=1, source_target_pairs={{2,1},{3,2},{6,5},{7,6},{10,9},{11,10},{14,13},{15,14},{18,17},{19... | collective-permute-start | bytes 2752520 | tf_op jit(solution)/shard_map/ppermute | solution.py:315
  215.2 30.0 %collective-permute-start.18 = (bf16[64,7168]{1,0:T(8,128)(2,1)S(1)}, bf16[64,7168]{1,0:T(8,128)(2,1)S(1)}, u32[]{:S(2)}, u32[]{:S(2)}) collective-permute-start(bf16[64,7168]{1,0:T(8,128)(2,1)S(1)} %get-tuple-element.78), channel_id=1, source_target_pairs={{2,3},{6,7},{10,11},{14,15},{18,19},{22,23},{26,27},{30,31}} | collective-permute-start | bytes 2752520 | tf_op jit(solution)/shard_map/ppermute | solution.py:300
  219.2 26.0 %collective-permute-start.19 = (bf16[64,7168]{1,0:T(8,128)(2,1)S(1)}, bf16[64,7168]{1,0:T(8,128)(2,1)S(1)}, u32[]{:S(2)}, u32[]{:S(2)}) collective-permute-start(bf16[64,7168]{1,0:T(8,128)(2,1)S(1)} %get-tuple-element.76), channel_id=1, source_target_pairs={{1,0},{5,4},{9,8},{13,12},{17,16},{21,20},{25,24},{29,28}} | collective-permute-start | bytes 2752520 | tf_op jit(solution)/shard_map/ppermute | solution.py:300
  219.9 21.9 %collective-permute-start.14 = (bf16[64,7168]{1,0:T(8,128)(2,1)S(1)}, bf16[64,7168]{1,0:T(8,128)(2,1)S(1)}, u32[]{:S(2)}, u32[]{:S(2)}) collective-permute-start(bf16[64,7168]{1,0:T(8,128)(2,1)S(1)} %get-tuple-element.81), channel_id=1, source_target_pairs={{0,1},{1,2},{4,5},{5,6},{8,9},{9,10},{12,13},{13,14},{16,17},{17,1... | collective-permute-start | bytes 2752520 | tf_op jit(solution)/shard_map/ppermute | solution.py:314
  236.9 31.6 %collective-permute-start.17 = (bf16[64,7168]{1,0:T(8,128)(2,1)}, bf16[64,7168]{1,0:T(8,128)(2,1)}, u32[]{:S(2)}, u32[]{:S(2)}) collective-permute-start(bf16[64,7168]{1,0:T(8,128)(2,1)} %add_convert_fusion.1), channel_id=1, source_target_pairs={{1,0},{2,1},{3,2},{5,4},{6,5},{7,6},{9,8},{10,9},{11,10},{13,12},{... | collective-permute-start | bytes 2752520 | tf_op jit(solution)/shard_map/ppermute | solution.py:315
  243.0 29.5 %copy-start.4 = (bf16[1,64,7168]{2,1,0:T(8,128)(2,1)S(1)}, bf16[1,64,7168]{2,1,0:T(8,128)(2,1)}, u32[]{:S(2)}) copy-start(bf16[1,64,7168]{2,1,0:T(8,128)(2,1)} %param.10) | copy-start | bytes 2752516
  243.0 29.5 %copy-start.7 = (f32[64,7168]{1,0:T(8,128)S(1)}, f32[64,7168]{1,0:T(8,128)}, u32[]{:S(2)}) copy-start(f32[64,7168]{1,0:T(8,128)} %get-tuple-element.43) | copy-start | bytes 5505028
  243.0 29.5 %copy-start.24 = (f32[1,64]{1,0:T(1,128)S(1)}, f32[1,64]{1,0:T(1,128)}, u32[]{:S(2)}) copy-start(f32[1,64]{1,0:T(1,128)} %param.12) | copy-start | bytes 772
  243.0 25.5 %collective-permute-start.15 = (bf16[64,7168]{1,0:T(8,128)(2,1)}, bf16[64,7168]{1,0:T(8,128)(2,1)}, u32[]{:S(2)}, u32[]{:S(2)}) collective-permute-start(bf16[64,7168]{1,0:T(8,128)(2,1)} %add_convert_fusion.2), channel_id=1, source_target_pairs={{0,1},{1,2},{2,3},{4,5},{5,6},{6,7},{8,9},{9,10},{10,11},{12,13},{... | collective-permute-start | bytes 2752520 | tf_op jit(solution)/shard_map/ppermute | solution.py:314
  268.5 25.9 %collective-permute-start.23 = (bf16[32,7168]{1,0:T(8,128)(2,1)}, bf16[32,7168]{1,0:T(8,128)(2,1)S(1)}, u32[]{:S(2)}, u32[]{:S(2)}) collective-permute-start(bf16[32,7168]{1,0:T(8,128)(2,1)} %get-tuple-element.63), channel_id=1, source_target_pairs={{3,2},{7,6},{11,10},{15,14},{19,18},{23,22},{27,26},{31,30}} | collective-permute-start | bytes 1376264 | tf_op jit(solution)/shard_map/ppermute | solution.py:315
  269.8 24.6 %collective-permute-start.21 = (bf16[32,7168]{1,0:T(8,128)(2,1)}, bf16[32,7168]{1,0:T(8,128)(2,1)S(1)}, u32[]{:S(2)}, u32[]{:S(2)}) collective-permute-start(bf16[32,7168]{1,0:T(8,128)(2,1)} %get-tuple-element.65), channel_id=1, source_target_pairs={{0,1},{4,5},{8,9},{12,13},{16,17},{20,21},{24,25},{28,29}} | collective-permute-start | bytes 1376264 | tf_op jit(solution)/shard_map/ppermute | solution.py:314
  270.5 19.2 %collective-permute-start.31 = (bf16[32,7168]{1,0:T(8,128)(2,1)}, bf16[32,7168]{1,0:T(8,128)(2,1)S(1)}, u32[]{:S(2)}, u32[]{:S(2)}) collective-permute-start(bf16[32,7168]{1,0:T(8,128)(2,1)} %get-tuple-element.71), channel_id=1, source_target_pairs={{3,2},{7,6},{11,10},{15,14},{19,18},{23,22},{27,26},{31,30}} | collective-permute-start | bytes 1376264 | tf_op jit(solution)/shard_map/ppermute | solution.py:315
  271.8 17.9 %collective-permute-start.28 = (bf16[32,7168]{1,0:T(8,128)(2,1)}, bf16[32,7168]{1,0:T(8,128)(2,1)S(1)}, u32[]{:S(2)}, u32[]{:S(2)}) collective-permute-start(bf16[32,7168]{1,0:T(8,128)(2,1)} %get-tuple-element.73), channel_id=1, source_target_pairs={{0,1},{4,5},{8,9},{12,13},{16,17},{20,21},{24,25},{28,29}} | collective-permute-start | bytes 1376264 | tf_op jit(solution)/shard_map/ppermute | solution.py:314
  274.5 30.9 %copy-start.21 = (bf16[32,7168]{1,0:T(8,128)(2,1)S(1)}, bf16[32,7168]{1,0:T(8,128)(2,1)}, u32[]{:S(2)}) copy-start(bf16[32,7168]{1,0:T(8,128)(2,1)} %get-tuple-element.73) | copy-start | bytes 1376260
  274.5 40.7 %collective-permute-start.20 = (bf16[64,7168]{1,0:T(8,128)(2,1)S(1)}, bf16[64,7168]{1,0:T(8,128)(2,1)S(1)}, u32[]{:S(2)}, u32[]{:S(2)}) collective-permute-start(bf16[64,7168]{1,0:T(8,128)(2,1)S(1)} %add_convert_fusion), channel_id=1, source_target_pairs={{16,0},{0,16},{17,1},{1,17},{18,2},{2,18},{19,3},{3,19},{20,4},{4,... | collective-permute-start | bytes 2752520 | tf_op jit(solution)/shard_map/ppermute | solution.py:30
  289.9 25.3 %copy-start.20 = (bf16[32,7168]{1,0:T(8,128)(2,1)S(1)}, bf16[32,7168]{1,0:T(8,128)(2,1)}, u32[]{:S(2)}) copy-start(bf16[32,7168]{1,0:T(8,128)(2,1)} %get-tuple-element.63) | copy-start | bytes 1376260
  289.9 15.5 %collective-permute-start.32 = (bf16[32,7168]{1,0:T(8,128)(2,1)S(1)}, bf16[32,7168]{1,0:T(8,128)(2,1)S(1)}, u32[]{:S(2)}, u32[]{:S(2)}) collective-permute-start(bf16[32,7168]{1,0:T(8,128)(2,1)S(1)} %get-tuple-element.84), channel_id=1, source_target_pairs={{2,1},{3,2},{6,5},{7,6},{10,9},{11,10},{14,13},{15,14},{18,17},{19... | collective-permute-start | bytes 1376264 | tf_op jit(solution)/shard_map/ppermute | solution.py:315
  294.6 20.6 %collective-permute-start.24 = (bf16[32,7168]{1,0:T(8,128)(2,1)S(1)}, bf16[32,7168]{1,0:T(8,128)(2,1)S(1)}, u32[]{:S(2)}, u32[]{:S(2)}) collective-permute-start(bf16[32,7168]{1,0:T(8,128)(2,1)S(1)} %get-tuple-element.82), channel_id=1, source_target_pairs={{2,1},{3,2},{6,5},{7,6},{10,9},{11,10},{14,13},{15,14},{18,17},{19... | collective-permute-start | bytes 1376264 | tf_op jit(solution)/shard_map/ppermute | solution.py:315
  296.7 18.6 %collective-permute-start.22 = (bf16[32,7168]{1,0:T(8,128)(2,1)S(1)}, bf16[32,7168]{1,0:T(8,128)(2,1)S(1)}, u32[]{:S(2)}, u32[]{:S(2)}) collective-permute-start(bf16[32,7168]{1,0:T(8,128)(2,1)S(1)} %get-tuple-element.83), channel_id=1, source_target_pairs={{0,1},{1,2},{4,5},{5,6},{8,9},{9,10},{12,13},{13,14},{16,17},{17,1... | collective-permute-start | bytes 1376264 | tf_op jit(solution)/shard_map/ppermute | solution.py:314
  298.0 23.9 %copy-start.18 = (bf16[32,7168]{1,0:T(8,128)(2,1)S(1)}, bf16[32,7168]{1,0:T(8,128)(2,1)}, u32[]{:S(2)}) copy-start(bf16[32,7168]{1,0:T(8,128)(2,1)} %get-tuple-element.71) | copy-start | bytes 1376260
  298.0 23.9 %collective-permute-start.29 = (bf16[32,7168]{1,0:T(8,128)(2,1)S(1)}, bf16[32,7168]{1,0:T(8,128)(2,1)S(1)}, u32[]{:S(2)}, u32[]{:S(2)}) collective-permute-start(bf16[32,7168]{1,0:T(8,128)(2,1)S(1)} %get-tuple-element.85), channel_id=1, source_target_pairs={{0,1},{1,2},{4,5},{5,6},{8,9},{9,10},{12,13},{13,14},{16,17},{17,1... | collective-permute-start | bytes 1376264 | tf_op jit(solution)/shard_map/ppermute | solution.py:314
  305.5 25.4 %copy-start.14 = (f32[32,7168]{1,0:T(8,128)S(1)}, f32[32,7168]{1,0:T(8,128)}, u32[]{:S(2)}) copy-start(f32[32,7168]{1,0:T(8,128)} %get-tuple-element.62) | copy-start | bytes 2752516
  305.5 26.2 %collective-permute-start.33 = (bf16[32,7168]{1,0:T(8,128)(2,1)S(1)}, bf16[32,7168]{1,0:T(8,128)(2,1)S(1)}, u32[]{:S(2)}, u32[]{:S(2)}) collective-permute-start(bf16[32,7168]{1,0:T(8,128)(2,1)S(1)} %add_convert_fusion.3), channel_id=1, source_target_pairs={{1,0},{2,1},{3,2},{5,4},{6,5},{7,6},{9,8},{10,9},{11,10},{13,12},{... | collective-permute-start | bytes 1376264 | tf_op jit(solution)/shard_map/ppermute | solution.py:315
  315.5 28.3 %copy-start.13 = (f32[32,7168]{1,0:T(8,128)S(1)}, f32[32,7168]{1,0:T(8,128)}, u32[]{:S(2)}) copy-start(f32[32,7168]{1,0:T(8,128)} %get-tuple-element.70) | copy-start | bytes 2752516
  315.5 14.3 %collective-permute-start.26 = (bf16[32,7168]{1,0:T(8,128)(2,1)S(1)}, bf16[32,7168]{1,0:T(8,128)(2,1)S(1)}, u32[]{:S(2)}, u32[]{:S(2)}) collective-permute-start(bf16[32,7168]{1,0:T(8,128)(2,1)S(1)} %add_convert_fusion.5), channel_id=1, source_target_pairs={{1,0},{2,1},{3,2},{5,4},{6,5},{7,6},{9,8},{10,9},{11,10},{13,12},{... | collective-permute-start | bytes 1376264 | tf_op jit(solution)/shard_map/ppermute | solution.py:315
  319.9 11.0 %collective-permute-start.25 = (bf16[32,7168]{1,0:T(8,128)(2,1)S(1)}, bf16[32,7168]{1,0:T(8,128)(2,1)S(1)}, u32[]{:S(2)}, u32[]{:S(2)}) collective-permute-start(bf16[32,7168]{1,0:T(8,128)(2,1)S(1)} %add_convert_fusion.6), channel_id=1, source_target_pairs={{0,1},{1,2},{2,3},{4,5},{5,6},{6,7},{8,9},{9,10},{10,11},{12,13},{... | collective-permute-start | bytes 1376264 | tf_op jit(solution)/shard_map/ppermute | solution.py:314
  322.0 13.8 %collective-permute-start.30 = (bf16[32,7168]{1,0:T(8,128)(2,1)S(1)}, bf16[32,7168]{1,0:T(8,128)(2,1)S(1)}, u32[]{:S(2)}, u32[]{:S(2)}) collective-permute-start(bf16[32,7168]{1,0:T(8,128)(2,1)S(1)} %add_convert_fusion.4), channel_id=1, source_target_pairs={{0,1},{1,2},{2,3},{4,5},{5,6},{6,7},{8,9},{9,10},{10,11},{12,13},{... | collective-permute-start | bytes 1376264 | tf_op jit(solution)/shard_map/ppermute | solution.py:314
  331.1 12.7 %collective-permute-start.27 = (bf16[32,7168]{1,0:T(8,128)(2,1)S(1)}, bf16[32,7168]{1,0:T(8,128)(2,1)S(1)}, u32[]{:S(2)}, u32[]{:S(2)}) collective-permute-start(bf16[32,7168]{1,0:T(8,128)(2,1)S(1)} %fusion.8), channel_id=1, source_target_pairs={{16,0},{0,16},{17,1},{1,17},{18,2},{2,18},{19,3},{3,19},{20,4},{4,... | collective-permute-start | bytes 1376264 | tf_op jit(solution)/shard_map/ppermute | solution.py:30
  344.0 8.5 %collective-permute-start.34 = (bf16[32,7168]{1,0:T(8,128)(2,1)S(1)}, bf16[32,7168]{1,0:T(8,128)(2,1)S(1)}, u32[]{:S(2)}, u32[]{:S(2)}) collective-permute-start(bf16[32,7168]{1,0:T(8,128)(2,1)S(1)} %fusion.7), channel_id=1, source_target_pairs={{16,0},{0,16},{17,1},{1,17},{18,2},{2,18},{19,3},{3,19},{20,4},{4,... | collective-permute-start | bytes 1376264 | tf_op jit(solution)/shard_map/ppermute | solution.py:30
  (14 other events, 104.4 us)
Sparse Core Ops, SparseCore 0:
  12.6 100.5 all-gather.2

commit v12 on v8

--- a/solution.py
+++ b/solution.py
@@ -9,7 +9,7 @@
 from jax.sharding import PartitionSpec as P
 
 BF16, F32 = jnp.bfloat16, jnp.float32
-VMEM_LIMIT = 56 * 1024 * 1024
+VMEM_LIMIT = 44 * 1024 * 1024
 ROW_PARTS = 2
 TAG_COLUMNS = 128
 

time: 346 us -> 341 us (0.986)
  waiting for transfers between devices: 213 us -> 219 us
  starting transfers between devices: 56.8 us -> 51.4 us
  Pallas kernels: 38.4 us -> 34.2 us
    ppermute x9, starting transfers between devices: 24.7 us -> 16 us  [step_home(): lax.ppermute(pair[1], axis, [(i, i - 1) for i in range(count - step, coun...]
    ppermute x9, waiting for transfers between devices: 49.3 us -> 53.1 us  [step_home(): lax.ppermute(pair[1], axis, [(i, i - 1) for i in range(count - step, coun...]
    unnamed x53 -> x33, local copies, waits for them, and re-layouts: 7.78 us -> 8.03 us
  transfers between devices with their start and end apart: 34 -> 34, of which waited for: 18 -> 16; matrix products, arithmetic and copies ran while one was open for 2% -> 2% of each run, Pallas kernels for 11% -> 10%
where the time goes in v12:
time: 341 us; the launch traced here: 340 us
  waiting for transfers between devices  219 us (64%)
  starting transfers between devices  51.4 us (15%)
  Pallas kernels  34.2 us (10%)
  between operations  14.5 us (4%)
  other arithmetic  10.7 us (3%)
  local copies, waits for them, and re-layouts  10.2 us (3%)
    ppermute x6, waiting for transfers between devices, hop(): return (lax.ppermute(below, axis, up), lax.ppermute(above, axis, down))  99.8 us
    ppermute x9, waiting for transfers between devices, step_home(): lax.ppermute(pair[1], axis, [(i, i - 1) for i in range(count - step, coun...  53.1 us
    ppermute x6, waiting for transfers between devices, flipped(): return lax.ppermute(block, axis, route)  44.2 us
    pallas_call x1, Pallas kernels, backward_call(): pl.pallas_call(functools.partial(backward_kernel, len(rows_in), count, pi...  20.1 us
    ppermute x6, starting transfers between devices, hop(): return (lax.ppermute(below, axis, up), lax.ppermute(above, axis, down))  16.1 us
    ppermute x3, waiting for transfers between devices, shifted(): lax.ppermute(block, axis, [((i - distance) % count, i) for i in range(cou...  16.1 us
    ppermute x9, starting transfers between devices, step_home(): lax.ppermute(pair[1], axis, [(i, i - 1) for i in range(count - step, coun...  16 us
    ppermute x9, starting transfers between devices, step_home(): up = lax.ppermute(pair[0], axis, [(i, i + 1) for i in range(step)])  13.9 us
  transfers between devices with their start and end apart: 34, of which 16 were waited for; matrix products, arithmetic and copies ran while one was open for 2% of the time, Pallas kernels for 10%

profile of v12, /device:TPU:20, one launch (start us, length us, event | category | flops | bytes accessed | tf_op | source)
XLA Modules:
  0.0 340.3 jit_solution(17662149396318134750)
XLA Ops:
  8.8 2.0 concatenate.12
  10.8 1.6 collective-permute-start
  12.7 1.5 pad_maximum_fusion.1.refs_4_.refs_11_
  15.0 2.1 pad_maximum_fusion.refs_8_.refs_18_
  17.1 35.8 %collective-permute-done.refs_2_.refs_24_ = bf16[128,7168]{1,0:T(8,128)(2,1)S(1)} collective-permute-done((bf16[128,7168]{1,0:T(8,128)(2,1)}, bf16[128,7168]{1,0:T(8,128)(2,1)S(1)}, u32[]{:S(2)}, u32[]{:S(2)}) %collective-permute-start) | collective-permute-done | bytes 1835040 | tf_op jit(solution)/shard_map/ppermute | solution.py:25
  52.9 1.5 collective-permute-start.4
  54.4 2.3 collective-permute-start.2
  56.7 3.6 %collective-permute-start.1 = (bf16[128,7168]{1,0:T(8,128)(2,1)S(1)}, bf16[128,7168]{1,0:T(8,128)(2,1)S(1)}, u32[]{:S(2)}, u32[]{:S(2)}) collective-permute-start(bf16[128,7168]{1,0:T(8,128)(2,1)S(1)} %pad_maximum_fusion.1.refs_4_.refs_11_), channel_id=1, source_target_pairs={{0,1},{1,2},{2,3},{4,5},{5,6},{6,7},{8,9},{9,10},{10,11},{12,13},{... | collective-permute-start | bytes 5505032 | tf_op jit(solution)/shard_map/ppermute | solution.py:295
  60.9 1.2 copy-done
  62.1 60.4 %collective-permute-done.2.refs_8_.refs_15_ = bf16[128,7168]{1,0:T(8,128)(2,1)S(1)} collective-permute-done((bf16[128,7168]{1,0:T(8,128)(2,1)S(1)}, bf16[128,7168]{1,0:T(8,128)(2,1)S(1)}, u32[]{:S(2)}, u32[]{:S(2)}) %collective-permute-start.2) | collective-permute-done | bytes 1835040 | tf_op jit(solution)/shard_map/ppermute | solution.py:295
  122.7 1.3 copy-done.4
  125.0 1.3 copy-done.7
  126.3 7.2 %collective-permute-done.4.refs_10_.refs_20_ = bf16[2,7168,128]{2,1,0:T(8,128)(2,1)} collective-permute-done((bf16[2,7168,128]{2,1,0:T(8,128)(2,1)}, bf16[2,7168,128]{2,1,0:T(8,128)(2,1)}, u32[]{:S(2)}, u32[]{:S(2)}) %collective-permute-start.4) | collective-permute-done | bytes 3670048 | tf_op jit(solution)/shard_map/ppermute | solution.py:25
  133.5 3.6 %collective-permute-start.11 = (bf16[128,7168]{1,0:T(8,128)(2,1)}, bf16[128,7168]{1,0:T(8,128)(2,1)}, u32[]{:S(2)}, u32[]{:S(2)}) collective-permute-start(bf16[128,7168]{1,0:T(8,128)(2,1)} %copy-done.6), channel_id=1, source_target_pairs={{1,0},{2,1},{5,4},{6,5},{9,8},{10,9},{13,12},{14,13},{17,16},{18,1... | collective-permute-start | bytes 5505032 | tf_op jit(solution)/shard_map/ppermute | solution.py:295
  137.1 1.9 collective-permute-start.10
  139.1 1.2 collective-permute-done.7.refs_11_.refs_21_
  140.2 9.5 %shard_map.113.hidden_ref = bf16[256,512]{1,0:T(8,128)(2,1)S(1)} custom-call(s32[2]{0:T(128)S(1)} %pad_add_fusion.at_ref, bf16[4,64,7296]{2,1,0:T(8,128)(2,1)} %bitcast.27, bf16[4,64,7296]{2,1,0:T(8,128)(2,1)} %bitcast.28, bf16[4,64,7296]{2,1,0:T(8,128)(2,1)} %bitcast.29, bf16[4,64,7296]{2,1,0:T(8,128)(2,1)} %bitcast.30, bf16[4,64,7296]{2,1,0:T(8,128)(2,1)} %bitcast.31, ...), custom_call_target="tpu_custom_call" | custom-call | flops 131072 | bytes 256 | tf_op jit(solution)/shard_map/pallas_call | solution.py:158
  149.7 4.7 %shard_map.114 = (f32[64,7168]{1,0:T(8,128)S(1)}, bf16[64,7168]{1,0:T(8,128)(2,1)S(1)}, bf16[64,7168]{1,0:T(8,128)(2,1)S(1)}, bf16[64,7168]{1,0:T(8,128)(2,1)S(1)}) custom-call(bf16[256,512]{1,0:T(8,128)(2,1)S(1)} %shard_map.113.hidden_ref, bf16[128,7168]{1,0:T(8,128)(2,1)} %bitcast.12.refs_0_.refs_22_, bf16[128,7168]{1,0:T(8,128)(2,1)S(1)} %copy-done.5, ...), custom_call_target="tpu_custom_call" | custom-call | flops 131072 | bytes 256 | tf_op jit(solution)/shard_map/pallas_call | solution.py:185
  154.4 1.3 collective-permute-start.9
  156.4 19.7 %collective-permute-done.11.refs_9_.refs_16_ = bf16[128,7168]{1,0:T(8,128)(2,1)} collective-permute-done((bf16[128,7168]{1,0:T(8,128)(2,1)}, bf16[128,7168]{1,0:T(8,128)(2,1)}, u32[]{:S(2)}, u32[]{:S(2)}) %collective-permute-start.11) | collective-permute-done | bytes 1835040 | tf_op jit(solution)/shard_map/ppermute | solution.py:295
  176.1 5.3 %collective-permute-done.10.refs_6_.refs_13_ = bf16[128,7168]{1,0:T(8,128)(2,1)} collective-permute-done((bf16[128,7168]{1,0:T(8,128)(2,1)}, bf16[128,7168]{1,0:T(8,128)(2,1)}, u32[]{:S(2)}, u32[]{:S(2)}) %collective-permute-start.10) | collective-permute-done | bytes 1835040 | tf_op jit(solution)/shard_map/ppermute | solution.py:295
  181.8 2.1 collective-permute-start.14
  184.7 3.9 %collective-permute-start.16 = (bf16[128,7168]{1,0:T(8,128)(2,1)}, bf16[128,7168]{1,0:T(8,128)(2,1)S(1)}, u32[]{:S(2)}, u32[]{:S(2)}) collective-permute-start(bf16[128,7168]{1,0:T(8,128)(2,1)} %collective-permute-done.10.refs_6_.refs_13_), channel_id=1, source_target_pairs={{2,3},{6,7},{10,11},{14,15},{18,19},{22,23},{26,27},{30,31}} | collective-permute-start | bytes 5505032 | tf_op jit(solution)/shard_map/ppermute | solution.py:295
  188.6 1.3 collective-permute-start.12
  189.9 15.4 %collective-permute-done.14 = bf16[64,7168]{1,0:T(8,128)(2,1)S(1)} collective-permute-done((bf16[64,7168]{1,0:T(8,128)(2,1)S(1)}, bf16[64,7168]{1,0:T(8,128)(2,1)S(1)}, u32[]{:S(2)}, u32[]{:S(2)}) %collective-permute-start.14) | collective-permute-done | bytes 917536 | tf_op jit(solution)/shard_map/ppermute | solution.py:310
  206.5 2.3 collective-permute-start.15
  208.9 2.8 collective-permute-done.12
  212.8 2.0 collective-permute-start.13
  214.9 14.4 %collective-permute-done.16.refs_7_.refs_14_ = bf16[128,7168]{1,0:T(8,128)(2,1)S(1)} collective-permute-done((bf16[128,7168]{1,0:T(8,128)(2,1)}, bf16[128,7168]{1,0:T(8,128)(2,1)S(1)}, u32[]{:S(2)}, u32[]{:S(2)}) %collective-permute-start.16) | collective-permute-done | bytes 1835040 | tf_op jit(solution)/shard_map/ppermute | solution.py:295
  229.3 1.3 copy-done.9
  230.6 20.1 %shard_map.115 = (f32[32,7168]{1,0:T(8,128)S(1)}, f32[32,7168]{1,0:T(8,128)S(1)}, bf16[32,7168]{1,0:T(8,128)(2,1)S(1)}, bf16[32,7168]{1,0:T(8,128)(2,1)S(1)}, bf...) custom-call(s32[2]{0:T(128)S(1)} %pad_add_fusion.at_ref, ...), custom_call_target="tpu_custom_call" | custom-call | flops 131072 | bytes 256 | tf_op jit(solution)/shard_map/pallas_call | solution.py:263
  250.8 1.3 collective-permute-start.21
  252.8 1.3 collective-permute-start.29
  255.9 15.3 %collective-permute-done.29 = bf16[32,7168]{1,0:T(8,128)(2,1)S(1)} collective-permute-done((bf16[32,7168]{1,0:T(8,128)(2,1)S(1)}, bf16[32,7168]{1,0:T(8,128)(2,1)S(1)}, u32[]{:S(2)}, u32[]{:S(2)}) %collective-permute-start.29) | collective-permute-done | bytes 458784 | tf_op jit(solution)/shard_map/ppermute | solution.py:310
  271.4 1.9 collective-permute-start.30
  273.6 1.9 collective-permute-start.22
  275.5 1.3 collective-permute-start.20
  276.8 1.3 collective-permute-start.27
  278.1 8.7 %collective-permute-done.30 = bf16[32,7168]{1,0:T(8,128)(2,1)S(1)} collective-permute-done((bf16[32,7168]{1,0:T(8,128)(2,1)S(1)}, bf16[32,7168]{1,0:T(8,128)(2,1)S(1)}, u32[]{:S(2)}, u32[]{:S(2)}) %collective-permute-start.30) | collective-permute-done | bytes 458784 | tf_op jit(solution)/shard_map/ppermute | solution.py:310
  286.9 1.9 collective-permute-start.31
  288.8 7.8 %collective-permute-done.22 = bf16[32,7168]{1,0:T(8,128)(2,1)S(1)} collective-permute-done((bf16[32,7168]{1,0:T(8,128)(2,1)S(1)}, bf16[32,7168]{1,0:T(8,128)(2,1)S(1)}, u32[]{:S(2)}, u32[]{:S(2)}) %collective-permute-start.22) | collective-permute-done | bytes 458784 | tf_op jit(solution)/shard_map/ppermute | solution.py:310
  296.8 1.9 collective-permute-start.24
  298.8 3.9 %collective-permute-start.23 = (bf16[32,7168]{1,0:T(8,128)(2,1)S(1)}, bf16[32,7168]{1,0:T(8,128)(2,1)S(1)}, u32[]{:S(2)}, u32[]{:S(2)}) collective-permute-start(bf16[32,7168]{1,0:T(8,128)(2,1)S(1)} %add_convert_fusion.6), channel_id=1, source_target_pairs={{0,1},{1,2},{2,3},{4,5},{5,6},{6,7},{8,9},{9,10},{10,11},{12,13},{... | collective-permute-start | bytes 1376264 | tf_op jit(solution)/shard_map/ppermute | solution.py:309
  302.9 1.9 collective-permute-start.28
  304.8 5.8 %collective-permute-done.24 = bf16[32,7168]{1,0:T(8,128)(2,1)S(1)} collective-permute-done((bf16[32,7168]{1,0:T(8,128)(2,1)S(1)}, bf16[32,7168]{1,0:T(8,128)(2,1)S(1)}, u32[]{:S(2)}, u32[]{:S(2)}) %collective-permute-start.24) | collective-permute-done | bytes 458784 | tf_op jit(solution)/shard_map/ppermute | solution.py:310
  311.4 3.3 collective-permute-done.28
  314.7 8.1 %collective-permute-done.25 = bf16[32,7168]{1,0:T(8,128)(2,1)S(1)} collective-permute-done((bf16[32,7168]{1,0:T(8,128)(2,1)S(1)}, bf16[32,7168]{1,0:T(8,128)(2,1)S(1)}, u32[]{:S(2)}, u32[]{:S(2)}) %collective-permute-start.25) | collective-permute-done | bytes 458784 | tf_op jit(solution)/shard_map/ppermute | solution.py:30
  323.6 8.0 %collective-permute-done.32 = bf16[32,7168]{1,0:T(8,128)(2,1)S(1)} collective-permute-done((bf16[32,7168]{1,0:T(8,128)(2,1)S(1)}, bf16[32,7168]{1,0:T(8,128)(2,1)S(1)}, u32[]{:S(2)}, u32[]{:S(2)}) %collective-permute-start.32) | collective-permute-done | bytes 458784 | tf_op jit(solution)/shard_map/ppermute | solution.py:30
  (79 shorter events, 15.4 us)
Async XLA Ops:
  7.2 5.2 %copy-start.11 = (bf16[1,64,7168]{2,1,0:T(8,128)(2,1)S(1)}, bf16[1,64,7168]{2,1,0:T(8,128)(2,1)}, u32[]{:S(2)}) copy-start(bf16[1,64,7168]{2,1,0:T(8,128)(2,1)} %param.16) | copy-start | bytes 2752516
  7.2 5.2 %copy-start.15 = (f32[1,64]{1,0:T(1,128)S(1)}, f32[1,64]{1,0:T(1,128)}, u32[]{:S(2)}) copy-start(f32[1,64]{1,0:T(1,128)} %param.15) | copy-start | bytes 772
  7.2 126.3 %all-gather.3.cloned.1.call-start = ((), (), s32[]{:S(2)}) async-start(), calls=%async_computation | async-start | bytes 4669440 | tf_op jit(solution)/shard_map/all_gather | solution.py:346
  10.8 42.0 %collective-permute-start = (bf16[128,7168]{1,0:T(8,128)(2,1)}, bf16[128,7168]{1,0:T(8,128)(2,1)S(1)}, u32[]{:S(2)}, u32[]{:S(2)}) collective-permute-start(bf16[128,7168]{1,0:T(8,128)(2,1)} %bitcast.12.refs_0_.refs_22_), channel_id=1, source_target_pairs={{0,8},{4,12},{8,0},{12,4},{1,9},{5,13},{9,1},{13,5},{2,10},{6,14},... | collective-permute-start | bytes 5505032 | tf_op jit(solution)/shard_map/ppermute | solution.py:25
  12.6 1.8 copy-start.12
  12.6 2.3 copy-start.13
  52.9 80.6 %collective-permute-start.4 = (bf16[2,7168,128]{2,1,0:T(8,128)(2,1)}, bf16[2,7168,128]{2,1,0:T(8,128)(2,1)}, u32[]{:S(2)}, u32[]{:S(2)}) collective-permute-start(bf16[2,7168,128]{2,1,0:T(8,128)(2,1)} %pad_maximum_fusion.refs_8_.refs_18_), channel_id=1, source_target_pairs={{0,8},{4,12},{8,0},{12,4},{1,9},{5,13},{9,1},{13,5},{2,10},{6,14},... | collective-permute-start | bytes 11010056 | tf_op jit(solution)/shard_map/ppermute | solution.py:25
  54.4 68.2 %collective-permute-start.2 = (bf16[128,7168]{1,0:T(8,128)(2,1)S(1)}, bf16[128,7168]{1,0:T(8,128)(2,1)S(1)}, u32[]{:S(2)}, u32[]{:S(2)}) collective-permute-start(bf16[128,7168]{1,0:T(8,128)(2,1)S(1)} %pad_maximum_fusion.1.refs_4_.refs_11_), channel_id=1, source_target_pairs={{1,0},{2,1},{3,2},{5,4},{6,5},{7,6},{9,8},{10,9},{11,10},{13,12},{... | collective-permute-start | bytes 5505032 | tf_op jit(solution)/shard_map/ppermute | solution.py:295
  56.7 65.8 %collective-permute-start.1 = (bf16[128,7168]{1,0:T(8,128)(2,1)S(1)}, bf16[128,7168]{1,0:T(8,128)(2,1)S(1)}, u32[]{:S(2)}, u32[]{:S(2)}) collective-permute-start(bf16[128,7168]{1,0:T(8,128)(2,1)S(1)} %pad_maximum_fusion.1.refs_4_.refs_11_), channel_id=1, source_target_pairs={{0,1},{1,2},{2,3},{4,5},{5,6},{6,7},{8,9},{9,10},{10,11},{12,13},{... | collective-permute-start | bytes 5505032 | tf_op jit(solution)/shard_map/ppermute | solution.py:295
  60.3 62.3 %collective-permute-start.5 = (bf16[128,7168]{1,0:T(8,128)(2,1)}, bf16[128,7168]{1,0:T(8,128)(2,1)S(1)}, u32[]{:S(2)}, u32[]{:S(2)}) collective-permute-start(bf16[128,7168]{1,0:T(8,128)(2,1)} %bitcast.12.refs_0_.refs_22_), channel_id=1, source_target_pairs={{0,4},{4,0},{8,12},{12,8},{1,5},{5,1},{9,13},{13,9},{2,6},{6,2},{1... | collective-permute-start | bytes 5505032 | tf_op jit(solution)/shard_map/ppermute | solution.py:25
  60.4 63.6 %collective-permute-start.6 = (bf16[128,7168]{1,0:T(8,128)(2,1)S(1)}, bf16[128,7168]{1,0:T(8,128)(2,1)S(1)}, u32[]{:S(2)}, u32[]{:S(2)}) collective-permute-start(bf16[128,7168]{1,0:T(8,128)(2,1)S(1)} %collective-permute-done.refs_2_.refs_24_), channel_id=1, source_target_pairs={{0,4},{4,0},{8,12},{12,8},{1,5},{5,1},{9,13},{13,9},{2,6},{6,2},{1... | collective-permute-start | bytes 5505032 | tf_op jit(solution)/shard_map/ppermute | solution.py:25
  122.6 1.8 copy-start.6
  122.6 2.4 copy-start.2
  122.6 16.5 %collective-permute-start.3 = (bf16[2,7168,128]{2,1,0:T(8,128)(2,1)}, bf16[2,7168,128]{2,1,0:T(8,128)(2,1)}, u32[]{:S(2)}, u32[]{:S(2)}) collective-permute-start(bf16[2,7168,128]{2,1,0:T(8,128)(2,1)} %pad_maximum_fusion.refs_8_.refs_18_), channel_id=1, source_target_pairs={{0,4},{4,0},{8,12},{12,8},{1,5},{5,1},{9,13},{13,9},{2,6},{6,2},{1... | collective-permute-start | bytes 11010056 | tf_op jit(solution)/shard_map/ppermute | solution.py:25
  125.0 1.3 copy-start.7
  133.5 6.8 %collective-permute-start.7 = (bf16[2,7168,128]{2,1,0:T(8,128)(2,1)}, bf16[2,7168,128]{2,1,0:T(8,128)(2,1)}, u32[]{:S(2)}, u32[]{:S(2)}) collective-permute-start(bf16[2,7168,128]{2,1,0:T(8,128)(2,1)} %collective-permute-done.4.refs_10_.refs_20_), channel_id=1, source_target_pairs={{0,4},{4,0},{8,12},{12,8},{1,5},{5,1},{9,13},{13,9},{2,6},{6,2},{1... | collective-permute-start | bytes 11010056 | tf_op jit(solution)/shard_map/ppermute | solution.py:25
  133.5 42.6 %collective-permute-start.11 = (bf16[128,7168]{1,0:T(8,128)(2,1)}, bf16[128,7168]{1,0:T(8,128)(2,1)}, u32[]{:S(2)}, u32[]{:S(2)}) collective-permute-start(bf16[128,7168]{1,0:T(8,128)(2,1)} %copy-done.6), channel_id=1, source_target_pairs={{1,0},{2,1},{5,4},{6,5},{9,8},{10,9},{13,12},{14,13},{17,16},{18,1... | collective-permute-start | bytes 5505032 | tf_op jit(solution)/shard_map/ppermute | solution.py:295
  137.1 44.3 %collective-permute-start.10 = (bf16[128,7168]{1,0:T(8,128)(2,1)}, bf16[128,7168]{1,0:T(8,128)(2,1)}, u32[]{:S(2)}, u32[]{:S(2)}) collective-permute-start(bf16[128,7168]{1,0:T(8,128)(2,1)} %copy-done.2), channel_id=1, source_target_pairs={{1,2},{2,3},{5,6},{6,7},{9,10},{10,11},{13,14},{14,15},{17,18},{18... | collective-permute-start | bytes 5505032 | tf_op jit(solution)/shard_map/ppermute | solution.py:295
  139.1 10.7 %copy-start.1 = (bf16[128,7168]{1,0:T(8,128)(2,1)S(1)}, bf16[128,7168]{1,0:T(8,128)(2,1)}, u32[]{:S(2)}) copy-start(bf16[128,7168]{1,0:T(8,128)(2,1)} %copy-done) | copy-start | bytes 5505028
  139.1 10.7 %copy-start.5 = (bf16[128,7168]{1,0:T(8,128)(2,1)S(1)}, bf16[128,7168]{1,0:T(8,128)(2,1)}, u32[]{:S(2)}) copy-start(bf16[128,7168]{1,0:T(8,128)(2,1)} %copy-done.4) | copy-start | bytes 5505028
  154.4 27.0 %collective-permute-start.9 = (bf16[64,7168]{1,0:T(8,128)(2,1)S(1)}, bf16[64,7168]{1,0:T(8,128)(2,1)S(1)}, u32[]{:S(2)}, u32[]{:S(2)}) collective-permute-start(bf16[64,7168]{1,0:T(8,128)(2,1)S(1)} %get-tuple-element.42), channel_id=1, source_target_pairs={{3,2},{7,6},{11,10},{15,14},{19,18},{23,22},{27,26},{31,30}} | collective-permute-start | bytes 2752520 | tf_op jit(solution)/shard_map/ppermute | solution.py:310
  155.7 25.7 %collective-permute-start.8 = (bf16[64,7168]{1,0:T(8,128)(2,1)S(1)}, bf16[64,7168]{1,0:T(8,128)(2,1)S(1)}, u32[]{:S(2)}, u32[]{:S(2)}) collective-permute-start(bf16[64,7168]{1,0:T(8,128)(2,1)S(1)} %get-tuple-element.44), channel_id=1, source_target_pairs={{0,1},{4,5},{8,9},{12,13},{16,17},{20,21},{24,25},{28,29}} | collective-permute-start | bytes 2752520 | tf_op jit(solution)/shard_map/ppermute | solution.py:309
  181.8 23.6 %collective-permute-start.14 = (bf16[64,7168]{1,0:T(8,128)(2,1)S(1)}, bf16[64,7168]{1,0:T(8,128)(2,1)S(1)}, u32[]{:S(2)}, u32[]{:S(2)}) collective-permute-start(bf16[64,7168]{1,0:T(8,128)(2,1)S(1)} %get-tuple-element.72), channel_id=1, source_target_pairs={{2,1},{3,2},{6,5},{7,6},{10,9},{11,10},{14,13},{15,14},{18,17},{19... | collective-permute-start | bytes 2752520 | tf_op jit(solution)/shard_map/ppermute | solution.py:310
  183.9 30.9 %collective-permute-start.17 = (bf16[128,7168]{1,0:T(8,128)(2,1)}, bf16[128,7168]{1,0:T(8,128)(2,1)S(1)}, u32[]{:S(2)}, u32[]{:S(2)}) collective-permute-start(bf16[128,7168]{1,0:T(8,128)(2,1)} %collective-permute-done.11.refs_9_.refs_16_), channel_id=1, source_target_pairs={{1,0},{5,4},{9,8},{13,12},{17,16},{21,20},{25,24},{29,28}} | collective-permute-start | bytes 5505032 | tf_op jit(solution)/shard_map/ppermute | solution.py:295
  184.7 44.6 %collective-permute-start.16 = (bf16[128,7168]{1,0:T(8,128)(2,1)}, bf16[128,7168]{1,0:T(8,128)(2,1)S(1)}, u32[]{:S(2)}, u32[]{:S(2)}) collective-permute-start(bf16[128,7168]{1,0:T(8,128)(2,1)} %collective-permute-done.10.refs_6_.refs_13_), channel_id=1, source_target_pairs={{2,3},{6,7},{10,11},{14,15},{18,19},{22,23},{26,27},{30,31}} | collective-permute-start | bytes 5505032 | tf_op jit(solution)/shard_map/ppermute | solution.py:295
  188.6 23.0 %collective-permute-start.12 = (bf16[64,7168]{1,0:T(8,128)(2,1)S(1)}, bf16[64,7168]{1,0:T(8,128)(2,1)S(1)}, u32[]{:S(2)}, u32[]{:S(2)}) collective-permute-start(bf16[64,7168]{1,0:T(8,128)(2,1)S(1)} %get-tuple-element.73), channel_id=1, source_target_pairs={{0,1},{1,2},{4,5},{5,6},{8,9},{9,10},{12,13},{13,14},{16,17},{17,1... | collective-permute-start | bytes 2752520 | tf_op jit(solution)/shard_map/ppermute | solution.py:309
  206.5 24.1 %copy-start.3 = (bf16[128,7168]{1,0:T(8,128)(2,1)S(1)}, bf16[128,7168]{1,0:T(8,128)(2,1)}, u32[]{:S(2)}) copy-start(bf16[128,7168]{1,0:T(8,128)(2,1)} %copy-done.2) | copy-start | bytes 5505028
  206.5 44.2 %collective-permute-start.15 = (bf16[64,7168]{1,0:T(8,128)(2,1)}, bf16[64,7168]{1,0:T(8,128)(2,1)S(1)}, u32[]{:S(2)}, u32[]{:S(2)}) collective-permute-start(bf16[64,7168]{1,0:T(8,128)(2,1)} %add_convert_fusion.1), channel_id=1, source_target_pairs={{1,0},{2,1},{3,2},{5,4},{6,5},{7,6},{9,8},{10,9},{11,10},{13,12},{... | collective-permute-start | bytes 2752520 | tf_op jit(solution)/shard_map/ppermute | solution.py:310
  212.8 42.0 %copy-start.10 = (bf16[1,64,7168]{2,1,0:T(8,128)(2,1)S(1)}, bf16[1,64,7168]{2,1,0:T(8,128)(2,1)}, u32[]{:S(2)}) copy-start(bf16[1,64,7168]{2,1,0:T(8,128)(2,1)} %param.10) | copy-start | bytes 2752516
  212.8 42.0 %copy-start.14 = (f32[1,64]{1,0:T(1,128)S(1)}, f32[1,64]{1,0:T(1,128)}, u32[]{:S(2)}) copy-start(f32[1,64]{1,0:T(1,128)} %param.12) | copy-start | bytes 772
  212.8 38.0 %collective-permute-start.13 = (bf16[64,7168]{1,0:T(8,128)(2,1)}, bf16[64,7168]{1,0:T(8,128)(2,1)S(1)}, u32[]{:S(2)}, u32[]{:S(2)}) collective-permute-start(bf16[64,7168]{1,0:T(8,128)(2,1)} %add_convert_fusion.2), channel_id=1, source_target_pairs={{0,1},{1,2},{2,3},{4,5},{5,6},{6,7},{8,9},{9,10},{10,11},{12,13},{... | collective-permute-start | bytes 2752520 | tf_op jit(solution)/shard_map/ppermute | solution.py:309
  214.8 14.5 %copy-start.8 = (bf16[128,7168]{1,0:T(8,128)(2,1)}, bf16[128,7168]{1,0:T(8,128)(2,1)S(1)}, u32[]{:S(2)}) copy-start(bf16[128,7168]{1,0:T(8,128)(2,1)S(1)} %collective-permute-done.17.refs_10_.refs_17_) | copy-start | bytes 5505028
  229.3 1.3 copy-start.9
  250.8 22.6 %collective-permute-start.21 = (bf16[32,7168]{1,0:T(8,128)(2,1)S(1)}, bf16[32,7168]{1,0:T(8,128)(2,1)S(1)}, u32[]{:S(2)}, u32[]{:S(2)}) collective-permute-start(bf16[32,7168]{1,0:T(8,128)(2,1)S(1)} %get-tuple-element.59), channel_id=1, source_target_pairs={{3,2},{7,6},{11,10},{15,14},{19,18},{23,22},{27,26},{31,30}} | collective-permute-start | bytes 1376264 | tf_op jit(solution)/shard_map/ppermute | solution.py:310
  252.1 21.3 %collective-permute-start.19 = (bf16[32,7168]{1,0:T(8,128)(2,1)S(1)}, bf16[32,7168]{1,0:T(8,128)(2,1)S(1)}, u32[]{:S(2)}, u32[]{:S(2)}) collective-permute-start(bf16[32,7168]{1,0:T(8,128)(2,1)S(1)} %get-tuple-element.61), channel_id=1, source_target_pairs={{0,1},{4,5},{8,9},{12,13},{16,17},{20,21},{24,25},{28,29}} | collective-permute-start | bytes 1376264 | tf_op jit(solution)/shard_map/ppermute | solution.py:309
  252.8 18.5 %collective-permute-start.29 = (bf16[32,7168]{1,0:T(8,128)(2,1)S(1)}, bf16[32,7168]{1,0:T(8,128)(2,1)S(1)}, u32[]{:S(2)}, u32[]{:S(2)}) collective-permute-start(bf16[32,7168]{1,0:T(8,128)(2,1)S(1)} %get-tuple-element.67), channel_id=1, source_target_pairs={{3,2},{7,6},{11,10},{15,14},{19,18},{23,22},{27,26},{31,30}} | collective-permute-start | bytes 1376264 | tf_op jit(solution)/shard_map/ppermute | solution.py:310
  254.1 17.2 %collective-permute-start.26 = (bf16[32,7168]{1,0:T(8,128)(2,1)S(1)}, bf16[32,7168]{1,0:T(8,128)(2,1)S(1)}, u32[]{:S(2)}, u32[]{:S(2)}) collective-permute-start(bf16[32,7168]{1,0:T(8,128)(2,1)S(1)} %get-tuple-element.69), channel_id=1, source_target_pairs={{0,1},{4,5},{8,9},{12,13},{16,17},{20,21},{24,25},{28,29}} | collective-permute-start | bytes 1376264 | tf_op jit(solution)/shard_map/ppermute | solution.py:309
  255.3 41.3 %collective-permute-start.18 = (bf16[64,7168]{1,0:T(8,128)(2,1)S(1)}, bf16[64,7168]{1,0:T(8,128)(2,1)S(1)}, u32[]{:S(2)}, u32[]{:S(2)}) collective-permute-start(bf16[64,7168]{1,0:T(8,128)(2,1)S(1)} %add_convert_fusion), channel_id=1, source_target_pairs={{16,0},{0,16},{17,1},{1,17},{18,2},{2,18},{19,3},{3,19},{20,4},{4,... | collective-permute-start | bytes 2752520 | tf_op jit(solution)/shard_map/ppermute | solution.py:30
  271.4 15.3 %collective-permute-start.30 = (bf16[32,7168]{1,0:T(8,128)(2,1)S(1)}, bf16[32,7168]{1,0:T(8,128)(2,1)S(1)}, u32[]{:S(2)}, u32[]{:S(2)}) collective-permute-start(bf16[32,7168]{1,0:T(8,128)(2,1)S(1)} %get-tuple-element.76), channel_id=1, source_target_pairs={{2,1},{3,2},{6,5},{7,6},{10,9},{11,10},{14,13},{15,14},{18,17},{19... | collective-permute-start | bytes 1376264 | tf_op jit(solution)/shard_map/ppermute | solution.py:310
  273.6 23.0 %collective-permute-start.22 = (bf16[32,7168]{1,0:T(8,128)(2,1)S(1)}, bf16[32,7168]{1,0:T(8,128)(2,1)S(1)}, u32[]{:S(2)}, u32[]{:S(2)}) collective-permute-start(bf16[32,7168]{1,0:T(8,128)(2,1)S(1)} %get-tuple-element.74), channel_id=1, source_target_pairs={{2,1},{3,2},{6,5},{7,6},{10,9},{11,10},{14,13},{15,14},{18,17},{19... | collective-permute-start | bytes 1376264 | tf_op jit(solution)/shard_map/ppermute | solution.py:310
  275.5 21.1 %collective-permute-start.20 = (bf16[32,7168]{1,0:T(8,128)(2,1)S(1)}, bf16[32,7168]{1,0:T(8,128)(2,1)S(1)}, u32[]{:S(2)}, u32[]{:S(2)}) collective-permute-start(bf16[32,7168]{1,0:T(8,128)(2,1)S(1)} %get-tuple-element.75), channel_id=1, source_target_pairs={{0,1},{1,2},{4,5},{5,6},{8,9},{9,10},{12,13},{13,14},{16,17},{17,1... | collective-permute-start | bytes 1376264 | tf_op jit(solution)/shard_map/ppermute | solution.py:309
  276.8 25.9 %collective-permute-start.27 = (bf16[32,7168]{1,0:T(8,128)(2,1)S(1)}, bf16[32,7168]{1,0:T(8,128)(2,1)S(1)}, u32[]{:S(2)}, u32[]{:S(2)}) collective-permute-start(bf16[32,7168]{1,0:T(8,128)(2,1)S(1)} %get-tuple-element.77), channel_id=1, source_target_pairs={{0,1},{1,2},{4,5},{5,6},{8,9},{9,10},{12,13},{13,14},{16,17},{17,1... | collective-permute-start | bytes 1376264 | tf_op jit(solution)/shard_map/ppermute | solution.py:309
  286.9 24.5 %collective-permute-start.31 = (bf16[32,7168]{1,0:T(8,128)(2,1)S(1)}, bf16[32,7168]{1,0:T(8,128)(2,1)S(1)}, u32[]{:S(2)}, u32[]{:S(2)}) collective-permute-start(bf16[32,7168]{1,0:T(8,128)(2,1)S(1)} %add_convert_fusion.3), channel_id=1, source_target_pairs={{1,0},{2,1},{3,2},{5,4},{6,5},{7,6},{9,8},{10,9},{11,10},{13,12},{... | collective-permute-start | bytes 1376264 | tf_op jit(solution)/shard_map/ppermute | solution.py:310
  296.8 13.8 %collective-permute-start.24 = (bf16[32,7168]{1,0:T(8,128)(2,1)S(1)}, bf16[32,7168]{1,0:T(8,128)(2,1)S(1)}, u32[]{:S(2)}, u32[]{:S(2)}) collective-permute-start(bf16[32,7168]{1,0:T(8,128)(2,1)S(1)} %add_convert_fusion.5), channel_id=1, source_target_pairs={{1,0},{2,1},{3,2},{5,4},{6,5},{7,6},{9,8},{10,9},{11,10},{13,12},{... | collective-permute-start | bytes 1376264 | tf_op jit(solution)/shard_map/ppermute | solution.py:310
  298.8 11.9 %collective-permute-start.23 = (bf16[32,7168]{1,0:T(8,128)(2,1)S(1)}, bf16[32,7168]{1,0:T(8,128)(2,1)S(1)}, u32[]{:S(2)}, u32[]{:S(2)}) collective-permute-start(bf16[32,7168]{1,0:T(8,128)(2,1)S(1)} %add_convert_fusion.6), channel_id=1, source_target_pairs={{0,1},{1,2},{2,3},{4,5},{5,6},{6,7},{8,9},{9,10},{10,11},{12,13},{... | collective-permute-start | bytes 1376264 | tf_op jit(solution)/shard_map/ppermute | solution.py:309
  302.9 11.8 %collective-permute-start.28 = (bf16[32,7168]{1,0:T(8,128)(2,1)S(1)}, bf16[32,7168]{1,0:T(8,128)(2,1)S(1)}, u32[]{:S(2)}, u32[]{:S(2)}) collective-permute-start(bf16[32,7168]{1,0:T(8,128)(2,1)S(1)} %add_convert_fusion.4), channel_id=1, source_target_pairs={{0,1},{1,2},{2,3},{4,5},{5,6},{6,7},{8,9},{9,10},{10,11},{12,13},{... | collective-permute-start | bytes 1376264 | tf_op jit(solution)/shard_map/ppermute | solution.py:309
  310.8 12.0 %collective-permute-start.25 = (bf16[32,7168]{1,0:T(8,128)(2,1)S(1)}, bf16[32,7168]{1,0:T(8,128)(2,1)S(1)}, u32[]{:S(2)}, u32[]{:S(2)}) collective-permute-start(bf16[32,7168]{1,0:T(8,128)(2,1)S(1)} %fusion.8), channel_id=1, source_target_pairs={{16,0},{0,16},{17,1},{1,17},{18,2},{2,18},{19,3},{3,19},{20,4},{4,... | collective-permute-start | bytes 1376264 | tf_op jit(solution)/shard_map/ppermute | solution.py:30
  323.0 8.5 %collective-permute-start.32 = (bf16[32,7168]{1,0:T(8,128)(2,1)S(1)}, bf16[32,7168]{1,0:T(8,128)(2,1)S(1)}, u32[]{:S(2)}, u32[]{:S(2)}) collective-permute-start(bf16[32,7168]{1,0:T(8,128)(2,1)S(1)} %fusion.7), channel_id=1, source_target_pairs={{16,0},{0,16},{17,1},{1,17},{18,2},{2,18},{19,3},{3,19},{20,4},{4,... | collective-permute-start | bytes 1376264 | tf_op jit(solution)/shard_map/ppermute | solution.py:30
  (2 other events, 2.5 us)
Sparse Core Ops, SparseCore 0:
  11.0 97.7 all-gather.2

commit v13 on v12

--- a/solution.py
+++ b/solution.py
@@ -9,7 +9,7 @@
 from jax.sharding import PartitionSpec as P
 
 BF16, F32 = jnp.bfloat16, jnp.float32
-VMEM_LIMIT = 44 * 1024 * 1024
+VMEM_LIMIT = 38 * 1024 * 1024
 ROW_PARTS = 2
 TAG_COLUMNS = 128
 

time: 341 us -> 339 us (level)
    unnamed x33 -> x35, local copies, waits for them, and re-layouts: 8.03 us -> 6.56 us
where the time goes in v13:
time: 339 us
  waiting for transfers between devices  221 us (65%)
  starting transfers between devices  51.6 us (15%)
  Pallas kernels  33.4 us (10%)
  between operations  14.5 us (4%)
  other arithmetic  8.82 us (3%)
  local copies, waits for them, and re-layouts  8.75 us (3%)
    ppermute x6, waiting for transfers between devices, hop(): return (lax.ppermute(below, axis, up), lax.ppermute(above, axis, down))  101 us
    ppermute x9, waiting for transfers between devices, step_home(): lax.ppermute(pair[1], axis, [(i, i - 1) for i in range(count - step, coun...  53.2 us
    ppermute x6, waiting for transfers between devices, flipped(): return lax.ppermute(block, axis, route)  44.3 us
    pallas_call x1, Pallas kernels, backward_call(): pl.pallas_call(functools.partial(backward_kernel, len(rows_in), count, pi...  19.6 us
    ppermute x6, starting transfers between devices, hop(): return (lax.ppermute(below, axis, up), lax.ppermute(above, axis, down))  16.3 us
    ppermute x3, waiting for transfers between devices, shifted(): lax.ppermute(block, axis, [((i - distance) % count, i) for i in range(cou...  16.1 us
    ppermute x9, starting transfers between devices, step_home(): lax.ppermute(pair[1], axis, [(i, i - 1) for i in range(count - step, coun...  15.9 us
    ppermute x9, starting transfers between devices, step_home(): up = lax.ppermute(pair[0], axis, [(i, i + 1) for i in range(step)])  13.9 us
  transfers between devices with their start and end apart: 34, of which 16 were waited for; matrix products, arithmetic and copies ran while one was open for 2% of the time, Pallas kernels for 10%

profile of v13, /device:TPU:20, one launch (start us, length us, event | category | flops | bytes accessed | tf_op | source)
XLA Modules:
  0.0 338.6 jit_solution(4662004251827565877)
XLA Ops:
  8.8 2.0 concatenate.12
  10.8 1.6 collective-permute-start
  12.6 1.5 pad_maximum_fusion.1.refs_4_.refs_11_
  15.0 2.1 pad_maximum_fusion.refs_8_.refs_18_
  17.1 35.8 %collective-permute-done.refs_2_.refs_24_ = bf16[128,7168]{1,0:T(8,128)(2,1)S(1)} collective-permute-done((bf16[128,7168]{1,0:T(8,128)(2,1)}, bf16[128,7168]{1,0:T(8,128)(2,1)S(1)}, u32[]{:S(2)}, u32[]{:S(2)}) %collective-permute-start) | collective-permute-done | bytes 1835040 | tf_op jit(solution)/shard_map/ppermute | solution.py:25
  52.9 1.5 collective-permute-start.4
  54.4 2.3 collective-permute-start.2
  56.7 3.6 %collective-permute-start.1 = (bf16[128,7168]{1,0:T(8,128)(2,1)S(1)}, bf16[128,7168]{1,0:T(8,128)(2,1)S(1)}, u32[]{:S(2)}, u32[]{:S(2)}) collective-permute-start(bf16[128,7168]{1,0:T(8,128)(2,1)S(1)} %pad_maximum_fusion.1.refs_4_.refs_11_), channel_id=1, source_target_pairs={{0,1},{1,2},{2,3},{4,5},{5,6},{6,7},{8,9},{9,10},{10,11},{12,13},{... | collective-permute-start | bytes 5505032 | tf_op jit(solution)/shard_map/ppermute | solution.py:295
  60.9 1.2 copy-done
  62.1 60.4 %collective-permute-done.2.refs_8_.refs_15_ = bf16[128,7168]{1,0:T(8,128)(2,1)S(1)} collective-permute-done((bf16[128,7168]{1,0:T(8,128)(2,1)S(1)}, bf16[128,7168]{1,0:T(8,128)(2,1)S(1)}, u32[]{:S(2)}, u32[]{:S(2)}) %collective-permute-start.2) | collective-permute-done | bytes 1835040 | tf_op jit(solution)/shard_map/ppermute | solution.py:295
  122.6 1.3 copy-done.6
  124.9 1.2 copy-done.8
  126.1 7.3 %collective-permute-done.4.refs_10_.refs_20_ = bf16[2,7168,128]{2,1,0:T(8,128)(2,1)} collective-permute-done((bf16[2,7168,128]{2,1,0:T(8,128)(2,1)}, bf16[2,7168,128]{2,1,0:T(8,128)(2,1)}, u32[]{:S(2)}, u32[]{:S(2)}) %collective-permute-start.4) | collective-permute-done | bytes 3670048 | tf_op jit(solution)/shard_map/ppermute | solution.py:25
  133.5 3.6 %collective-permute-start.11 = (bf16[128,7168]{1,0:T(8,128)(2,1)}, bf16[128,7168]{1,0:T(8,128)(2,1)}, u32[]{:S(2)}, u32[]{:S(2)}) collective-permute-start(bf16[128,7168]{1,0:T(8,128)(2,1)} %copy-done.2), channel_id=1, source_target_pairs={{1,0},{2,1},{5,4},{6,5},{9,8},{10,9},{13,12},{14,13},{17,16},{18,1... | collective-permute-start | bytes 5505032 | tf_op jit(solution)/shard_map/ppermute | solution.py:295
  137.1 1.9 collective-permute-start.10
  139.1 1.2 collective-permute-done.7.refs_11_.refs_21_
  140.2 9.5 %shard_map.113.hidden_ref = bf16[256,512]{1,0:T(8,128)(2,1)S(1)} custom-call(s32[2]{0:T(128)S(1)} %pad_add_fusion.at_ref, bf16[4,64,7296]{2,1,0:T(8,128)(2,1)} %bitcast.27, bf16[4,64,7296]{2,1,0:T(8,128)(2,1)} %bitcast.28, bf16[4,64,7296]{2,1,0:T(8,128)(2,1)} %bitcast.29, bf16[4,64,7296]{2,1,0:T(8,128)(2,1)} %bitcast.30, bf16[4,64,7296]{2,1,0:T(8,128)(2,1)} %bitcast.31, ...), custom_call_target="tpu_custom_call" | custom-call | flops 131072 | bytes 256 | tf_op jit(solution)/shard_map/pallas_call | solution.py:158
  149.7 4.4 %shard_map.114 = (f32[64,7168]{1,0:T(8,128)S(1)}, bf16[64,7168]{1,0:T(8,128)(2,1)S(1)}, bf16[64,7168]{1,0:T(8,128)(2,1)S(1)}, bf16[64,7168]{1,0:T(8,128)(2,1)S(1)}) custom-call(bf16[256,512]{1,0:T(8,128)(2,1)S(1)} %shard_map.113.hidden_ref, bf16[128,7168]{1,0:T(8,128)(2,1)} %bitcast.12.refs_0_.refs_22_, bf16[128,7168]{1,0:T(8,128)(2,1)S(1)} %copy-done.7, ...), custom_call_target="tpu_custom_call" | custom-call | flops 131072 | bytes 256 | tf_op jit(solution)/shard_map/pallas_call | solution.py:185
  154.1 1.3 collective-permute-start.9
  156.1 19.9 %collective-permute-done.11.refs_9_.refs_16_ = bf16[128,7168]{1,0:T(8,128)(2,1)} collective-permute-done((bf16[128,7168]{1,0:T(8,128)(2,1)}, bf16[128,7168]{1,0:T(8,128)(2,1)}, u32[]{:S(2)}, u32[]{:S(2)}) %collective-permute-start.11) | collective-permute-done | bytes 1835040 | tf_op jit(solution)/shard_map/ppermute | solution.py:295
  176.1 5.3 %collective-permute-done.10.refs_6_.refs_13_ = bf16[128,7168]{1,0:T(8,128)(2,1)} collective-permute-done((bf16[128,7168]{1,0:T(8,128)(2,1)}, bf16[128,7168]{1,0:T(8,128)(2,1)}, u32[]{:S(2)}, u32[]{:S(2)}) %collective-permute-start.10) | collective-permute-done | bytes 1835040 | tf_op jit(solution)/shard_map/ppermute | solution.py:295
  181.8 1.9 collective-permute-start.14
  184.6 4.1 %collective-permute-start.16 = (bf16[128,7168]{1,0:T(8,128)(2,1)}, bf16[128,7168]{1,0:T(8,128)(2,1)S(1)}, u32[]{:S(2)}, u32[]{:S(2)}) collective-permute-start(bf16[128,7168]{1,0:T(8,128)(2,1)} %collective-permute-done.10.refs_6_.refs_13_), channel_id=1, source_target_pairs={{2,3},{6,7},{10,11},{14,15},{18,19},{22,23},{26,27},{30,31}} | collective-permute-start | bytes 5505032 | tf_op jit(solution)/shard_map/ppermute | solution.py:295
  188.7 1.3 collective-permute-start.12
  190.0 15.4 %collective-permute-done.14 = bf16[64,7168]{1,0:T(8,128)(2,1)S(1)} collective-permute-done((bf16[64,7168]{1,0:T(8,128)(2,1)S(1)}, bf16[64,7168]{1,0:T(8,128)(2,1)S(1)}, u32[]{:S(2)}, u32[]{:S(2)}) %collective-permute-start.14) | collective-permute-done | bytes 917536 | tf_op jit(solution)/shard_map/ppermute | solution.py:310
  205.6 2.5 collective-permute-start.15
  208.1 3.6 %collective-permute-done.12 = bf16[64,7168]{1,0:T(8,128)(2,1)S(1)} collective-permute-done((bf16[64,7168]{1,0:T(8,128)(2,1)S(1)}, bf16[64,7168]{1,0:T(8,128)(2,1)S(1)}, u32[]{:S(2)}, u32[]{:S(2)}) %collective-permute-start.12) | collective-permute-done | bytes 917536 | tf_op jit(solution)/shard_map/ppermute | solution.py:309
  211.9 2.1 collective-permute-start.13
  214.0 15.3 %collective-permute-done.16.refs_7_.refs_14_ = bf16[128,7168]{1,0:T(8,128)(2,1)S(1)} collective-permute-done((bf16[128,7168]{1,0:T(8,128)(2,1)}, bf16[128,7168]{1,0:T(8,128)(2,1)S(1)}, u32[]{:S(2)}, u32[]{:S(2)}) %collective-permute-start.16) | collective-permute-done | bytes 1835040 | tf_op jit(solution)/shard_map/ppermute | solution.py:295
  229.3 19.6 %shard_map.115 = (f32[32,7168]{1,0:T(8,128)S(1)}, f32[32,7168]{1,0:T(8,128)S(1)}, bf16[32,7168]{1,0:T(8,128)(2,1)S(1)}, bf16[32,7168]{1,0:T(8,128)(2,1)S(1)}, bf...) custom-call(s32[2]{0:T(128)S(1)} %pad_add_fusion.at_ref, ...), custom_call_target="tpu_custom_call" | custom-call | flops 131072 | bytes 256 | tf_op jit(solution)/shard_map/pallas_call | solution.py:263
  248.9 1.3 collective-permute-start.21
  250.9 1.3 collective-permute-start.29
  254.0 15.4 %collective-permute-done.29 = bf16[32,7168]{1,0:T(8,128)(2,1)S(1)} collective-permute-done((bf16[32,7168]{1,0:T(8,128)(2,1)S(1)}, bf16[32,7168]{1,0:T(8,128)(2,1)S(1)}, u32[]{:S(2)}, u32[]{:S(2)}) %collective-permute-start.29) | collective-permute-done | bytes 458784 | tf_op jit(solution)/shard_map/ppermute | solution.py:310
  269.6 1.9 collective-permute-start.30
  271.8 1.9 collective-permute-start.22
  273.7 1.3 collective-permute-start.20
  275.0 1.3 collective-permute-start.27
  276.3 8.7 %collective-permute-done.30 = bf16[32,7168]{1,0:T(8,128)(2,1)S(1)} collective-permute-done((bf16[32,7168]{1,0:T(8,128)(2,1)S(1)}, bf16[32,7168]{1,0:T(8,128)(2,1)S(1)}, u32[]{:S(2)}, u32[]{:S(2)}) %collective-permute-start.30) | collective-permute-done | bytes 458784 | tf_op jit(solution)/shard_map/ppermute | solution.py:310
  285.1 1.9 collective-permute-start.31
  287.0 7.8 %collective-permute-done.22 = bf16[32,7168]{1,0:T(8,128)(2,1)S(1)} collective-permute-done((bf16[32,7168]{1,0:T(8,128)(2,1)S(1)}, bf16[32,7168]{1,0:T(8,128)(2,1)S(1)}, u32[]{:S(2)}, u32[]{:S(2)}) %collective-permute-start.22) | collective-permute-done | bytes 458784 | tf_op jit(solution)/shard_map/ppermute | solution.py:310
  295.1 1.9 collective-permute-start.24
  297.0 3.9 %collective-permute-start.23 = (bf16[32,7168]{1,0:T(8,128)(2,1)S(1)}, bf16[32,7168]{1,0:T(8,128)(2,1)S(1)}, u32[]{:S(2)}, u32[]{:S(2)}) collective-permute-start(bf16[32,7168]{1,0:T(8,128)(2,1)S(1)} %add_convert_fusion.6), channel_id=1, source_target_pairs={{0,1},{1,2},{2,3},{4,5},{5,6},{6,7},{8,9},{9,10},{10,11},{12,13},{... | collective-permute-start | bytes 1376264 | tf_op jit(solution)/shard_map/ppermute | solution.py:309
  301.1 1.9 collective-permute-start.28
  303.0 5.9 %collective-permute-done.24 = bf16[32,7168]{1,0:T(8,128)(2,1)S(1)} collective-permute-done((bf16[32,7168]{1,0:T(8,128)(2,1)S(1)}, bf16[32,7168]{1,0:T(8,128)(2,1)S(1)}, u32[]{:S(2)}, u32[]{:S(2)}) %collective-permute-start.24) | collective-permute-done | bytes 458784 | tf_op jit(solution)/shard_map/ppermute | solution.py:310
  309.7 3.3 collective-permute-done.28
  313.0 8.1 %collective-permute-done.25 = bf16[32,7168]{1,0:T(8,128)(2,1)S(1)} collective-permute-done((bf16[32,7168]{1,0:T(8,128)(2,1)S(1)}, bf16[32,7168]{1,0:T(8,128)(2,1)S(1)}, u32[]{:S(2)}, u32[]{:S(2)}) %collective-permute-start.25) | collective-permute-done | bytes 458784 | tf_op jit(solution)/shard_map/ppermute | solution.py:30
  321.8 8.0 %collective-permute-done.32 = bf16[32,7168]{1,0:T(8,128)(2,1)S(1)} collective-permute-done((bf16[32,7168]{1,0:T(8,128)(2,1)S(1)}, bf16[32,7168]{1,0:T(8,128)(2,1)S(1)}, u32[]{:S(2)}, u32[]{:S(2)}) %collective-permute-start.32) | collective-permute-done | bytes 458784 | tf_op jit(solution)/shard_map/ppermute | solution.py:30
  329.8 1.0 maximum_bitcast_fusion
  (81 shorter events, 12.5 us)
Async XLA Ops:
  7.2 5.2 %copy-start.12 = (bf16[1,64,7168]{2,1,0:T(8,128)(2,1)S(1)}, bf16[1,64,7168]{2,1,0:T(8,128)(2,1)}, u32[]{:S(2)}) copy-start(bf16[1,64,7168]{2,1,0:T(8,128)(2,1)} %param.16) | copy-start | bytes 2752516
  7.2 5.2 %copy-start.16 = (f32[1,64]{1,0:T(1,128)S(1)}, f32[1,64]{1,0:T(1,128)}, u32[]{:S(2)}) copy-start(f32[1,64]{1,0:T(1,128)} %param.15) | copy-start | bytes 772
  7.2 126.3 %all-gather.3.cloned.1.call-start = ((), (), s32[]{:S(2)}) async-start(), calls=%async_computation | async-start | bytes 4669440 | tf_op jit(solution)/shard_map/all_gather | solution.py:346
  10.8 42.0 %collective-permute-start = (bf16[128,7168]{1,0:T(8,128)(2,1)}, bf16[128,7168]{1,0:T(8,128)(2,1)S(1)}, u32[]{:S(2)}, u32[]{:S(2)}) collective-permute-start(bf16[128,7168]{1,0:T(8,128)(2,1)} %bitcast.12.refs_0_.refs_22_), channel_id=1, source_target_pairs={{0,8},{4,12},{8,0},{12,4},{1,9},{5,13},{9,1},{13,5},{2,10},{6,14},... | collective-permute-start | bytes 5505032 | tf_op jit(solution)/shard_map/ppermute | solution.py:25
  12.6 1.8 copy-start.13
  12.6 2.3 copy-start.14
  52.9 80.6 %collective-permute-start.4 = (bf16[2,7168,128]{2,1,0:T(8,128)(2,1)}, bf16[2,7168,128]{2,1,0:T(8,128)(2,1)}, u32[]{:S(2)}, u32[]{:S(2)}) collective-permute-start(bf16[2,7168,128]{2,1,0:T(8,128)(2,1)} %pad_maximum_fusion.refs_8_.refs_18_), channel_id=1, source_target_pairs={{0,8},{4,12},{8,0},{12,4},{1,9},{5,13},{9,1},{13,5},{2,10},{6,14},... | collective-permute-start | bytes 11010056 | tf_op jit(solution)/shard_map/ppermute | solution.py:25
  54.4 68.2 %collective-permute-start.2 = (bf16[128,7168]{1,0:T(8,128)(2,1)S(1)}, bf16[128,7168]{1,0:T(8,128)(2,1)S(1)}, u32[]{:S(2)}, u32[]{:S(2)}) collective-permute-start(bf16[128,7168]{1,0:T(8,128)(2,1)S(1)} %pad_maximum_fusion.1.refs_4_.refs_11_), channel_id=1, source_target_pairs={{1,0},{2,1},{3,2},{5,4},{6,5},{7,6},{9,8},{10,9},{11,10},{13,12},{... | collective-permute-start | bytes 5505032 | tf_op jit(solution)/shard_map/ppermute | solution.py:295
  56.7 65.8 %collective-permute-start.1 = (bf16[128,7168]{1,0:T(8,128)(2,1)S(1)}, bf16[128,7168]{1,0:T(8,128)(2,1)S(1)}, u32[]{:S(2)}, u32[]{:S(2)}) collective-permute-start(bf16[128,7168]{1,0:T(8,128)(2,1)S(1)} %pad_maximum_fusion.1.refs_4_.refs_11_), channel_id=1, source_target_pairs={{0,1},{1,2},{2,3},{4,5},{5,6},{6,7},{8,9},{9,10},{10,11},{12,13},{... | collective-permute-start | bytes 5505032 | tf_op jit(solution)/shard_map/ppermute | solution.py:295
  60.3 62.3 %collective-permute-start.5 = (bf16[128,7168]{1,0:T(8,128)(2,1)}, bf16[128,7168]{1,0:T(8,128)(2,1)S(1)}, u32[]{:S(2)}, u32[]{:S(2)}) collective-permute-start(bf16[128,7168]{1,0:T(8,128)(2,1)} %bitcast.12.refs_0_.refs_22_), channel_id=1, source_target_pairs={{0,4},{4,0},{8,12},{12,8},{1,5},{5,1},{9,13},{13,9},{2,6},{6,2},{1... | collective-permute-start | bytes 5505032 | tf_op jit(solution)/shard_map/ppermute | solution.py:25
  60.4 63.6 %collective-permute-start.6 = (bf16[128,7168]{1,0:T(8,128)(2,1)S(1)}, bf16[128,7168]{1,0:T(8,128)(2,1)S(1)}, u32[]{:S(2)}, u32[]{:S(2)}) collective-permute-start(bf16[128,7168]{1,0:T(8,128)(2,1)S(1)} %collective-permute-done.refs_2_.refs_24_), channel_id=1, source_target_pairs={{0,4},{4,0},{8,12},{12,8},{1,5},{5,1},{9,13},{13,9},{2,6},{6,2},{1... | collective-permute-start | bytes 5505032 | tf_op jit(solution)/shard_map/ppermute | solution.py:25
  122.5 1.8 copy-start.2
  122.6 2.4 copy-start.4
  122.6 16.5 %collective-permute-start.3 = (bf16[2,7168,128]{2,1,0:T(8,128)(2,1)}, bf16[2,7168,128]{2,1,0:T(8,128)(2,1)}, u32[]{:S(2)}, u32[]{:S(2)}) collective-permute-start(bf16[2,7168,128]{2,1,0:T(8,128)(2,1)} %pad_maximum_fusion.refs_8_.refs_18_), channel_id=1, source_target_pairs={{0,4},{4,0},{8,12},{12,8},{1,5},{5,1},{9,13},{13,9},{2,6},{6,2},{1... | collective-permute-start | bytes 11010056 | tf_op jit(solution)/shard_map/ppermute | solution.py:25
  133.5 6.8 %collective-permute-start.7 = (bf16[2,7168,128]{2,1,0:T(8,128)(2,1)}, bf16[2,7168,128]{2,1,0:T(8,128)(2,1)}, u32[]{:S(2)}, u32[]{:S(2)}) collective-permute-start(bf16[2,7168,128]{2,1,0:T(8,128)(2,1)} %collective-permute-done.4.refs_10_.refs_20_), channel_id=1, source_target_pairs={{0,4},{4,0},{8,12},{12,8},{1,5},{5,1},{9,13},{13,9},{2,6},{6,2},{1... | collective-permute-start | bytes 11010056 | tf_op jit(solution)/shard_map/ppermute | solution.py:25
  133.5 42.6 %collective-permute-start.11 = (bf16[128,7168]{1,0:T(8,128)(2,1)}, bf16[128,7168]{1,0:T(8,128)(2,1)}, u32[]{:S(2)}, u32[]{:S(2)}) collective-permute-start(bf16[128,7168]{1,0:T(8,128)(2,1)} %copy-done.2), channel_id=1, source_target_pairs={{1,0},{2,1},{5,4},{6,5},{9,8},{10,9},{13,12},{14,13},{17,16},{18,1... | collective-permute-start | bytes 5505032 | tf_op jit(solution)/shard_map/ppermute | solution.py:295
  137.1 44.3 %collective-permute-start.10 = (bf16[128,7168]{1,0:T(8,128)(2,1)}, bf16[128,7168]{1,0:T(8,128)(2,1)}, u32[]{:S(2)}, u32[]{:S(2)}) collective-permute-start(bf16[128,7168]{1,0:T(8,128)(2,1)} %copy-done.4), channel_id=1, source_target_pairs={{1,2},{2,3},{5,6},{6,7},{9,10},{10,11},{13,14},{14,15},{17,18},{18... | collective-permute-start | bytes 5505032 | tf_op jit(solution)/shard_map/ppermute | solution.py:295
  139.1 10.6 %copy-start.1 = (bf16[128,7168]{1,0:T(8,128)(2,1)S(1)}, bf16[128,7168]{1,0:T(8,128)(2,1)}, u32[]{:S(2)}) copy-start(bf16[128,7168]{1,0:T(8,128)(2,1)} %copy-done) | copy-start | bytes 5505028
  139.1 10.7 %copy-start.7 = (bf16[128,7168]{1,0:T(8,128)(2,1)S(1)}, bf16[128,7168]{1,0:T(8,128)(2,1)}, u32[]{:S(2)}) copy-start(bf16[128,7168]{1,0:T(8,128)(2,1)} %copy-done.6) | copy-start | bytes 5505028
  139.1 10.7 %copy-start.9 = (bf16[128,7168]{1,0:T(8,128)(2,1)S(1)}, bf16[128,7168]{1,0:T(8,128)(2,1)}, u32[]{:S(2)}) copy-start(bf16[128,7168]{1,0:T(8,128)(2,1)} %copy-done.8) | copy-start | bytes 5505028
  154.1 27.3 %collective-permute-start.9 = (bf16[64,7168]{1,0:T(8,128)(2,1)S(1)}, bf16[64,7168]{1,0:T(8,128)(2,1)S(1)}, u32[]{:S(2)}, u32[]{:S(2)}) collective-permute-start(bf16[64,7168]{1,0:T(8,128)(2,1)S(1)} %get-tuple-element.42), channel_id=1, source_target_pairs={{3,2},{7,6},{11,10},{15,14},{19,18},{23,22},{27,26},{31,30}} | collective-permute-start | bytes 2752520 | tf_op jit(solution)/shard_map/ppermute | solution.py:310
  155.4 26.0 %collective-permute-start.8 = (bf16[64,7168]{1,0:T(8,128)(2,1)S(1)}, bf16[64,7168]{1,0:T(8,128)(2,1)S(1)}, u32[]{:S(2)}, u32[]{:S(2)}) collective-permute-start(bf16[64,7168]{1,0:T(8,128)(2,1)S(1)} %get-tuple-element.44), channel_id=1, source_target_pairs={{0,1},{4,5},{8,9},{12,13},{16,17},{20,21},{24,25},{28,29}} | collective-permute-start | bytes 2752520 | tf_op jit(solution)/shard_map/ppermute | solution.py:309
  181.8 23.6 %collective-permute-start.14 = (bf16[64,7168]{1,0:T(8,128)(2,1)S(1)}, bf16[64,7168]{1,0:T(8,128)(2,1)S(1)}, u32[]{:S(2)}, u32[]{:S(2)}) collective-permute-start(bf16[64,7168]{1,0:T(8,128)(2,1)S(1)} %get-tuple-element.72), channel_id=1, source_target_pairs={{2,1},{3,2},{6,5},{7,6},{10,9},{11,10},{14,13},{15,14},{18,17},{19... | collective-permute-start | bytes 2752520 | tf_op jit(solution)/shard_map/ppermute | solution.py:310
  183.8 30.2 %collective-permute-start.17 = (bf16[128,7168]{1,0:T(8,128)(2,1)}, bf16[128,7168]{1,0:T(8,128)(2,1)S(1)}, u32[]{:S(2)}, u32[]{:S(2)}) collective-permute-start(bf16[128,7168]{1,0:T(8,128)(2,1)} %collective-permute-done.11.refs_9_.refs_16_), channel_id=1, source_target_pairs={{1,0},{5,4},{9,8},{13,12},{17,16},{21,20},{25,24},{29,28}} | collective-permute-start | bytes 5505032 | tf_op jit(solution)/shard_map/ppermute | solution.py:295
  184.6 44.7 %collective-permute-start.16 = (bf16[128,7168]{1,0:T(8,128)(2,1)}, bf16[128,7168]{1,0:T(8,128)(2,1)S(1)}, u32[]{:S(2)}, u32[]{:S(2)}) collective-permute-start(bf16[128,7168]{1,0:T(8,128)(2,1)} %collective-permute-done.10.refs_6_.refs_13_), channel_id=1, source_target_pairs={{2,3},{6,7},{10,11},{14,15},{18,19},{22,23},{26,27},{30,31}} | collective-permute-start | bytes 5505032 | tf_op jit(solution)/shard_map/ppermute | solution.py:295
  188.7 23.0 %collective-permute-start.12 = (bf16[64,7168]{1,0:T(8,128)(2,1)S(1)}, bf16[64,7168]{1,0:T(8,128)(2,1)S(1)}, u32[]{:S(2)}, u32[]{:S(2)}) collective-permute-start(bf16[64,7168]{1,0:T(8,128)(2,1)S(1)} %get-tuple-element.73), channel_id=1, source_target_pairs={{0,1},{1,2},{4,5},{5,6},{8,9},{9,10},{12,13},{13,14},{16,17},{17,1... | collective-permute-start | bytes 2752520 | tf_op jit(solution)/shard_map/ppermute | solution.py:309
  205.4 23.9 %copy-start.5 = (bf16[128,7168]{1,0:T(8,128)(2,1)S(1)}, bf16[128,7168]{1,0:T(8,128)(2,1)}, u32[]{:S(2)}) copy-start(bf16[128,7168]{1,0:T(8,128)(2,1)} %copy-done.4) | copy-start | bytes 5505028
  205.6 23.7 %copy-start.3 = (bf16[128,7168]{1,0:T(8,128)(2,1)S(1)}, bf16[128,7168]{1,0:T(8,128)(2,1)}, u32[]{:S(2)}) copy-start(bf16[128,7168]{1,0:T(8,128)(2,1)} %copy-done.2) | copy-start | bytes 5505028
  205.6 43.3 %collective-permute-start.15 = (bf16[64,7168]{1,0:T(8,128)(2,1)S(1)}, bf16[64,7168]{1,0:T(8,128)(2,1)S(1)}, u32[]{:S(2)}, u32[]{:S(2)}) collective-permute-start(bf16[64,7168]{1,0:T(8,128)(2,1)S(1)} %add_convert_fusion.1), channel_id=1, source_target_pairs={{1,0},{2,1},{3,2},{5,4},{6,5},{7,6},{9,8},{10,9},{11,10},{13,12},{... | collective-permute-start | bytes 2752520 | tf_op jit(solution)/shard_map/ppermute | solution.py:310
  211.9 41.0 %copy-start.11 = (bf16[1,64,7168]{2,1,0:T(8,128)(2,1)S(1)}, bf16[1,64,7168]{2,1,0:T(8,128)(2,1)}, u32[]{:S(2)}) copy-start(bf16[1,64,7168]{2,1,0:T(8,128)(2,1)} %param.10) | copy-start | bytes 2752516
  211.9 41.0 %copy-start.15 = (f32[1,64]{1,0:T(1,128)S(1)}, f32[1,64]{1,0:T(1,128)}, u32[]{:S(2)}) copy-start(f32[1,64]{1,0:T(1,128)} %param.12) | copy-start | bytes 772
  211.9 37.0 %collective-permute-start.13 = (bf16[64,7168]{1,0:T(8,128)(2,1)S(1)}, bf16[64,7168]{1,0:T(8,128)(2,1)S(1)}, u32[]{:S(2)}, u32[]{:S(2)}) collective-permute-start(bf16[64,7168]{1,0:T(8,128)(2,1)S(1)} %add_convert_fusion.2), channel_id=1, source_target_pairs={{0,1},{1,2},{2,3},{4,5},{5,6},{6,7},{8,9},{9,10},{10,11},{12,13},{... | collective-permute-start | bytes 2752520 | tf_op jit(solution)/shard_map/ppermute | solution.py:309
  214.0 15.3 %copy-start.10 = (bf16[128,7168]{1,0:T(8,128)(2,1)}, bf16[128,7168]{1,0:T(8,128)(2,1)S(1)}, u32[]{:S(2)}) copy-start(bf16[128,7168]{1,0:T(8,128)(2,1)S(1)} %collective-permute-done.17.refs_10_.refs_17_) | copy-start | bytes 5505028
  248.9 22.6 %collective-permute-start.21 = (bf16[32,7168]{1,0:T(8,128)(2,1)S(1)}, bf16[32,7168]{1,0:T(8,128)(2,1)S(1)}, u32[]{:S(2)}, u32[]{:S(2)}) collective-permute-start(bf16[32,7168]{1,0:T(8,128)(2,1)S(1)} %get-tuple-element.59), channel_id=1, source_target_pairs={{3,2},{7,6},{11,10},{15,14},{19,18},{23,22},{27,26},{31,30}} | collective-permute-start | bytes 1376264 | tf_op jit(solution)/shard_map/ppermute | solution.py:310
  250.2 21.4 %collective-permute-start.19 = (bf16[32,7168]{1,0:T(8,128)(2,1)S(1)}, bf16[32,7168]{1,0:T(8,128)(2,1)S(1)}, u32[]{:S(2)}, u32[]{:S(2)}) collective-permute-start(bf16[32,7168]{1,0:T(8,128)(2,1)S(1)} %get-tuple-element.61), channel_id=1, source_target_pairs={{0,1},{4,5},{8,9},{12,13},{16,17},{20,21},{24,25},{28,29}} | collective-permute-start | bytes 1376264 | tf_op jit(solution)/shard_map/ppermute | solution.py:309
  250.9 18.5 %collective-permute-start.29 = (bf16[32,7168]{1,0:T(8,128)(2,1)S(1)}, bf16[32,7168]{1,0:T(8,128)(2,1)S(1)}, u32[]{:S(2)}, u32[]{:S(2)}) collective-permute-start(bf16[32,7168]{1,0:T(8,128)(2,1)S(1)} %get-tuple-element.67), channel_id=1, source_target_pairs={{3,2},{7,6},{11,10},{15,14},{19,18},{23,22},{27,26},{31,30}} | collective-permute-start | bytes 1376264 | tf_op jit(solution)/shard_map/ppermute | solution.py:310
  252.2 17.2 %collective-permute-start.26 = (bf16[32,7168]{1,0:T(8,128)(2,1)S(1)}, bf16[32,7168]{1,0:T(8,128)(2,1)S(1)}, u32[]{:S(2)}, u32[]{:S(2)}) collective-permute-start(bf16[32,7168]{1,0:T(8,128)(2,1)S(1)} %get-tuple-element.69), channel_id=1, source_target_pairs={{0,1},{4,5},{8,9},{12,13},{16,17},{20,21},{24,25},{28,29}} | collective-permute-start | bytes 1376264 | tf_op jit(solution)/shard_map/ppermute | solution.py:309
  253.5 41.4 %collective-permute-start.18 = (bf16[64,7168]{1,0:T(8,128)(2,1)S(1)}, bf16[64,7168]{1,0:T(8,128)(2,1)S(1)}, u32[]{:S(2)}, u32[]{:S(2)}) collective-permute-start(bf16[64,7168]{1,0:T(8,128)(2,1)S(1)} %add_convert_fusion), channel_id=1, source_target_pairs={{16,0},{0,16},{17,1},{1,17},{18,2},{2,18},{19,3},{3,19},{20,4},{4,... | collective-permute-start | bytes 2752520 | tf_op jit(solution)/shard_map/ppermute | solution.py:30
  269.6 15.3 %collective-permute-start.30 = (bf16[32,7168]{1,0:T(8,128)(2,1)S(1)}, bf16[32,7168]{1,0:T(8,128)(2,1)S(1)}, u32[]{:S(2)}, u32[]{:S(2)}) collective-permute-start(bf16[32,7168]{1,0:T(8,128)(2,1)S(1)} %get-tuple-element.76), channel_id=1, source_target_pairs={{2,1},{3,2},{6,5},{7,6},{10,9},{11,10},{14,13},{15,14},{18,17},{19... | collective-permute-start | bytes 1376264 | tf_op jit(solution)/shard_map/ppermute | solution.py:310
  271.8 23.0 %collective-permute-start.22 = (bf16[32,7168]{1,0:T(8,128)(2,1)S(1)}, bf16[32,7168]{1,0:T(8,128)(2,1)S(1)}, u32[]{:S(2)}, u32[]{:S(2)}) collective-permute-start(bf16[32,7168]{1,0:T(8,128)(2,1)S(1)} %get-tuple-element.74), channel_id=1, source_target_pairs={{2,1},{3,2},{6,5},{7,6},{10,9},{11,10},{14,13},{15,14},{18,17},{19... | collective-permute-start | bytes 1376264 | tf_op jit(solution)/shard_map/ppermute | solution.py:310
  273.7 21.1 %collective-permute-start.20 = (bf16[32,7168]{1,0:T(8,128)(2,1)S(1)}, bf16[32,7168]{1,0:T(8,128)(2,1)S(1)}, u32[]{:S(2)}, u32[]{:S(2)}) collective-permute-start(bf16[32,7168]{1,0:T(8,128)(2,1)S(1)} %get-tuple-element.75), channel_id=1, source_target_pairs={{0,1},{1,2},{4,5},{5,6},{8,9},{9,10},{12,13},{13,14},{16,17},{17,1... | collective-permute-start | bytes 1376264 | tf_op jit(solution)/shard_map/ppermute | solution.py:309
  275.0 25.9 %collective-permute-start.27 = (bf16[32,7168]{1,0:T(8,128)(2,1)S(1)}, bf16[32,7168]{1,0:T(8,128)(2,1)S(1)}, u32[]{:S(2)}, u32[]{:S(2)}) collective-permute-start(bf16[32,7168]{1,0:T(8,128)(2,1)S(1)} %get-tuple-element.77), channel_id=1, source_target_pairs={{0,1},{1,2},{4,5},{5,6},{8,9},{9,10},{12,13},{13,14},{16,17},{17,1... | collective-permute-start | bytes 1376264 | tf_op jit(solution)/shard_map/ppermute | solution.py:309
  285.1 24.6 %collective-permute-start.31 = (bf16[32,7168]{1,0:T(8,128)(2,1)S(1)}, bf16[32,7168]{1,0:T(8,128)(2,1)S(1)}, u32[]{:S(2)}, u32[]{:S(2)}) collective-permute-start(bf16[32,7168]{1,0:T(8,128)(2,1)S(1)} %add_convert_fusion.3), channel_id=1, source_target_pairs={{1,0},{2,1},{3,2},{5,4},{6,5},{7,6},{9,8},{10,9},{11,10},{13,12},{... | collective-permute-start | bytes 1376264 | tf_op jit(solution)/shard_map/ppermute | solution.py:310
  295.1 13.8 %collective-permute-start.24 = (bf16[32,7168]{1,0:T(8,128)(2,1)S(1)}, bf16[32,7168]{1,0:T(8,128)(2,1)S(1)}, u32[]{:S(2)}, u32[]{:S(2)}) collective-permute-start(bf16[32,7168]{1,0:T(8,128)(2,1)S(1)} %add_convert_fusion.5), channel_id=1, source_target_pairs={{1,0},{2,1},{3,2},{5,4},{6,5},{7,6},{9,8},{10,9},{11,10},{13,12},{... | collective-permute-start | bytes 1376264 | tf_op jit(solution)/shard_map/ppermute | solution.py:310
  297.0 11.9 %collective-permute-start.23 = (bf16[32,7168]{1,0:T(8,128)(2,1)S(1)}, bf16[32,7168]{1,0:T(8,128)(2,1)S(1)}, u32[]{:S(2)}, u32[]{:S(2)}) collective-permute-start(bf16[32,7168]{1,0:T(8,128)(2,1)S(1)} %add_convert_fusion.6), channel_id=1, source_target_pairs={{0,1},{1,2},{2,3},{4,5},{5,6},{6,7},{8,9},{9,10},{10,11},{12,13},{... | collective-permute-start | bytes 1376264 | tf_op jit(solution)/shard_map/ppermute | solution.py:309
  301.1 11.9 %collective-permute-start.28 = (bf16[32,7168]{1,0:T(8,128)(2,1)S(1)}, bf16[32,7168]{1,0:T(8,128)(2,1)S(1)}, u32[]{:S(2)}, u32[]{:S(2)}) collective-permute-start(bf16[32,7168]{1,0:T(8,128)(2,1)S(1)} %add_convert_fusion.4), channel_id=1, source_target_pairs={{0,1},{1,2},{2,3},{4,5},{5,6},{6,7},{8,9},{9,10},{10,11},{12,13},{... | collective-permute-start | bytes 1376264 | tf_op jit(solution)/shard_map/ppermute | solution.py:309
  309.1 11.9 %collective-permute-start.25 = (bf16[32,7168]{1,0:T(8,128)(2,1)S(1)}, bf16[32,7168]{1,0:T(8,128)(2,1)S(1)}, u32[]{:S(2)}, u32[]{:S(2)}) collective-permute-start(bf16[32,7168]{1,0:T(8,128)(2,1)S(1)} %fusion.8), channel_id=1, source_target_pairs={{16,0},{0,16},{17,1},{1,17},{18,2},{2,18},{19,3},{3,19},{20,4},{4,... | collective-permute-start | bytes 1376264 | tf_op jit(solution)/shard_map/ppermute | solution.py:30
  321.3 8.5 %collective-permute-start.32 = (bf16[32,7168]{1,0:T(8,128)(2,1)S(1)}, bf16[32,7168]{1,0:T(8,128)(2,1)S(1)}, u32[]{:S(2)}, u32[]{:S(2)}) collective-permute-start(bf16[32,7168]{1,0:T(8,128)(2,1)S(1)} %fusion.7), channel_id=1, source_target_pairs={{16,0},{0,16},{17,1},{1,17},{18,2},{2,18},{19,3},{3,19},{20,4},{4,... | collective-permute-start | bytes 1376264 | tf_op jit(solution)/shard_map/ppermute | solution.py:30
  (3 other events, 3.8 us)
Sparse Core Ops, SparseCore 0:
  11.0 97.7 all-gather.2
